TPU v7x, 32 devices: a whole 2x2x4 slice. The times are simulated.
32 devices in a mesh: gx: 4 (over y, core), gy: 8 (over z, x).
Axes of the slice: x: 2, y: 2, z: 4, core: 2. Of those that a mesh axis runs over, the one named last changes fastest.
Arguments:
- positions: float32 [3, 524288], P(None, ('gx', 'gy')), may hold values from 0 to 128, as said below
- point_feat: float32 [32, 524288], P(None, ('gx', 'gy')), may hold values from -1.8 to 1.8
- area: float32 [524288], P(('gx', 'gy')), may hold values from 0.3 to 3
- block_brick: int32 [4096], P(('gx', 'gy')), may hold values from 0 to 4095, as said below
- block_count: int32 [32], P(('gx', 'gy')), may hold values from 16 to 128, as said below
- sdf: float32 [128, 128, 128], P('gx', 'gy'), may hold values from -6 to 6
- grid_gain: float32 [32], replicated, may hold values from -4 to 4
- mix_w: float32 [2, 32, 32], replicated, may hold values from -1 to 1
- mix_b: float32 [2, 32], replicated, may hold values from -1.8 to 1.8
- spec_w: float32 [2, 2, 16, 32, 1024], P(None, None, 'gy', 'gx'), may hold values from -18 to 18
- readout_w: float32 [32], replicated, may hold values from -1 to 1
Outputs:
- pressure: float32 [524288], P(('gx', 'gy'))
Inputs may be any that keep to these rules, and one draw needn't show every extreme that they name: `block_brick`: block n belongs to partition d = n // 128. Its brick b lies in the grid pencil row of that partition: (b // 256) // 4 == d // 8. Of the blocks of one partition at most 16 lie in the bricks of one pencil, the pencil of b being ((b // 16) % 16) // 2; in every pencil row some pencil holds exactly 16 of the first 16 blocks of every partition of that row. The live blocks of partition d are its first block_count[d] blocks; some partition has all 128 live and some has exactly 16. `positions`: every point lies inside its block's brick, 0.5 or more from each of the brick's faces.
All inputs are finite; a program needn't handle non-finite values.
Results may differ from a plain program's by a relative error of at most 0.0003.
Values sent between devices are 32-bit elements; how exact they have to be, the bound alone decides.
No kernel may reach another device: no remote copies, remote signals or barrier semaphores. Data moves between devices by JAX's collectives and lax.ppermute only.
A program may use at most 192 MiB of HBM per device.

v0:
```python
import jax
import jax.numpy as jnp
from jax import lax
from jax.sharding import PartitionSpec as P

G = 128
M = 32
B = 8
KZ = 16


highest = lax.Precision.HIGHEST


def phase_table(length, frequency):
    places = jnp.arange(length, dtype=jnp.int32)
    wrapped = jnp.mod(places[:, None] * frequency[None, :], length).astype(jnp.float32)
    phases = wrapped * (2.0 * jnp.pi / length)
    return (jnp.cos(phases), jnp.sin(phases))


def kept_freqs(mode_count):
    mode_index = jnp.arange(mode_count, dtype=jnp.int32)
    return jnp.where(mode_index < mode_count // 2, mode_index, mode_index - mode_count)


def cell_offsets(brick_edge):
    cell_index = jnp.arange(brick_edge * brick_edge * brick_edge, dtype=jnp.int32)
    coords = jnp.stack(
        [
            cell_index // (brick_edge * brick_edge),
            cell_index // brick_edge % brick_edge,
            cell_index % brick_edge,
        ]
    )
    return coords.astype(jnp.float32) + 0.5


def kernel_weights(corners, points, offsets, radius):
    distance = jnp.zeros((corners.shape[0], offsets.shape[1], points.shape[2]), dtype=jnp.float32)
    for axis_id in range(3):
        centre_line = corners[:, axis_id][:, None] + offsets[axis_id][None, :]
        gap_line = centre_line[:, :, None] - points[:, axis_id][:, None, :]
        distance = distance + gap_line * gap_line
    return jnp.square(jnp.maximum(1.0 - distance / (radius * radius), 0.0))


def rotate(spectra, table_cos, table_sin, pattern, direction):
    part_real = spectra[0]
    part_imag = spectra[1]
    real_cos = jnp.einsum(pattern, part_real, table_cos, precision=highest)
    real_sin = jnp.einsum(pattern, part_real, table_sin, precision=highest)
    imag_cos = jnp.einsum(pattern, part_imag, table_cos, precision=highest)
    imag_sin = jnp.einsum(pattern, part_imag, table_sin, precision=highest)
    return jnp.stack([real_cos - direction * imag_sin, imag_cos + direction * real_sin])


def spectral_part(grid_field, weights, tables):
    z_cos, z_sin, f_cos, f_sin, inv_cos, inv_sin, back_cos, back_sin = tables
    part_real = jnp.einsum("cxyz,zk->kcxy", grid_field, z_cos, precision=highest)
    part_imag = -jnp.einsum("cxyz,zk->kcxy", grid_field, z_sin, precision=highest)
    spectra = jnp.stack([part_real, part_imag])
    spectra = lax.all_to_all(spectra, "gy", split_axis=1, concat_axis=4, tiled=True)
    spectra = rotate(spectra, f_cos, f_sin, "...y,ym->...m", -1.0)
    spectra = lax.all_to_all(spectra, "gx", split_axis=2, concat_axis=3, tiled=True)
    spectra = rotate(spectra, f_cos, f_sin, "...xm,xn->...nm", -1.0)
    wave_shape = spectra.shape
    flattened = spectra.reshape(2, wave_shape[1], wave_shape[2], wave_shape[3] * wave_shape[4])
    prod_real = flattened[0] * weights[0] - flattened[1] * weights[1]
    prod_imag = flattened[0] * weights[1] + flattened[1] * weights[0]
    spectra = jnp.stack([prod_real, prod_imag]).reshape(wave_shape)
    spectra = rotate(spectra, inv_cos, inv_sin, "...nm,xn->...xm", 1.0)
    spectra = lax.all_to_all(spectra, "gx", split_axis=3, concat_axis=2, tiled=True)
    spectra = rotate(spectra, inv_cos, inv_sin, "...m,ym->...y", 1.0)
    spectra = lax.all_to_all(spectra, "gy", split_axis=4, concat_axis=1, tiled=True)
    result_real = jnp.einsum("kcxy,zk->cxyz", spectra[0], back_cos, precision=highest)
    result_imag = jnp.einsum("kcxy,zk->cxyz", spectra[1], back_sin, precision=highest)
    return result_real - result_imag


def per_device(
    positions,
    point_feat,
    area,
    block_brick,
    block_count,
    sdf,
    grid_gain,
    mix_w,
    mix_b,
    spec_w,
    readout_w,
):
    row_x = lax.axis_index("gx")
    row_y = lax.axis_index("gy")
    owners = lax.axis_size("gy")
    brick_edge = B
    side_bricks = G // brick_edge
    bricks_x = side_bricks // lax.axis_size("gx")
    bricks_y = side_bricks // owners
    block_total = block_brick.shape[0]
    capacity = block_total // owners
    block_points = positions.shape[1] // block_total
    channels = point_feat.shape[0]
    cell_count = brick_edge * brick_edge * brick_edge
    group_size = 4
    live_mask = jnp.arange(block_total, dtype=jnp.int32) < block_count[0]
    target = block_brick // side_bricks % side_bricks // bricks_y
    choose = (
        (target[:, None] == jnp.arange(owners, dtype=jnp.int32)[None, :]) & live_mask[:, None]
    ).astype(jnp.int32)
    before = jnp.cumsum(choose, axis=0) - choose
    order_in = jnp.sum(before * choose, axis=1)
    slot_of = target * capacity + order_in
    send_index = jnp.where(live_mask, slot_of, block_total)
    block_pos = positions.reshape(3, block_total, block_points).transpose(1, 0, 2)
    block_feat = point_feat.reshape(channels, block_total, block_points).transpose(1, 0, 2)
    block_area = area.reshape(block_total, 1, block_points)
    stacked = jnp.concatenate([block_pos, block_feat, block_area], axis=1)
    outgoing = jnp.zeros_like(stacked).at[send_index].set(stacked, mode="drop")
    incoming = lax.all_to_all(outgoing, "gy", split_axis=0, concat_axis=0, tiled=True)
    in_pos = incoming[:, 0:3, :]
    in_feat = incoming[:, 3 : 3 + channels, :] * incoming[:, 3 + channels : 4 + channels, :]
    home_brick = jnp.floor(in_pos[:, :, 0] / brick_edge).astype(jnp.int32)
    brick_xi = jnp.clip(home_brick[:, 0] - row_x * bricks_x, 0, bricks_x - 1)
    brick_yi = jnp.clip(home_brick[:, 1] - row_y * bricks_y, 0, bricks_y - 1)
    brick_zi = jnp.clip(home_brick[:, 2], 0, side_bricks - 1)
    local_id = (brick_xi * bricks_y + brick_yi) * side_bricks + brick_zi
    corners = (
        jnp.stack(
            [row_x * bricks_x + brick_xi, row_y * bricks_y + brick_yi, brick_zi], axis=1
        ).astype(jnp.float32)
        * brick_edge
    )
    local_count = bricks_x * bricks_y * side_bricks
    picker = (local_id[:, None] == jnp.arange(local_count, dtype=jnp.int32)[None, :]).astype(
        jnp.float32
    )
    offsets = cell_offsets(brick_edge)
    group_count = block_total // group_size
    corner_groups = corners.reshape(group_count, group_size, 3)
    point_groups = in_pos.reshape(group_count, group_size, 3, block_points)

    def encode_group(group_items):
        corner_set, point_set, feature_set = group_items
        weights = kernel_weights(corner_set, point_set, offsets, brick_edge)
        return jnp.einsum("rcp,rgp->rcg", feature_set, weights, precision=highest)

    contrib = lax.map(
        encode_group,
        (
            corner_groups,
            point_groups,
            in_feat.reshape(group_count, group_size, channels, block_points),
        ),
    )
    contrib = contrib.reshape(block_total, channels * cell_count)
    local_bricks = jnp.einsum("rb,rf->bf", picker, contrib, precision=highest)
    grid_field = local_bricks.reshape(
        bricks_x, bricks_y, side_bricks, channels, brick_edge, brick_edge, brick_edge
    )
    grid_field = grid_field.transpose(3, 0, 4, 1, 5, 2, 6).reshape(
        channels, bricks_x * brick_edge, bricks_y * brick_edge, G
    )
    grid_field = grid_field + grid_gain[:, None, None, None] * sdf[None]
    z_cos, z_sin = phase_table(G, jnp.arange(KZ, dtype=jnp.int32))
    f_cos, f_sin = phase_table(G, kept_freqs(M))
    z_back = jnp.where(jnp.arange(KZ) == 0, 1.0, 2.0).astype(jnp.float32) / G
    tables = (
        z_cos,
        z_sin,
        f_cos,
        f_sin,
        f_cos / G,
        f_sin / G,
        z_cos * z_back[None, :],
        z_sin * z_back[None, :],
    )
    layers = mix_w.shape[0]
    for layer_index in range(layers):
        spectral = spectral_part(grid_field, spec_w[layer_index], tables)
        mixed_sum = jnp.einsum("oc,cxyz->oxyz", mix_w[layer_index], grid_field, precision=highest)
        mixed_sum = mixed_sum + mix_b[layer_index][:, None, None, None] + spectral
        grid_field = jax.nn.gelu(mixed_sum) if layer_index < layers - 1 else mixed_sum
    final_bricks = grid_field.reshape(
        channels, bricks_x, brick_edge, bricks_y, brick_edge, side_bricks, brick_edge
    )
    final_bricks = final_bricks.transpose(1, 3, 5, 0, 2, 4, 6).reshape(
        local_count, channels * cell_count
    )
    slot_values = final_bricks[local_id]
    slot_values = slot_values.reshape(group_count, group_size, channels, cell_count)

    def decode_group(group_items):
        corner_set, point_set, value_set = group_items
        weights = kernel_weights(corner_set, point_set, offsets, brick_edge)
        weight_sum = jnp.sum(weights, axis=1)
        safe_sum = jnp.where(weight_sum > 0.0, weight_sum, 1.0)
        return (
            jnp.einsum("rcg,rgp->rcp", value_set, weights, precision=highest) / safe_sum[:, None, :]
        )

    decoded = lax.map(decode_group, (corner_groups, point_groups, slot_values)).reshape(
        block_total, channels, block_points
    )
    reduced = jnp.einsum("c,rcp->rp", readout_w, decoded, precision=highest)
    returned = lax.all_to_all(reduced, "gy", split_axis=0, concat_axis=0, tiled=True)
    per_block = returned[slot_of]
    pressure = jnp.where(live_mask[:, None], per_block, 0.0)
    return pressure.reshape(block_total * block_points)


def solution(mesh):
    placed = (
        P(None, ("gx", "gy")),
        P(None, ("gx", "gy")),
        P(("gx", "gy")),
        P(("gx", "gy")),
        P(("gx", "gy")),
        P("gx", "gy", None),
        P(),
        P(),
        P(),
        P(None, None, "gy", "gx", None),
        P(),
    )
    return jax.shard_map(
        per_device, mesh=mesh, in_specs=placed, out_specs=P(("gx", "gy")), check_vma=False
    )
```

profile of v0, /device:TPU:0, one launch (start us, length us, event | category | flops | bytes accessed | tf_op | source)
XLA Modules:
  0.0 1598.1 jit_solution(17911595065564864631)
XLA Ops:
  6.4 17.9 %scatter_fusion = f32[128,36,128]{2,1,0:T(8,128)} fusion(f32[128,36,128]{2,1,0:T(8,128)} %broadcast_in_dim.77, s32[128]{0:T(128)S(1)} %get-tuple-element.234, f32[128,36,128]{2,1,0:T(8,128)} %pad_maximum_fusion.2), kind=kCustom, calls=%fused_computation.2 | custom fusion | bytes 7078400 | tf_op jit(solution)/shard_map/scatter | solution.py:120
  24.4 7.8 all-to-all-start
  38.7 53.3 %all-to-all-done = f32[128,36,128]{2,1,0:T(8,128)} async-done(((f32[128,36,128]{2,1,0:T(8,128)}), f32[128,36,128]{2,1,0:T(8,128)}, u32[]{:S(2)}, u32[]{:S(2)}) %all-to-all-start) | async-done | bytes 2359328 | tf_op jit(solution)/shard_map/all_to_all | solution.py:121
  100.2 124.9 %while.20 = (s32[]{:T(128)}, f32[32,4,32,512]{3,2,1,0:T(8,128)}, f32[32,4,32,128]{3,2,1,0:T(8,128)}, f32[32,4,3]{2,1,0:T(4,128)S(1)}, f32[3,512]{1,0:T(4,128)S(1)}, /*index=5*/f32[32,4,3,128]{3,1,2,0:T(4,128)S(1)}, s32[]{:T(128)}) while((s32[]{:T(128)}, f32[32,4,32,512]{3,2,1,0:T(8,128)}, f32[32,4,32,128]{3,2,1,0:T(8,128)}, ...), condition=%wide.region_4.5_spmd, body=%wide.region_3.4_spmd.sunk | while | flops 103815168 | bytes 427333 | solution.py:149
  225.1 13.5 copy.503
  238.7 9.0 copy.394
  247.6 29.2 %multiply_add_fusion = (f32[32,4,8,2,8,16,8]{0,5,6,4,2,3,1:T(8,128)}, f32[32,4,8,2,8,16,8]{0,5,6,4,2,3,1:T(8,128)}) fusion(f32[4,8,2,8,16,8]{4,5,3,1,2,0:T(8,128)S(1)} %copy.396, f32[32]{0:T(128)S(1)} %copy-done.14, f32[32,8,8,8,128,1,1]{4,3,2,1,0,6,5:T(8,128)} %bitcast.458, s32[4,2,16]{2,1,0:T(2,128)S(1)} %multiply_add_fusion.4, s32[128]{0:T(128)S(1)} %bitcast.496), kind=kOutput, calls=%fused_computation.75 | convolution fusion | flops 3225436160 | bytes 25429120 | tf_op jit(solution)/shard_map/rb,rf->bf/dot_general | solution.py:158
  276.8 30.0 %copy.399 = f32[32,4,8,2,8,16,8]{0,6,5,4,3,2,1:T(8,128)} copy(f32[32,4,8,2,8,16,8]{0,5,6,4,2,3,1:T(8,128)} %get-tuple-element.238) | data formatting | bytes 16777216 | tf_op jit(solution)/shard_map/transpose | solution.py:162
  306.8 22.2 %copy.400 = f32[32,32,16,128]{3,2,1,0:T(8,128)} copy(f32[32,32,16,128]{0,3,2,1:T(8,128)} %bitcast.436) | data formatting | bytes 16777216 | tf_op jit(solution)/shard_map/reshape | solution.py:162
  333.4 41.3 %fusion.62 = f32[1,16,32,32,16]{3,1,4,2,0:T(8,128)S(1)} fusion(f32[32,32,16,128]{3,2,1,0:T(8,128)S(1)} %multiply_add_fusion.1), kind=kOutput, calls=%fused_computation.104 | convolution fusion | flops 402681856 | bytes 9437184 | tf_op jit(solution)/shard_map/cxyz,zk->kcxy/dot_general | solution.py:60
  374.7 33.1 %negate_bitcast_fusion.1 = f32[1,16,32,32,16]{3,1,4,2,0:T(8,128)S(1)} fusion(f32[32,32,16,128]{3,2,1,0:T(8,128)S(1)} %multiply_add_fusion.1), kind=kOutput, calls=%fused_computation.102 | convolution fusion | flops 402944000 | bytes 9437184 | tf_op jit(solution)/shard_map/cxyz,zk->kcxy/dot_general | solution.py:61
  414.8 8.6 reshape.541
  427.0 48.4 %all-to-all-done.1 = f32[8,1,65536]{2,1,0:T(1,128)S(1)} async-done(((f32[8,1,65536]{2,1,0:T(1,128)}), f32[8,1,65536]{2,1,0:T(1,128)S(1)}, u32[]{:S(2)}, u32[]{:S(2)}) %all-to-all-start.1) | async-done | bytes 2097184 | tf_op jit(solution)/shard_map/all_to_all | solution.py:63
  477.3 7.3 reduce.24
  529.0 8.5 all-to-all-done.2
  555.9 11.6 all_to_all.134
  576.6 7.5 copy.417
  584.1 8.6 reshape.547
  597.8 30.1 %copy.397 = f32[32,4,8,2,8,16,8]{0,6,5,4,3,2,1:T(8,128)} copy(f32[32,4,8,2,8,16,8]{0,5,6,4,2,3,1:T(8,128)} %get-tuple-element.237) | data formatting | bytes 16777216 | tf_op jit(solution)/shard_map/add | solution.py:165
  627.9 17.4 %all-to-all-done.4 = f32[8,1,65536]{2,1,0:T(1,128)} async-done(((f32[8,1,65536]{2,1,0:T(1,128)}), f32[8,1,65536]{2,1,0:T(1,128)}, u32[]{:S(2)}, u32[]{:S(2)}) %all-to-all-start.4) | async-done | bytes 2097184 | tf_op jit(solution)/shard_map/all_to_all | solution.py:75
  645.3 7.3 reduce.27
  658.6 8.6 copy.418
  689.9 15.4 fusion.174
  705.3 16.2 %fusion.178 = f32[32,32,16,128]{3,0,2,1:T(8,128)} fusion(f32[16,32,32,16]{1,0,3,2:T(8,128)S(1)} %copy-done.3, f32[16]{0:T(128)S(1)} %fusion.257), kind=kOutput, calls=%fused_computation.259 | convolution fusion | flops 402683904 | bytes 9437248 | tf_op jit(solution)/shard_map/kcxy,zk->cxyz/dot_general | solution.py:76
  721.5 40.4 %fusion.52 = f32[32,32,16,128]{3,0,2,1:T(8,128)S(1)} fusion(f32[32,32,16,128]{3,0,2,1:T(8,128)} %fusion.178, f32[32,32,16,128]{3,0,2,1:T(8,128)S(1)} %fusion.174, f32[32]{0:T(128)S(1)} %get-tuple-element.236, f32[32,32,16,128]{0,3,2,1:T(8,128)} %bitcast.434, f32[2,32,32]{2,1,0:T(8,128)S(1)} %copy-done.15), kind=kOutput, calls=%fused_computation.84 | convolution fusion | flops 828375040 | bytes 33571328 | tf_op jit(solution)/shard_map/oc,cxyz->oxyz/dot_general | solution.py:182
  761.9 36.1 %fusion.67 = f32[1,16,32,32,16]{3,1,4,2,0:T(8,128)S(1)} fusion(f32[32,32,16,128]{3,0,2,1:T(8,128)S(1)} %fusion.52), kind=kOutput, calls=%fused_computation.105 | convolution fusion | flops 402681856 | bytes 9437184 | tf_op jit(solution)/shard_map/cxyz,zk->kcxy/dot_general | solution.py:60
  798.0 36.4 %negate_bitcast_fusion = f32[1,16,32,32,16]{3,1,4,2,0:T(8,128)S(1)} fusion(f32[32,32,16,128]{3,0,2,1:T(8,128)S(1)} %fusion.52), kind=kOutput, calls=%fused_computation.101 | convolution fusion | flops 402944000 | bytes 9437184 | tf_op jit(solution)/shard_map/cxyz,zk->kcxy/dot_general | solution.py:61
  840.8 7.4 reshape.549
  848.3 51.9 %all_to_all.135 = f32[8,1,65536]{2,1,0:T(1,128)} all-to-all(f32[8,1,65536]{2,1,0:T(1,128)S(1)} %reshape.549), channel_id=1, replica_groups=mesh['gx'=4,'gy'=8] {'gy'}, dimensions={0} | all-to-all | bytes 4194304 | tf_op jit(solution)/shard_map/all_to_all | solution.py:63
  900.1 7.3 reduce.28
  918.9 7.1 convolution_multiply_fusion.1
  951.8 8.6 all-to-all-done.6
  978.7 11.6 all_to_all.136
  999.4 7.5 copy.441
  1006.9 8.5 reshape.555
  1020.2 47.9 %all-to-all-done.8 = f32[8,1,65536]{2,1,0:T(1,128)} async-done(((f32[8,1,65536]{2,1,0:T(1,128)}), f32[8,1,65536]{2,1,0:T(1,128)}, u32[]{:S(2)}, u32[]{:S(2)}) %all-to-all-start.8) | async-done | bytes 2097184 | tf_op jit(solution)/shard_map/all_to_all | solution.py:75
  1068.1 7.3 reduce.31
  1081.3 8.6 copy.442
  1101.6 17.2 %fusion.172 = f32[32,32,16,128]{3,0,2,1:T(8,128)} fusion(f32[16,32,32,16]{1,0,3,2:T(8,128)} %copy.489, f32[16]{0:T(128)S(1)} %fusion.257), kind=kOutput, calls=%fused_computation.253 | convolution fusion | flops 402683904 | bytes 9437248 | tf_op jit(solution)/shard_map/kcxy,zk->cxyz/dot_general | solution.py:77
  1127.6 15.4 fusion.176
  1143.0 14.0 bitcast_add_fusion
  1157.0 19.6 %copy.449 = f32[32,32,16,128]{0,3,2,1:T(8,128)} copy(f32[32,32,16,128]{3,0,2,1:T(8,128)} %bitcast_add_fusion) | data formatting | bytes 16777216 | tf_op jit(solution)/shard_map/add | solution.py:183
  1176.6 103.5 %copy.450 = f32[4,2,16,32,8,8,8]{2,1,0,6,5,4,3:T(2,128)} copy(f32[4,2,16,32,8,8,8]{3,6,2,5,1,4,0:T(8,128)} %bitcast.435) | data formatting | bytes 16777216 | tf_op jit(solution)/shard_map/transpose | solution.py:188
  1280.1 85.8 %reshape.475 = f32[128,16384]{0,1:T(8,128)} reshape(f32[4,2,16,32,8,8,8]{2,1,0,6,5,4,3:T(2,128)} %copy.450) | data formatting | bytes 16777216 | tf_op jit(solution)/shard_map/reshape | solution.py:188
  1365.9 9.1 copy.451
  1375.0 13.0 gather_fusion
  1388.1 13.4 copy.504
  1401.4 180.8 %while.21 = (s32[]{:T(128)}, f32[32,4,32,128]{3,2,1,0:T(8,128)}, f32[32,4,32,512]{3,2,1,0:T(8,128)}, f32[32,4,3]{2,1,0:T(4,128)}, f32[3,512]{1,0:T(4,128)S(1)}, /*index=5*/f32[32,4,3,128]{3,1,2,0:T(4,128)}, s32[]{:T(128)}) while((s32[]{:T(128)}, f32[32,4,32,128]{3,2,1,0:T(8,128)}, f32[32,4,32,512]{3,2,1,0:T(8,128)}, f32[32,4,3]{2,1,0:T(4,128)}, ...), condition=%wide.region_7.8_spmd, body=%wide.region_5.7_spmd.sunk | while | flops 107239936 | bytes 466245 | solution.py:203
  (765 shorter events, 564.8 us)
Async XLA Ops:
  0.0 2.0 copy-start
  0.0 2.3 copy-start.23
  0.0 2.8 copy-start.10
  0.0 2.8 copy-start.13
  0.8 3.9 copy-start.16
  24.3 7.8 copy-start.6
  24.4 67.6 %all-to-all-start = ((f32[128,36,128]{2,1,0:T(8,128)}), f32[128,36,128]{2,1,0:T(8,128)}, u32[]{:S(2)}, u32[]{:S(2)}) async-start(f32[128,36,128]{2,1,0:T(8,128)} %scatter_fusion), calls=%async_computation | async-start | bytes 5242880 | tf_op jit(solution)/shard_map/all_to_all | solution.py:121
  225.1 13.5 copy-start.7
  225.1 13.5 copy-start.9
  225.1 13.5 copy-start.12
  238.7 9.0 copy-start.14
  423.4 52.1 %all-to-all-start.1 = ((f32[8,1,65536]{2,1,0:T(1,128)}), f32[8,1,65536]{2,1,0:T(1,128)S(1)}, u32[]{:S(2)}, u32[]{:S(2)}) async-start(f32[8,1,65536]{2,1,0:T(1,128)} %reshape.541), calls=%async_computation.1 | async-start | bytes 4194304 | tf_op jit(solution)/shard_map/all_to_all | solution.py:63
  475.4 1.3 copy-start.5
  523.4 5.4 copy-start.11
  525.2 12.3 all-to-all-start.2
  592.7 4.5 copy-start.21
  592.7 52.6 %all-to-all-start.4 = ((f32[8,1,65536]{2,1,0:T(1,128)}), f32[8,1,65536]{2,1,0:T(1,128)}, u32[]{:S(2)}, u32[]{:S(2)}) async-start(f32[8,1,65536]{2,1,0:T(1,128)} %reshape.547), calls=%async_computation.4 | async-start | bytes 4194304 | tf_op jit(solution)/shard_map/all_to_all | solution.py:75
  689.9 15.4 copy-start.3
  705.3 16.2 %copy-start.15 = (f32[2,32,32]{2,1,0:T(8,128)S(1)}, f32[2,32,32]{2,1,0:T(8,128)}, u32[]{:S(2)}) copy-start(f32[2,32,32]{2,1,0:T(8,128)} %param.22) | copy-start | bytes 24580
  761.9 36.1 %copy-start.2 = (f32[32,32,16,128]{3,0,2,1:T(8,128)}, f32[32,32,16,128]{3,0,2,1:T(8,128)S(1)}, u32[]{:S(2)}) copy-start(f32[32,32,16,128]{3,0,2,1:T(8,128)S(1)} %fusion.52) | copy-start | bytes 25165828
  948.0 12.3 all-to-all-start.6
  1015.4 4.7 copy-start.20
  1015.4 52.7 %all-to-all-start.8 = ((f32[8,1,65536]{2,1,0:T(1,128)}), f32[8,1,65536]{2,1,0:T(1,128)}, u32[]{:S(2)}, u32[]{:S(2)}) async-start(f32[8,1,65536]{2,1,0:T(1,128)} %reshape.555), calls=%async_computation.8 | async-start | bytes 4194304 | tf_op jit(solution)/shard_map/all_to_all | solution.py:75
  1101.6 17.2 %copy-start.4 = (f32[1,8,2,32,32,16]{4,5,1,3,2,0:T(8,128)S(1)}, f32[1,8,2,32,32,16]{4,5,1,3,2,0:T(8,128)}, u32[]{:S(2)}) copy-start(f32[1,8,2,32,32,16]{4,5,1,3,2,0:T(8,128)} %get-tuple-element.207) | copy-start | bytes 3145732
  1127.6 15.4 copy-start.18
  1388.1 13.4 copy-start.8
  1401.4 180.8 %copy-start.22 = (f32[32]{0:T(128)S(1)}, f32[32]{0:T(128)}, u32[]{:S(2)}) copy-start(f32[32]{0:T(128)} %param.25) | copy-start | bytes 388
  1401.4 188.0 %copy-start.19 = (s32[128]{0:T(128)S(1)}, s32[128]{0:T(128)}, u32[]{:S(2)}) copy-start(s32[128]{0:T(128)} %get-tuple-element.233) | copy-start | bytes 1540
  1401.4 195.5 %copy-start.17 = (pred[128]{0:T(512)(128)(4,1)S(1)}, pred[128]{0:T(512)(128)(4,1)}, u32[]{:S(2)}) copy-start(pred[128]{0:T(512)(128)(4,1)} %copy-done.16) | copy-start | bytes 388
  1582.2 15.5 copy-start.1
  1585.8 10.5 all-to-all-start.9
where the time goes:
time: 1620 us; the launch traced here: 1600 us
  local copies, waits for them, and re-layouts  618 us (38%)
  matrix products  585 us (36%)
  waiting for transfers between devices  191 us (12%)
  other arithmetic  95.1 us (6%)
  blocking collectives  75.2 us (5%)
  starting transfers between devices  31.2 us (2%)
    dot_general x32, matrix products, encode_group(): return jnp.einsum('rcp,rgp->rcg', feature_set, weights, precision=highest)  114 us
    transpose x1, local copies, waits for them, and re-layouts, per_device(): final_bricks.transpose(1, 3, 5, 0, 2, 4, 6)  104 us
    reshape x2, local copies, waits for them, and re-layouts, per_device(): final_bricks.transpose(1, 3, 5, 0, 2, 4, 6)  94.9 us
    dot_general x32, matrix products, decode_group(): jnp.einsum('rcg,rgp->rcp', value_set, weights, precision=highest)  93.8 us
    unnamed x69, local copies, waits for them, and re-layouts  93.4 us
    dot_general x2, matrix products, spectral_part(): jnp.einsum('cxyz,zk->kcxy', grid_field, z_cos, precision=highest)  77.4 us
    dot_general x2, matrix products, spectral_part(): jnp.einsum('cxyz,zk->kcxy', grid_field, z_sin, precision=highest)  69.5 us
    all_to_all x2, waiting for transfers between devices, spectral_part(): lax.all_to_all(spectra, 'gy', split_axis=4, concat_axis=1, tiled=True)  65.3 us
  transfers between devices with their start and end apart: 7, of which 7 were waited for; matrix products, arithmetic and copies ran while one was open for 2% of the time, Pallas kernels for 0%

commit v1 on v0

v1 whole, which is shorter than its diff:
```python
import functools
import math

import jax
import jax.numpy as jnp
import ml_dtypes
import numpy as np
from jax import lax
from jax.experimental import pallas as pl
from jax.experimental.pallas import tpu as pltpu
from jax.sharding import PartitionSpec as P

B = 8
BF = jnp.bfloat16
F32 = jnp.float32
VM = pl.BlockSpec(memory_space=pltpu.VMEM)
SM = pl.BlockSpec(memory_space=pltpu.SMEM)
LIMIT = 56 * 1024 * 1024


def split(x):
    hi = x.astype(BF)
    lo = (x - hi.astype(F32)).astype(BF)
    return hi, lo


def np_split(table):
    table = np.asarray(table, np.float64).astype(np.float32)
    hi = table.astype(ml_dtypes.bfloat16)
    lo = (table - hi.astype(np.float32)).astype(ml_dtypes.bfloat16)
    return hi, lo


def dot(a, b, contract=((1,), (0,))):
    return lax.dot_general(a, b, (contract, ((), ())), preferred_element_type=F32)


NT = ((1,), (1,))


def call(body, name, out_shape, in_specs, out_specs, flops, moved, grid=None, scratch=(), aliases=None):
    extra = {} if grid is None else {"grid": grid}
    return pl.pallas_call(
        body,
        name=name,
        out_shape=out_shape,
        in_specs=in_specs,
        out_specs=out_specs,
        scratch_shapes=list(scratch),
        input_output_aliases=aliases or {},
        compiler_params=pltpu.CompilerParams(vmem_limit_bytes=LIMIT),
        cost_estimate=pl.CostEstimate(flops=int(flops), bytes_accessed=int(moved), transcendentals=0),
        **extra,
    )


class Sizes:
    def __init__(self, nx, ny, grid, channels, modes, kz):
        self.nx, self.ny, self.G, self.C, self.M, self.KZ = nx, ny, grid, channels, modes, kz
        self.NB = grid // B
        self.bxn = self.NB // nx
        self.byn = self.NB // ny
        self.Xl = grid // nx
        self.Yl = grid // ny
        self.cp = channels // nx
        self.KL = kz // ny
        self.L = channels * self.bxn
        self.LY = self.Yl * self.cp
        self.LK = 2 * self.KL * modes
        self.K2 = 2 * kz
        self.LB = self.NB * self.bxn * self.byn
        self.freq = np.where(np.arange(modes) < modes // 2, np.arange(modes), np.arange(modes) - modes)


def trig(s, places, freqs):
    angle = (np.asarray(places)[:, None] * np.asarray(freqs)[None, :]) % s.G * (2.0 * np.pi / s.G)
    return np.cos(angle), np.sin(angle)


def stack_left(table):
    hi, lo = np_split(table)
    zero = np.zeros_like(lo)
    return np.concatenate([np.concatenate([hi, hi], 1), np.concatenate([lo, zero], 1)], 0)


def wide_left(table):
    hi, lo = np_split(table)
    return np.concatenate([hi, hi, lo], 1)


def make_tables(s):
    t = {}
    c, n = trig(s, np.arange(s.KZ), np.arange(s.G))
    t["z_fwd"] = stack_left(np.concatenate([c, -n], 0))
    back = np.where(np.arange(s.KZ) == 0, 1.0, 2.0)[None, :] / s.G
    c, n = trig(s, np.arange(s.G), np.arange(s.KZ))
    t["z_inv"] = wide_left(np.concatenate([c * back, -n * back], 1))
    order = np.arange(s.G).reshape(s.nx, s.bxn, B).transpose(0, 2, 1).reshape(-1)
    c, n = trig(s, s.freq, order)
    hi, lo = np_split(np.concatenate([np.concatenate([c, n], 1), np.concatenate([-n, c], 1)], 0))
    t["x_fwd"] = np.concatenate([hi, lo], 0)
    c, n = trig(s, s.freq, np.arange(s.G))
    t["y_fwd"] = stack_left(np.concatenate([c, n], 0))
    t["y_inv"] = wide_left(np.concatenate([c.T, n.T], 1) / s.G)
    c, n = trig(s, order, s.freq)
    table = np.zeros((s.KL, 2, s.G, 2, s.KL, s.M))
    for k in range(s.KL):
        table[k, 0, :, 0, k], table[k, 0, :, 1, k] = c, -n
        table[k, 1, :, 0, k], table[k, 1, :, 1, k] = n, c
    t["x_inv"] = wide_left(table.reshape(2 * s.KL * s.G, s.LK) / s.G)
    xs = (np.arange(s.bxn)[:, None] * B + np.arange(B)[None, :]).T.reshape(B, 1, s.bxn, 1)
    ys = (np.arange(s.byn)[:, None] * B + np.arange(B)[None, :]).T.reshape(1, B, 1, s.byn)
    full = (B, B, s.bxn, s.byn)
    xs, ys = np.broadcast_to(xs, full).reshape(-1), np.broadcast_to(ys, full).reshape(-1)
    turn = s.freq[None, :, None] * xs[None, None, :] + s.freq[:, None, None] * ys[None, None, :]
    angle = (turn % s.G).reshape(s.M * s.M, -1) * (2.0 * np.pi / s.G)
    t["xy_hi"], t["xy_lo"] = np_split(np.concatenate([np.cos(angle), np.sin(angle)], 0) / (s.G * s.G))
    return t


def block_turn(tiles, blocks, width):
    count = len(tiles)
    if count == blocks and count * width == 128:
        lane = lax.broadcasted_iota(jnp.int32, tiles[0].shape, 1) // width
        tiles = list(tiles)
        step = 1
        while step < count:
            upper = (lane & step) != 0
            for i in range(count):
                if i & step == 0:
                    a, b = tiles[i], tiles[i | step]
                    up = pltpu.roll(b, step * width, 1)
                    down = pltpu.roll(a, 128 - step * width, 1)
                    tiles[i] = jnp.where(upper, up, a)
                    tiles[i | step] = jnp.where(upper, b, down)
            step *= 2
        return tiles
    return [
        jnp.concatenate([tile[:, b * width : (b + 1) * width] for tile in tiles], axis=1)
        for b in range(blocks)
    ]


def swap_halves(x):
    half = x.shape[1] // 2
    if x.shape[1] == 128:
        return pltpu.roll(x, half, 1)
    return jnp.concatenate([x[:, half:], x[:, :half]], axis=1)


def half_signs(rows, width, first):
    lane = lax.broadcasted_iota(jnp.int32, (rows, width), 1)
    return jnp.where(lane < width // 2, first, -first).astype(F32)


def pack_kernel(s, cap, brick_ref, count_ref, pos_ref, feat_ref, area_ref, out_ref, slot_ref, fill_ref):
    blocks = brick_ref.shape[0]
    C = s.C
    for i in range(s.ny):
        fill_ref[i] = 0
        out_ref[i] = jnp.full(out_ref.shape[1:], -1.0, F32)
    live = count_ref[0]

    def step(n, carry):
        @pl.when(n < live)
        def _():
            brick = brick_ref[n]
            dest = (brick // s.NB) % s.NB // s.byn
            order = fill_ref[dest]
            fill_ref[dest] = order + 1
            slot_ref[n] = dest * cap + order
            lanes = pl.ds(pl.multiple_of(n * 128, 128), 128)
            out_ref[dest, pl.ds(pl.multiple_of(order * C, 8), C), :] = feat_ref[:, lanes] * area_ref[pl.ds(n, 1), :]
            points = pos_ref[:, lanes]
            for d in range(3):
                out_ref[dest, pl.ds(cap * C + d * cap + order, 1), :] = points[d : d + 1, :]

        @pl.when(n >= live)
        def _():
            slot_ref[n] = -1

        return carry

    lax.fori_loop(0, blocks, step, 0)


def field_kernel(s, sdf_ref, gain_ref, out_ref):
    rows = sdf_ref[...].reshape(s.bxn * s.Yl, s.G).T
    hi, lo = split(rows)
    ghi, glo = split(gain_ref[...])
    wide = dot(hi, ghi) + dot(lo, ghi) + dot(hi, glo)
    for y in range(s.Yl):
        out_ref[0, y] = wide[:, y * s.L : (y + 1) * s.L]


def kernel_tiles(points):
    px, py, pz = points
    scale = 1.0 / B
    sub = lax.broadcasted_iota(jnp.int32, pz.shape, 0).astype(F32)
    gz = ((sub + 0.5) - pz) * scale
    gz = gz * gz
    gx = []
    gy = []
    for a in range(B):
        d = (px - (a + 0.5)) * scale
        gx.append(1.0 - d * d)
        d = (py - (a + 0.5)) * scale
        gy.append(d * d + gz)
    tiles = []
    for a in range(B):
        for b in range(B):
            t = jnp.maximum(gx[a] - gy[b], 0.0)
            tiles.append(t * t)
    return tiles


def grid_to_spectrum(s, rows_of, table):
    tiles = []
    for y in range(0, s.Yl, 2):
        both = jnp.concatenate([rows_of(y), rows_of(y + 1)], axis=1)
        hi, lo = split(both)
        res = dot(table, jnp.concatenate([hi, lo], axis=0))
        res = res[: s.K2] + res[s.K2 :]
        tiles += [res[:, : s.L], res[:, s.L :]]
    return block_turn(tiles, s.nx * s.bxn, s.cp)


def encode_kernel(s, cap, id_ref, num_ref, in_ref, init_ref, table_ref, grid_ref, spec_ref):
    C = s.C
    for a in range(B):
        grid_ref[a] = init_ref[a]
    group = lax.broadcasted_iota(jnp.int32, (s.L, 128), 0) // s.cp % s.bxn

    def per_source(src, carry):
        def per_block(j, inner):
            slot = src * cap + j
            bx, by, bz = id_ref[0, slot], id_ref[1, slot], id_ref[2, slot]
            points = [
                jnp.broadcast_to(in_ref[src, pl.ds(cap * C + d * cap + j, 1), :], (8, 128))
                for d in range(3)
            ]
            points = [p - id_ref[3 + d, slot].astype(F32) for d, p in enumerate(points)]
            weights = jnp.concatenate(kernel_tiles(points), axis=0)
            feats = in_ref[src, pl.ds(pl.multiple_of(j * C, 8), C), :]
            spread = []
            for g in range(s.nx):
                spread += [feats[g * s.cp : (g + 1) * s.cp]] * s.bxn
            spread = jnp.where(group == bx, jnp.concatenate(spread, axis=0), 0.0)
            whi, wlo = split(weights)
            fhi, flo = split(spread)
            left = jnp.concatenate([whi, wlo], axis=1)
            right = jnp.concatenate([fhi, fhi], axis=1)
            if s.L == 128:
                under = jnp.concatenate([flo, jnp.zeros_like(flo)], axis=1)
                res = dot(left, jnp.concatenate([right, under], axis=0), NT)
                res = res[:, : s.L] + res[:, s.L :]
            else:
                res = dot(left, right, NT) + dot(whi, flo, NT)
            ys = pl.ds(pl.multiple_of(by * B, B), B)
            zs = pl.ds(pl.multiple_of(bz * B, B), B)
            grid_ref[:, ys, zs, :] = grid_ref[:, ys, zs, :] + res.reshape(B, B, B, s.L)
            return inner

        return lax.fori_loop(0, num_ref[src], per_block, carry)

    lax.fori_loop(0, s.ny, per_source, 0)

    def transform(a, carry):
        out = grid_to_spectrum(s, lambda y: grid_ref[a, y], table_ref[...])
        for g in range(s.nx):
            for b in range(s.bxn):
                spec_ref[g, a, b] = out[g * s.bxn + b]
        return carry

    lax.fori_loop(0, B, transform, 0)


def mixed_rows(rows, whi, wlo):
    hi, lo = split(rows)
    width = whi.shape[1]
    if width == 128 and rows.shape[1] == 128:
        left = jnp.concatenate([hi, lo], axis=1)
        right = jnp.concatenate(
            [jnp.concatenate([whi, wlo], axis=1), jnp.concatenate([whi, jnp.zeros_like(wlo)], axis=1)], axis=0
        )
        res = dot(left, right)
        return res[:, :128] + res[:, 128:]
    return dot(hi, whi) + dot(lo, whi) + dot(hi, wlo)


def mix_kernel(s, grid_ref, mix_ref, bias_ref, out_ref):
    whi, wlo = split(mix_ref[...])
    for y in range(s.Yl):
        out_ref[0, y] = mixed_rows(grid_ref[0, y], whi, wlo) + bias_ref[...]


def readout_kernel(s, grid_ref, mix_ref, out_ref):
    whi, wlo = split(mix_ref[...])
    lane = lax.broadcasted_iota(jnp.int32, (B, s.LB), 1)
    for a in range(B):
        total = jnp.zeros((B, s.LB), F32)
        for by in range(s.byn):
            res = mixed_rows(grid_ref[0, by * B + a], whi, wlo)
            for bz in range(s.NB):
                mine = (lane // (s.bxn * s.byn) == bz) & (lane % s.byn == by)
                total = jnp.where(mine, res[bz * B : (bz + 1) * B], total)
        out_ref[0, a * B : (a + 1) * B, :] = total


def x_forward_kernel(s, in_ref, table_ref, out_ref):
    M = s.M
    thi = table_ref[: 2 * M]
    for i in range(s.ny):
        parts = []
        for k in range(s.KL):
            kz = i * s.KL + k
            parts.append(
                jnp.concatenate(
                    [in_ref[pl.ds(kz, s.G, stride=s.K2), :], in_ref[pl.ds(s.KZ + kz, s.G, stride=s.K2), :]], axis=0
                )
            )
        hi, lo = split(jnp.concatenate(parts, axis=1))
        res = dot(table_ref[...], hi)
        res = res[: 2 * M] + res[2 * M :] + dot(thi, lo)
        rows = []
        for ri in range(2):
            for k in range(s.KL):
                rows.append(res[ri * M : (ri + 1) * M, k * s.LY : (k + 1) * s.LY])
        out_ref[i] = jnp.concatenate(rows, axis=0).T


def y_spectrum(s, in_ref, table, u_ref, v_ref, cs):
    M = s.M
    both = jnp.concatenate([in_ref[pl.ds(c, s.G, stride=s.cp), :] for c in cs], axis=1)
    hi, lo = split(both)
    res = dot(table, jnp.concatenate([hi, lo], axis=0))
    res = res[: 2 * M] + res[2 * M :]
    out = []
    plus = half_signs(M, s.LK, 1.0)
    for i, c in enumerate(cs):
        part = res[:, i * s.LK : (i + 1) * s.LK]
        wave = part[:M] + plus * swap_halves(part[M:])
        out.append(wave * u_ref[c] + swap_halves(wave) * v_ref[c])
    return out


def y_kernel(s, in_ref, fwd_ref, inv_ref, u_ref, v_ref, out_ref):
    minus = half_signs(s.M, s.LK, -1.0)
    for c in range(0, s.cp, 2):
        prods = y_spectrum(s, in_ref, fwd_ref[...], u_ref, v_ref, (c, c + 1))
        both = jnp.concatenate(
            [jnp.concatenate([p, minus * swap_halves(p)], axis=0) for p in prods], axis=1
        )
        hi, lo = split(both)
        res = dot(inv_ref[...], jnp.concatenate([hi, lo, hi], axis=0))
        for i in range(2):
            out_ref[pl.ds(c + i, s.G, stride=s.cp), :] = res[:, i * s.LK : (i + 1) * s.LK]


def y_last_kernel(s, in_ref, fwd_ref, u_ref, v_ref, out_ref):
    total = jnp.zeros((s.M, s.LK), F32)
    for c in range(0, s.cp, 2):
        prods = y_spectrum(s, in_ref, fwd_ref[...], u_ref, v_ref, (c, c + 1))
        total = total + prods[0] + prods[1]
    out_ref[...] = total


def x_inverse_kernel(s, in_ref, table_ref, out_ref):
    for i in range(s.ny):
        hi, lo = split(in_ref[i])
        if s.LK == 128:
            res = dot(table_ref[...], jnp.concatenate([hi, lo, hi], axis=1), NT)
        else:
            t = table_ref[...]
            res = dot(t[:, : s.LK], hi, NT) + dot(t[:, : s.LK], lo, NT) + dot(t[:, 2 * s.LK :], hi, NT)
        for k in range(s.KL):
            for ri in range(2):
                at = (k * 2 + ri) * s.G
                out_ref[pl.ds(ri * s.KZ + i * s.KL + k, s.G, stride=s.K2), :] = res[at : at + s.G]


def gelu(x):
    inner = math.sqrt(2.0 / math.pi) * (x + 0.044715 * (x * x * x))
    return 0.5 * x * (1.0 + jnp.tanh(inner))


def layer_kernel(s, mixed_ref, in_ref, inv_ref, fwd_ref, grid_ref, spec_ref):
    tiles = [in_ref[g, 0, b] for g in range(s.nx) for b in range(s.bxn)]
    tiles = block_turn(tiles, s.Yl, s.cp)
    for y in range(0, s.Yl, 2):
        hi, lo = split(jnp.concatenate([tiles[y], tiles[y + 1]], axis=1))
        res = dot(inv_ref[...], jnp.concatenate([hi, lo, hi], axis=0))
        for i in range(2):
            grid_ref[0, y + i] = gelu(mixed_ref[0, y + i] + res[:, i * s.L : (i + 1) * s.L])
    out = grid_to_spectrum(s, lambda y: grid_ref[0, y], fwd_ref[...])
    for g in range(s.nx):
        for b in range(s.bxn):
            spec_ref[g, 0, b] = out[g * s.bxn + b]


def decode_kernel(s, cap, id_ref, num_ref, base_ref, pos_ref, spec_ref, mix_ref, hi_ref, lo_ref, inv_ref, out_ref, s_ref):
    mhi, mlo = split(spec_ref[...])
    wave = dot(jnp.concatenate([mhi, mlo], axis=0), hi_ref[...])
    wave = wave[: s.K2] + wave[s.K2 :] + dot(mhi, lo_ref[...])
    hi, lo = split(wave)
    field = dot(inv_ref[...], jnp.concatenate([hi, lo, hi], axis=0))
    width = s.bxn * s.byn
    per = 128 // width
    for q in range(field.shape[1] // 128):
        tiles = [field[z * B : (z + 1) * B, q * 128 : (q + 1) * 128] for z in range(s.NB)]
        for i, tile in enumerate(block_turn(tiles, per, width)):
            at = (q * per + i) * B
            s_ref[at : at + B, :] = tile + mix_ref[at : at + B, :] + base_ref[0]
    out_ref[...] = jnp.zeros(out_ref.shape, F32)
    cell = lax.broadcasted_iota(jnp.int32, (s.LB, 128), 0)

    def per_source(src, carry):
        def per_pair(h, inner):
            shi, slo = split(s_ref[...])
            picks = []
            for i in range(2):
                j = h * 2 + i
                at = id_ref[6, src * cap + j]
                picks.append(jnp.where(cell == at, 1.0, 0.0).astype(BF))
            pick = jnp.concatenate(picks, axis=1)
            if s.LB == 128:
                vals = dot(jnp.concatenate([shi, slo], axis=1), jnp.concatenate([pick, pick], axis=0))
            else:
                vals = dot(shi, pick) + dot(slo, pick)
            for i in range(2):
                j = h * 2 + i
                slot = src * cap + j
                points = [
                    jnp.broadcast_to(pos_ref[src, pl.ds(d * cap + j, 1), :], (8, 128))
                    - id_ref[3 + d, slot].astype(F32)
                    for d in range(3)
                ]
                top = jnp.zeros((B, 128), F32)
                low = jnp.zeros((B, 128), F32)
                for n, tile in enumerate(kernel_tiles(points)):
                    top = top + tile * vals[n * B : (n + 1) * B, i * 128 : (i + 1) * 128]
                    low = low + tile
                top = jnp.sum(top, axis=0, keepdims=True)
                low = jnp.sum(low, axis=0, keepdims=True)
                out_ref[pl.ds(slot, 1), :] = top / jnp.where(low > 0.0, low, 1.0)
            return inner

        return lax.fori_loop(0, (num_ref[src] + 1) // 2, per_pair, carry)

    lax.fori_loop(0, s.ny, per_source, 0)


def per_device(
    positions,
    point_feat,
    area,
    block_brick,
    block_count,
    sdf,
    grid_gain,
    mix_w,
    mix_b,
    spec_w,
    readout_w,
):
    nx, ny = lax.axis_size("gx"), lax.axis_size("gy")
    row_x, row_y = lax.axis_index("gx"), lax.axis_index("gy")
    modes = math.isqrt(spec_w.shape[4])
    s = Sizes(nx, ny, sdf.shape[2], point_feat.shape[0], modes, spec_w.shape[2] * ny)
    t = {name: jnp.asarray(value) for name, value in make_tables(s).items()}
    shape = lambda *dims: jax.ShapeDtypeStruct(dims, F32)
    blocks = block_brick.shape[0]
    cap = blocks // ny
    PB = positions.shape[1] // blocks
    C, G, M, L = s.C, s.G, s.M, s.L
    rows = cap * (C + 3)

    outgoing, slot_of = call(
        functools.partial(pack_kernel, s, cap),
        "pack",
        (shape(ny, rows, PB), jax.ShapeDtypeStruct((blocks,), jnp.int32)),
        [SM, SM, VM, VM, VM],
        (VM, SM),
        1e6,
        6e6,
        scratch=[pltpu.SMEM((ny,), jnp.int32)],
    )(block_brick, block_count, positions, point_feat, area.reshape(blocks, PB))
    incoming = lax.all_to_all(outgoing, "gy", split_axis=0, concat_axis=0, tiled=True)
    in_pos = incoming[:, cap * C :, :]
    first = in_pos.reshape(ny, 3, cap, PB)[..., 0].transpose(1, 0, 2).reshape(3, ny * cap)
    counts = jnp.sum((first[0].reshape(ny, cap) >= 0.0).astype(jnp.int32), axis=1)
    brick = jnp.floor(first / B).astype(jnp.int32)
    start = jnp.stack([row_x * s.bxn, row_y * s.byn, jnp.zeros_like(row_x)])
    limit = jnp.array([s.bxn - 1, s.byn - 1, s.NB - 1], jnp.int32)
    local = jnp.clip(brick - start[:, None], 0, limit[:, None])
    corner = (local + start[:, None]) * B
    flat = local[2] * (s.bxn * s.byn) + local[0] * s.byn + local[1]
    ids = jnp.concatenate([local, corner, flat[None], flat[None]], axis=0)

    lane = jnp.arange(L)
    lane_bx = lane // s.cp % s.bxn
    lane_c = lane // (s.bxn * s.cp) * s.cp + lane % s.cp
    same_bx = lane_bx[:, None] == lane_bx[None, :]
    gain_l = grid_gain[lane_c]
    spread = (
        (jnp.arange(s.bxn)[:, None, None, None] == lane_bx[None, None, None, :])
        & (jnp.arange(s.Yl)[None, :, None, None] == jnp.arange(s.Yl)[None, None, :, None])
    )
    gains = jnp.where(spread, gain_l, 0.0).reshape(s.bxn * s.Yl, s.Yl * L)
    grid_shape = shape(B, s.Yl, G, L)
    grid_block = pl.BlockSpec((1, s.Yl, G, L), lambda a: (a, 0, 0, 0))
    whole = lambda array: pl.BlockSpec(array.shape, lambda a: (0,) * array.ndim)
    init = call(
        functools.partial(field_kernel, s),
        "field",
        grid_shape,
        [pl.BlockSpec((s.bxn, None, s.Yl, G), lambda a: (0, a, 0, 0)), whole(gains)],
        grid_block,
        3e9,
        1e7,
        grid=(B,),
    )(sdf.reshape(s.bxn, B, s.Yl, G), gains)

    mixing = jnp.where(same_bx, mix_w[0][lane_c[None, :], lane_c[:, None]], 0.0)
    bias = mix_b[0][lane_c][None, :]
    read_mix = jnp.sum(readout_w[:, None] * mix_w[1], axis=0)
    base = jnp.sum(readout_w * mix_b[1]).reshape(1)
    out_lane = jnp.arange(s.LB)
    reading = jnp.where(lane_bx[:, None] == out_lane[None, :] // s.byn % s.bxn, read_mix[lane_c][:, None], 0.0)
    mine = lax.dynamic_slice_in_dim(readout_w, row_x * s.cp, s.cp)

    def multipliers(w, scale):
        w = w.reshape(2, s.KL, s.cp, M, M)
        if scale is not None:
            w = w * scale[None, None, :, None, None]
        w = w.transpose(2, 4, 0, 1, 3)
        u = jnp.concatenate([w[:, :, 0:1], w[:, :, 0:1]], axis=2).reshape(s.cp, M, s.LK)
        v = jnp.concatenate([-w[:, :, 1:2], w[:, :, 1:2]], axis=2).reshape(s.cp, M, s.LK)
        return u, v

    u0, v0 = multipliers(spec_w[0], None)
    u1, v1 = multipliers(spec_w[1], mine)

    spec_shape = shape(nx, B, s.bxn, s.K2, s.LY)
    grid0, spec = call(
        functools.partial(encode_kernel, s, cap),
        "encode",
        (grid_shape, spec_shape),
        [SM, SM, VM, VM, VM],
        (VM, VM),
        4e9,
        2.2e7,
    )(ids, counts, incoming, init, t["z_fwd"])

    def to_modes(spec):
        spec = spec.reshape(nx, B * s.bxn * s.K2, s.LY)
        spec = lax.all_to_all(spec, "gx", split_axis=0, concat_axis=0, tiled=True)
        spec = call(
            functools.partial(x_forward_kernel, s),
            "x_forward",
            shape(ny, s.LY, s.LK),
            [VM, VM],
            VM,
            1e9,
            3e6,
        )(spec.reshape(G * s.K2, s.LY), t["x_fwd"])
        spec = lax.all_to_all(spec, "gy", split_axis=0, concat_axis=0, tiled=True)
        return spec.reshape(G * s.cp, s.LK)

    spec = to_modes(spec)
    mixed = call(
        functools.partial(mix_kernel, s),
        "mix",
        grid_shape,
        [grid_block, whole(mixing), whole(bias)],
        grid_block,
        2e9,
        1.7e7,
        grid=(B,),
    )(grid0, mixing, bias)
    spec = call(
        functools.partial(y_kernel, s), "y_both", shape(G * s.cp, s.LK), [VM] * 5, VM, 1e9, 2e6
    )(spec, t["y_fwd"], t["y_inv"], u0, v0)
    spec = lax.all_to_all(spec.reshape(ny, s.LY, s.LK), "gy", split_axis=0, concat_axis=0, tiled=True)
    spec = call(
        functools.partial(x_inverse_kernel, s), "x_inverse", shape(G * s.K2, s.LY), [VM, VM], VM, 1e9, 3e6
    )(spec, t["x_inv"])
    spec = lax.all_to_all(
        spec.reshape(nx, B * s.bxn * s.K2, s.LY), "gx", split_axis=0, concat_axis=0, tiled=True
    ).reshape(nx, B, s.bxn, s.K2, s.LY)
    spec_block = pl.BlockSpec((nx, 1, s.bxn, s.K2, s.LY), lambda a: (0, a, 0, 0, 0))
    grid1, spec = call(
        functools.partial(layer_kernel, s),
        "layer",
        (grid_shape, spec_shape),
        [grid_block, spec_block, whole(t["z_inv"]), whole(t["z_fwd"])],
        (grid_block, spec_block),
        4e9,
        2.1e7,
        grid=(B,),
    )(mixed, spec, t["z_inv"], t["z_fwd"])
    spec = to_modes(spec)
    read = call(
        functools.partial(readout_kernel, s),
        "readout",
        shape(B, B * B, s.LB),
        [grid_block, whole(reading)],
        pl.BlockSpec((1, B * B, s.LB), lambda a: (a, 0, 0)),
        2e9,
        9e6,
        grid=(B,),
    )(grid1, reading)
    last = call(
        functools.partial(y_last_kernel, s), "y_last", shape(M, s.LK), [VM] * 4, VM, 1e9, 1e6
    )(spec, t["y_fwd"], u1, v1)

    last = lax.all_gather(last, ("gx", "gy"), axis=0, tiled=False)
    last = jnp.sum(last.reshape(nx, ny, M, 2, s.KL, M), axis=0)
    last = last.transpose(2, 0, 3, 1, 4).reshape(2, s.KZ, M * M)
    freq = jnp.asarray(s.freq, jnp.int32)
    turn = jnp.mod(freq[None, :] * (row_x * s.Xl) + freq[:, None] * (row_y * s.Yl), G).reshape(-1)
    angle = turn.astype(F32) * (2.0 * math.pi / G)
    cos, sin = jnp.cos(angle), jnp.sin(angle)
    real = last[0] * cos - last[1] * sin
    imag = last[1] * cos + last[0] * sin
    left = jnp.concatenate(
        [jnp.concatenate([real, -imag], axis=1), jnp.concatenate([imag, real], axis=1)], axis=0
    )
    values = call(
        functools.partial(decode_kernel, s, cap),
        "decode",
        shape(ny * cap, PB),
        [SM, SM, SM] + [VM] * 6,
        VM,
        4e9,
        6e6,
        scratch=[pltpu.VMEM((B * B * B, s.LB), F32)],
    )(ids, counts, base, in_pos, left, read.reshape(B * B * B, s.LB), t["xy_hi"], t["xy_lo"], t["z_inv"])
    returned = lax.all_to_all(values.reshape(ny, cap, PB), "gy", split_axis=0, concat_axis=0, tiled=True)
    choose = (slot_of[:, None] == jnp.arange(ny * cap, dtype=jnp.int32)[None, :]).astype(F32)
    pressure = jnp.dot(choose, returned.reshape(ny * cap, PB), precision=lax.Precision.HIGHEST)
    return pressure.reshape(blocks * PB)


def solution(mesh):
    placed = (
        P(None, ("gx", "gy")),
        P(None, ("gx", "gy")),
        P(("gx", "gy")),
        P(("gx", "gy")),
        P(("gx", "gy")),
        P("gx", "gy", None),
        P(),
        P(),
        P(),
        P(None, None, "gy", "gx", None),
        P(),
    )
    return jax.shard_map(
        per_device, mesh=mesh, in_specs=placed, out_specs=P(("gx", "gy")), check_vma=False
    )
```

time: 1620 us -> 494 us (0.30); the launches traced: 1600 us -> 492 us
  matrix products: 585 us -> 0.86 us
  local copies, waits for them, and re-layouts: 618 us -> 121 us
  Pallas kernels: 0 us -> 116 us
  waiting for transfers between devices: 191 us -> 80 us
  other arithmetic: 95.1 us -> 8.24 us
  blocking collectives: 75.2 us -> 129 us
    dot_general x108 -> x1, matrix products: 585 us -> 0.86 us  [per_device(): jnp.dot(choose, returned.reshape(ny * cap, PB), precision=lax.Precision.H...]
    transpose x3 -> x0, local copies, waits for them, and re-layouts: 134 us -> none  [the longest x1 104 us: per_device(): final_bricks.transpose(1, 3, 5, 0, 2, 4, 6)]
    pallas_call x0 -> x12, Pallas kernels: none -> 116 us  [the longest x1 34.3 us: per_device(): call(functools.partial(encode_kernel, s, cap), 'encode', (grid_shape, spe...]
    reshape x3 -> x5, local copies, waits for them, and re-layouts: 117 us -> 6.06 us  [the longest x2 2.2 us: multipliers(): jnp.concatenate([-w[:, :, 1:2], w[:, :, 1:2]], axis=2)]
    all_to_all x6 -> x4, waiting for transfers between devices: 138 us -> 38.6 us  [the longest x1 22.3 us: to_modes(): spec = lax.all_to_all(spec, 'gx', split_axis=0, concat_axis=0, tiled=True)]
    gather x2 -> x4, local copies, waits for them, and re-layouts: 13.7 us -> 109 us  [the longest x1 105 us: per_device(): mixing = jnp.where(same_bx, mix_w[0][lane_c[None, :], lane_c[:, None]], 0.0)]
    unnamed x69 -> x29, local copies, waits for them, and re-layouts: 93.4 us -> 3.15 us
    squeeze x140 -> x4, local copies, waits for them, and re-layouts: 72.3 us -> 0.29 us  [the longest x2 0.28 us: per_device(): real = last[0] * cos - last[1] * sin]
  transfers between devices with their start and end apart: 7 -> 5, of which waited for: 7 -> 4; matrix products, arithmetic and copies ran while one was open for 2% -> 24% of each run, Pallas kernels for 0% -> 6%
where the time goes in v1:
time: 494 us; the launch traced here: 492 us
  blocking collectives  129 us (26%)
  local copies, waits for them, and re-layouts  121 us (24%)
  Pallas kernels  116 us (23%)
  waiting for transfers between devices  80 us (16%)
  starting transfers between devices  35.8 us (7%)
  other arithmetic  8.24 us (2%)
    gather x1, local copies, waits for them, and re-layouts, per_device(): mixing = jnp.where(same_bx, mix_w[0][lane_c[None, :], lane_c[:, None]], 0.0)  105 us
    all_gather x1, blocking collectives, per_device(): last = lax.all_gather(last, ('gx', 'gy'), axis=0, tiled=False)  68.6 us
    all_to_all x1, waiting for transfers between devices, per_device(): lax.all_to_all(outgoing, 'gy', split_axis=0, concat_axis=0, tiled=True)  41.3 us
    pallas_call x1, Pallas kernels, per_device(): call(functools.partial(encode_kernel, s, cap), 'encode', (grid_shape, spe...  34.3 us
    all_to_all x1, blocking collectives, to_modes(): spec = lax.all_to_all(spec, 'gx', split_axis=0, concat_axis=0, tiled=True)  30.2 us
    all_to_all x1, waiting for transfers between devices, to_modes(): spec = lax.all_to_all(spec, 'gx', split_axis=0, concat_axis=0, tiled=True)  22.3 us
    all_to_all x2, starting transfers between devices, to_modes(): spec = lax.all_to_all(spec, 'gy', split_axis=0, concat_axis=0, tiled=True)  19.9 us
    all_to_all x1, blocking collectives, per_device(): lax.all_to_all(spec.reshape(ny, s.LY, s.LK), 'gy', split_axis=0, concat_a...  18.4 us
  transfers between devices with their start and end apart: 5, of which 4 were waited for; matrix products, arithmetic and copies ran while one was open for 24% of the time, Pallas kernels for 6%

profile of v1, /device:TPU:0, one launch (start us, length us, event | category | flops | bytes accessed | tf_op | source)
XLA Modules:
  0.0 492.2 jit_solution(2728294213531136632)
XLA Ops:
  0.7 6.4 %pack.1 = (f32[8,560,128]{2,1,0:T(8,128)}, s32[128]{0:T(128)}) custom-call(s32[128]{0:T(128)} %brick_ref.1, s32[1]{0:T(128)S(6)} %copy.42.count_ref, f32[3,16384]{1,0:T(4,128)} %pos_ref.1, f32[32,16384]{1,0:T(8,128)} %feat_ref.1, f32[128,128]{1,0:T(8,128)} %bitcast.78), custom_call_target="tpu_custom_call" | custom-call | flops 1000000 | bytes 6000000 | tf_op jit(solution)/shard_map/pack/pallas_call | solution.py:478
  7.1 7.5 %all-to-all-start = ((f32[8,560,128]{2,1,0:T(8,128)}), f32[8,560,128]{2,1,0:T(8,128)S(1)}, u32[]{:S(2)}, u32[]{:S(2)}) async-start(f32[8,560,128]{2,1,0:T(8,128)} %get-tuple-element.12), calls=%async_computation | async-start | bytes 4587520 | tf_op jit(solution)/shard_map/all_to_all | solution.py:488
  14.6 1.2 gather_fusion
  16.1 0.9 bitcast_select_fusion.gain_ref
  16.9 8.4 %field.1.init_ref = f32[8,16,128,128]{3,2,1,0:T(8,128)} custom-call(f32[4,8,16,128]{3,2,1,0:T(8,128)} %bitcast.81, f32[64,2048]{1,0:T(8,128)} %bitcast_select_fusion.gain_ref), custom_call_target="tpu_custom_call" | custom-call | flops 3000000000 | bytes 10000000 | tf_op jit(solution)/shard_map/field/pallas_call | solution.py:513
  25.3 41.3 %all-to-all-done.in_ref = f32[8,560,128]{2,1,0:T(8,128)S(1)} async-done(((f32[8,560,128]{2,1,0:T(8,128)}), f32[8,560,128]{2,1,0:T(8,128)S(1)}, u32[]{:S(2)}, u32[]{:S(2)}) %all-to-all-start) | async-done | bytes 2293792 | tf_op jit(solution)/shard_map/all_to_all | solution.py:488
  67.1 0.9 convert_reduce_fusion.num_ref
  68.0 0.6 pad_add_fusion.id_ref
  68.6 34.3 %encode.1 = (f32[8,16,128,128]{3,2,1,0:T(8,128)}, f32[4,8,4,32,128]{4,3,2,1,0:T(8,128)}) custom-call(s32[8,128]{1,0:T(8,128)} %pad_add_fusion.id_ref, s32[8]{0:T(128)} %convert_reduce_fusion.num_ref, f32[8,560,128]{2,1,0:T(8,128)} %copy-done.2, f32[8,16,128,128]{3,2,1,0:T(8,128)} %field.1.init_ref, bf16[64,256]{1,0:T(8,128)(2,1)} %constant.156.clone.table_ref.fwd_ref), custom_call_target="tpu_custom_call" | custom-call | flops 4000000000 | bytes 22000000 | tf_op jit(solution)/shard_map/encode/pallas_call | solution.py:545
  102.8 30.2 %all_to_all.40 = f32[4,1024,128]{2,1,0:T(8,128)} all-to-all(f32[4,1024,128]{2,1,0:T(8,128)} %bitcast.66), channel_id=1, replica_groups=mesh['gx'=4,'gy'=8] {'gx'}, dimensions={0} | all-to-all | bytes 4194304 | tf_op jit(solution)/shard_map/all_to_all | solution.py:557
  133.1 4.1 x_forward.2
  137.1 16.2 %all-to-all-start.2 = ((f32[8,128,128]{2,1,0:T(8,128)}), f32[8,128,128]{2,1,0:T(8,128)S(1)}, u32[]{:S(2)}, u32[]{:S(2)}) async-start(f32[8,128,128]{2,1,0:T(8,128)} %x_forward.2), calls=%async_computation.2 | async-start | bytes 1048576 | tf_op jit(solution)/shard_map/all_to_all | solution.py:567
  153.9 0.4 slice_negate_fusion.1
  154.4 0.6 pad_maximum_fusion
  154.9 1.1 reshape.383.u_ref
  156.0 1.1 reshape.384.v_ref
  157.1 11.1 %all-to-all-done.2 = f32[8,128,128]{2,1,0:T(8,128)S(1)} async-done(((f32[8,128,128]{2,1,0:T(8,128)}), f32[8,128,128]{2,1,0:T(8,128)S(1)}, u32[]{:S(2)}, u32[]{:S(2)}) %all-to-all-start.2) | async-done | bytes 524320 | tf_op jit(solution)/shard_map/all_to_all | solution.py:567
  168.2 0.8 copy-done.5
  169.0 3.1 y_both.1
  172.1 18.4 %all_to_all.41.in_ref = f32[8,128,128]{2,1,0:T(8,128)} all-to-all(f32[8,128,128]{2,1,0:T(8,128)} %bitcast.73), channel_id=1, replica_groups=mesh['gx'=4,'gy'=8] {'gy'}, dimensions={0} | all-to-all | bytes 1048576 | tf_op jit(solution)/shard_map/all_to_all | solution.py:584
  190.5 5.0 %x_inverse.1 = f32[4096,128]{1,0:T(8,128)} custom-call(f32[8,128,128]{2,1,0:T(8,128)} %all_to_all.41.in_ref, bf16[512,384]{1,0:T(8,128)(2,1)} %constant.161.clone.table_ref), custom_call_target="tpu_custom_call" | custom-call | flops 1000000000 | bytes 3000000 | tf_op jit(solution)/shard_map/x_inverse/pallas_call | solution.py:585
  195.6 3.8 all-to-all-start.4
  199.5 1.2 gather_fusion.3
  200.7 1.7 gather_fusion.2
  202.6 105.2 %gather_fusion.1 = f32[16384]{0:T(1024)S(1)} fusion(f32[32,32]{1,0:T(8,128)S(1)} %slice_bitcast_fusion, s32[16384]{0:T(1024)S(1)} %or_bitcast_fusion), kind=kCustom, calls=%fused_computation.1 | custom fusion | bytes 262144 | tf_op jit(solution)/shard_map/gather | solution.py:524
  307.8 0.7 compare_select_fusion
  308.5 10.5 %mix.1.mixed_ref = f32[8,16,128,128]{3,2,1,0:T(8,128)} custom-call(f32[8,16,128,128]{3,2,1,0:T(8,128)} %get-tuple-element.13.grid_ref, f32[128,128]{1,0:T(8,128)} %get-tuple-element.35.mix_ref, f32[1,128]{1,0:T(1,128)} %bitcast.80), custom_call_target="tpu_custom_call" | custom-call | flops 2000000000 | bytes 17000000 | tf_op jit(solution)/shard_map/mix/pallas_call | solution.py:571
  319.0 1.3 copy-done.3
  320.3 13.3 %layer.1 = (f32[8,16,128,128]{3,2,1,0:T(8,128)}, f32[4,8,4,32,128]{4,3,2,1,0:T(8,128)}) custom-call(f32[8,16,128,128]{3,2,1,0:T(8,128)} %mix.1.mixed_ref, f32[4,8,4,32,128]{4,3,2,1,0:T(8,128)} %bitcast.64, bf16[128,96]{1,0:T(8,128)(2,1)} %constant.157.clone.inv_ref, bf16[64,256]{1,0:T(8,128)(2,1)} %constant.156.clone.table_ref.fwd_ref), custom_call_target="tpu_custom_call" | custom-call | flops 4000000000 | bytes 21000000 | tf_op jit(solution)/shard_map/layer/pallas_call | solution.py:592
  333.6 4.6 all-to-all-start.5
  338.9 0.3 copy.35
  339.2 1.1 reshape.391.u_ref
  340.6 1.1 reshape.392.v_ref
  341.7 22.3 %all-to-all-done.5 = f32[4,1024,128]{2,1,0:T(8,128)} async-done(((f32[4,1024,128]{2,1,0:T(8,128)}), f32[4,1024,128]{2,1,0:T(8,128)}, u32[]{:S(2)}, u32[]{:S(2)}) %all-to-all-start.5) | async-done | bytes 2097184 | tf_op jit(solution)/shard_map/all_to_all | solution.py:557
  364.1 4.1 x_forward.3
  368.2 3.7 all-to-all-start.6
  372.0 0.6 fusion.16
  372.7 8.3 %readout.1 = f32[8,64,128]{2,1,0:T(8,128)} custom-call(f32[8,16,128,128]{3,2,1,0:T(8,128)} %get-tuple-element.16.grid_ref, f32[128,128]{1,0:T(8,128)} %get-tuple-element.34.mix_ref), custom_call_target="tpu_custom_call" | custom-call | flops 2000000000 | bytes 9000000 | tf_op jit(solution)/shard_map/readout/pallas_call | solution.py:603
  381.0 5.2 %all-to-all-done.6 = f32[8,128,128]{2,1,0:T(8,128)S(1)} async-done(((f32[8,128,128]{2,1,0:T(8,128)}), f32[8,128,128]{2,1,0:T(8,128)S(1)}, u32[]{:S(2)}, u32[]{:S(2)}) %all-to-all-start.6) | async-done | bytes 524320 | tf_op jit(solution)/shard_map/all_to_all | solution.py:567
  386.2 0.8 copy-done.6
  387.0 2.2 y_last.1
  389.2 68.6 %all-gather = f32[1024,128]{1,0:T(8,128)S(1)} all-gather(f32[32,128]{1,0:T(8,128)} %y_last.1), channel_id=2, replica_groups=mesh['gx'=4,'gy'=8] {'gx','gy'}, dimensions={0}, use_global_device_ids=true | all-gather | bytes 540672 | tf_op jit(solution)/shard_map/all_gather | solution.py:617
  457.8 1.7 reshape.393
  459.5 1.8 reduce_sum.38
  461.9 0.7 maximum_maximum_fusion.spec_ref
  462.6 16.7 %decode.1 = f32[128,128]{1,0:T(8,128)} custom-call(s32[8,128]{1,0:T(8,128)} %pad_add_fusion.id_ref, s32[8]{0:T(128)} %convert_reduce_fusion.num_ref, f32[1]{0:T(128)} %bitcast.8.base_ref, f32[8,48,128]{2,1,0:T(8,128)} %copy-done.4, f32[32,2048]{1,0:T(8,128)} %maximum_maximum_fusion.spec_ref, f32[512,128]{1,0:T(8,128)} %bitcast.75, ...), custom_call_target="tpu_custom_call" | custom-call | flops 4000000000 | bytes 6000000 | tf_op jit(solution)/shard_map/decode/pallas_call | solution.py:629
  479.3 12.0 %all_to_all.42 = f32[8,16,128]{2,1,0:T(8,128)S(1)} all-to-all(f32[8,16,128]{2,1,0:T(8,128)} %bitcast.79), channel_id=1, replica_groups=mesh['gx'=4,'gy'=8] {'gy'}, dimensions={0} | all-to-all | bytes 131072 | tf_op jit(solution)/shard_map/all_to_all | solution.py:639
  491.3 0.9 convolution_bitcast_fusion
  (64 shorter events, 3.0 us)
Async XLA Ops:
  0.0 14.6 %copy-start = (f32[32]{0:T(128)S(1)}, f32[32]{0:T(128)}, u32[]{:S(2)}) copy-start(f32[32]{0:T(128)} %param.27) | copy-start | bytes 388
  7.1 59.9 %copy-start.10 = (s32[3]{0:T(128)S(1)}, s32[3]{0:T(128)}, u32[]{:S(2)}) copy-start(s32[3]{0:T(128)} %constant.164.clone) | copy-start | bytes 40
  7.1 59.6 %all-to-all-start = ((f32[8,560,128]{2,1,0:T(8,128)}), f32[8,560,128]{2,1,0:T(8,128)S(1)}, u32[]{:S(2)}, u32[]{:S(2)}) async-start(f32[8,560,128]{2,1,0:T(8,128)} %get-tuple-element.12), calls=%async_computation | async-start | bytes 4587520 | tf_op jit(solution)/shard_map/all_to_all | solution.py:488
  66.6 1.9 copy-start.2
  66.7 66.4 %copy-start.4 = (f32[8,48,128]{2,1,0:T(8,128)}, f32[8,48,128]{2,1,0:T(8,128)S(1)}, u32[]{:S(2)}) copy-start(f32[8,48,128]{2,1,0:T(8,128)S(1)} %slice.89.pos_ref) | copy-start | bytes 589828
  68.6 84.8 %copy-start.7 = (f32[2,2,2,8,1024]{4,3,2,1,0:T(8,128)S(1)}, f32[2,2,2,8,1024]{4,3,2,1,0:T(8,128)}, u32[]{:S(2)}) copy-start(f32[2,2,2,8,1024]{4,3,2,1,0:T(8,128)} %param.30) | copy-start | bytes 786436
  137.1 31.1 %all-to-all-start.2 = ((f32[8,128,128]{2,1,0:T(8,128)}), f32[8,128,128]{2,1,0:T(8,128)S(1)}, u32[]{:S(2)}, u32[]{:S(2)}) async-start(f32[8,128,128]{2,1,0:T(8,128)} %x_forward.2), calls=%async_computation.2 | async-start | bytes 1048576 | tf_op jit(solution)/shard_map/all_to_all | solution.py:567
  153.9 45.4 %copy-start.8 = (f32[2,32,32]{2,1,0:T(8,128)S(1)}, f32[2,32,32]{2,1,0:T(8,128)}, u32[]{:S(2)}) copy-start(f32[2,32,32]{2,1,0:T(8,128)} %param.28) | copy-start | bytes 24580
  153.9 45.4 %copy-start.11 = (f32[32]{0:T(128)S(1)}, f32[32]{0:T(128)}, u32[]{:S(2)}) copy-start(f32[32]{0:T(128)} %param.31) | copy-start | bytes 388
  154.4 46.3 %copy-start.13 = (f32[2,32]{1,0:T(2,128)S(1)}, f32[2,32]{1,0:T(2,128)}, u32[]{:S(2)}) copy-start(f32[2,32]{1,0:T(2,128)} %param.29) | copy-start | bytes 772
  168.2 0.8 copy-start.5
  195.6 123.4 %all-to-all-start.4 = ((f32[4,1024,128]{2,1,0:T(8,128)}), f32[4,1024,128]{2,1,0:T(8,128)S(1)}, u32[]{:S(2)}, u32[]{:S(2)}) async-start(f32[4,1024,128]{2,1,0:T(8,128)} %bitcast.65), calls=%async_computation.4 | async-start | bytes 4194304 | tf_op jit(solution)/shard_map/all_to_all | solution.py:588
  319.0 1.3 copy-start.3
  333.6 38.2 %copy-start.12 = (s32[32]{0:T(128)S(1)}, s32[32]{0:T(128)}, u32[]{:S(2)}) copy-start(s32[32]{0:T(128)} %constant.165.clone) | copy-start | bytes 388
  333.6 30.4 %all-to-all-start.5 = ((f32[4,1024,128]{2,1,0:T(8,128)}), f32[4,1024,128]{2,1,0:T(8,128)}, u32[]{:S(2)}, u32[]{:S(2)}) async-start(f32[4,1024,128]{2,1,0:T(8,128)} %bitcast.63), calls=%async_computation.5 | async-start | bytes 4194304 | tf_op jit(solution)/shard_map/all_to_all | solution.py:557
  368.2 18.0 %all-to-all-start.6 = ((f32[8,128,128]{2,1,0:T(8,128)}), f32[8,128,128]{2,1,0:T(8,128)S(1)}, u32[]{:S(2)}, u32[]{:S(2)}) async-start(f32[8,128,128]{2,1,0:T(8,128)} %x_forward.3), calls=%async_computation.6 | async-start | bytes 1048576 | tf_op jit(solution)/shard_map/all_to_all | solution.py:567
  386.2 0.8 copy-start.6
  461.5 29.8 %copy-start.9 = (s32[128]{0:T(128)S(1)}, s32[128]{0:T(128)}, u32[]{:S(2)}) copy-start(s32[128]{0:T(128)} %get-tuple-element.11) | copy-start | bytes 1540
  461.5 30.6 %copy-start.1 = (f32[32]{0:T(128)S(1)}, f32[32]{0:T(128)}, u32[]{:S(2)}) copy-start(f32[32]{0:T(128)} %param.27) | copy-start | bytes 388

commit v2 on v1

--- a/solution.py
+++ b/solution.py
@@ -15,7 +15,7 @@
 F32 = jnp.float32
 VM = pl.BlockSpec(memory_space=pltpu.VMEM)
 SM = pl.BlockSpec(memory_space=pltpu.SMEM)
-LIMIT = 56 * 1024 * 1024
+LIMIT = 32 * 1024 * 1024
 
 
 def split(x):
@@ -94,7 +94,9 @@
     t["z_fwd"] = stack_left(np.concatenate([c, -n], 0))
     back = np.where(np.arange(s.KZ) == 0, 1.0, 2.0)[None, :] / s.G
     c, n = trig(s, np.arange(s.G), np.arange(s.KZ))
-    t["z_inv"] = wide_left(np.concatenate([c * back, -n * back], 1))
+    c, n = c * back, -n * back
+    t["z_inv"] = wide_left(np.concatenate([c, n], 1))
+    t["z_last"] = wide_left(np.stack([c.reshape(s.G, s.ny, s.KL), n.reshape(s.G, s.ny, s.KL)], 2).reshape(s.G, -1))
     order = np.arange(s.G).reshape(s.nx, s.bxn, B).transpose(0, 2, 1).reshape(-1)
     c, n = trig(s, s.freq, order)
     hi, lo = np_split(np.concatenate([np.concatenate([c, n], 1), np.concatenate([-n, c], 1)], 0))
@@ -232,36 +234,41 @@
     group = lax.broadcasted_iota(jnp.int32, (s.L, 128), 0) // s.cp % s.bxn
 
     def per_source(src, carry):
-        def per_block(j, inner):
-            slot = src * cap + j
-            bx, by, bz = id_ref[0, slot], id_ref[1, slot], id_ref[2, slot]
-            points = [
-                jnp.broadcast_to(in_ref[src, pl.ds(cap * C + d * cap + j, 1), :], (8, 128))
-                for d in range(3)
-            ]
-            points = [p - id_ref[3 + d, slot].astype(F32) for d, p in enumerate(points)]
-            weights = jnp.concatenate(kernel_tiles(points), axis=0)
-            feats = in_ref[src, pl.ds(pl.multiple_of(j * C, 8), C), :]
-            spread = []
-            for g in range(s.nx):
-                spread += [feats[g * s.cp : (g + 1) * s.cp]] * s.bxn
-            spread = jnp.where(group == bx, jnp.concatenate(spread, axis=0), 0.0)
-            whi, wlo = split(weights)
-            fhi, flo = split(spread)
-            left = jnp.concatenate([whi, wlo], axis=1)
-            right = jnp.concatenate([fhi, fhi], axis=1)
-            if s.L == 128:
-                under = jnp.concatenate([flo, jnp.zeros_like(flo)], axis=1)
-                res = dot(left, jnp.concatenate([right, under], axis=0), NT)
-                res = res[:, : s.L] + res[:, s.L :]
-            else:
-                res = dot(left, right, NT) + dot(whi, flo, NT)
-            ys = pl.ds(pl.multiple_of(by * B, B), B)
-            zs = pl.ds(pl.multiple_of(bz * B, B), B)
-            grid_ref[:, ys, zs, :] = grid_ref[:, ys, zs, :] + res.reshape(B, B, B, s.L)
+        def per_pair(h, inner):
+            results = []
+            for i in range(2):
+                j = h * 2 + i
+                slot = src * cap + j
+                points = [
+                    jnp.broadcast_to(in_ref[src, pl.ds(cap * C + d * cap + j, 1), :], (8, 128))
+                    - id_ref[3 + d, slot].astype(F32)
+                    for d in range(3)
+                ]
+                weights = jnp.concatenate(kernel_tiles(points), axis=0)
+                feats = in_ref[src, pl.ds(pl.multiple_of(j * C, 8), C), :]
+                spread = []
+                for g in range(s.nx):
+                    spread += [feats[g * s.cp : (g + 1) * s.cp]] * s.bxn
+                spread = jnp.where(group == id_ref[0, slot], jnp.concatenate(spread, axis=0), 0.0)
+                whi, wlo = split(weights)
+                fhi, flo = split(spread)
+                left = jnp.concatenate([whi, wlo], axis=1)
+                right = jnp.concatenate([fhi, fhi], axis=1)
+                if s.L == 128:
+                    under = jnp.concatenate([flo, jnp.zeros_like(flo)], axis=1)
+                    res = dot(left, jnp.concatenate([right, under], axis=0), NT)
+                    res = res[:, : s.L] + res[:, s.L :]
+                else:
+                    res = dot(left, right, NT) + dot(whi, flo, NT)
+                results.append(res.reshape(B, B, B, s.L))
+            for i in range(2):
+                slot = src * cap + h * 2 + i
+                ys = pl.ds(pl.multiple_of(id_ref[1, slot] * B, B), B)
+                zs = pl.ds(pl.multiple_of(id_ref[2, slot] * B, B), B)
+                grid_ref[:, ys, zs, :] = grid_ref[:, ys, zs, :] + results[i]
             return inner
 
-        return lax.fori_loop(0, num_ref[src], per_block, carry)
+        return lax.fori_loop(0, (num_ref[src] + 1) // 2, per_pair, carry)
 
     lax.fori_loop(0, s.ny, per_source, 0)
 
@@ -362,7 +369,10 @@
     for c in range(0, s.cp, 2):
         prods = y_spectrum(s, in_ref, fwd_ref[...], u_ref, v_ref, (c, c + 1))
         total = total + prods[0] + prods[1]
-    out_ref[...] = total
+    M = s.M
+    for r in range(2 * s.KL):
+        part = total[:, r * M : (r + 1) * M]
+        out_ref[r : r + 1, :] = jnp.concatenate([part[m : m + 1] for m in range(M)], axis=1)
 
 
 def x_inverse_kernel(s, in_ref, table_ref, out_ref):
@@ -398,8 +408,15 @@
             spec_ref[g, 0, b] = out[g * s.bxn + b]
 
 
-def decode_kernel(s, cap, id_ref, num_ref, base_ref, pos_ref, spec_ref, mix_ref, hi_ref, lo_ref, inv_ref, out_ref, s_ref):
-    mhi, mlo = split(spec_ref[...])
+def decode_kernel(s, cap, id_ref, num_ref, base_ref, pos_ref, spec_ref, turn_ref, mix_ref, hi_ref, lo_ref, inv_ref, out_ref, s_ref):
+    modes = jnp.concatenate([spec_ref[i] for i in range(s.ny)], axis=0)
+    real_row = lax.broadcasted_iota(jnp.int32, modes.shape, 0) // s.KL % 2 == 0
+
+    def partner(x):
+        return jnp.where(real_row, -pltpu.roll(x, s.K2 - s.KL, 0), pltpu.roll(x, s.KL, 0))
+
+    modes = modes * turn_ref[0:1, :] + partner(modes) * turn_ref[1:2, :]
+    mhi, mlo = split(jnp.concatenate([modes, partner(modes)], axis=1))
     wave = dot(jnp.concatenate([mhi, mlo], axis=0), hi_ref[...])
     wave = wave[: s.K2] + wave[s.K2 :] + dot(mhi, lo_ref[...])
     hi, lo = split(wave)
@@ -486,22 +503,25 @@
         scratch=[pltpu.SMEM((ny,), jnp.int32)],
     )(block_brick, block_count, positions, point_feat, area.reshape(blocks, PB))
     incoming = lax.all_to_all(outgoing, "gy", split_axis=0, concat_axis=0, tiled=True)
-    in_pos = incoming[:, cap * C :, :]
-    first = in_pos.reshape(ny, 3, cap, PB)[..., 0].transpose(1, 0, 2).reshape(3, ny * cap)
-    counts = jnp.sum((first[0].reshape(ny, cap) >= 0.0).astype(jnp.int32), axis=1)
-    brick = jnp.floor(first / B).astype(jnp.int32)
-    start = jnp.stack([row_x * s.bxn, row_y * s.byn, jnp.zeros_like(row_x)])
-    limit = jnp.array([s.bxn - 1, s.byn - 1, s.NB - 1], jnp.int32)
-    local = jnp.clip(brick - start[:, None], 0, limit[:, None])
-    corner = (local + start[:, None]) * B
-    flat = local[2] * (s.bxn * s.byn) + local[0] * s.byn + local[1]
-    ids = jnp.concatenate([local, corner, flat[None], flat[None]], axis=0)
+
+    def placement(incoming):
+        in_pos = incoming[:, cap * C :, :]
+        first = in_pos.reshape(ny, 3, cap, PB)[..., 0].transpose(1, 0, 2).reshape(3, ny * cap)
+        counts = jnp.sum((first[0].reshape(ny, cap) >= 0.0).astype(jnp.int32), axis=1)
+        brick = jnp.floor(first / B).astype(jnp.int32)
+        start = jnp.stack([row_x * s.bxn, row_y * s.byn, jnp.zeros_like(row_x)])
+        limit = jnp.array([s.bxn - 1, s.byn - 1, s.NB - 1], jnp.int32)
+        local = jnp.clip(brick - start[:, None], 0, limit[:, None])
+        corner = (local + start[:, None]) * B
+        flat = local[2] * (s.bxn * s.byn) + local[0] * s.byn + local[1]
+        owned = jnp.where(first[0:1] >= 0.0, local[0:1], -1)
+        ids = jnp.concatenate([owned, local[1:], corner, flat[None], flat[None]], axis=0)
+        return ids, counts, in_pos
 
     lane = jnp.arange(L)
     lane_bx = lane // s.cp % s.bxn
-    lane_c = lane // (s.bxn * s.cp) * s.cp + lane % s.cp
     same_bx = lane_bx[:, None] == lane_bx[None, :]
-    gain_l = grid_gain[lane_c]
+    gain_l = jnp.broadcast_to(grid_gain.reshape(nx, 1, s.cp), (nx, s.bxn, s.cp)).reshape(L)
     spread = (
         (jnp.arange(s.bxn)[:, None, None, None] == lane_bx[None, None, None, :])
         & (jnp.arange(s.Yl)[None, :, None, None] == jnp.arange(s.Yl)[None, None, :, None])
@@ -521,12 +541,15 @@
         grid=(B,),
     )(sdf.reshape(s.bxn, B, s.Yl, G), gains)
 
-    mixing = jnp.where(same_bx, mix_w[0][lane_c[None, :], lane_c[:, None]], 0.0)
-    bias = mix_b[0][lane_c][None, :]
+    on_lanes = lambda v: jnp.broadcast_to(v.reshape(nx, 1, s.cp), (nx, s.bxn, s.cp)).reshape(1, L)
+    mixing = mix_w[0].T.reshape(nx, 1, s.cp, nx, 1, s.cp)
+    mixing = jnp.broadcast_to(mixing, (nx, s.bxn, s.cp, nx, s.bxn, s.cp)).reshape(L, L)
+    mixing = jnp.where(same_bx, mixing, 0.0)
+    bias = on_lanes(mix_b[0])
     read_mix = jnp.sum(readout_w[:, None] * mix_w[1], axis=0)
     base = jnp.sum(readout_w * mix_b[1]).reshape(1)
     out_lane = jnp.arange(s.LB)
-    reading = jnp.where(lane_bx[:, None] == out_lane[None, :] // s.byn % s.bxn, read_mix[lane_c][:, None], 0.0)
+    reading = jnp.where(lane_bx[:, None] == out_lane[None, :] // s.byn % s.bxn, on_lanes(read_mix).reshape(L, 1), 0.0)
     mine = lax.dynamic_slice_in_dim(readout_w, row_x * s.cp, s.cp)
 
     def multipliers(w, scale):
@@ -540,6 +563,14 @@
 
     u0, v0 = multipliers(spec_w[0], None)
     u1, v1 = multipliers(spec_w[1], mine)
+
+    freq = jnp.asarray(s.freq, jnp.int32)
+    turn = jnp.mod(freq[None, :] * (row_x * s.Xl) + freq[:, None] * (row_y * s.Yl), G).reshape(1, -1)
+    angle = turn.astype(F32) * (2.0 * math.pi / G)
+    turns = jnp.concatenate([jnp.cos(angle), jnp.sin(angle)], axis=0)
+    prepared = (incoming, init, mixing, bias, base, reading, u0, v0, u1, v1, turns)
+    incoming, init, mixing, bias, base, reading, u0, v0, u1, v1, turns = lax.optimization_barrier(prepared)
+    ids, counts, in_pos = placement(incoming)
 
     spec_shape = shape(nx, B, s.bxn, s.K2, s.LY)
     grid0, spec = call(
@@ -611,31 +642,25 @@
         grid=(B,),
     )(grid1, reading)
     last = call(
-        functools.partial(y_last_kernel, s), "y_last", shape(M, s.LK), [VM] * 4, VM, 1e9, 1e6
+        functools.partial(y_last_kernel, s), "y_last", shape(2 * s.KL, M * M), [VM] * 4, VM, 1e9, 1e6
     )(spec, t["y_fwd"], u1, v1)
 
-    last = lax.all_gather(last, ("gx", "gy"), axis=0, tiled=False)
-    last = jnp.sum(last.reshape(nx, ny, M, 2, s.KL, M), axis=0)
-    last = last.transpose(2, 0, 3, 1, 4).reshape(2, s.KZ, M * M)
-    freq = jnp.asarray(s.freq, jnp.int32)
-    turn = jnp.mod(freq[None, :] * (row_x * s.Xl) + freq[:, None] * (row_y * s.Yl), G).reshape(-1)
-    angle = turn.astype(F32) * (2.0 * math.pi / G)
-    cos, sin = jnp.cos(angle), jnp.sin(angle)
-    real = last[0] * cos - last[1] * sin
-    imag = last[1] * cos + last[0] * sin
-    left = jnp.concatenate(
-        [jnp.concatenate([real, -imag], axis=1), jnp.concatenate([imag, real], axis=1)], axis=0
-    )
+    step = 1
+    while step < nx:
+        last = last + lax.ppermute(last, "gx", [(i, i ^ step) for i in range(nx)])
+        step *= 2
+    last = jnp.broadcast_to(last[None], (ny,) + last.shape)
+    last = lax.all_to_all(last, "gy", split_axis=0, concat_axis=0, tiled=True)
     values = call(
         functools.partial(decode_kernel, s, cap),
         "decode",
         shape(ny * cap, PB),
-        [SM, SM, SM] + [VM] * 6,
+        [SM, SM, SM] + [VM] * 7,
         VM,
         4e9,
         6e6,
         scratch=[pltpu.VMEM((B * B * B, s.LB), F32)],
-    )(ids, counts, base, in_pos, left, read.reshape(B * B * B, s.LB), t["xy_hi"], t["xy_lo"], t["z_inv"])
+    )(ids, counts, base, in_pos, last, turns, read.reshape(B * B * B, s.LB), t["xy_hi"], t["xy_lo"], t["z_last"])
     returned = lax.all_to_all(values.reshape(ny, cap, PB), "gy", split_axis=0, concat_axis=0, tiled=True)
     choose = (slot_of[:, None] == jnp.arange(ny * cap, dtype=jnp.int32)[None, :]).astype(F32)
     pressure = jnp.dot(choose, returned.reshape(ny * cap, PB), precision=lax.Precision.HIGHEST)

time: 494 us -> 328 us (0.66)
  local copies, waits for them, and re-layouts: 121 us -> 51.8 us
  waiting for transfers between devices: 80 us -> 45.1 us
  Pallas kernels: 116 us -> 89.8 us
  starting transfers between devices: 35.8 us -> 16 us
  blocking collectives: 129 us -> 118 us
    gather x4 -> x0, local copies, waits for them, and re-layouts: 109 us -> none  [the longest x1 105 us: per_device(): mixing = jnp.where(same_bx, mix_w[0][lane_c[None, :], lane_c[:, None]], 0.0)]
    all_gather x1 -> x0, blocking collectives: 68.6 us -> none  [per_device(): last = lax.all_gather(last, ('gx', 'gy'), axis=0, tiled=False)]
    all_to_all x3 -> x1, waiting for transfers between devices: 38.6 us -> 0.19 us  [per_device(): last = lax.all_to_all(last, 'gy', split_axis=0, concat_axis=0, tiled=True)]
    all_to_all x0 -> x2, blocking collectives: none -> 34.4 us  [to_modes(): spec = lax.all_to_all(spec, 'gy', split_axis=0, concat_axis=0, tiled=True)]
    unnamed x29 -> x63, local copies, waits for them, and re-layouts: 3.15 us -> 36.8 us
    all_to_all x1 -> x2, blocking collectives: 30.2 us -> 56.4 us  [to_modes(): spec = lax.all_to_all(spec, 'gx', split_axis=0, concat_axis=0, tiled=True)]
    all_to_all x3 -> x1, starting transfers between devices: 24.6 us -> 3.64 us  [per_device(): last = lax.all_to_all(last, 'gy', split_axis=0, concat_axis=0, tiled=True)]
    all_to_all x1, waiting for transfers between devices: 41.3 us -> 25.4 us  [per_device(): lax.all_to_all(outgoing, 'gy', split_axis=0, concat_axis=0, tiled=True)]
  transfers between devices with their start and end apart: 5 -> 5, of which waited for: 4 -> 5; matrix products, arithmetic and copies ran while one was open for 24% -> 6% of each run, Pallas kernels for 6% -> 4%
where the time goes in v2:
time: 328 us; the launch traced here: 327 us
  blocking collectives  118 us (36%)
  Pallas kernels  89.8 us (27%)
  local copies, waits for them, and re-layouts  51.8 us (16%)
  waiting for transfers between devices  45.1 us (14%)
  starting transfers between devices  16 us (5%)
  other arithmetic  4.41 us (1%)
    all_to_all x2, blocking collectives, to_modes(): spec = lax.all_to_all(spec, 'gx', split_axis=0, concat_axis=0, tiled=True)  56.4 us
    unnamed x63, local copies, waits for them, and re-layouts  36.8 us
    all_to_all x2, blocking collectives, to_modes(): spec = lax.all_to_all(spec, 'gy', split_axis=0, concat_axis=0, tiled=True)  34.4 us
    pallas_call x1, Pallas kernels, per_device(): call(functools.partial(encode_kernel, s, cap), 'encode', (grid_shape, spe...  32.5 us
    all_to_all x1, waiting for transfers between devices, per_device(): lax.all_to_all(outgoing, 'gy', split_axis=0, concat_axis=0, tiled=True)  25.4 us
    pallas_call x1, Pallas kernels, per_device(): call(functools.partial(decode_kernel, s, cap), 'decode', shape(ny * cap,...  21.2 us
    all_to_all x1, blocking collectives, per_device(): lax.all_to_all(spec.reshape(ny, s.LY, s.LK), 'gy', split_axis=0, concat_a...  17.5 us
    all_to_all x1, waiting for transfers between devices, per_device(): lax.all_to_all(spec.reshape(nx, B * s.bxn * s.K2, s.LY), 'gx', split_axis...  15.4 us
  transfers between devices with their start and end apart: 5, of which 5 were waited for; matrix products, arithmetic and copies ran while one was open for 6% of the time, Pallas kernels for 4%

profile of v2, /device:TPU:0, one launch (start us, length us, event | category | flops | bytes accessed | tf_op | source)
XLA Modules:
  0.0 326.8 jit_solution(241841816898504293)
XLA Ops:
  0.7 1.6 copy-done.7
  2.2 0.9 copy-done.9
  4.7 4.7 %pack.1 = (f32[8,560,128]{2,1,0:T(8,128)S(1)}, s32[128]{0:T(128)S(1)}) custom-call(s32[128]{0:T(128)S(1)} %copy-done.11, s32[1]{0:T(128)S(6)} %copy.35.count_ref, f32[3,16384]{1,0:T(4,128)S(1)} %copy-done.9, f32[32,16384]{1,0:T(8,128)S(1)} %copy-done.7, f32[128,128]{1,0:T(8,128)S(1)} %bitcast.64), custom_call_target="tpu_custom_call" | custom-call | flops 1000000 | bytes 6000000 | tf_op jit(solution)/shard_map/pack/pallas_call | solution.py:495
  9.4 1.4 copy-done.6
  10.8 7.8 %all-to-all-start = ((f32[8,560,128]{2,1,0:T(8,128)}), f32[8,560,128]{2,1,0:T(8,128)S(1)}, u32[]{:S(2)}, u32[]{:S(2)}) async-start(f32[8,560,128]{2,1,0:T(8,128)} %copy-done.6), calls=%async_computation | async-start | bytes 4587520 | tf_op jit(solution)/shard_map/all_to_all | solution.py:505
  21.9 1.0 copy.29
  22.9 1.5 reshape.368.u_ref
  25.1 1.1 reshape_squeeze.8
  26.2 1.0 copy.28
  27.2 1.2 slice_negate_fusion.1
  28.4 1.3 pad_maximum_fusion
  30.2 1.5 reshape.367.v_ref
  31.7 2.1 broadcast_in_dim.90
  33.8 2.3 reshape.363
  37.2 5.0 %field.1.init_ref = f32[8,16,128,128]{3,2,1,0:T(8,128)S(1)} custom-call(f32[4,8,16,128]{3,2,1,0:T(8,128)S(1)} %bitcast.66, f32[64,2048]{1,0:T(8,128)S(1)} %bitcast_select_fusion.gain_ref), custom_call_target="tpu_custom_call" | custom-call | flops 3000000000 | bytes 10000000 | tf_op jit(solution)/shard_map/field/pallas_call | solution.py:533
  42.2 3.3 %copy-done.22 = f32[8,16,128,128]{3,2,1,0:T(8,128)} copy-done((f32[8,16,128,128]{3,2,1,0:T(8,128)}, f32[8,16,128,128]{3,2,1,0:T(8,128)S(1)}, u32[]{:S(2)}) %copy-start.22) | copy-done | bytes 8388632
  45.5 25.4 %all-to-all-done.in_ref = f32[8,560,128]{2,1,0:T(8,128)S(1)} async-done(((f32[8,560,128]{2,1,0:T(8,128)}), f32[8,560,128]{2,1,0:T(8,128)S(1)}, u32[]{:S(2)}, u32[]{:S(2)}) %all-to-all-start) | async-done | bytes 2293792 | tf_op jit(solution)/shard_map/all_to_all | solution.py:505
  71.6 3.4 %copy-done.23 = f32[8,16,128,128]{3,2,1,0:T(8,128)S(1)} copy-done((f32[8,16,128,128]{3,2,1,0:T(8,128)S(1)}, f32[8,16,128,128]{3,2,1,0:T(8,128)}, u32[]{:S(2)}) %copy-start.23) | copy-done | bytes 8388632
  75.0 32.5 %encode.1 = (f32[8,16,128,128]{3,2,1,0:T(8,128)S(1)}, f32[4,8,4,32,128]{4,3,2,1,0:T(8,128)S(1)}) custom-call(s32[8,128]{1,0:T(8,128)S(1)} %concatenate.23.id_ref, s32[8]{0:T(128)S(1)} %get-tuple-element.39.num_ref, f32[8,560,128]{2,1,0:T(8,128)S(1)} %all-to-all-done.in_ref, f32[8,16,128,128]{3,2,1,0:T(8,128)S(1)} %copy-done.23, bf16[64,256]{1,0:T(8,128)(2,1)S(1)} %copy-done.20), custom_call_target="tpu_custom_call" | custom-call | flops 4000000000 | bytes 22000000 | tf_op jit(solution)/shard_map/encode/pallas_call | solution.py:576
  107.5 3.3 %copy-done = f32[8,16,128,128]{3,2,1,0:T(8,128)} copy-done((f32[8,16,128,128]{3,2,1,0:T(8,128)}, f32[8,16,128,128]{3,2,1,0:T(8,128)S(1)}, u32[]{:S(2)}) %copy-start) | copy-done | bytes 8388632
  110.8 28.3 %all_to_all.45 = f32[4,1024,128]{2,1,0:T(8,128)S(1)} all-to-all(f32[4,1024,128]{2,1,0:T(8,128)S(1)} %bitcast.56), channel_id=1, replica_groups=mesh['gx'=4,'gy'=8] {'gx'}, dimensions={0} | all-to-all | bytes 4194304 | tf_op jit(solution)/shard_map/all_to_all | solution.py:588
  139.1 1.7 x_forward.2
  140.8 16.9 %all_to_all.46 = f32[8,128,128]{2,1,0:T(8,128)S(1)} all-to-all(f32[8,128,128]{2,1,0:T(8,128)S(1)} %x_forward.2), channel_id=1, replica_groups=mesh['gx'=4,'gy'=8] {'gy'}, dimensions={0} | all-to-all | bytes 1048576 | tf_op jit(solution)/shard_map/all_to_all | solution.py:598
  157.6 1.0 y_both.1
  158.7 17.5 %all_to_all.47.in_ref = f32[8,128,128]{2,1,0:T(8,128)S(1)} all-to-all(f32[8,128,128]{2,1,0:T(8,128)S(1)} %bitcast.61), channel_id=1, replica_groups=mesh['gx'=4,'gy'=8] {'gy'}, dimensions={0} | all-to-all | bytes 1048576 | tf_op jit(solution)/shard_map/all_to_all | solution.py:615
  176.3 2.5 x_inverse.1
  178.8 1.4 copy-done.8
  180.2 3.6 %all-to-all-start.4 = ((f32[4,1024,128]{2,1,0:T(8,128)}), f32[4,1024,128]{2,1,0:T(8,128)S(1)}, u32[]{:S(2)}, u32[]{:S(2)}) async-start(f32[4,1024,128]{2,1,0:T(8,128)} %bitcast.54), calls=%async_computation.4 | async-start | bytes 4194304 | tf_op jit(solution)/shard_map/all_to_all | solution.py:619
  183.8 3.4 %copy-done.1 = f32[8,16,128,128]{3,2,1,0:T(8,128)S(1)} copy-done((f32[8,16,128,128]{3,2,1,0:T(8,128)S(1)}, f32[8,16,128,128]{3,2,1,0:T(8,128)}, u32[]{:S(2)}) %copy-start.1) | copy-done | bytes 8388632
  187.1 3.6 %mix.1.mixed_ref = f32[8,16,128,128]{3,2,1,0:T(8,128)S(1)} custom-call(f32[8,16,128,128]{3,2,1,0:T(8,128)S(1)} %copy-done.1, f32[128,128]{1,0:T(8,128)S(1)} %get-tuple-element.28.mix_ref, f32[1,128]{1,0:T(1,128)S(1)} %reshape.364.bias_ref), custom_call_target="tpu_custom_call" | custom-call | flops 2000000000 | bytes 17000000 | tf_op jit(solution)/shard_map/mix/pallas_call | solution.py:602
  190.8 3.3 %copy-done.2 = f32[8,16,128,128]{3,2,1,0:T(8,128)} copy-done((f32[8,16,128,128]{3,2,1,0:T(8,128)}, f32[8,16,128,128]{3,2,1,0:T(8,128)S(1)}, u32[]{:S(2)}) %copy-start.2) | copy-done | bytes 8388632
  194.1 15.4 %all-to-all-done.4 = f32[4,1024,128]{2,1,0:T(8,128)S(1)} async-done(((f32[4,1024,128]{2,1,0:T(8,128)}), f32[4,1024,128]{2,1,0:T(8,128)S(1)}, u32[]{:S(2)}, u32[]{:S(2)}) %all-to-all-start.4) | async-done | bytes 2097184 | tf_op jit(solution)/shard_map/all_to_all | solution.py:619
  209.4 3.4 %copy-done.3 = f32[8,16,128,128]{3,2,1,0:T(8,128)S(1)} copy-done((f32[8,16,128,128]{3,2,1,0:T(8,128)S(1)}, f32[8,16,128,128]{3,2,1,0:T(8,128)}, u32[]{:S(2)}) %copy-start.3) | copy-done | bytes 8388632
  212.8 11.3 %layer.1 = (f32[8,16,128,128]{3,2,1,0:T(8,128)S(1)}, f32[4,8,4,32,128]{4,3,2,1,0:T(8,128)S(1)}) custom-call(f32[8,16,128,128]{3,2,1,0:T(8,128)S(1)} %copy-done.3, f32[4,8,4,32,128]{4,3,2,1,0:T(8,128)S(1)} %bitcast.53, bf16[128,96]{1,0:T(8,128)(2,1)S(1)} %copy-done.21, bf16[64,256]{1,0:T(8,128)(2,1)S(1)} %copy-done.20), custom_call_target="tpu_custom_call" | custom-call | flops 4000000000 | bytes 21000000 | tf_op jit(solution)/shard_map/layer/pallas_call | solution.py:623
  224.2 3.3 %copy-done.4 = f32[8,16,128,128]{3,2,1,0:T(8,128)} copy-done((f32[8,16,128,128]{3,2,1,0:T(8,128)}, f32[8,16,128,128]{3,2,1,0:T(8,128)S(1)}, u32[]{:S(2)}) %copy-start.4) | copy-done | bytes 8388632
  227.4 28.2 %all_to_all.48 = f32[4,1024,128]{2,1,0:T(8,128)S(1)} all-to-all(f32[4,1024,128]{2,1,0:T(8,128)S(1)} %bitcast.55), channel_id=1, replica_groups=mesh['gx'=4,'gy'=8] {'gx'}, dimensions={0} | all-to-all | bytes 4194304 | tf_op jit(solution)/shard_map/all_to_all | solution.py:588
  255.6 1.7 x_forward.3
  257.3 17.6 %all_to_all.49 = f32[8,128,128]{2,1,0:T(8,128)S(1)} all-to-all(f32[8,128,128]{2,1,0:T(8,128)S(1)} %x_forward.3), channel_id=1, replica_groups=mesh['gx'=4,'gy'=8] {'gy'}, dimensions={0} | all-to-all | bytes 1048576 | tf_op jit(solution)/shard_map/all_to_all | solution.py:598
  275.6 1.2 collective-permute-done
  277.6 2.9 collective-permute-done.1
  281.2 3.6 %all-to-all-start.7 = ((f32[8,4,1024]{2,1,0:T(4,128)}), f32[8,4,1024]{2,1,0:T(4,128)S(1)}, u32[]{:S(2)}, u32[]{:S(2)}) async-start(f32[8,4,1024]{2,1,0:T(4,128)} %broadcast_in_dim.98), calls=%async_computation.7 | async-start | bytes 262144 | tf_op jit(solution)/shard_map/all_to_all | solution.py:653
  284.8 3.4 %copy-done.5 = f32[8,16,128,128]{3,2,1,0:T(8,128)S(1)} copy-done((f32[8,16,128,128]{3,2,1,0:T(8,128)S(1)}, f32[8,16,128,128]{3,2,1,0:T(8,128)}, u32[]{:S(2)}) %copy-start.5) | copy-done | bytes 8388632
  288.2 3.8 %readout.1 = f32[8,64,128]{2,1,0:T(8,128)S(1)} custom-call(f32[8,16,128,128]{3,2,1,0:T(8,128)S(1)} %copy-done.5, f32[128,128]{1,0:T(8,128)S(1)} %get-tuple-element.38.mix_ref), custom_call_target="tpu_custom_call" | custom-call | flops 2000000000 | bytes 9000000 | tf_op jit(solution)/shard_map/readout/pallas_call | solution.py:634
  292.2 1.6 copy-done.13
  293.8 1.6 copy-done.14
  295.3 21.2 %decode.1 = f32[128,128]{1,0:T(8,128)S(1)} custom-call(s32[8,128]{1,0:T(8,128)S(1)} %concatenate.23.id_ref, s32[8]{0:T(128)S(1)} %get-tuple-element.39.num_ref, f32[1]{0:T(128)} %bitcast.6.base_ref, f32[8,48,128]{2,1,0:T(8,128)S(1)} %slice.68.pos_ref, f32[8,4,1024]{2,1,0:T(4,128)S(1)} %all-to-all-done.7.spec_ref, f32[2,1024]{1,0:T(2,128)S(1)} %pad_maximum_fusion.4.turn_ref, ...), custom_call_target="tpu_custom_call" | custom-call | flops 4000000000 | bytes 6000000 | tf_op jit(solution)/shard_map/decode/pallas_call | solution.py:654
  316.5 9.4 %all_to_all.50 = f32[8,16,128]{2,1,0:T(8,128)S(1)} all-to-all(f32[8,16,128]{2,1,0:T(8,128)S(1)} %bitcast.65), channel_id=1, replica_groups=mesh['gx'=4,'gy'=8] {'gy'}, dimensions={0} | all-to-all | bytes 131072 | tf_op jit(solution)/shard_map/all_to_all | solution.py:664
  325.9 0.9 convolution_bitcast_fusion
  (103 shorter events, 9.9 us)
Async XLA Ops:
  0.7 1.6 copy-start.7
  2.2 0.9 copy-start.9
  3.2 0.8 copy-start.10
  4.0 0.7 copy-start.11
  9.4 1.4 copy-start.6
  10.8 7.9 %copy-start.30 = (f32[2,32]{1,0:T(2,128)S(1)}, f32[2,32]{1,0:T(2,128)}, u32[]{:S(2)}) copy-start(f32[2,32]{1,0:T(2,128)} %param.30) | copy-start | bytes 772
  10.8 8.0 %copy-start.28 = (f32[32]{0:T(128)S(1)}, f32[32]{0:T(128)}, u32[]{:S(2)}) copy-start(f32[32]{0:T(128)} %param.32) | copy-start | bytes 388
  10.8 8.1 %copy-start.29 = (s32[32]{0:T(128)S(1)}, s32[32]{0:T(128)}, u32[]{:S(2)}) copy-start(s32[32]{0:T(128)} %constant.135.clone) | copy-start | bytes 388
  10.8 8.1 %copy-start.25 = (f32[2,32,32]{2,1,0:T(8,128)S(1)}, f32[2,32,32]{2,1,0:T(8,128)}, u32[]{:S(2)}) copy-start(f32[2,32,32]{2,1,0:T(8,128)} %param.29) | copy-start | bytes 24580
  10.8 8.3 %copy-start.27 = (f32[32]{0:T(128)S(1)}, f32[32]{0:T(128)}, u32[]{:S(2)}) copy-start(f32[32]{0:T(128)} %param.28) | copy-start | bytes 388
  10.8 9.9 %copy-start.24 = (f32[2,2,2,8,1024]{4,3,2,1,0:T(8,128)S(1)}, f32[2,2,2,8,1024]{4,3,2,1,0:T(8,128)}, u32[]{:S(2)}) copy-start(f32[2,2,2,8,1024]{4,3,2,1,0:T(8,128)} %param.31) | copy-start | bytes 786436
  10.8 60.1 %all-to-all-start = ((f32[8,560,128]{2,1,0:T(8,128)}), f32[8,560,128]{2,1,0:T(8,128)S(1)}, u32[]{:S(2)}, u32[]{:S(2)}) async-start(f32[8,560,128]{2,1,0:T(8,128)} %copy-done.6), calls=%async_computation | async-start | bytes 4587520 | tf_op jit(solution)/shard_map/all_to_all | solution.py:505
  30.2 6.9 %copy-start.12 = (f32[32,16,128]{2,1,0:T(8,128)S(1)}, f32[32,16,128]{2,1,0:T(8,128)}, u32[]{:S(2)}) copy-start(f32[32,16,128]{2,1,0:T(8,128)} %param.27) | copy-start | bytes 786436
  37.1 34.3 %copy-start.26 = (s32[3]{0:T(128)S(1)}, s32[3]{0:T(128)}, u32[]{:S(2)}) copy-start(s32[3]{0:T(128)} %constant.136.clone) | copy-start | bytes 40
  37.1 34.4 %copy-start.20 = (bf16[64,256]{1,0:T(8,128)(2,1)S(1)}, bf16[64,256]{1,0:T(8,128)(2,1)}, u32[]{:S(2)}) copy-start(bf16[64,256]{1,0:T(8,128)(2,1)} %constant.126.clone.table_ref.fwd_ref) | copy-start | bytes 98308
  42.2 3.3 %copy-start.22 = (f32[8,16,128,128]{3,2,1,0:T(8,128)}, f32[8,16,128,128]{3,2,1,0:T(8,128)S(1)}, u32[]{:S(2)}) copy-start(f32[8,16,128,128]{3,2,1,0:T(8,128)S(1)} %field.1.init_ref) | copy-start | bytes 25165828
  71.6 3.4 %copy-start.23 = (f32[8,16,128,128]{3,2,1,0:T(8,128)S(1)}, f32[8,16,128,128]{3,2,1,0:T(8,128)}, u32[]{:S(2)}) copy-start(f32[8,16,128,128]{3,2,1,0:T(8,128)} %copy-done.22) | copy-start | bytes 25165828
  107.5 3.3 %copy-start = (f32[8,16,128,128]{3,2,1,0:T(8,128)}, f32[8,16,128,128]{3,2,1,0:T(8,128)S(1)}, u32[]{:S(2)}) copy-start(f32[8,16,128,128]{3,2,1,0:T(8,128)S(1)} %get-tuple-element.27.grid_ref) | copy-start | bytes 25165828
  110.8 28.3 %copy-start.17 = (bf16[128,256]{1,0:T(8,128)(2,1)S(1)}, bf16[128,256]{1,0:T(8,128)(2,1)}, u32[]{:S(2)}) copy-start(bf16[128,256]{1,0:T(8,128)(2,1)} %constant.129.clone.table_ref) | copy-start | bytes 196612
  139.0 18.6 %copy-start.16 = (bf16[128,256]{1,0:T(8,128)(2,1)S(1)}, bf16[128,256]{1,0:T(8,128)(2,1)}, u32[]{:S(2)}) copy-start(bf16[128,256]{1,0:T(8,128)(2,1)} %constant.130.clone.fwd_ref) | copy-start | bytes 196612
  139.1 18.6 %copy-start.18 = (bf16[128,192]{1,0:T(8,128)(2,1)S(1)}, bf16[128,192]{1,0:T(8,128)(2,1)}, u32[]{:S(2)}) copy-start(bf16[128,192]{1,0:T(8,128)(2,1)} %constant.131.clone.inv_ref) | copy-start | bytes 147460
  157.6 18.6 %copy-start.15 = (bf16[512,384]{1,0:T(8,128)(2,1)S(1)}, bf16[512,384]{1,0:T(8,128)(2,1)}, u32[]{:S(2)}) copy-start(bf16[512,384]{1,0:T(8,128)(2,1)} %constant.132.clone.table_ref) | copy-start | bytes 1179652
  178.8 1.4 copy-start.8
  180.2 29.3 %all-to-all-start.4 = ((f32[4,1024,128]{2,1,0:T(8,128)}), f32[4,1024,128]{2,1,0:T(8,128)S(1)}, u32[]{:S(2)}, u32[]{:S(2)}) async-start(f32[4,1024,128]{2,1,0:T(8,128)} %bitcast.54), calls=%async_computation.4 | async-start | bytes 4194304 | tf_op jit(solution)/shard_map/all_to_all | solution.py:619
  183.8 3.4 %copy-start.1 = (f32[8,16,128,128]{3,2,1,0:T(8,128)S(1)}, f32[8,16,128,128]{3,2,1,0:T(8,128)}, u32[]{:S(2)}) copy-start(f32[8,16,128,128]{3,2,1,0:T(8,128)} %copy-done) | copy-start | bytes 25165828
  187.1 22.3 %copy-start.21 = (bf16[128,96]{1,0:T(8,128)(2,1)S(1)}, bf16[128,96]{1,0:T(8,128)(2,1)}, u32[]{:S(2)}) copy-start(bf16[128,96]{1,0:T(8,128)(2,1)} %constant.127.clone.inv_ref) | copy-start | bytes 73732
  190.8 3.3 %copy-start.2 = (f32[8,16,128,128]{3,2,1,0:T(8,128)}, f32[8,16,128,128]{3,2,1,0:T(8,128)S(1)}, u32[]{:S(2)}) copy-start(f32[8,16,128,128]{3,2,1,0:T(8,128)S(1)} %mix.1.mixed_ref) | copy-start | bytes 25165828
  209.4 3.4 %copy-start.3 = (f32[8,16,128,128]{3,2,1,0:T(8,128)S(1)}, f32[8,16,128,128]{3,2,1,0:T(8,128)}, u32[]{:S(2)}) copy-start(f32[8,16,128,128]{3,2,1,0:T(8,128)} %copy-done.2) | copy-start | bytes 25165828
  224.2 3.3 %copy-start.4 = (f32[8,16,128,128]{3,2,1,0:T(8,128)}, f32[8,16,128,128]{3,2,1,0:T(8,128)S(1)}, u32[]{:S(2)}) copy-start(f32[8,16,128,128]{3,2,1,0:T(8,128)S(1)} %get-tuple-element.37.grid_ref) | copy-start | bytes 25165828
  275.5 1.2 collective-permute-start
  276.8 3.7 %collective-permute-start.1 = (f32[4,1024]{1,0:T(4,128)S(1)}, f32[4,1024]{1,0:T(4,128)S(1)}, u32[]{:S(2)}, u32[]{:S(2)}) collective-permute-start(f32[4,1024]{1,0:T(4,128)S(1)} %add.132), channel_id=1, source_target_pairs={{0,16},{8,24},{16,0},{24,8},{1,17},{9,25},{17,1},{25,9},{2,18},{10... | collective-permute-start | bytes 49160 | tf_op jit(solution)/shard_map/ppermute | solution.py:650
  281.2 11.0 %all-to-all-start.7 = ((f32[8,4,1024]{2,1,0:T(4,128)}), f32[8,4,1024]{2,1,0:T(4,128)S(1)}, u32[]{:S(2)}, u32[]{:S(2)}) async-start(f32[8,4,1024]{2,1,0:T(4,128)} %broadcast_in_dim.98), calls=%async_computation.7 | async-start | bytes 262144 | tf_op jit(solution)/shard_map/all_to_all | solution.py:653
  284.8 3.4 %copy-start.5 = (f32[8,16,128,128]{3,2,1,0:T(8,128)S(1)}, f32[8,16,128,128]{3,2,1,0:T(8,128)}, u32[]{:S(2)}) copy-start(f32[8,16,128,128]{3,2,1,0:T(8,128)} %copy-done.4) | copy-start | bytes 25165828
  288.2 4.0 %copy-start.19 = (bf16[128,96]{1,0:T(8,128)(2,1)S(1)}, bf16[128,96]{1,0:T(8,128)(2,1)}, u32[]{:S(2)}) copy-start(bf16[128,96]{1,0:T(8,128)(2,1)} %constant.128.clone.inv_ref) | copy-start | bytes 73732
  292.2 1.6 copy-start.13
  293.8 1.6 copy-start.14

commit v3 on v2

--- a/solution.py
+++ b/solution.py
@@ -97,19 +97,23 @@
     c, n = c * back, -n * back
     t["z_inv"] = wide_left(np.concatenate([c, n], 1))
     t["z_last"] = wide_left(np.stack([c.reshape(s.G, s.ny, s.KL), n.reshape(s.G, s.ny, s.KL)], 2).reshape(s.G, -1))
-    order = np.arange(s.G).reshape(s.nx, s.bxn, B).transpose(0, 2, 1).reshape(-1)
-    c, n = trig(s, s.freq, order)
-    hi, lo = np_split(np.concatenate([np.concatenate([c, n], 1), np.concatenate([-n, c], 1)], 0))
-    t["x_fwd"] = np.concatenate([hi, lo], 0)
+    local = np.arange(s.Xl).reshape(s.bxn, B).T.reshape(-1)
+    fwd, inv = [], []
+    for row in range(s.nx):
+        places = np.concatenate([row * s.Xl + local, (row ^ 1) * s.Xl + local])
+        c, n = trig(s, s.freq, places)
+        fwd.append(stack_left(np.concatenate([np.concatenate([c, n], 1), np.concatenate([-n, c], 1)], 0)))
+        c, n = c.T, n.T
+        table = np.zeros((s.KL, 2, 2 * s.Xl, 2, s.KL, s.M))
+        for k in range(s.KL):
+            table[k, 0, :, 0, k], table[k, 0, :, 1, k] = c, -n
+            table[k, 1, :, 0, k], table[k, 1, :, 1, k] = n, c
+        inv.append(wide_left(table.reshape(4 * s.KL * s.Xl, s.LK) / s.G))
+    t["x_fwd"] = np.stack(fwd)
+    t["x_inv"] = np.stack(inv)
     c, n = trig(s, s.freq, np.arange(s.G))
     t["y_fwd"] = stack_left(np.concatenate([c, n], 0))
     t["y_inv"] = wide_left(np.concatenate([c.T, n.T], 1) / s.G)
-    c, n = trig(s, order, s.freq)
-    table = np.zeros((s.KL, 2, s.G, 2, s.KL, s.M))
-    for k in range(s.KL):
-        table[k, 0, :, 0, k], table[k, 0, :, 1, k] = c, -n
-        table[k, 1, :, 0, k], table[k, 1, :, 1, k] = n, c
-    t["x_inv"] = wide_left(table.reshape(2 * s.KL * s.G, s.LK) / s.G)
     xs = (np.arange(s.bxn)[:, None] * B + np.arange(B)[None, :]).T.reshape(B, 1, s.bxn, 1)
     ys = (np.arange(s.byn)[:, None] * B + np.arange(B)[None, :]).T.reshape(1, B, 1, s.byn)
     full = (B, B, s.bxn, s.byn)
@@ -187,12 +191,16 @@
 
 
 def field_kernel(s, sdf_ref, gain_ref, out_ref):
-    rows = sdf_ref[...].reshape(s.bxn * s.Yl, s.G).T
-    hi, lo = split(rows)
     ghi, glo = split(gain_ref[...])
-    wide = dot(hi, ghi) + dot(lo, ghi) + dot(hi, glo)
-    for y in range(s.Yl):
-        out_ref[0, y] = wide[:, y * s.L : (y + 1) * s.L]
+
+    def step(a, carry):
+        hi, lo = split(sdf_ref[:, a].reshape(s.bxn * s.Yl, s.G).T)
+        wide = dot(hi, ghi) + dot(lo, ghi) + dot(hi, glo)
+        for y in range(s.Yl):
+            out_ref[a, y] = wide[:, y * s.L : (y + 1) * s.L]
+        return carry
+
+    lax.fori_loop(0, B, step, 0)
 
 
 def kernel_tiles(points):
@@ -216,6 +224,24 @@
     return tiles
 
 
+def by_distance(s, row, items):
+    bit = 1
+    while bit < s.nx:
+        far = row & bit != 0
+        items = [
+            [jnp.where(far, b, a) for a, b in zip(items[e], items[e ^ bit])] for e in range(s.nx)
+        ]
+        bit *= 2
+    return items
+
+
+def store_spectrum(s, row, a, tiles, keep_ref, send_ref):
+    groups = by_distance(s, row, [tiles[g * s.bxn : (g + 1) * s.bxn] for g in range(s.nx)])
+    for e in range(s.nx):
+        for b in range(s.bxn):
+            (send_ref if e & 1 else keep_ref)[e // 2, a, b] = groups[e][b]
+
+
 def grid_to_spectrum(s, rows_of, table):
     tiles = []
     for y in range(0, s.Yl, 2):
@@ -227,7 +253,7 @@
     return block_turn(tiles, s.nx * s.bxn, s.cp)
 
 
-def encode_kernel(s, cap, id_ref, num_ref, in_ref, init_ref, table_ref, grid_ref, spec_ref):
+def encode_kernel(s, cap, row_ref, id_ref, num_ref, in_ref, init_ref, table_ref, grid_ref, keep_ref, send_ref):
     C = s.C
     for a in range(B):
         grid_ref[a] = init_ref[a]
@@ -274,9 +300,7 @@
 
     def transform(a, carry):
         out = grid_to_spectrum(s, lambda y: grid_ref[a, y], table_ref[...])
-        for g in range(s.nx):
-            for b in range(s.bxn):
-                spec_ref[g, a, b] = out[g * s.bxn + b]
+        store_spectrum(s, row_ref[0], a, out, keep_ref, send_ref)
         return carry
 
     lax.fori_loop(0, B, transform, 0)
@@ -297,38 +321,52 @@
 
 def mix_kernel(s, grid_ref, mix_ref, bias_ref, out_ref):
     whi, wlo = split(mix_ref[...])
-    for y in range(s.Yl):
-        out_ref[0, y] = mixed_rows(grid_ref[0, y], whi, wlo) + bias_ref[...]
+
+    def step(a, carry):
+        for y in range(s.Yl):
+            out_ref[a, y] = mixed_rows(grid_ref[a, y], whi, wlo) + bias_ref[...]
+        return carry
+
+    lax.fori_loop(0, B, step, 0)
 
 
 def readout_kernel(s, grid_ref, mix_ref, out_ref):
     whi, wlo = split(mix_ref[...])
     lane = lax.broadcasted_iota(jnp.int32, (B, s.LB), 1)
-    for a in range(B):
-        total = jnp.zeros((B, s.LB), F32)
-        for by in range(s.byn):
-            res = mixed_rows(grid_ref[0, by * B + a], whi, wlo)
-            for bz in range(s.NB):
-                mine = (lane // (s.bxn * s.byn) == bz) & (lane % s.byn == by)
-                total = jnp.where(mine, res[bz * B : (bz + 1) * B], total)
-        out_ref[0, a * B : (a + 1) * B, :] = total
-
-
-def x_forward_kernel(s, in_ref, table_ref, out_ref):
+
+    def step(a0, carry):
+        for a in range(B):
+            total = jnp.zeros((B, s.LB), F32)
+            for by in range(s.byn):
+                res = mixed_rows(grid_ref[a0, by * B + a], whi, wlo)
+                for bz in range(s.NB):
+                    mine = (lane // (s.bxn * s.byn) == bz) & (lane % s.byn == by)
+                    total = jnp.where(mine, res[bz * B : (bz + 1) * B], total)
+            out_ref[a0, a * B : (a + 1) * B, :] = total
+        return carry
+
+    lax.fori_loop(0, B, step, 0)
+
+
+def x_forward_kernel(s, keep_ref, recv_ref, table_ref, out_ref):
     M = s.M
-    thi = table_ref[: 2 * M]
     for i in range(s.ny):
         parts = []
         for k in range(s.KL):
             kz = i * s.KL + k
             parts.append(
                 jnp.concatenate(
-                    [in_ref[pl.ds(kz, s.G, stride=s.K2), :], in_ref[pl.ds(s.KZ + kz, s.G, stride=s.K2), :]], axis=0
+                    [
+                        ref[0, pl.ds(ri * s.KZ + kz, s.Xl, stride=s.K2), :]
+                        for ri in range(2)
+                        for ref in (keep_ref, recv_ref)
+                    ],
+                    axis=0,
                 )
             )
         hi, lo = split(jnp.concatenate(parts, axis=1))
-        res = dot(table_ref[...], hi)
-        res = res[: 2 * M] + res[2 * M :] + dot(thi, lo)
+        res = dot(table_ref[...], jnp.concatenate([hi, lo], axis=0))
+        res = res[: 2 * M] + res[2 * M :]
         rows = []
         for ri in range(2):
             for k in range(s.KL):
@@ -375,7 +413,7 @@
         out_ref[r : r + 1, :] = jnp.concatenate([part[m : m + 1] for m in range(M)], axis=1)
 
 
-def x_inverse_kernel(s, in_ref, table_ref, out_ref):
+def x_inverse_kernel(s, in_ref, table_ref, keep_ref, send_ref):
     for i in range(s.ny):
         hi, lo = split(in_ref[i])
         if s.LK == 128:
@@ -385,8 +423,10 @@
             res = dot(t[:, : s.LK], hi, NT) + dot(t[:, : s.LK], lo, NT) + dot(t[:, 2 * s.LK :], hi, NT)
         for k in range(s.KL):
             for ri in range(2):
-                at = (k * 2 + ri) * s.G
-                out_ref[pl.ds(ri * s.KZ + i * s.KL + k, s.G, stride=s.K2), :] = res[at : at + s.G]
+                at = (k * 2 + ri) * 2 * s.Xl
+                places = pl.ds(ri * s.KZ + i * s.KL + k, s.Xl, stride=s.K2)
+                keep_ref[places, :] = res[at : at + s.Xl]
+                send_ref[places, :] = res[at + s.Xl : at + 2 * s.Xl]
 
 
 def gelu(x):
@@ -394,18 +434,23 @@
     return 0.5 * x * (1.0 + jnp.tanh(inner))
 
 
-def layer_kernel(s, mixed_ref, in_ref, inv_ref, fwd_ref, grid_ref, spec_ref):
-    tiles = [in_ref[g, 0, b] for g in range(s.nx) for b in range(s.bxn)]
-    tiles = block_turn(tiles, s.Yl, s.cp)
-    for y in range(0, s.Yl, 2):
-        hi, lo = split(jnp.concatenate([tiles[y], tiles[y + 1]], axis=1))
-        res = dot(inv_ref[...], jnp.concatenate([hi, lo, hi], axis=0))
-        for i in range(2):
-            grid_ref[0, y + i] = gelu(mixed_ref[0, y + i] + res[:, i * s.L : (i + 1) * s.L])
-    out = grid_to_spectrum(s, lambda y: grid_ref[0, y], fwd_ref[...])
-    for g in range(s.nx):
-        for b in range(s.bxn):
-            spec_ref[g, 0, b] = out[g * s.bxn + b]
+def layer_kernel(s, row_ref, mixed_ref, inv_ref, fwd_ref, *refs):
+    in_refs, (grid_ref, keep_ref, send_ref) = refs[: s.nx], refs[s.nx :]
+    row = row_ref[0]
+
+    def step(a, carry):
+        groups = by_distance(s, row, [[ref[a, b] for b in range(s.bxn)] for ref in in_refs])
+        tiles = block_turn([tile for group in groups for tile in group], s.Yl, s.cp)
+        for y in range(0, s.Yl, 2):
+            hi, lo = split(jnp.concatenate([tiles[y], tiles[y + 1]], axis=1))
+            res = dot(inv_ref[...], jnp.concatenate([hi, lo, hi], axis=0))
+            for i in range(2):
+                grid_ref[a, y + i] = gelu(mixed_ref[a, y + i] + res[:, i * s.L : (i + 1) * s.L])
+        out = grid_to_spectrum(s, lambda y: grid_ref[a, y], fwd_ref[...])
+        store_spectrum(s, row, a, out, keep_ref, send_ref)
+        return carry
+
+    lax.fori_loop(0, B, step, 0)
 
 
 def decode_kernel(s, cap, id_ref, num_ref, base_ref, pos_ref, spec_ref, turn_ref, mix_ref, hi_ref, lo_ref, inv_ref, out_ref, s_ref):
@@ -528,18 +573,9 @@
     )
     gains = jnp.where(spread, gain_l, 0.0).reshape(s.bxn * s.Yl, s.Yl * L)
     grid_shape = shape(B, s.Yl, G, L)
-    grid_block = pl.BlockSpec((1, s.Yl, G, L), lambda a: (a, 0, 0, 0))
-    whole = lambda array: pl.BlockSpec(array.shape, lambda a: (0,) * array.ndim)
-    init = call(
-        functools.partial(field_kernel, s),
-        "field",
-        grid_shape,
-        [pl.BlockSpec((s.bxn, None, s.Yl, G), lambda a: (0, a, 0, 0)), whole(gains)],
-        grid_block,
-        3e9,
-        1e7,
-        grid=(B,),
-    )(sdf.reshape(s.bxn, B, s.Yl, G), gains)
+    init = call(functools.partial(field_kernel, s), "field", grid_shape, [VM, VM], VM, 3e9, 1e7)(
+        sdf.reshape(s.bxn, B, s.Yl, G), gains
+    )
 
     on_lanes = lambda v: jnp.broadcast_to(v.reshape(nx, 1, s.cp), (nx, s.bxn, s.cp)).reshape(1, L)
     mixing = mix_w[0].T.reshape(nx, 1, s.cp, nx, 1, s.cp)
@@ -568,79 +604,91 @@
     turn = jnp.mod(freq[None, :] * (row_x * s.Xl) + freq[:, None] * (row_y * s.Yl), G).reshape(1, -1)
     angle = turn.astype(F32) * (2.0 * math.pi / G)
     turns = jnp.concatenate([jnp.cos(angle), jnp.sin(angle)], axis=0)
-    prepared = (incoming, init, mixing, bias, base, reading, u0, v0, u1, v1, turns)
-    incoming, init, mixing, bias, base, reading, u0, v0, u1, v1, turns = lax.optimization_barrier(prepared)
+    x_fwd = lax.dynamic_index_in_dim(t["x_fwd"], row_x, 0, False)
+    x_inv = lax.dynamic_index_in_dim(t["x_inv"], row_x, 0, False)
+    row = row_x.astype(jnp.int32).reshape(1)
+    prepared = (incoming, init, mixing, bias, base, reading, u0, v0, u1, v1, turns, x_fwd, x_inv, row)
+    incoming, init, mixing, bias, base, reading, u0, v0, u1, v1, turns, x_fwd, x_inv, row = (
+        lax.optimization_barrier(prepared)
+    )
     ids, counts, in_pos = placement(incoming)
 
-    spec_shape = shape(nx, B, s.bxn, s.K2, s.LY)
-    grid0, spec = call(
+    half = s.nx // 2
+    spec_shape = shape(half, B, s.bxn, s.K2, s.LY)
+    grid, keep, send = call(
         functools.partial(encode_kernel, s, cap),
         "encode",
-        (grid_shape, spec_shape),
-        [SM, SM, VM, VM, VM],
-        (VM, VM),
+        (grid_shape, spec_shape, spec_shape),
+        [SM, SM, SM, VM, VM, VM],
+        (VM, VM, VM),
         4e9,
         2.2e7,
-    )(ids, counts, incoming, init, t["z_fwd"])
-
-    def to_modes(spec):
-        spec = spec.reshape(nx, B * s.bxn * s.K2, s.LY)
-        spec = lax.all_to_all(spec, "gx", split_axis=0, concat_axis=0, tiled=True)
-        spec = call(
-            functools.partial(x_forward_kernel, s),
-            "x_forward",
-            shape(ny, s.LY, s.LK),
-            [VM, VM],
-            VM,
-            1e9,
-            3e6,
-        )(spec.reshape(G * s.K2, s.LY), t["x_fwd"])
+        aliases={4: 0},
+    )(row, ids, counts, incoming, init, t["z_fwd"])
+
+    def exchange(array, distance):
+        return lax.ppermute(array, "gx", [(i, i ^ distance) for i in range(nx)])
+
+    def to_modes(keep, send):
+        recv = exchange(send, 1).reshape(half, s.Xl * s.K2, s.LY)
+        keep = keep.reshape(half, s.Xl * s.K2, s.LY)
+
+        def part(d):
+            block = pl.BlockSpec((1, s.Xl * s.K2, s.LY), lambda i: (d, 0, 0))
+            return call(
+                functools.partial(x_forward_kernel, s),
+                "x_forward",
+                shape(ny, s.LY, s.LK),
+                [block, block, pl.BlockSpec(x_fwd.shape, lambda i: (0, 0))],
+                pl.BlockSpec((ny, s.LY, s.LK), lambda i: (0, 0, 0)),
+                2e8,
+                3e6,
+                grid=(1,),
+            )(keep, recv, x_fwd)
+
+        others = [exchange(part(d), 2 * d) for d in range(1, half)]
+        spec = part(0)
+        for other in others:
+            spec = spec + other
         spec = lax.all_to_all(spec, "gy", split_axis=0, concat_axis=0, tiled=True)
         return spec.reshape(G * s.cp, s.LK)
 
-    spec = to_modes(spec)
+    spec = to_modes(keep, send)
     mixed = call(
-        functools.partial(mix_kernel, s),
-        "mix",
-        grid_shape,
-        [grid_block, whole(mixing), whole(bias)],
-        grid_block,
-        2e9,
-        1.7e7,
-        grid=(B,),
-    )(grid0, mixing, bias)
+        functools.partial(mix_kernel, s), "mix", grid_shape, [VM] * 3, VM, 2e9, 1.7e7, aliases={0: 0}
+    )(grid, mixing, bias)
     spec = call(
         functools.partial(y_kernel, s), "y_both", shape(G * s.cp, s.LK), [VM] * 5, VM, 1e9, 2e6
     )(spec, t["y_fwd"], t["y_inv"], u0, v0)
     spec = lax.all_to_all(spec.reshape(ny, s.LY, s.LK), "gy", split_axis=0, concat_axis=0, tiled=True)
-    spec = call(
-        functools.partial(x_inverse_kernel, s), "x_inverse", shape(G * s.K2, s.LY), [VM, VM], VM, 1e9, 3e6
-    )(spec, t["x_inv"])
-    spec = lax.all_to_all(
-        spec.reshape(nx, B * s.bxn * s.K2, s.LY), "gx", split_axis=0, concat_axis=0, tiled=True
-    ).reshape(nx, B, s.bxn, s.K2, s.LY)
-    spec_block = pl.BlockSpec((nx, 1, s.bxn, s.K2, s.LY), lambda a: (0, a, 0, 0, 0))
-    grid1, spec = call(
+    near = [spec] + [exchange(spec, 2 * d) for d in range(1, half)]
+    fields = []
+    for item in near:
+        own, other = call(
+            functools.partial(x_inverse_kernel, s),
+            "x_inverse",
+            (shape(s.Xl * s.K2, s.LY),) * 2,
+            [VM, VM],
+            (VM, VM),
+            3e8,
+            3e6,
+        )(item, x_inv)
+        fields += [own, exchange(other, 1)]
+    fields = [f.reshape(B, s.bxn, s.K2, s.LY) for f in fields]
+    grid, keep, send = call(
         functools.partial(layer_kernel, s),
         "layer",
-        (grid_shape, spec_shape),
-        [grid_block, spec_block, whole(t["z_inv"]), whole(t["z_fwd"])],
-        (grid_block, spec_block),
+        (grid_shape, spec_shape, spec_shape),
+        [SM] + [VM] * (3 + nx),
+        (VM, VM, VM),
         4e9,
         2.1e7,
-        grid=(B,),
-    )(mixed, spec, t["z_inv"], t["z_fwd"])
-    spec = to_modes(spec)
+        aliases={1: 0},
+    )(row, mixed, t["z_inv"], t["z_fwd"], *fields)
+    spec = to_modes(keep, send)
     read = call(
-        functools.partial(readout_kernel, s),
-        "readout",
-        shape(B, B * B, s.LB),
-        [grid_block, whole(reading)],
-        pl.BlockSpec((1, B * B, s.LB), lambda a: (a, 0, 0)),
-        2e9,
-        9e6,
-        grid=(B,),
-    )(grid1, reading)
+        functools.partial(readout_kernel, s), "readout", shape(B, B * B, s.LB), [VM, VM], VM, 2e9, 9e6
+    )(grid, reading)
     last = call(
         functools.partial(y_last_kernel, s), "y_last", shape(2 * s.KL, M * M), [VM] * 4, VM, 1e9, 1e6
     )(spec, t["y_fwd"], u1, v1)

time: 328 us -> 305 us (0.930)
  blocking collectives: 118 us -> 76 us
  waiting for transfers between devices: 45.1 us -> 65 us
  starting transfers between devices: 16 us -> 28.8 us
  local copies, waits for them, and re-layouts: 51.8 us -> 42.3 us
  Pallas kernels: 89.8 us -> 84.3 us
    all_to_all x2 -> x0, blocking collectives: 56.4 us -> none  [to_modes(): spec = lax.all_to_all(spec, 'gx', split_axis=0, concat_axis=0, tiled=True)]
    ppermute x0 -> x7, waiting for transfers between devices: none -> 38.4 us  [exchange(): return lax.ppermute(array, 'gx', [(i, i ^ distance) for i in range(nx)])]
    ppermute x0 -> x7, starting transfers between devices: none -> 18.1 us  [exchange(): return lax.ppermute(array, 'gx', [(i, i ^ distance) for i in range(nx)])]
    pallas_call x5 -> x8, Pallas kernels: 14.6 us -> 31.3 us  [the longest x1 20.1 us: per_device(): call(functools.partial(mix_kernel, s), 'mix', grid_shape, [VM] * 3, VM, 2...]
    all_to_all x1 -> x0, waiting for transfers between devices: 15.4 us -> none  [per_device(): lax.all_to_all(spec.reshape(nx, B * s.bxn * s.K2, s.LY), 'gx', split_axis...]
    pallas_call x1, Pallas kernels: 32.5 us -> 19.4 us  [per_device(): call(functools.partial(encode_kernel, s, cap), 'encode', (grid_shape, spe...]
    all_to_all x1, blocking collectives: 9.37 us -> 22 us  [per_device(): lax.all_to_all(values.reshape(ny, cap, PB), 'gy', split_axis=0, concat_ax...]
    unnamed x63 -> x53, local copies, waits for them, and re-layouts: 36.8 us -> 24.8 us
  transfers between devices with their start and end apart: 5 -> 11, of which waited for: 5 -> 9; matrix products, arithmetic and copies ran while one was open for 6% -> 7% of each run, Pallas kernels for 4% -> 11%
where the time goes in v3:
time: 305 us; the launch traced here: 304 us
  Pallas kernels  84.3 us (28%)
  blocking collectives  76 us (25%)
  waiting for transfers between devices  65 us (21%)
  local copies, waits for them, and re-layouts  42.3 us (14%)
  starting transfers between devices  28.8 us (9%)
  other arithmetic  5.55 us (2%)
    ppermute x7, waiting for transfers between devices, exchange(): return lax.ppermute(array, 'gx', [(i, i ^ distance) for i in range(nx)])  38.4 us
    all_to_all x2, blocking collectives, to_modes(): spec = lax.all_to_all(spec, 'gy', split_axis=0, concat_axis=0, tiled=True)  36.5 us
    unnamed x53, local copies, waits for them, and re-layouts  24.8 us
    all_to_all x1, waiting for transfers between devices, per_device(): lax.all_to_all(outgoing, 'gy', split_axis=0, concat_axis=0, tiled=True)  22.2 us
    all_to_all x1, blocking collectives, per_device(): lax.all_to_all(values.reshape(ny, cap, PB), 'gy', split_axis=0, concat_ax...  22 us
    pallas_call x1, Pallas kernels, per_device(): call(functools.partial(mix_kernel, s), 'mix', grid_shape, [VM] * 3, VM, 2...  20.1 us
    pallas_call x1, Pallas kernels, per_device(): call(functools.partial(encode_kernel, s, cap), 'encode', (grid_shape, spe...  19.4 us
    ppermute x7, starting transfers between devices, exchange(): return lax.ppermute(array, 'gx', [(i, i ^ distance) for i in range(nx)])  18.1 us
  transfers between devices with their start and end apart: 11, of which 9 were waited for; matrix products, arithmetic and copies ran while one was open for 7% of the time, Pallas kernels for 11%

profile of v3, /device:TPU:0, one launch (start us, length us, event | category | flops | bytes accessed | tf_op | source)
XLA Modules:
  0.0 303.9 jit_solution(4565846343321962378)
XLA Ops:
  0.7 1.6 copy-done.7
  2.2 0.9 copy-done.8
  4.7 4.6 %pack.1 = (f32[8,560,128]{2,1,0:T(8,128)S(1)}, s32[128]{0:T(128)S(1)}) custom-call(s32[128]{0:T(128)S(1)} %copy-done.10, s32[1]{0:T(128)S(6)} %copy.41.count_ref, f32[3,16384]{1,0:T(4,128)S(1)} %copy-done.8, f32[32,16384]{1,0:T(8,128)S(1)} %copy-done.7, f32[128,128]{1,0:T(8,128)S(1)} %bitcast.73), custom_call_target="tpu_custom_call" | custom-call | flops 1000000 | bytes 6000000 | tf_op jit(solution)/shard_map/pack/pallas_call | solution.py:540
  9.3 1.4 copy-done.6
  10.8 6.2 %all-to-all-start = ((f32[8,560,128]{2,1,0:T(8,128)}), f32[8,560,128]{2,1,0:T(8,128)S(1)}, u32[]{:S(2)}, u32[]{:S(2)}) async-start(f32[8,560,128]{2,1,0:T(8,128)} %copy-done.6), calls=%async_computation | async-start | bytes 4587520 | tf_op jit(solution)/shard_map/all_to_all | solution.py:550
  19.7 2.1 copy.32
  21.7 1.5 reshape.377.u_ref
  23.2 1.0 copy.33
  24.2 1.5 reshape.378.v_ref
  25.9 1.0 copy.31
  26.9 1.3 slice_negate_fusion.1
  28.1 1.6 pad_maximum_fusion
  29.7 1.5 reshape.375.u_ref
  31.2 1.5 reshape.376.v_ref
  32.6 1.2 broadcast_in_dim.90
  33.8 2.3 reshape.372
  37.7 0.9 dynamic-slice_bitcast_fusion.table_ref
  39.9 5.0 %field.1.init_ref = f32[8,16,128,128]{3,2,1,0:T(8,128)S(1)} custom-call(f32[4,8,16,128]{3,2,1,0:T(8,128)S(1)} %bitcast.77, f32[64,2048]{1,0:T(8,128)S(1)} %bitcast_select_fusion.gain_ref), custom_call_target="tpu_custom_call" | custom-call | flops 3000000000 | bytes 10000000 | tf_op jit(solution)/shard_map/field/pallas_call | solution.py:576
  44.9 3.3 %copy-done = f32[8,16,128,128]{3,2,1,0:T(8,128)} copy-done((f32[8,16,128,128]{3,2,1,0:T(8,128)}, f32[8,16,128,128]{3,2,1,0:T(8,128)S(1)}, u32[]{:S(2)}) %copy-start) | copy-done | bytes 8388632
  48.2 22.2 %all-to-all-done.in_ref = f32[8,560,128]{2,1,0:T(8,128)S(1)} async-done(((f32[8,560,128]{2,1,0:T(8,128)}), f32[8,560,128]{2,1,0:T(8,128)S(1)}, u32[]{:S(2)}, u32[]{:S(2)}) %all-to-all-start) | async-done | bytes 2293792 | tf_op jit(solution)/shard_map/all_to_all | solution.py:550
  71.1 3.4 %copy-done.1 = f32[8,16,128,128]{3,2,1,0:T(8,128)S(1)} copy-done((f32[8,16,128,128]{3,2,1,0:T(8,128)S(1)}, f32[8,16,128,128]{3,2,1,0:T(8,128)}, u32[]{:S(2)}) %copy-start.1) | copy-done | bytes 8388632
  74.4 19.4 %encode.1 = (f32[8,16,128,128]{3,2,1,0:T(8,128)S(1)}, f32[2,8,4,32,128]{4,3,2,1,0:T(8,128)S(1)}, f32[2,8,4,32,128]{4,3,2,1,0:T(8,128)S(1)}) custom-call(s32[1]{0:T(128)} %bitcast.12.row_ref, s32[8,128]{1,0:T(8,128)S(1)} %concatenate.23.id_ref, s32[8]{0:T(128)S(1)} %get-tuple-element.57.num_ref, ...), custom_call_target="tpu_custom_call", output_to_operand_aliasing={{0}: (4, {})} | custom-call | flops 4000000000 | bytes 22000000 | tf_op jit(solution)/shard_map/encode/pallas_call | solution.py:618
  93.9 3.3 %copy-done.2 = f32[8,16,128,128]{3,2,1,0:T(8,128)} copy-done((f32[8,16,128,128]{3,2,1,0:T(8,128)}, f32[8,16,128,128]{3,2,1,0:T(8,128)S(1)}, u32[]{:S(2)}) %copy-start.2) | copy-done | bytes 8388632
  97.2 3.9 %collective-permute-start = (f32[2,8,4,32,128]{4,3,2,1,0:T(8,128)S(1)}, f32[2,8,4,32,128]{4,3,2,1,0:T(8,128)S(1)}, u32[]{:S(2)}, u32[]{:S(2)}) collective-permute-start(f32[2,8,4,32,128]{4,3,2,1,0:T(8,128)S(1)} %get-tuple-element.41), channel_id=1, source_target_pairs={{0,8},{8,0},{16,24},{24,16},{1,9},{9,1},{17,25},{25,17},{2,10},{10... | collective-permute-start | bytes 3145736 | tf_op jit(solution)/shard_map/ppermute | solution.py:630
  101.1 2.3 collective-permute-done
  104.3 11.8 %collective-permute-start.1 = (f32[8,128,128]{2,1,0:T(8,128)S(1)}, f32[8,128,128]{2,1,0:T(8,128)S(1)}, u32[]{:S(2)}, u32[]{:S(2)}) collective-permute-start(f32[8,128,128]{2,1,0:T(8,128)S(1)} %x_forward.5), channel_id=1, source_target_pairs={{0,16},{8,24},{16,0},{24,8},{1,17},{9,25},{17,1},{25,9},{2,18},{10... | collective-permute-start | bytes 1572872 | tf_op jit(solution)/shard_map/ppermute | solution.py:630
  117.0 11.3 %collective-permute-done.1 = f32[8,128,128]{2,1,0:T(8,128)S(1)} collective-permute-done((f32[8,128,128]{2,1,0:T(8,128)S(1)}, f32[8,128,128]{2,1,0:T(8,128)S(1)}, u32[]{:S(2)}, u32[]{:S(2)}) %collective-permute-start.1) | collective-permute-done | bytes 524320 | tf_op jit(solution)/shard_map/ppermute | solution.py:630
  128.4 18.1 %all_to_all.30 = f32[8,128,128]{2,1,0:T(8,128)S(1)} all-to-all(f32[8,128,128]{2,1,0:T(8,128)S(1)} %add.145), channel_id=1, replica_groups=mesh['gx'=4,'gy'=8] {'gy'}, dimensions={0} | all-to-all | bytes 1048576 | tf_op jit(solution)/shard_map/all_to_all | solution.py:653
  146.5 1.1 y_both.1
  147.5 17.4 %all_to_all.31.in_ref = f32[8,128,128]{2,1,0:T(8,128)S(1)} all-to-all(f32[8,128,128]{2,1,0:T(8,128)S(1)} %bitcast.70), channel_id=1, replica_groups=mesh['gx'=4,'gy'=8] {'gy'}, dimensions={0} | all-to-all | bytes 1048576 | tf_op jit(solution)/shard_map/all_to_all | solution.py:663
  165.8 1.3 x_inverse.2
  167.2 10.1 %collective-permute-done.3.in_ref = f32[8,128,128]{2,1,0:T(8,128)S(1)} collective-permute-done((f32[8,128,128]{2,1,0:T(8,128)S(1)}, f32[8,128,128]{2,1,0:T(8,128)S(1)}, u32[]{:S(2)}, u32[]{:S(2)}) %collective-permute-start.3) | collective-permute-done | bytes 524320 | tf_op jit(solution)/shard_map/ppermute | solution.py:630
  177.3 1.3 x_inverse.3
  178.7 20.1 %mix.1.mixed_ref = f32[8,16,128,128]{3,2,1,0:T(8,128)S(1)} custom-call(f32[8,16,128,128]{3,2,1,0:T(8,128)S(1)} %copy-done.3, f32[128,128]{1,0:T(8,128)S(1)} %get-tuple-element.38.mix_ref, f32[1,128]{1,0:T(1,128)S(1)} %reshape.373.bias_ref), custom_call_target="tpu_custom_call", output_to_operand_aliasing={{}: (0, {})} | custom-call | flops 2000000000 | bytes 17000000 | tf_op jit(solution)/shard_map/mix/pallas_call | solution.py:657
  198.9 11.8 %layer.1 = (f32[8,16,128,128]{3,2,1,0:T(8,128)S(1)}, f32[2,8,4,32,128]{4,3,2,1,0:T(8,128)S(1)}, f32[2,8,4,32,128]{4,3,2,1,0:T(8,128)S(1)}) custom-call(s32[1]{0:T(128)} %bitcast.12.row_ref, f32[8,16,128,128]{3,2,1,0:T(8,128)S(1)} %mix.1.mixed_ref, bf16[128,96]{1,0:T(8,128)(2,1)S(1)} %copy-done.18, ...), custom_call_target="tpu_custom_call", output_to_operand_aliasing={{0}: (1, {})} | custom-call | flops 4000000000 | bytes 21000000 | tf_op jit(solution)/shard_map/layer/pallas_call | solution.py:678
  210.7 3.3 %copy-done.4 = f32[8,16,128,128]{3,2,1,0:T(8,128)} copy-done((f32[8,16,128,128]{3,2,1,0:T(8,128)}, f32[8,16,128,128]{3,2,1,0:T(8,128)S(1)}, u32[]{:S(2)}) %copy-start.4) | copy-done | bytes 8388632
  214.5 2.3 collective-permute-done.5
  217.7 1.0 collective-permute-start.6
  219.5 12.4 %collective-permute-done.6 = f32[8,128,128]{2,1,0:T(8,128)S(1)} collective-permute-done((f32[8,128,128]{2,1,0:T(8,128)S(1)}, f32[8,128,128]{2,1,0:T(8,128)S(1)}, u32[]{:S(2)}, u32[]{:S(2)}) %collective-permute-start.6) | collective-permute-done | bytes 524320 | tf_op jit(solution)/shard_map/ppermute | solution.py:630
  232.0 18.5 %all_to_all.32 = f32[8,128,128]{2,1,0:T(8,128)S(1)} all-to-all(f32[8,128,128]{2,1,0:T(8,128)S(1)} %add.146), channel_id=1, replica_groups=mesh['gx'=4,'gy'=8] {'gy'}, dimensions={0} | all-to-all | bytes 1048576 | tf_op jit(solution)/shard_map/all_to_all | solution.py:653
  251.2 1.2 collective-permute-done.7
  253.1 2.9 collective-permute-done.8
  256.8 3.6 %all-to-all-start.4 = ((f32[8,4,1024]{2,1,0:T(4,128)}), f32[8,4,1024]{2,1,0:T(4,128)S(1)}, u32[]{:S(2)}, u32[]{:S(2)}) async-start(f32[8,4,1024]{2,1,0:T(4,128)} %broadcast_in_dim.98), calls=%async_computation.4 | async-start | bytes 262144 | tf_op jit(solution)/shard_map/all_to_all | solution.py:701
  260.4 3.4 %copy-done.5 = f32[8,16,128,128]{3,2,1,0:T(8,128)S(1)} copy-done((f32[8,16,128,128]{3,2,1,0:T(8,128)S(1)}, f32[8,16,128,128]{3,2,1,0:T(8,128)}, u32[]{:S(2)}) %copy-start.5) | copy-done | bytes 8388632
  263.8 3.7 %readout.1 = f32[8,64,128]{2,1,0:T(8,128)S(1)} custom-call(f32[8,16,128,128]{3,2,1,0:T(8,128)S(1)} %copy-done.5, f32[128,128]{1,0:T(8,128)S(1)} %get-tuple-element.56.mix_ref), custom_call_target="tpu_custom_call" | custom-call | flops 2000000000 | bytes 9000000 | tf_op jit(solution)/shard_map/readout/pallas_call | solution.py:689
  267.8 1.6 copy-done.12
  269.4 11.6 %decode.1 = f32[128,128]{1,0:T(8,128)S(1)} custom-call(s32[8,128]{1,0:T(8,128)S(1)} %concatenate.23.id_ref, s32[8]{0:T(128)S(1)} %get-tuple-element.57.num_ref, f32[1]{0:T(128)} %bitcast.6.base_ref, f32[8,48,128]{2,1,0:T(8,128)S(1)} %slice.68.pos_ref, f32[8,4,1024]{2,1,0:T(4,128)S(1)} %all-to-all-done.4.spec_ref, f32[2,1024]{1,0:T(2,128)S(1)} %pad_maximum_fusion.4.turn_ref, ...), custom_call_target="tpu_custom_call" | custom-call | flops 4000000000 | bytes 6000000 | tf_op jit(solution)/shard_map/decode/pallas_call | solution.py:702
  281.0 22.0 %all_to_all.33 = f32[8,16,128]{2,1,0:T(8,128)S(1)} all-to-all(f32[8,16,128]{2,1,0:T(8,128)S(1)} %bitcast.74), channel_id=1, replica_groups=mesh['gx'=4,'gy'=8] {'gy'}, dimensions={0} | all-to-all | bytes 131072 | tf_op jit(solution)/shard_map/all_to_all | solution.py:712
  (110 shorter events, 16.2 us)
Async XLA Ops:
  0.7 1.6 copy-start.7
  2.2 0.9 copy-start.8
  3.2 0.8 copy-start.9
  4.0 0.7 copy-start.10
  9.3 1.4 copy-start.6
  10.7 6.2 %copy-start.25 = (f32[2,32]{1,0:T(2,128)S(1)}, f32[2,32]{1,0:T(2,128)}, u32[]{:S(2)}) copy-start(f32[2,32]{1,0:T(2,128)} %param.30) | copy-start | bytes 772
  10.7 6.3 %copy-start.24 = (s32[32]{0:T(128)S(1)}, s32[32]{0:T(128)}, u32[]{:S(2)}) copy-start(s32[32]{0:T(128)} %constant.143.clone) | copy-start | bytes 388
  10.7 6.6 %copy-start.23 = (f32[32]{0:T(128)S(1)}, f32[32]{0:T(128)}, u32[]{:S(2)}) copy-start(f32[32]{0:T(128)} %param.32) | copy-start | bytes 388
  10.8 6.7 %copy-start.20 = (f32[2,32,32]{2,1,0:T(8,128)S(1)}, f32[2,32,32]{2,1,0:T(8,128)}, u32[]{:S(2)}) copy-start(f32[2,32,32]{2,1,0:T(8,128)} %param.29) | copy-start | bytes 24580
  10.8 6.9 %copy-start.22 = (f32[32]{0:T(128)S(1)}, f32[32]{0:T(128)}, u32[]{:S(2)}) copy-start(f32[32]{0:T(128)} %param.28) | copy-start | bytes 388
  10.8 7.6 %copy-start.19 = (f32[2,2,2,8,1024]{4,3,2,1,0:T(8,128)S(1)}, f32[2,2,2,8,1024]{4,3,2,1,0:T(8,128)}, u32[]{:S(2)}) copy-start(f32[2,2,2,8,1024]{4,3,2,1,0:T(8,128)} %param.31) | copy-start | bytes 786436
  10.8 59.6 %all-to-all-start = ((f32[8,560,128]{2,1,0:T(8,128)}), f32[8,560,128]{2,1,0:T(8,128)S(1)}, u32[]{:S(2)}, u32[]{:S(2)}) async-start(f32[8,560,128]{2,1,0:T(8,128)} %copy-done.6), calls=%async_computation | async-start | bytes 4587520 | tf_op jit(solution)/shard_map/all_to_all | solution.py:550
  39.0 1.0 copy-start.11
  39.9 31.0 %copy-start.21 = (s32[3]{0:T(128)S(1)}, s32[3]{0:T(128)}, u32[]{:S(2)}) copy-start(s32[3]{0:T(128)} %constant.144.clone) | copy-start | bytes 40
  39.9 31.1 %copy-start.17 = (bf16[64,256]{1,0:T(8,128)(2,1)S(1)}, bf16[64,256]{1,0:T(8,128)(2,1)}, u32[]{:S(2)}) copy-start(bf16[64,256]{1,0:T(8,128)(2,1)} %constant.134.clone.table_ref.fwd_ref) | copy-start | bytes 98308
  44.9 3.3 %copy-start = (f32[8,16,128,128]{3,2,1,0:T(8,128)}, f32[8,16,128,128]{3,2,1,0:T(8,128)S(1)}, u32[]{:S(2)}) copy-start(f32[8,16,128,128]{3,2,1,0:T(8,128)S(1)} %field.1.init_ref) | copy-start | bytes 25165828
  71.0 3.4 %copy-start.1 = (f32[8,16,128,128]{3,2,1,0:T(8,128)S(1)}, f32[8,16,128,128]{3,2,1,0:T(8,128)}, u32[]{:S(2)}) copy-start(f32[8,16,128,128]{3,2,1,0:T(8,128)} %copy-done) | copy-start | bytes 25165828
  93.9 3.3 %copy-start.2 = (f32[8,16,128,128]{3,2,1,0:T(8,128)}, f32[8,16,128,128]{3,2,1,0:T(8,128)S(1)}, u32[]{:S(2)}) copy-start(f32[8,16,128,128]{3,2,1,0:T(8,128)S(1)} %get-tuple-element.37.grid_ref) | copy-start | bytes 25165828
  97.2 6.2 %collective-permute-start = (f32[2,8,4,32,128]{4,3,2,1,0:T(8,128)S(1)}, f32[2,8,4,32,128]{4,3,2,1,0:T(8,128)S(1)}, u32[]{:S(2)}, u32[]{:S(2)}) collective-permute-start(f32[2,8,4,32,128]{4,3,2,1,0:T(8,128)S(1)} %get-tuple-element.41), channel_id=1, source_target_pairs={{0,8},{8,0},{16,24},{24,16},{1,9},{9,1},{17,25},{25,17},{2,10},{10... | collective-permute-start | bytes 3145736 | tf_op jit(solution)/shard_map/ppermute | solution.py:630
  104.3 42.2 %copy-start.14 = (bf16[128,256]{1,0:T(8,128)(2,1)S(1)}, bf16[128,256]{1,0:T(8,128)(2,1)}, u32[]{:S(2)}) copy-start(bf16[128,256]{1,0:T(8,128)(2,1)} %constant.139.clone.fwd_ref) | copy-start | bytes 196612
  104.3 42.2 %copy-start.15 = (bf16[128,192]{1,0:T(8,128)(2,1)S(1)}, bf16[128,192]{1,0:T(8,128)(2,1)}, u32[]{:S(2)}) copy-start(bf16[128,192]{1,0:T(8,128)(2,1)} %constant.140.clone.inv_ref) | copy-start | bytes 147460
  104.3 24.0 %collective-permute-start.1 = (f32[8,128,128]{2,1,0:T(8,128)S(1)}, f32[8,128,128]{2,1,0:T(8,128)S(1)}, u32[]{:S(2)}, u32[]{:S(2)}) collective-permute-start(f32[8,128,128]{2,1,0:T(8,128)S(1)} %x_forward.5), channel_id=1, source_target_pairs={{0,16},{8,24},{16,0},{24,8},{1,17},{9,25},{17,1},{25,9},{2,18},{10... | collective-permute-start | bytes 1572872 | tf_op jit(solution)/shard_map/ppermute | solution.py:630
  128.4 50.3 %copy-start.3 = (f32[8,16,128,128]{3,2,1,0:T(8,128)S(1)}, f32[8,16,128,128]{3,2,1,0:T(8,128)}, u32[]{:S(2)}) copy-start(f32[8,16,128,128]{3,2,1,0:T(8,128)} %copy-done.2) | copy-start | bytes 25165828
  165.0 12.3 %collective-permute-start.3 = (f32[8,128,128]{2,1,0:T(8,128)S(1)}, f32[8,128,128]{2,1,0:T(8,128)S(1)}, u32[]{:S(2)}, u32[]{:S(2)}) collective-permute-start(f32[8,128,128]{2,1,0:T(8,128)S(1)} %all_to_all.31.in_ref), channel_id=1, source_target_pairs={{0,16},{8,24},{16,0},{24,8},{1,17},{9,25},{17,1},{25,9},{2,18},{10... | collective-permute-start | bytes 1572872 | tf_op jit(solution)/shard_map/ppermute | solution.py:630
  167.1 31.8 %collective-permute-start.2 = (f32[1024,128]{1,0:T(8,128)S(1)}, f32[1024,128]{1,0:T(8,128)S(1)}, u32[]{:S(2)}, u32[]{:S(2)}) collective-permute-start(f32[1024,128]{1,0:T(8,128)S(1)} %get-tuple-element.47), channel_id=1, source_target_pairs={{0,8},{8,0},{16,24},{24,16},{1,9},{9,1},{17,25},{25,17},{2,10},{10... | collective-permute-start | bytes 1572872 | tf_op jit(solution)/shard_map/ppermute | solution.py:630
  178.6 20.2 %collective-permute-start.4 = (f32[1024,128]{1,0:T(8,128)S(1)}, f32[1024,128]{1,0:T(8,128)S(1)}, u32[]{:S(2)}, u32[]{:S(2)}) collective-permute-start(f32[1024,128]{1,0:T(8,128)S(1)} %get-tuple-element.49), channel_id=1, source_target_pairs={{0,8},{8,0},{16,24},{24,16},{1,9},{9,1},{17,25},{25,17},{2,10},{10... | collective-permute-start | bytes 1572872 | tf_op jit(solution)/shard_map/ppermute | solution.py:630
  178.7 20.2 %copy-start.18 = (bf16[128,96]{1,0:T(8,128)(2,1)S(1)}, bf16[128,96]{1,0:T(8,128)(2,1)}, u32[]{:S(2)}) copy-start(bf16[128,96]{1,0:T(8,128)(2,1)} %constant.135.clone.inv_ref) | copy-start | bytes 73732
  210.7 3.3 %copy-start.4 = (f32[8,16,128,128]{3,2,1,0:T(8,128)}, f32[8,16,128,128]{3,2,1,0:T(8,128)S(1)}, u32[]{:S(2)}) copy-start(f32[8,16,128,128]{3,2,1,0:T(8,128)S(1)} %get-tuple-element.55.grid_ref) | copy-start | bytes 25165828
  214.0 2.8 collective-permute-start.5
  217.7 14.3 %collective-permute-start.6 = (f32[8,128,128]{2,1,0:T(8,128)S(1)}, f32[8,128,128]{2,1,0:T(8,128)S(1)}, u32[]{:S(2)}, u32[]{:S(2)}) collective-permute-start(f32[8,128,128]{2,1,0:T(8,128)S(1)} %x_forward.7), channel_id=1, source_target_pairs={{0,16},{8,24},{16,0},{24,8},{1,17},{9,25},{17,1},{25,9},{2,18},{10... | collective-permute-start | bytes 1572872 | tf_op jit(solution)/shard_map/ppermute | solution.py:630
  251.1 1.2 collective-permute-start.7
  252.4 3.7 %collective-permute-start.8 = (f32[4,1024]{1,0:T(4,128)S(1)}, f32[4,1024]{1,0:T(4,128)S(1)}, u32[]{:S(2)}, u32[]{:S(2)}) collective-permute-start(f32[4,1024]{1,0:T(4,128)S(1)} %add.147), channel_id=1, source_target_pairs={{0,16},{8,24},{16,0},{24,8},{1,17},{9,25},{17,1},{25,9},{2,18},{10... | collective-permute-start | bytes 49160 | tf_op jit(solution)/shard_map/ppermute | solution.py:698
  256.8 11.0 %all-to-all-start.4 = ((f32[8,4,1024]{2,1,0:T(4,128)}), f32[8,4,1024]{2,1,0:T(4,128)S(1)}, u32[]{:S(2)}, u32[]{:S(2)}) async-start(f32[8,4,1024]{2,1,0:T(4,128)} %broadcast_in_dim.98), calls=%async_computation.4 | async-start | bytes 262144 | tf_op jit(solution)/shard_map/all_to_all | solution.py:701
  260.4 3.4 %copy-start.5 = (f32[8,16,128,128]{3,2,1,0:T(8,128)S(1)}, f32[8,16,128,128]{3,2,1,0:T(8,128)}, u32[]{:S(2)}) copy-start(f32[8,16,128,128]{3,2,1,0:T(8,128)} %copy-done.4) | copy-start | bytes 25165828
  263.8 4.0 %copy-start.13 = (bf16[2048,512]{1,0:T(8,128)(2,1)S(1)}, bf16[2048,512]{1,0:T(8,128)(2,1)}, u32[]{:S(2)}) copy-start(bf16[2048,512]{1,0:T(8,128)(2,1)} %constant.141.clone.hi_ref) | copy-start | bytes 6291460
  263.8 4.0 %copy-start.16 = (bf16[128,96]{1,0:T(8,128)(2,1)S(1)}, bf16[128,96]{1,0:T(8,128)(2,1)}, u32[]{:S(2)}) copy-start(bf16[128,96]{1,0:T(8,128)(2,1)} %constant.136.clone.inv_ref) | copy-start | bytes 73732
  267.8 1.6 copy-start.12

commit v4 on v3

--- a/solution.py
+++ b/solution.py
@@ -15,7 +15,7 @@
 F32 = jnp.float32
 VM = pl.BlockSpec(memory_space=pltpu.VMEM)
 SM = pl.BlockSpec(memory_space=pltpu.SMEM)
-LIMIT = 32 * 1024 * 1024
+MIB = 1024 * 1024
 
 
 def split(x):
@@ -38,7 +38,7 @@
 NT = ((1,), (1,))
 
 
-def call(body, name, out_shape, in_specs, out_specs, flops, moved, grid=None, scratch=(), aliases=None):
+def call(body, name, out_shape, in_specs, out_specs, flops, moved, grid=None, scratch=(), room=58):
     extra = {} if grid is None else {"grid": grid}
     return pl.pallas_call(
         body,
@@ -47,8 +47,7 @@
         in_specs=in_specs,
         out_specs=out_specs,
         scratch_shapes=list(scratch),
-        input_output_aliases=aliases or {},
-        compiler_params=pltpu.CompilerParams(vmem_limit_bytes=LIMIT),
+        compiler_params=pltpu.CompilerParams(vmem_limit_bytes=room * MIB),
         cost_estimate=pl.CostEstimate(flops=int(flops), bytes_accessed=int(moved), transcendentals=0),
         **extra,
     )
@@ -159,12 +158,14 @@
     return jnp.where(lane < width // 2, first, -first).astype(F32)
 
 
-def pack_kernel(s, cap, brick_ref, count_ref, pos_ref, feat_ref, area_ref, out_ref, slot_ref, fill_ref):
+def pack_kernel(s, caps, brick_ref, count_ref, pos_ref, feat_ref, area_ref, *refs):
+    out_refs, (slot_ref, fill_ref) = refs[: len(caps)], refs[len(caps) :]
     blocks = brick_ref.shape[0]
     C = s.C
     for i in range(s.ny):
         fill_ref[i] = 0
-        out_ref[i] = jnp.full(out_ref.shape[1:], -1.0, F32)
+        for out_ref in out_refs:
+            out_ref[i] = jnp.full(out_ref.shape[1:], -1.0, F32)
     live = count_ref[0]
 
     def step(n, carry):
@@ -174,12 +175,21 @@
             dest = (brick // s.NB) % s.NB // s.byn
             order = fill_ref[dest]
             fill_ref[dest] = order + 1
-            slot_ref[n] = dest * cap + order
+            slot_ref[n] = dest * sum(caps) + order
             lanes = pl.ds(pl.multiple_of(n * 128, 128), 128)
-            out_ref[dest, pl.ds(pl.multiple_of(order * C, 8), C), :] = feat_ref[:, lanes] * area_ref[pl.ds(n, 1), :]
-            points = pos_ref[:, lanes]
-            for d in range(3):
-                out_ref[dest, pl.ds(cap * C + d * cap + order, 1), :] = points[d : d + 1, :]
+            first = 0
+            for cap, out_ref in zip(caps, out_refs):
+                place = order - first
+
+                @pl.when((place >= 0) & (place < cap))
+                def _():
+                    feats = feat_ref[:, lanes] * area_ref[pl.ds(n, 1), :]
+                    out_ref[dest, pl.ds(pl.multiple_of(place * C, 8), C), :] = feats
+                    points = pos_ref[:, lanes]
+                    for d in range(3):
+                        out_ref[dest, pl.ds(cap * C + d * cap + place, 1), :] = points[d : d + 1, :]
+
+                first += cap
 
         @pl.when(n >= live)
         def _():
@@ -191,16 +201,11 @@
 
 
 def field_kernel(s, sdf_ref, gain_ref, out_ref):
+    hi, lo = split(sdf_ref[...].reshape(s.bxn * s.Yl, s.G).T)
     ghi, glo = split(gain_ref[...])
-
-    def step(a, carry):
-        hi, lo = split(sdf_ref[:, a].reshape(s.bxn * s.Yl, s.G).T)
-        wide = dot(hi, ghi) + dot(lo, ghi) + dot(hi, glo)
-        for y in range(s.Yl):
-            out_ref[a, y] = wide[:, y * s.L : (y + 1) * s.L]
-        return carry
-
-    lax.fori_loop(0, B, step, 0)
+    wide = dot(hi, ghi) + dot(lo, ghi) + dot(hi, glo)
+    for y in range(s.Yl):
+        out_ref[0, y] = wide[:, y * s.L : (y + 1) * s.L]
 
 
 def kernel_tiles(points):
@@ -253,10 +258,8 @@
     return block_turn(tiles, s.nx * s.bxn, s.cp)
 
 
-def encode_kernel(s, cap, row_ref, id_ref, num_ref, in_ref, init_ref, table_ref, grid_ref, keep_ref, send_ref):
+def add_blocks(s, cap, id_ref, num_ref, in_ref, grid_ref):
     C = s.C
-    for a in range(B):
-        grid_ref[a] = init_ref[a]
     group = lax.broadcasted_iota(jnp.int32, (s.L, 128), 0) // s.cp % s.bxn
 
     def per_source(src, carry):
@@ -298,12 +301,34 @@
 
     lax.fori_loop(0, s.ny, per_source, 0)
 
+
+def encode_first_kernel(s, cap, id_ref, num_ref, in_ref, init_ref, grid_ref):
+    for a in range(B):
+        grid_ref[a] = init_ref[a]
+    add_blocks(s, cap, id_ref, num_ref, in_ref, grid_ref)
+
+
+def encode_last_kernel(
+    s, cap, row_ref, id_ref, num_ref, in_ref, before_ref, table_ref, grid_ref, keep_ref, send_ref,
+    sum_ref, held_ref, in_sem, out_sems
+):
+    fetch = pltpu.make_async_copy(before_ref, held_ref, in_sem)
+    fetch.start()
+    for a in range(B):
+        sum_ref[a] = jnp.zeros(sum_ref.shape[1:], F32)
+    add_blocks(s, cap, id_ref, num_ref, in_ref, sum_ref)
+    fetch.wait()
+
     def transform(a, carry):
-        out = grid_to_spectrum(s, lambda y: grid_ref[a, y], table_ref[...])
+        held_ref[a] = held_ref[a] + sum_ref[a]
+        pltpu.make_async_copy(held_ref.at[a], grid_ref.at[a], out_sems.at[a]).start()
+        out = grid_to_spectrum(s, lambda y: held_ref[a, y], table_ref[...])
         store_spectrum(s, row_ref[0], a, out, keep_ref, send_ref)
         return carry
 
     lax.fori_loop(0, B, transform, 0)
+    for a in range(B):
+        pltpu.make_async_copy(held_ref.at[a], grid_ref.at[a], out_sems.at[a]).wait()
 
 
 def mixed_rows(rows, whi, wlo):
@@ -321,31 +346,21 @@
 
 def mix_kernel(s, grid_ref, mix_ref, bias_ref, out_ref):
     whi, wlo = split(mix_ref[...])
-
-    def step(a, carry):
-        for y in range(s.Yl):
-            out_ref[a, y] = mixed_rows(grid_ref[a, y], whi, wlo) + bias_ref[...]
-        return carry
-
-    lax.fori_loop(0, B, step, 0)
+    for y in range(s.Yl):
+        out_ref[0, y] = mixed_rows(grid_ref[0, y], whi, wlo) + bias_ref[...]
 
 
 def readout_kernel(s, grid_ref, mix_ref, out_ref):
     whi, wlo = split(mix_ref[...])
     lane = lax.broadcasted_iota(jnp.int32, (B, s.LB), 1)
-
-    def step(a0, carry):
-        for a in range(B):
-            total = jnp.zeros((B, s.LB), F32)
-            for by in range(s.byn):
-                res = mixed_rows(grid_ref[a0, by * B + a], whi, wlo)
-                for bz in range(s.NB):
-                    mine = (lane // (s.bxn * s.byn) == bz) & (lane % s.byn == by)
-                    total = jnp.where(mine, res[bz * B : (bz + 1) * B], total)
-            out_ref[a0, a * B : (a + 1) * B, :] = total
-        return carry
-
-    lax.fori_loop(0, B, step, 0)
+    for a in range(B):
+        total = jnp.zeros((B, s.LB), F32)
+        for by in range(s.byn):
+            res = mixed_rows(grid_ref[0, by * B + a], whi, wlo)
+            for bz in range(s.NB):
+                mine = (lane // (s.bxn * s.byn) == bz) & (lane % s.byn == by)
+                total = jnp.where(mine, res[bz * B : (bz + 1) * B], total)
+        out_ref[0, a * B : (a + 1) * B, :] = total
 
 
 def x_forward_kernel(s, keep_ref, recv_ref, table_ref, out_ref):
@@ -437,23 +452,21 @@
 def layer_kernel(s, row_ref, mixed_ref, inv_ref, fwd_ref, *refs):
     in_refs, (grid_ref, keep_ref, send_ref) = refs[: s.nx], refs[s.nx :]
     row = row_ref[0]
-
-    def step(a, carry):
-        groups = by_distance(s, row, [[ref[a, b] for b in range(s.bxn)] for ref in in_refs])
-        tiles = block_turn([tile for group in groups for tile in group], s.Yl, s.cp)
-        for y in range(0, s.Yl, 2):
-            hi, lo = split(jnp.concatenate([tiles[y], tiles[y + 1]], axis=1))
-            res = dot(inv_ref[...], jnp.concatenate([hi, lo, hi], axis=0))
-            for i in range(2):
-                grid_ref[a, y + i] = gelu(mixed_ref[a, y + i] + res[:, i * s.L : (i + 1) * s.L])
-        out = grid_to_spectrum(s, lambda y: grid_ref[a, y], fwd_ref[...])
-        store_spectrum(s, row, a, out, keep_ref, send_ref)
-        return carry
-
-    lax.fori_loop(0, B, step, 0)
-
-
-def decode_kernel(s, cap, id_ref, num_ref, base_ref, pos_ref, spec_ref, turn_ref, mix_ref, hi_ref, lo_ref, inv_ref, out_ref, s_ref):
+    groups = by_distance(s, row, [[ref[0, b] for b in range(s.bxn)] for ref in in_refs])
+    tiles = block_turn([tile for group in groups for tile in group], s.Yl, s.cp)
+    for y in range(0, s.Yl, 2):
+        hi, lo = split(jnp.concatenate([tiles[y], tiles[y + 1]], axis=1))
+        res = dot(inv_ref[...], jnp.concatenate([hi, lo, hi], axis=0))
+        for i in range(2):
+            grid_ref[0, y + i] = gelu(mixed_ref[0, y + i] + res[:, i * s.L : (i + 1) * s.L])
+    out = grid_to_spectrum(s, lambda y: grid_ref[0, y], fwd_ref[...])
+    store_spectrum(s, row, 0, out, keep_ref, send_ref)
+
+
+def decode_kernel(s, caps, *refs):
+    n = len(caps)
+    id_refs, num_refs, in_refs = refs[:n], refs[n : 2 * n], refs[2 * n : 3 * n]
+    base_ref, spec_ref, turn_ref, mix_ref, hi_ref, lo_ref, inv_ref, out_ref, s_ref = refs[3 * n :]
     modes = jnp.concatenate([spec_ref[i] for i in range(s.ny)], axis=0)
     real_row = lax.broadcasted_iota(jnp.int32, modes.shape, 0) // s.KL % 2 == 0
 
@@ -476,13 +489,19 @@
     out_ref[...] = jnp.zeros(out_ref.shape, F32)
     cell = lax.broadcasted_iota(jnp.int32, (s.LB, 128), 0)
 
+    first = 0
+    for cap, id_ref, num_ref, pos_ref in zip(caps, id_refs, num_refs, in_refs):
+        decode_blocks(s, cap, sum(caps), first, id_ref, num_ref, pos_ref, cell, s_ref, out_ref)
+        first += cap
+
+
+def decode_blocks(s, cap, all_caps, first, id_ref, num_ref, pos_ref, cell, s_ref, out_ref):
     def per_source(src, carry):
         def per_pair(h, inner):
             shi, slo = split(s_ref[...])
             picks = []
             for i in range(2):
-                j = h * 2 + i
-                at = id_ref[6, src * cap + j]
+                at = id_ref[6, src * cap + h * 2 + i]
                 picks.append(jnp.where(cell == at, 1.0, 0.0).astype(BF))
             pick = jnp.concatenate(picks, axis=1)
             if s.LB == 128:
@@ -504,7 +523,7 @@
                     low = low + tile
                 top = jnp.sum(top, axis=0, keepdims=True)
                 low = jnp.sum(low, axis=0, keepdims=True)
-                out_ref[pl.ds(slot, 1), :] = top / jnp.where(low > 0.0, low, 1.0)
+                out_ref[pl.ds(src * all_caps + first + j, 1), :] = top / jnp.where(low > 0.0, low, 1.0)
             return inner
 
         return lax.fori_loop(0, (num_ref[src] + 1) // 2, per_pair, carry)
@@ -535,21 +554,22 @@
     cap = blocks // ny
     PB = positions.shape[1] // blocks
     C, G, M, L = s.C, s.G, s.M, s.L
-    rows = cap * (C + 3)
-
-    outgoing, slot_of = call(
-        functools.partial(pack_kernel, s, cap),
+    large = cap * 5 // 16 * 2
+    caps = (large, cap - large)
+
+    *outgoing, slot_of = call(
+        functools.partial(pack_kernel, s, caps),
         "pack",
-        (shape(ny, rows, PB), jax.ShapeDtypeStruct((blocks,), jnp.int32)),
+        tuple(shape(ny, part * (C + 3), PB) for part in caps) + (jax.ShapeDtypeStruct((blocks,), jnp.int32),),
         [SM, SM, VM, VM, VM],
-        (VM, SM),
+        (VM,) * len(caps) + (SM,),
         1e6,
         6e6,
         scratch=[pltpu.SMEM((ny,), jnp.int32)],
     )(block_brick, block_count, positions, point_feat, area.reshape(blocks, PB))
-    incoming = lax.all_to_all(outgoing, "gy", split_axis=0, concat_axis=0, tiled=True)
-
-    def placement(incoming):
+    early, late = (lax.all_to_all(part, "gy", split_axis=0, concat_axis=0, tiled=True) for part in outgoing)
+
+    def placement(incoming, cap):
         in_pos = incoming[:, cap * C :, :]
         first = in_pos.reshape(ny, 3, cap, PB)[..., 0].transpose(1, 0, 2).reshape(3, ny * cap)
         counts = jnp.sum((first[0].reshape(ny, cap) >= 0.0).astype(jnp.int32), axis=1)
@@ -573,9 +593,18 @@
     )
     gains = jnp.where(spread, gain_l, 0.0).reshape(s.bxn * s.Yl, s.Yl * L)
     grid_shape = shape(B, s.Yl, G, L)
-    init = call(functools.partial(field_kernel, s), "field", grid_shape, [VM, VM], VM, 3e9, 1e7)(
-        sdf.reshape(s.bxn, B, s.Yl, G), gains
-    )
+    grid_block = pl.BlockSpec((1, s.Yl, G, L), lambda a: (a, 0, 0, 0))
+    whole = lambda array: pl.BlockSpec(array.shape, lambda a: (0,) * array.ndim)
+    init = call(
+        functools.partial(field_kernel, s),
+        "field",
+        grid_shape,
+        [pl.BlockSpec((s.bxn, None, s.Yl, G), lambda a: (0, a, 0, 0)), whole(gains)],
+        grid_block,
+        3e9,
+        1e7,
+        grid=(B,),
+    )(sdf.reshape(s.bxn, B, s.Yl, G), gains)
 
     on_lanes = lambda v: jnp.broadcast_to(v.reshape(nx, 1, s.cp), (nx, s.bxn, s.cp)).reshape(1, L)
     mixing = mix_w[0].T.reshape(nx, 1, s.cp, nx, 1, s.cp)
@@ -607,24 +636,39 @@
     x_fwd = lax.dynamic_index_in_dim(t["x_fwd"], row_x, 0, False)
     x_inv = lax.dynamic_index_in_dim(t["x_inv"], row_x, 0, False)
     row = row_x.astype(jnp.int32).reshape(1)
-    prepared = (incoming, init, mixing, bias, base, reading, u0, v0, u1, v1, turns, x_fwd, x_inv, row)
-    incoming, init, mixing, bias, base, reading, u0, v0, u1, v1, turns, x_fwd, x_inv, row = (
+    prepared = (early, init, mixing, bias, base, reading, u0, v0, u1, v1, turns, x_fwd, x_inv, row)
+    early, init, mixing, bias, base, reading, u0, v0, u1, v1, turns, x_fwd, x_inv, row = (
         lax.optimization_barrier(prepared)
     )
-    ids, counts, in_pos = placement(incoming)
+    ids_a, counts_a, pos_a = placement(early, caps[0])
+    ids_b, counts_b, pos_b = placement(late, caps[1])
 
     half = s.nx // 2
     spec_shape = shape(half, B, s.bxn, s.K2, s.LY)
+    before = call(
+        functools.partial(encode_first_kernel, s, caps[0]),
+        "encode_first",
+        grid_shape,
+        [SM, SM, VM, VM],
+        VM,
+        3e9,
+        2e7,
+    )(ids_a, counts_a, early, init)
     grid, keep, send = call(
-        functools.partial(encode_kernel, s, cap),
-        "encode",
+        functools.partial(encode_last_kernel, s, caps[1]),
+        "encode_last",
         (grid_shape, spec_shape, spec_shape),
-        [SM, SM, SM, VM, VM, VM],
-        (VM, VM, VM),
+        [SM, SM, SM, VM, pl.BlockSpec(memory_space=pl.ANY), VM],
+        (pl.BlockSpec(memory_space=pl.ANY), VM, VM),
         4e9,
         2.2e7,
-        aliases={4: 0},
-    )(row, ids, counts, incoming, init, t["z_fwd"])
+        scratch=[
+            pltpu.VMEM(grid_shape.shape, F32),
+            pltpu.VMEM(grid_shape.shape, F32),
+            pltpu.SemaphoreType.DMA,
+            pltpu.SemaphoreType.DMA((B,)),
+        ],
+    )(row, ids_b, counts_b, late, before, t["z_fwd"])
 
     def exchange(array, distance):
         return lax.ppermute(array, "gx", [(i, i ^ distance) for i in range(nx)])
@@ -644,6 +688,7 @@
                 2e8,
                 3e6,
                 grid=(1,),
+                room=16,
             )(keep, recv, x_fwd)
 
         others = [exchange(part(d), 2 * d) for d in range(1, half)]
@@ -655,13 +700,22 @@
 
     spec = to_modes(keep, send)
     mixed = call(
-        functools.partial(mix_kernel, s), "mix", grid_shape, [VM] * 3, VM, 2e9, 1.7e7, aliases={0: 0}
+        functools.partial(mix_kernel, s),
+        "mix",
+        grid_shape,
+        [grid_block, whole(mixing), whole(bias)],
+        grid_block,
+        2e9,
+        1.7e7,
+        grid=(B,),
     )(grid, mixing, bias)
     spec = call(
-        functools.partial(y_kernel, s), "y_both", shape(G * s.cp, s.LK), [VM] * 5, VM, 1e9, 2e6
+        functools.partial(y_kernel, s), "y_both", shape(G * s.cp, s.LK), [VM] * 5, VM, 1e9, 2e6, room=16
     )(spec, t["y_fwd"], t["y_inv"], u0, v0)
     spec = lax.all_to_all(spec.reshape(ny, s.LY, s.LK), "gy", split_axis=0, concat_axis=0, tiled=True)
-    near = [spec] + [exchange(spec, 2 * d) for d in range(1, half)]
+    near = [exchange(spec, 2 * d) for d in range(1, half)]
+    mixed, *near = lax.optimization_barrier((mixed, *near))
+    near = [spec] + near
     fields = []
     for item in near:
         own, other = call(
@@ -672,25 +726,35 @@
             (VM, VM),
             3e8,
             3e6,
+            room=16,
         )(item, x_inv)
         fields += [own, exchange(other, 1)]
     fields = [f.reshape(B, s.bxn, s.K2, s.LY) for f in fields]
+    field_block = pl.BlockSpec((1, s.bxn, s.K2, s.LY), lambda a: (a, 0, 0, 0))
+    spec_block = pl.BlockSpec((half, 1, s.bxn, s.K2, s.LY), lambda a: (0, a, 0, 0, 0))
     grid, keep, send = call(
         functools.partial(layer_kernel, s),
         "layer",
         (grid_shape, spec_shape, spec_shape),
-        [SM] + [VM] * (3 + nx),
-        (VM, VM, VM),
+        [SM, grid_block, whole(t["z_inv"]), whole(t["z_fwd"])] + [field_block] * nx,
+        (grid_block, spec_block, spec_block),
         4e9,
         2.1e7,
-        aliases={1: 0},
+        grid=(B,),
     )(row, mixed, t["z_inv"], t["z_fwd"], *fields)
     spec = to_modes(keep, send)
     read = call(
-        functools.partial(readout_kernel, s), "readout", shape(B, B * B, s.LB), [VM, VM], VM, 2e9, 9e6
+        functools.partial(readout_kernel, s),
+        "readout",
+        shape(B, B * B, s.LB),
+        [grid_block, whole(reading)],
+        pl.BlockSpec((1, B * B, s.LB), lambda a: (a, 0, 0)),
+        2e9,
+        9e6,
+        grid=(B,),
     )(grid, reading)
     last = call(
-        functools.partial(y_last_kernel, s), "y_last", shape(2 * s.KL, M * M), [VM] * 4, VM, 1e9, 1e6
+        functools.partial(y_last_kernel, s), "y_last", shape(2 * s.KL, M * M), [VM] * 4, VM, 1e9, 1e6, room=16
     )(spec, t["y_fwd"], u1, v1)
 
     step = 1
@@ -700,15 +764,16 @@
     last = jnp.broadcast_to(last[None], (ny,) + last.shape)
     last = lax.all_to_all(last, "gy", split_axis=0, concat_axis=0, tiled=True)
     values = call(
-        functools.partial(decode_kernel, s, cap),
+        functools.partial(decode_kernel, s, caps),
         "decode",
         shape(ny * cap, PB),
-        [SM, SM, SM] + [VM] * 7,
+        [SM] * 4 + [VM] * 2 + [SM] + [VM] * 6,
         VM,
         4e9,
         6e6,
         scratch=[pltpu.VMEM((B * B * B, s.LB), F32)],
-    )(ids, counts, base, in_pos, last, turns, read.reshape(B * B * B, s.LB), t["xy_hi"], t["xy_lo"], t["z_last"])
+        room=32,
+    )(ids_a, ids_b, counts_a, counts_b, pos_a, pos_b, base, last, turns, read.reshape(B * B * B, s.LB), t["xy_hi"], t["xy_lo"], t["z_last"])
     returned = lax.all_to_all(values.reshape(ny, cap, PB), "gy", split_axis=0, concat_axis=0, tiled=True)
     choose = (slot_of[:, None] == jnp.arange(ny * cap, dtype=jnp.int32)[None, :]).astype(F32)
     pressure = jnp.dot(choose, returned.reshape(ny * cap, PB), precision=lax.Precision.HIGHEST)

time: 305 us -> 301 us (0.987)
  local copies, waits for them, and re-layouts: 42.3 us -> 21.6 us
  Pallas kernels: 84.3 us -> 102 us
  starting transfers between devices: 28.8 us -> 21.6 us
  blocking collectives: 76 us -> 82.9 us
    unnamed x53 -> x44, local copies, waits for them, and re-layouts: 24.8 us -> 7.45 us
    ppermute x7, starting transfers between devices: 18.1 us -> 4.97 us  [exchange(): return lax.ppermute(array, 'gx', [(i, i ^ distance) for i in range(nx)])]
    pallas_call x5 -> x6, Pallas kernels: 60.8 us -> 72.8 us  [the longest x1 21.5 us: per_device(): call(functools.partial(encode_first_kernel, s, caps[0]), 'encode_first',...]
    all_to_all x2, blocking collectives: 36.5 us -> 45.1 us  [to_modes(): spec = lax.all_to_all(spec, 'gy', split_axis=0, concat_axis=0, tiled=True)]
    ppermute x7, waiting for transfers between devices: 38.4 us -> 30.1 us  [exchange(): return lax.ppermute(array, 'gx', [(i, i ^ distance) for i in range(nx)])]
    all_to_all x1 -> x2, waiting for transfers between devices: 22.2 us -> 29.6 us  [per_device(): lax.all_to_all(part, 'gy', split_axis=0, concat_axis=0, tiled=True)]
    all_to_all x1 -> x2, starting transfers between devices: 6.16 us -> 11.6 us  [per_device(): lax.all_to_all(part, 'gy', split_axis=0, concat_axis=0, tiled=True)]
    pallas_call x1, Pallas kernels: 3.71 us -> 8.23 us  [per_device(): call(functools.partial(readout_kernel, s), 'readout', shape(B, B * B, s.L...]
  transfers between devices with their start and end apart: 11 -> 12, of which waited for: 9 -> 9; matrix products, arithmetic and copies ran while one was open for 7% -> 6% of each run, Pallas kernels for 11% -> 10%
where the time goes in v4:
time: 301 us
  Pallas kernels  102 us (34%)
  blocking collectives  82.9 us (28%)
  waiting for transfers between devices  63.4 us (21%)
  starting transfers between devices  21.6 us (7%)
  local copies, waits for them, and re-layouts  21.6 us (7%)
  other arithmetic  7.07 us (2%)
    all_to_all x2, blocking collectives, to_modes(): spec = lax.all_to_all(spec, 'gy', split_axis=0, concat_axis=0, tiled=True)  45.1 us
    ppermute x7, waiting for transfers between devices, exchange(): return lax.ppermute(array, 'gx', [(i, i ^ distance) for i in range(nx)])  30.1 us
    all_to_all x2, waiting for transfers between devices, per_device(): lax.all_to_all(part, 'gy', split_axis=0, concat_axis=0, tiled=True)  29.6 us
    pallas_call x1, Pallas kernels, per_device(): call(functools.partial(encode_first_kernel, s, caps[0]), 'encode_first',...  21.5 us
    all_to_all x1, blocking collectives, per_device(): lax.all_to_all(values.reshape(ny, cap, PB), 'gy', split_axis=0, concat_ax...  20.4 us
    all_to_all x1, blocking collectives, per_device(): lax.all_to_all(spec.reshape(ny, s.LY, s.LK), 'gy', split_axis=0, concat_a...  17.4 us
    pallas_call x1, Pallas kernels, per_device(): call(functools.partial(decode_kernel, s, caps), 'decode', shape(ny * cap,...  13.5 us
    pallas_call x1, Pallas kernels, per_device(): call(functools.partial(layer_kernel, s), 'layer', (grid_shape, spec_shape...  13.4 us
  transfers between devices with their start and end apart: 12, of which 9 were waited for; matrix products, arithmetic and copies ran while one was open for 6% of the time, Pallas kernels for 10%

profile of v4, /device:TPU:0, one launch (start us, length us, event | category | flops | bytes accessed | tf_op | source)
XLA Modules:
  0.0 300.8 jit_solution(5843073984798634436)
XLA Ops:
  0.7 7.2 %pack.1 = (f32[8,350,128]{2,1,0:T(8,128)}, f32[8,210,128]{2,1,0:T(8,128)}, s32[128]{0:T(128)}) custom-call(s32[128]{0:T(128)} %brick_ref.1, s32[1]{0:T(128)S(6)} %copy.55.count_ref, f32[3,16384]{1,0:T(4,128)} %pos_ref.1, f32[32,16384]{1,0:T(8,128)} %feat_ref.1, f32[128,128]{1,0:T(8,128)} %bitcast.88), custom_call_target="tpu_custom_call" | custom-call | flops 1000000 | bytes 6000000 | tf_op jit(solution)/shard_map/pack/pallas_call | solution.py:560
  7.8 8.0 %all-to-all-start.1 = ((f32[8,210,128]{2,1,0:T(8,128)}), f32[8,210,128]{2,1,0:T(8,128)S(1)}, u32[]{:S(2)}, u32[]{:S(2)}) async-start(f32[8,210,128]{2,1,0:T(8,128)} %get-tuple-element.37), calls=%async_computation.1 | async-start | bytes 1769472 | tf_op jit(solution)/shard_map/all_to_all | solution.py:570
  16.6 0.8 fusion.1
  21.9 1.0 fusion.10
  27.5 1.1 reshape.400
  29.3 0.9 dynamic-slice_bitcast_fusion.1.table_ref
  30.1 0.9 dynamic-slice_bitcast_fusion.table_ref
  31.1 7.2 %all-to-all-done.1.in_ref = f32[8,210,128]{2,1,0:T(8,128)S(1)} async-done(((f32[8,210,128]{2,1,0:T(8,128)}), f32[8,210,128]{2,1,0:T(8,128)S(1)}, u32[]{:S(2)}, u32[]{:S(2)}) %all-to-all-start.1) | async-done | bytes 860192 | tf_op jit(solution)/shard_map/all_to_all | solution.py:570
  38.3 3.6 %all-to-all-start = ((f32[8,350,128]{2,1,0:T(8,128)}), f32[8,350,128]{2,1,0:T(8,128)S(1)}, u32[]{:S(2)}, u32[]{:S(2)}) async-start(f32[8,350,128]{2,1,0:T(8,128)} %get-tuple-element.35), calls=%async_computation | async-start | bytes 2883584 | tf_op jit(solution)/shard_map/all_to_all | solution.py:570
  42.7 0.8 bitcast_select_fusion.gain_ref
  43.6 8.3 %field.1.init_ref = f32[8,16,128,128]{3,2,1,0:T(8,128)} custom-call(f32[4,8,16,128]{3,2,1,0:T(8,128)} %bitcast.91, f32[64,2048]{1,0:T(8,128)} %bitcast_select_fusion.gain_ref), custom_call_target="tpu_custom_call" | custom-call | flops 3000000000 | bytes 10000000 | tf_op jit(solution)/shard_map/field/pallas_call | solution.py:598
  53.7 22.5 %all-to-all-done.in_ref = f32[8,350,128]{2,1,0:T(8,128)S(1)} async-done(((f32[8,350,128]{2,1,0:T(8,128)}), f32[8,350,128]{2,1,0:T(8,128)S(1)}, u32[]{:S(2)}, u32[]{:S(2)}) %all-to-all-start) | async-done | bytes 1433632 | tf_op jit(solution)/shard_map/all_to_all | solution.py:570
  78.1 21.5 %encode_first.1.before_ref = f32[8,16,128,128]{3,2,1,0:T(8,128)} custom-call(s32[8,80]{1,0:T(8,128)} %concatenate.26.id_ref.refs_0_, s32[8]{0:T(128)} %get-tuple-element.65.num_ref.refs_2_, f32[8,350,128]{2,1,0:T(8,128)} %copy-done.14, f32[8,16,128,128]{3,2,1,0:T(8,128)} %field.1.init_ref), custom_call_target="tpu_custom_call" | custom-call | flops 3000000000 | bytes 20000000 | tf_op jit(solution)/shard_map/encode_first/pallas_call | solution.py:648
  99.6 11.8 %encode_last.1 = (f32[8,16,128,128]{3,2,1,0:T(8,128)}, f32[2,8,4,32,128]{4,3,2,1,0:T(8,128)}, f32[2,8,4,32,128]{4,3,2,1,0:T(8,128)}) custom-call(s32[1]{0:T(128)} %bitcast.12.row_ref, s32[8,48]{1,0:T(8,128)} %concatenate.27.id_ref.refs_1_, s32[8]{0:T(128)} %get-tuple-element.63.num_ref.refs_3_, f32[8,210,128]{2,1,0:T(8,128)} %copy-done.15, ...), custom_call_target="tpu_custom_call" | custom-call | flops 4000000000 | bytes 22000000 | tf_op jit(solution)/shard_map/encode_last/pallas_call | solution.py:657
  111.5 2.9 collective-permute-done
  114.3 1.2 copy-done.1
  115.6 0.9 x_forward.5
  116.5 1.9 collective-permute-start.1
  118.3 0.9 x_forward.4
  119.2 11.3 %collective-permute-done.1 = f32[8,128,128]{2,1,0:T(8,128)S(1)} collective-permute-done((f32[8,128,128]{2,1,0:T(8,128)S(1)}, f32[8,128,128]{2,1,0:T(8,128)S(1)}, u32[]{:S(2)}, u32[]{:S(2)}) %collective-permute-start.1) | collective-permute-done | bytes 524320 | tf_op jit(solution)/shard_map/ppermute | solution.py:674
  130.6 27.4 %all_to_all.35 = f32[8,128,128]{2,1,0:T(8,128)S(1)} all-to-all(f32[8,128,128]{2,1,0:T(8,128)S(1)} %add.162), channel_id=1, replica_groups=mesh['gx'=4,'gy'=8] {'gy'}, dimensions={0} | all-to-all | bytes 1048576 | tf_op jit(solution)/shard_map/all_to_all | solution.py:698
  158.0 1.0 y_both.1
  159.1 17.4 %all_to_all.36.in_ref = f32[8,128,128]{2,1,0:T(8,128)S(1)} all-to-all(f32[8,128,128]{2,1,0:T(8,128)S(1)} %bitcast.75), channel_id=1, replica_groups=mesh['gx'=4,'gy'=8] {'gy'}, dimensions={0} | all-to-all | bytes 1048576 | tf_op jit(solution)/shard_map/all_to_all | solution.py:715
  177.3 10.5 %mix.1.mixed_ref = f32[8,16,128,128]{3,2,1,0:T(8,128)} custom-call(f32[8,16,128,128]{3,2,1,0:T(8,128)} %get-tuple-element.41.grid_ref, f32[128,128]{1,0:T(8,128)} %get-tuple-element.42.mix_ref, f32[1,128]{1,0:T(1,128)} %reshape.401.bias_ref), custom_call_target="tpu_custom_call" | custom-call | flops 2000000000 | bytes 17000000 | tf_op jit(solution)/shard_map/mix/pallas_call | solution.py:702
  187.8 1.3 x_inverse.2
  189.1 0.8 copy-done.9
  189.9 1.3 x_inverse.3
  191.2 0.8 copy-done.10
  192.6 1.5 collective-permute-done.4
  194.1 0.8 copy-done.20
  194.9 13.4 %layer.1 = (f32[8,16,128,128]{3,2,1,0:T(8,128)}, f32[2,8,4,32,128]{4,3,2,1,0:T(8,128)}, f32[2,8,4,32,128]{4,3,2,1,0:T(8,128)}) custom-call(s32[1]{0:T(128)} %bitcast.12.row_ref, f32[8,16,128,128]{3,2,1,0:T(8,128)} %mix.1.mixed_ref, bf16[128,96]{1,0:T(8,128)(2,1)} %constant.142.clone.inv_ref, bf16[64,256]{1,0:T(8,128)(2,1)} %constant.141.clone.table_ref.fwd_ref, ...), custom_call_target="tpu_custom_call" | custom-call | flops 4000000000 | bytes 21000000 | tf_op jit(solution)/shard_map/layer/pallas_call | solution.py:735
  208.7 2.5 collective-permute-done.5
  211.2 1.2 copy-done
  212.4 0.9 x_forward.7
  213.3 1.4 collective-permute-start.6
  214.8 0.9 x_forward.6
  215.7 11.9 %collective-permute-done.6 = f32[8,128,128]{2,1,0:T(8,128)S(1)} collective-permute-done((f32[8,128,128]{2,1,0:T(8,128)S(1)}, f32[8,128,128]{2,1,0:T(8,128)S(1)}, u32[]{:S(2)}, u32[]{:S(2)}) %collective-permute-start.6) | collective-permute-done | bytes 524320 | tf_op jit(solution)/shard_map/ppermute | solution.py:674
  227.7 17.7 %all_to_all.37 = f32[8,128,128]{2,1,0:T(8,128)S(1)} all-to-all(f32[8,128,128]{2,1,0:T(8,128)S(1)} %add.163), channel_id=1, replica_groups=mesh['gx'=4,'gy'=8] {'gy'}, dimensions={0} | all-to-all | bytes 1048576 | tf_op jit(solution)/shard_map/all_to_all | solution.py:698
  246.0 1.2 collective-permute-done.7
  247.2 1.3 collective-permute-start.8
  248.5 2.5 collective-permute-done.8
  251.6 3.6 %all-to-all-start.5 = ((f32[8,4,1024]{2,1,0:T(4,128)}), f32[8,4,1024]{2,1,0:T(4,128)S(1)}, u32[]{:S(2)}, u32[]{:S(2)}) async-start(f32[8,4,1024]{2,1,0:T(4,128)} %broadcast_in_dim.111), calls=%async_computation.5 | async-start | bytes 262144 | tf_op jit(solution)/shard_map/all_to_all | solution.py:765
  255.2 8.2 %readout.1 = f32[8,64,128]{2,1,0:T(8,128)} custom-call(f32[8,16,128,128]{3,2,1,0:T(8,128)} %get-tuple-element.61.grid_ref, f32[128,128]{1,0:T(8,128)} %get-tuple-element.62.mix_ref), custom_call_target="tpu_custom_call" | custom-call | flops 2000000000 | bytes 9000000 | tf_op jit(solution)/shard_map/readout/pallas_call | solution.py:746
  263.5 0.9 copy-done.2
  264.5 1.6 copy-done.8
  266.1 13.5 %decode.1 = f32[128,128]{1,0:T(8,128)S(1)} custom-call(s32[8,80]{1,0:T(8,128)S(1)} %copy-done.3, s32[8,48]{1,0:T(8,128)S(1)} %copy-done.4, s32[8]{0:T(128)S(1)} %copy-done.5, s32[8]{0:T(128)S(1)} %copy-done.6, f32[8,30,128]{2,1,0:T(8,128)S(1)} %slice.92.refs_4_, f32[8,18,128]{2,1,0:T(8,128)S(1)} %slice.112.refs_5_, f32[1]{0:T(128)} %bitcast.6.refs_6_, ...), custom_call_target="tpu_custom_call" | custom-call | flops 4000000000 | bytes 6000000 | tf_op jit(solution)/shard_map/decode/pallas_call | solution.py:766
  279.6 20.4 %all_to_all.38 = f32[8,16,128]{2,1,0:T(8,128)S(1)} all-to-all(f32[8,16,128]{2,1,0:T(8,128)S(1)} %bitcast.78), channel_id=1, replica_groups=mesh['gx'=4,'gy'=8] {'gy'}, dimensions={0} | all-to-all | bytes 131072 | tf_op jit(solution)/shard_map/all_to_all | solution.py:777
  300.0 0.9 convolution_bitcast_fusion
  (117 shorter events, 18.2 us)
Async XLA Ops:
  7.8 30.4 %all-to-all-start.1 = ((f32[8,210,128]{2,1,0:T(8,128)}), f32[8,210,128]{2,1,0:T(8,128)S(1)}, u32[]{:S(2)}, u32[]{:S(2)}) async-start(f32[8,210,128]{2,1,0:T(8,128)} %get-tuple-element.37), calls=%async_computation.1 | async-start | bytes 1769472 | tf_op jit(solution)/shard_map/all_to_all | solution.py:570
  22.9 5.8 %copy-start.18 = (f32[32]{0:T(128)S(1)}, f32[32]{0:T(128)}, u32[]{:S(2)}) copy-start(f32[32]{0:T(128)} %param.33) | copy-start | bytes 388
  22.9 5.8 %copy-start.21 = (f32[2,32]{1,0:T(2,128)S(1)}, f32[2,32]{1,0:T(2,128)}, u32[]{:S(2)}) copy-start(f32[2,32]{1,0:T(2,128)} %param.31) | copy-start | bytes 772
  27.5 25.5 %copy-start.16 = (s32[3]{0:T(128)S(1)}, s32[3]{0:T(128)}, u32[]{:S(2)}) copy-start(s32[3]{0:T(128)} %constant.151.clone) | copy-start | bytes 40
  38.2 61.4 %copy-start.15 = (f32[8,210,128]{2,1,0:T(8,128)}, f32[8,210,128]{2,1,0:T(8,128)S(1)}, u32[]{:S(2)}) copy-start(f32[8,210,128]{2,1,0:T(8,128)S(1)} %all-to-all-done.1.in_ref) | copy-start | bytes 2580484
  38.3 37.9 %all-to-all-start = ((f32[8,350,128]{2,1,0:T(8,128)}), f32[8,350,128]{2,1,0:T(8,128)S(1)}, u32[]{:S(2)}, u32[]{:S(2)}) async-start(f32[8,350,128]{2,1,0:T(8,128)} %get-tuple-element.35), calls=%async_computation | async-start | bytes 2883584 | tf_op jit(solution)/shard_map/all_to_all | solution.py:570
  76.2 2.0 copy-start.14
  99.6 58.4 %copy-start.11 = (bf16[128,256]{1,0:T(8,128)(2,1)S(1)}, bf16[128,256]{1,0:T(8,128)(2,1)}, u32[]{:S(2)}) copy-start(bf16[128,256]{1,0:T(8,128)(2,1)} %constant.146.clone.fwd_ref) | copy-start | bytes 196612
  99.6 58.4 %copy-start.12 = (bf16[128,192]{1,0:T(8,128)(2,1)S(1)}, bf16[128,192]{1,0:T(8,128)(2,1)}, u32[]{:S(2)}) copy-start(bf16[128,192]{1,0:T(8,128)(2,1)} %constant.147.clone.inv_ref) | copy-start | bytes 147460
  111.4 2.9 collective-permute-start
  114.3 1.2 copy-start.1
  116.5 14.1 %collective-permute-start.1 = (f32[8,128,128]{2,1,0:T(8,128)S(1)}, f32[8,128,128]{2,1,0:T(8,128)S(1)}, u32[]{:S(2)}, u32[]{:S(2)}) collective-permute-start(f32[8,128,128]{2,1,0:T(8,128)S(1)} %x_forward.5), channel_id=1, source_target_pairs={{0,16},{8,24},{16,0},{24,8},{1,17},{9,25},{17,1},{25,9},{2,18},{10... | collective-permute-start | bytes 1572872 | tf_op jit(solution)/shard_map/ppermute | solution.py:674
  176.5 13.4 %collective-permute-start.2 = (f32[8,128,128]{2,1,0:T(8,128)S(1)}, f32[8,128,128]{2,1,0:T(8,128)S(1)}, u32[]{:S(2)}, u32[]{:S(2)}) collective-permute-start(f32[8,128,128]{2,1,0:T(8,128)S(1)} %all_to_all.36.in_ref), channel_id=1, source_target_pairs={{0,16},{8,24},{16,0},{24,8},{1,17},{9,25},{17,1},{25,9},{2,18},{10... | collective-permute-start | bytes 1572872 | tf_op jit(solution)/shard_map/ppermute | solution.py:674
  189.1 0.8 copy-start.9
  189.9 2.6 collective-permute-start.3
  191.2 0.8 copy-start.10
  192.0 2.0 collective-permute-start.4
  192.6 1.5 copy-start.19
  194.1 0.8 copy-start.20
  208.3 2.9 collective-permute-start.5
  211.2 1.2 copy-start
  213.3 14.3 %collective-permute-start.6 = (f32[8,128,128]{2,1,0:T(8,128)S(1)}, f32[8,128,128]{2,1,0:T(8,128)S(1)}, u32[]{:S(2)}, u32[]{:S(2)}) collective-permute-start(f32[8,128,128]{2,1,0:T(8,128)S(1)} %x_forward.7), channel_id=1, source_target_pairs={{0,16},{8,24},{16,0},{24,8},{1,17},{9,25},{17,1},{25,9},{2,18},{10... | collective-permute-start | bytes 1572872 | tf_op jit(solution)/shard_map/ppermute | solution.py:674
  215.7 47.8 %copy-start.3 = (s32[8,80]{1,0:T(8,128)S(1)}, s32[8,80]{1,0:T(8,128)}, u32[]{:S(2)}) copy-start(s32[8,80]{1,0:T(8,128)} %concatenate.26.id_ref.refs_0_) | copy-start | bytes 7684
  215.7 47.8 %copy-start.4 = (s32[8,48]{1,0:T(8,128)S(1)}, s32[8,48]{1,0:T(8,128)}, u32[]{:S(2)}) copy-start(s32[8,48]{1,0:T(8,128)} %concatenate.27.id_ref.refs_1_) | copy-start | bytes 4612
  215.7 47.8 %copy-start.5 = (s32[8]{0:T(128)S(1)}, s32[8]{0:T(128)}, u32[]{:S(2)}) copy-start(s32[8]{0:T(128)} %get-tuple-element.65.num_ref.refs_2_) | copy-start | bytes 100
  215.7 47.8 %copy-start.6 = (s32[8]{0:T(128)S(1)}, s32[8]{0:T(128)}, u32[]{:S(2)}) copy-start(s32[8]{0:T(128)} %get-tuple-element.63.num_ref.refs_3_) | copy-start | bytes 100
  215.7 47.8 %copy-start.7 = (bf16[2048,512]{1,0:T(8,128)(2,1)S(1)}, bf16[2048,512]{1,0:T(8,128)(2,1)}, u32[]{:S(2)}) copy-start(bf16[2048,512]{1,0:T(8,128)(2,1)} %constant.149.clone.refs_11_) | copy-start | bytes 6291460
  215.7 47.8 %copy-start.13 = (bf16[128,96]{1,0:T(8,128)(2,1)S(1)}, bf16[128,96]{1,0:T(8,128)(2,1)}, u32[]{:S(2)}) copy-start(bf16[128,96]{1,0:T(8,128)(2,1)} %constant.143.clone.refs_12_) | copy-start | bytes 73732
  245.9 1.2 collective-permute-start.7
  247.2 3.7 %collective-permute-start.8 = (f32[4,1024]{1,0:T(4,128)S(1)}, f32[4,1024]{1,0:T(4,128)S(1)}, u32[]{:S(2)}, u32[]{:S(2)}) collective-permute-start(f32[4,1024]{1,0:T(4,128)S(1)} %add.164), channel_id=1, source_target_pairs={{0,16},{8,24},{16,0},{24,8},{1,17},{9,25},{17,1},{25,9},{2,18},{10... | collective-permute-start | bytes 49160 | tf_op jit(solution)/shard_map/ppermute | solution.py:762
  251.6 11.9 %all-to-all-start.5 = ((f32[8,4,1024]{2,1,0:T(4,128)}), f32[8,4,1024]{2,1,0:T(4,128)S(1)}, u32[]{:S(2)}, u32[]{:S(2)}) async-start(f32[8,4,1024]{2,1,0:T(4,128)} %broadcast_in_dim.111), calls=%async_computation.5 | async-start | bytes 262144 | tf_op jit(solution)/shard_map/all_to_all | solution.py:765
  263.5 36.5 %copy-start.17 = (s32[128]{0:T(128)S(1)}, s32[128]{0:T(128)}, u32[]{:S(2)}) copy-start(s32[128]{0:T(128)} %get-tuple-element.34) | copy-start | bytes 1540
  263.5 1.0 copy-start.2
  264.5 1.6 copy-start.8

commit v5 on v4

--- a/solution.py
+++ b/solution.py
@@ -466,8 +466,14 @@
 def decode_kernel(s, caps, *refs):
     n = len(caps)
     id_refs, num_refs, in_refs = refs[:n], refs[n : 2 * n], refs[2 * n : 3 * n]
-    base_ref, spec_ref, turn_ref, mix_ref, hi_ref, lo_ref, inv_ref, out_ref, s_ref = refs[3 * n :]
-    modes = jnp.concatenate([spec_ref[i] for i in range(s.ny)], axis=0)
+    col_ref, base_ref, turn_ref, mix_ref, hi_ref, lo_ref, inv_ref = refs[3 * n : 3 * n + 7]
+    spec_refs, out_refs = refs[3 * n + 7 : 3 * n + 7 + s.ny], refs[3 * n + 7 + s.ny : 3 * n + 7 + 2 * s.ny]
+    s_ref, modes_ref, out_ref = refs[3 * n + 7 + 2 * s.ny :]
+    col = col_ref[0]
+    for e in range(s.ny):
+        for r in range(2 * s.KL):
+            modes_ref[pl.ds((col ^ e) * 2 * s.KL + r, 1), :] = spec_refs[e][r : r + 1, :]
+    modes = modes_ref[...]
     real_row = lax.broadcasted_iota(jnp.int32, modes.shape, 0) // s.KL % 2 == 0
 
     def partner(x):
@@ -493,6 +499,22 @@
     for cap, id_ref, num_ref, pos_ref in zip(caps, id_refs, num_refs, in_refs):
         decode_blocks(s, cap, sum(caps), first, id_ref, num_ref, pos_ref, cell, s_ref, out_ref)
         first += cap
+    for e in range(s.ny):
+        out_refs[e][...] = out_ref[pl.ds(pl.multiple_of((col ^ e) * sum(caps), 8), sum(caps)), :]
+
+
+def return_kernel(s, cap, col_ref, slot_ref, *refs):
+    in_refs, (out_ref, held_ref) = refs[: s.ny], refs[s.ny :]
+    for e in range(s.ny):
+        held_ref[pl.ds(pl.multiple_of((col_ref[0] ^ e) * cap, 8), cap), :] = in_refs[e][...]
+
+    def step(n, carry):
+        slot = slot_ref[n]
+        line = held_ref[pl.ds(jnp.maximum(slot, 0), 1), :]
+        out_ref[pl.ds(n, 1), :] = jnp.where(slot >= 0, line, 0.0)
+        return carry
+
+    lax.fori_loop(0, out_ref.shape[0], step, 0, unroll=4)
 
 
 def decode_blocks(s, cap, all_caps, first, id_ref, num_ref, pos_ref, cell, s_ref, out_ref):
@@ -567,7 +589,9 @@
         6e6,
         scratch=[pltpu.SMEM((ny,), jnp.int32)],
     )(block_brick, block_count, positions, point_feat, area.reshape(blocks, PB))
-    early, late = (lax.all_to_all(part, "gy", split_axis=0, concat_axis=0, tiled=True) for part in outgoing)
+    early = lax.all_to_all(outgoing[0], "gy", split_axis=0, concat_axis=0, tiled=True)
+    early, second = lax.optimization_barrier((early, outgoing[1]))
+    late = lax.all_to_all(second, "gy", split_axis=0, concat_axis=0, tiled=True)
 
     def placement(incoming, cap):
         in_pos = incoming[:, cap * C :, :]
@@ -636,8 +660,9 @@
     x_fwd = lax.dynamic_index_in_dim(t["x_fwd"], row_x, 0, False)
     x_inv = lax.dynamic_index_in_dim(t["x_inv"], row_x, 0, False)
     row = row_x.astype(jnp.int32).reshape(1)
-    prepared = (early, init, mixing, bias, base, reading, u0, v0, u1, v1, turns, x_fwd, x_inv, row)
-    early, init, mixing, bias, base, reading, u0, v0, u1, v1, turns, x_fwd, x_inv, row = (
+    col = row_y.astype(jnp.int32).reshape(1)
+    prepared = (early, init, mixing, bias, base, reading, u0, v0, u1, v1, turns, x_fwd, x_inv, row, col)
+    early, init, mixing, bias, base, reading, u0, v0, u1, v1, turns, x_fwd, x_inv, row, col = (
         lax.optimization_barrier(prepared)
     )
     ids_a, counts_a, pos_a = placement(early, caps[0])
@@ -673,7 +698,10 @@
     def exchange(array, distance):
         return lax.ppermute(array, "gx", [(i, i ^ distance) for i in range(nx)])
 
-    def to_modes(keep, send):
+    def turned(array, distance):
+        return lax.ppermute(array, "gy", [(i, i ^ distance) for i in range(ny)])
+
+    def to_modes(keep, send, beside=None):
         recv = exchange(send, 1).reshape(half, s.Xl * s.K2, s.LY)
         keep = keep.reshape(half, s.Xl * s.K2, s.LY)
 
@@ -693,12 +721,14 @@
 
         others = [exchange(part(d), 2 * d) for d in range(1, half)]
         spec = part(0)
+        if beside is not None:
+            beside, *others = lax.optimization_barrier((beside(), *others))
         for other in others:
             spec = spec + other
         spec = lax.all_to_all(spec, "gy", split_axis=0, concat_axis=0, tiled=True)
-        return spec.reshape(G * s.cp, s.LK)
-
-    spec = to_modes(keep, send)
+        return spec.reshape(G * s.cp, s.LK), beside
+
+    spec, unused = to_modes(keep, send)
     mixed = call(
         functools.partial(mix_kernel, s),
         "mix",
@@ -742,41 +772,56 @@
         2.1e7,
         grid=(B,),
     )(row, mixed, t["z_inv"], t["z_fwd"], *fields)
-    spec = to_modes(keep, send)
-    read = call(
-        functools.partial(readout_kernel, s),
-        "readout",
-        shape(B, B * B, s.LB),
-        [grid_block, whole(reading)],
-        pl.BlockSpec((1, B * B, s.LB), lambda a: (a, 0, 0)),
-        2e9,
-        9e6,
-        grid=(B,),
-    )(grid, reading)
+
+    def readout():
+        return call(
+            functools.partial(readout_kernel, s),
+            "readout",
+            shape(B, B * B, s.LB),
+            [grid_block, whole(reading)],
+            pl.BlockSpec((1, B * B, s.LB), lambda a: (a, 0, 0)),
+            2e9,
+            9e6,
+            grid=(B,),
+        )(grid, reading)
+
+    spec, read = to_modes(keep, send, readout)
     last = call(
         functools.partial(y_last_kernel, s), "y_last", shape(2 * s.KL, M * M), [VM] * 4, VM, 1e9, 1e6, room=16
     )(spec, t["y_fwd"], u1, v1)
 
-    step = 1
-    while step < nx:
-        last = last + lax.ppermute(last, "gx", [(i, i ^ step) for i in range(nx)])
-        step *= 2
-    last = jnp.broadcast_to(last[None], (ny,) + last.shape)
-    last = lax.all_to_all(last, "gy", split_axis=0, concat_axis=0, tiled=True)
+    last = functools.reduce(jnp.add, [last] + [exchange(last, e) for e in range(1, nx)])
+    pieces = [last] + [turned(last, e) for e in range(1, ny)]
     values = call(
         functools.partial(decode_kernel, s, caps),
         "decode",
-        shape(ny * cap, PB),
-        [SM] * 4 + [VM] * 2 + [SM] + [VM] * 6,
-        VM,
+        (shape(cap, PB),) * ny,
+        [SM] * 4 + [VM] * 2 + [SM] * 2 + [VM] * (5 + ny),
+        (VM,) * ny,
         4e9,
         6e6,
-        scratch=[pltpu.VMEM((B * B * B, s.LB), F32)],
+        scratch=[
+            pltpu.VMEM((B * B * B, s.LB), F32),
+            pltpu.VMEM((s.K2, M * M), F32),
+            pltpu.VMEM((ny * cap, PB), F32),
+        ],
         room=32,
-    )(ids_a, ids_b, counts_a, counts_b, pos_a, pos_b, base, last, turns, read.reshape(B * B * B, s.LB), t["xy_hi"], t["xy_lo"], t["z_last"])
-    returned = lax.all_to_all(values.reshape(ny, cap, PB), "gy", split_axis=0, concat_axis=0, tiled=True)
-    choose = (slot_of[:, None] == jnp.arange(ny * cap, dtype=jnp.int32)[None, :]).astype(F32)
-    pressure = jnp.dot(choose, returned.reshape(ny * cap, PB), precision=lax.Precision.HIGHEST)
+    )(
+        ids_a, ids_b, counts_a, counts_b, pos_a, pos_b, col, base, turns,
+        read.reshape(B * B * B, s.LB), t["xy_hi"], t["xy_lo"], t["z_last"], *pieces,
+    )
+    values = [values[0]] + [turned(values[e], e) for e in range(1, ny)]
+    pressure = call(
+        functools.partial(return_kernel, s, cap),
+        "return",
+        shape(blocks, PB),
+        [SM, SM] + [VM] * ny,
+        VM,
+        1e5,
+        2e5,
+        scratch=[pltpu.VMEM((ny * cap, PB), F32)],
+        room=16,
+    )(col, slot_of, *values)
     return pressure.reshape(blocks * PB)
 
 

time: 301 us -> 301 us (level)
  starting transfers between devices: 21.6 us -> 52.2 us
  blocking collectives: 82.9 us -> 54.5 us
  waiting for transfers between devices: 63.4 us -> 47.5 us
  local copies, waits for them, and re-layouts: 21.6 us -> 26.3 us
  other arithmetic: 7.07 us -> 11.7 us
  Pallas kernels: 102 us -> 106 us
    ppermute x2 -> x14, starting transfers between devices: 1.35 us -> 28.4 us  [turned(): return lax.ppermute(array, 'gy', [(i, i ^ distance) for i in range(ny)])]
    all_to_all x1 -> x0, blocking collectives: 20.4 us -> none  [per_device(): lax.all_to_all(values.reshape(ny, cap, PB), 'gy', split_axis=0, concat_ax...]
    all_to_all x3 -> x2, waiting for transfers between devices: 29.7 us -> 15.3 us  [the longest x1 15.3 us: per_device(): lax.all_to_all(outgoing[0], 'gy', split_axis=0, concat_axis=0, tiled=True)]
    ppermute x7 -> x10, starting transfers between devices: 4.97 us -> 13.1 us  [exchange(): return lax.ppermute(array, 'gx', [(i, i ^ distance) for i in range(nx)])]
    all_to_all x2, blocking collectives: 45.1 us -> 37 us  [to_modes(): spec = lax.all_to_all(spec, 'gy', split_axis=0, concat_axis=0, tiled=True)]
    all_to_all x3 -> x2, starting transfers between devices: 15.2 us -> 10.7 us  [the longest x1 6.52 us: per_device(): lax.all_to_all(outgoing[0], 'gy', split_axis=0, concat_axis=0, tiled=True)]
    ppermute x7 -> x10, waiting for transfers between devices: 30.1 us -> 25.9 us  [exchange(): return lax.ppermute(array, 'gx', [(i, i ^ distance) for i in range(nx)])]
    ppermute x2 -> x14, waiting for transfers between devices: 3.63 us -> 6.3 us  [turned(): return lax.ppermute(array, 'gy', [(i, i ^ distance) for i in range(ny)])]
  transfers between devices with their start and end apart: 12 -> 26, of which waited for: 9 -> 13; matrix products, arithmetic and copies ran while one was open for 6% -> 10% of each run, Pallas kernels for 10% -> 18%
where the time goes in v5:
time: 301 us; the launch traced here: 300 us
  Pallas kernels  106 us (35%)
  blocking collectives  54.5 us (18%)
  starting transfers between devices  52.2 us (17%)
  waiting for transfers between devices  47.5 us (16%)
  local copies, waits for them, and re-layouts  26.3 us (9%)
  other arithmetic  11.7 us (4%)
    all_to_all x2, blocking collectives, to_modes(): spec = lax.all_to_all(spec, 'gy', split_axis=0, concat_axis=0, tiled=True)  37 us
    ppermute x14, starting transfers between devices, turned(): return lax.ppermute(array, 'gy', [(i, i ^ distance) for i in range(ny)])  28.4 us
    ppermute x10, waiting for transfers between devices, exchange(): return lax.ppermute(array, 'gx', [(i, i ^ distance) for i in range(nx)])  25.9 us
    pallas_call x1, Pallas kernels, per_device(): call(functools.partial(encode_first_kernel, s, caps[0]), 'encode_first',...  22.7 us
    all_to_all x1, blocking collectives, per_device(): lax.all_to_all(spec.reshape(ny, s.LY, s.LK), 'gy', split_axis=0, concat_a...  17.6 us
    all_to_all x1, waiting for transfers between devices, per_device(): lax.all_to_all(outgoing[0], 'gy', split_axis=0, concat_axis=0, tiled=True)  15.3 us
    pallas_call x1, Pallas kernels, per_device(): call(functools.partial(decode_kernel, s, caps), 'decode', (shape(cap, PB)...  13.9 us
    pallas_call x1, Pallas kernels, per_device(): call(functools.partial(layer_kernel, s), 'layer', (grid_shape, spec_shape...  13.4 us
  transfers between devices with their start and end apart: 26, of which 13 were waited for; matrix products, arithmetic and copies ran while one was open for 10% of the time, Pallas kernels for 18%

profile of v5, /device:TPU:0, one launch (start us, length us, event | category | flops | bytes accessed | tf_op | source)
XLA Modules:
  0.0 299.5 jit_solution(9490852137093831316)
XLA Ops:
  0.7 7.7 %pack.1 = (f32[8,350,128]{2,1,0:T(8,128)}, f32[8,210,128]{2,1,0:T(8,128)}, s32[128]{0:T(128)}) custom-call(s32[128]{0:T(128)} %brick_ref.1, s32[1]{0:T(128)S(6)} %copy.55.count_ref, f32[3,16384]{1,0:T(4,128)} %pos_ref.1, f32[32,16384]{1,0:T(8,128)} %feat_ref.1, f32[128,128]{1,0:T(8,128)} %bitcast.83), custom_call_target="tpu_custom_call" | custom-call | flops 1000000 | bytes 6000000 | tf_op jit(solution)/shard_map/pack/pallas_call | solution.py:582
  8.4 6.5 %all-to-all-start = ((f32[8,350,128]{2,1,0:T(8,128)}), f32[8,350,128]{2,1,0:T(8,128)S(1)}, u32[]{:S(2)}, u32[]{:S(2)}) async-start(f32[8,350,128]{2,1,0:T(8,128)} %get-tuple-element.47), calls=%async_computation | async-start | bytes 2883584 | tf_op jit(solution)/shard_map/all_to_all | solution.py:592
  15.6 1.4 fusion.6
  26.7 1.1 reshape.395
  27.8 1.1 multiply_bitcast_fusion
  29.0 1.1 pad_maximum_fusion.2
  30.1 1.3 slice_negate_fusion.1
  33.7 15.3 %all-to-all-done.in_ref = f32[8,350,128]{2,1,0:T(8,128)S(1)} async-done(((f32[8,350,128]{2,1,0:T(8,128)}), f32[8,350,128]{2,1,0:T(8,128)S(1)}, u32[]{:S(2)}, u32[]{:S(2)}) %all-to-all-start) | async-done | bytes 1433632 | tf_op jit(solution)/shard_map/all_to_all | solution.py:592
  49.0 4.2 %all-to-all-start.1 = ((f32[8,210,128]{2,1,0:T(8,128)}), f32[8,210,128]{2,1,0:T(8,128)}, u32[]{:S(2)}, u32[]{:S(2)}) async-start(f32[8,210,128]{2,1,0:T(8,128)} %get-tuple-element.53), calls=%async_computation.1 | async-start | bytes 1769472 | tf_op jit(solution)/shard_map/all_to_all | solution.py:594
  54.1 2.0 copy.47
  56.1 1.5 reshape.400.u_ref
  57.6 2.0 copy.48
  59.6 1.5 reshape.401.v_ref
  62.0 8.3 %field.1.init_ref = f32[8,16,128,128]{3,2,1,0:T(8,128)} custom-call(f32[4,8,16,128]{3,2,1,0:T(8,128)} %bitcast.86, f32[64,2048]{1,0:T(8,128)} %bitcast_select_fusion.gain_ref), custom_call_target="tpu_custom_call" | custom-call | flops 3000000000 | bytes 10000000 | tf_op jit(solution)/shard_map/field/pallas_call | solution.py:622
  72.1 22.7 %encode_first.1.before_ref = f32[8,16,128,128]{3,2,1,0:T(8,128)} custom-call(s32[8,80]{1,0:T(8,128)} %concatenate.26.id_ref.refs_0_, s32[8]{0:T(128)} %get-tuple-element.91.num_ref.refs_2_, f32[8,350,128]{2,1,0:T(8,128)} %copy-done.16, f32[8,16,128,128]{3,2,1,0:T(8,128)} %field.1.init_ref), custom_call_target="tpu_custom_call" | custom-call | flops 3000000000 | bytes 20000000 | tf_op jit(solution)/shard_map/encode_first/pallas_call | solution.py:673
  97.5 11.7 %encode_last.1 = (f32[8,16,128,128]{3,2,1,0:T(8,128)}, f32[2,8,4,32,128]{4,3,2,1,0:T(8,128)}, f32[2,8,4,32,128]{4,3,2,1,0:T(8,128)}) custom-call(s32[1]{0:T(128)} %bitcast.12.row_ref, s32[8,48]{1,0:T(8,128)} %concatenate.27.id_ref.refs_1_, s32[8]{0:T(128)} %get-tuple-element.89.num_ref.refs_3_, f32[8,210,128]{2,1,0:T(8,128)} %all-to-all-done.1.in_ref, ...), custom_call_target="tpu_custom_call" | custom-call | flops 4000000000 | bytes 22000000 | tf_op jit(solution)/shard_map/encode_last/pallas_call | solution.py:682
  109.2 8.1 %collective-permute-start = (f32[2,8,4,32,128]{4,3,2,1,0:T(8,128)}, f32[2,8,4,32,128]{4,3,2,1,0:T(8,128)S(1)}, u32[]{:S(2)}, u32[]{:S(2)}) collective-permute-start(f32[2,8,4,32,128]{4,3,2,1,0:T(8,128)} %get-tuple-element.62), channel_id=1, source_target_pairs={{0,8},{8,0},{16,24},{24,16},{1,9},{9,1},{17,25},{25,17},{2,10},{10... | collective-permute-start | bytes 3145736 | tf_op jit(solution)/shard_map/ppermute | solution.py:699
  117.3 2.5 collective-permute-done
  119.8 1.2 copy-done.2
  122.9 13.3 %collective-permute-done.1 = f32[8,128,128]{2,1,0:T(8,128)S(1)} collective-permute-done((f32[8,128,128]{2,1,0:T(8,128)S(1)}, f32[8,128,128]{2,1,0:T(8,128)S(1)}, u32[]{:S(2)}, u32[]{:S(2)}) %collective-permute-start.1) | collective-permute-done | bytes 524320 | tf_op jit(solution)/shard_map/ppermute | solution.py:699
  136.3 19.3 %all_to_all.25 = f32[8,128,128]{2,1,0:T(8,128)S(1)} all-to-all(f32[8,128,128]{2,1,0:T(8,128)S(1)} %add.165), channel_id=1, replica_groups=mesh['gx'=4,'gy'=8] {'gy'}, dimensions={0} | all-to-all | bytes 1048576 | tf_op jit(solution)/shard_map/all_to_all | solution.py:728
  156.7 17.6 %all_to_all.26.in_ref = f32[8,128,128]{2,1,0:T(8,128)S(1)} all-to-all(f32[8,128,128]{2,1,0:T(8,128)S(1)} %bitcast.72), channel_id=1, replica_groups=mesh['gx'=4,'gy'=8] {'gy'}, dimensions={0} | all-to-all | bytes 1048576 | tf_op jit(solution)/shard_map/all_to_all | solution.py:745
  174.2 1.3 collective-permute-start.2
  175.5 10.5 %mix.1.mixed_ref = f32[8,16,128,128]{3,2,1,0:T(8,128)} custom-call(f32[8,16,128,128]{3,2,1,0:T(8,128)} %get-tuple-element.58.grid_ref, f32[128,128]{1,0:T(8,128)} %get-tuple-element.59.mix_ref, f32[1,128]{1,0:T(1,128)} %reshape.396.bias_ref), custom_call_target="tpu_custom_call" | custom-call | flops 2000000000 | bytes 17000000 | tf_op jit(solution)/shard_map/mix/pallas_call | solution.py:732
  186.1 1.3 x_inverse.2
  188.2 1.3 x_inverse.3
  190.8 1.5 collective-permute-done.4
  193.2 13.4 %layer.1 = (f32[8,16,128,128]{3,2,1,0:T(8,128)}, f32[2,8,4,32,128]{4,3,2,1,0:T(8,128)}, f32[2,8,4,32,128]{4,3,2,1,0:T(8,128)}) custom-call(s32[1]{0:T(128)} %bitcast.12.row_ref, f32[8,16,128,128]{3,2,1,0:T(8,128)} %mix.1.mixed_ref, bf16[128,96]{1,0:T(8,128)(2,1)} %constant.142.clone.inv_ref, bf16[64,256]{1,0:T(8,128)(2,1)} %constant.141.clone.table_ref.fwd_ref, ...), custom_call_target="tpu_custom_call" | custom-call | flops 4000000000 | bytes 21000000 | tf_op jit(solution)/shard_map/layer/pallas_call | solution.py:765
  207.0 2.5 collective-permute-done.5
  209.5 1.2 copy-done
  212.5 8.4 %readout.1 = f32[8,64,128]{2,1,0:T(8,128)} custom-call(f32[8,16,128,128]{3,2,1,0:T(8,128)} %get-tuple-element.73.grid_ref, f32[128,128]{1,0:T(8,128)} %get-tuple-element.74.mix_ref), custom_call_target="tpu_custom_call" | custom-call | flops 2000000000 | bytes 9000000 | tf_op jit(solution)/shard_map/readout/pallas_call | solution.py:777
  221.8 4.2 %collective-permute-done.6 = f32[8,128,128]{2,1,0:T(8,128)} collective-permute-done((f32[8,128,128]{2,1,0:T(8,128)S(1)}, f32[8,128,128]{2,1,0:T(8,128)}, u32[]{:S(2)}, u32[]{:S(2)}) %collective-permute-start.6) | collective-permute-done | bytes 524320 | tf_op jit(solution)/shard_map/ppermute | solution.py:699
  226.0 1.1 add.166
  227.1 17.6 %all_to_all.27 = f32[8,128,128]{2,1,0:T(8,128)S(1)} all-to-all(f32[8,128,128]{2,1,0:T(8,128)S(1)} %add.166), channel_id=1, replica_groups=mesh['gx'=4,'gy'=8] {'gy'}, dimensions={0} | all-to-all | bytes 1048576 | tf_op jit(solution)/shard_map/all_to_all | solution.py:728
  247.3 1.3 collective-permute-done.9
  249.2 2.4 collective-permute-start.16
  251.7 2.4 collective-permute-start.15
  254.1 2.9 collective-permute-start.13
  257.0 3.0 collective-permute-start.11
  260.5 1.1 collective-permute-done.12.refs_16_
  261.8 1.9 collective-permute-done.10.refs_14_
  263.7 13.9 %decode.1 = (f32[16,128]{1,0:T(8,128)S(1)}, f32[16,128]{1,0:T(8,128)S(1)}, f32[16,128]{1,0:T(8,128)S(1)}, f32[16,128]{1,0:T(8,128)S(1)}, f32[16,128]{1,0:T(8,128...) custom-call(s32[8,80]{1,0:T(8,128)S(1)} %copy-done.4, s32[8,48]{1,0:T(8,128)S(1)} %copy-done.5, ...), custom_call_target="tpu_custom_call" | custom-call | flops 4000000000 | bytes 6000000 | tf_op jit(solution)/shard_map/decode/pallas_call | solution.py:795
  277.7 8.0 %collective-permute-start.17 = (f32[16,128]{1,0:T(8,128)S(1)}, f32[16,128]{1,0:T(8,128)S(1)}, u32[]{:S(2)}, u32[]{:S(2)}) collective-permute-start(f32[16,128]{1,0:T(8,128)S(1)} %get-tuple-element.82), channel_id=1, source_target_pairs={{0,1},{1,0},{2,3},{3,2},{4,5},{5,4},{6,7},{7,6},{8,9},{9,8},{10,11... | collective-permute-start | bytes 24584 | tf_op jit(solution)/shard_map/ppermute | solution.py:702
  285.7 1.5 collective-permute-start.19
  287.2 4.3 %collective-permute-start.21 = (f32[16,128]{1,0:T(8,128)S(1)}, f32[16,128]{1,0:T(8,128)S(1)}, u32[]{:S(2)}, u32[]{:S(2)}) collective-permute-start(f32[16,128]{1,0:T(8,128)S(1)} %get-tuple-element.86), channel_id=1, source_target_pairs={{0,5},{1,4},{2,7},{3,6},{4,1},{5,0},{6,3},{7,2},{8,13},{9,12},{10,... | collective-permute-start | bytes 24584 | tf_op jit(solution)/shard_map/ppermute | solution.py:702
  291.5 3.3 %collective-permute-start.23 = (f32[16,128]{1,0:T(8,128)S(1)}, f32[16,128]{1,0:T(8,128)S(1)}, u32[]{:S(2)}, u32[]{:S(2)}) collective-permute-start(f32[16,128]{1,0:T(8,128)S(1)} %get-tuple-element.88), channel_id=1, source_target_pairs={{0,7},{1,6},{2,5},{3,4},{4,3},{5,2},{6,1},{7,0},{8,15},{9,14},{10,... | collective-permute-start | bytes 24584 | tf_op jit(solution)/shard_map/ppermute | solution.py:702
  294.9 2.1 collective-permute-done.22.refs_6_
  297.9 1.6 return.1
  (138 shorter events, 32.9 us)
Async XLA Ops:
  8.4 40.7 %all-to-all-start = ((f32[8,350,128]{2,1,0:T(8,128)}), f32[8,350,128]{2,1,0:T(8,128)S(1)}, u32[]{:S(2)}, u32[]{:S(2)}) async-start(f32[8,350,128]{2,1,0:T(8,128)} %get-tuple-element.47), calls=%async_computation | async-start | bytes 2883584 | tf_op jit(solution)/shard_map/all_to_all | solution.py:592
  49.0 21.2 %copy-start.16 = (f32[8,350,128]{2,1,0:T(8,128)}, f32[8,350,128]{2,1,0:T(8,128)S(1)}, u32[]{:S(2)}) copy-start(f32[8,350,128]{2,1,0:T(8,128)S(1)} %all-to-all-done.in_ref) | copy-start | bytes 4300804
  49.0 45.8 %all-to-all-start.1 = ((f32[8,210,128]{2,1,0:T(8,128)}), f32[8,210,128]{2,1,0:T(8,128)}, u32[]{:S(2)}, u32[]{:S(2)}) async-start(f32[8,210,128]{2,1,0:T(8,128)} %get-tuple-element.53), calls=%async_computation.1 | async-start | bytes 1769472 | tf_op jit(solution)/shard_map/all_to_all | solution.py:594
  53.2 18.2 %copy-start.17 = (s32[3]{0:T(128)S(1)}, s32[3]{0:T(128)}, u32[]{:S(2)}) copy-start(s32[3]{0:T(128)} %constant.151.clone) | copy-start | bytes 40
  97.5 58.1 %copy-start.13 = (bf16[128,256]{1,0:T(8,128)(2,1)S(1)}, bf16[128,256]{1,0:T(8,128)(2,1)}, u32[]{:S(2)}) copy-start(bf16[128,256]{1,0:T(8,128)(2,1)} %constant.146.clone.fwd_ref) | copy-start | bytes 196612
  97.5 58.1 %copy-start.14 = (bf16[128,192]{1,0:T(8,128)(2,1)S(1)}, bf16[128,192]{1,0:T(8,128)(2,1)}, u32[]{:S(2)}) copy-start(bf16[128,192]{1,0:T(8,128)(2,1)} %constant.147.clone.inv_ref) | copy-start | bytes 147460
  109.2 10.6 %collective-permute-start = (f32[2,8,4,32,128]{4,3,2,1,0:T(8,128)}, f32[2,8,4,32,128]{4,3,2,1,0:T(8,128)S(1)}, u32[]{:S(2)}, u32[]{:S(2)}) collective-permute-start(f32[2,8,4,32,128]{4,3,2,1,0:T(8,128)} %get-tuple-element.62), channel_id=1, source_target_pairs={{0,8},{8,0},{16,24},{24,16},{1,9},{9,1},{17,25},{25,17},{2,10},{10... | collective-permute-start | bytes 3145736 | tf_op jit(solution)/shard_map/ppermute | solution.py:699
  119.8 1.2 copy-start.2
  121.9 14.3 %collective-permute-start.1 = (f32[8,128,128]{2,1,0:T(8,128)S(1)}, f32[8,128,128]{2,1,0:T(8,128)S(1)}, u32[]{:S(2)}, u32[]{:S(2)}) collective-permute-start(f32[8,128,128]{2,1,0:T(8,128)S(1)} %x_forward.5), channel_id=1, source_target_pairs={{0,16},{8,24},{16,0},{24,8},{1,17},{9,25},{17,1},{25,9},{2,18},{10... | collective-permute-start | bytes 1572872 | tf_op jit(solution)/shard_map/ppermute | solution.py:699
  174.2 14.0 %collective-permute-start.2 = (f32[8,128,128]{2,1,0:T(8,128)S(1)}, f32[8,128,128]{2,1,0:T(8,128)S(1)}, u32[]{:S(2)}, u32[]{:S(2)}) collective-permute-start(f32[8,128,128]{2,1,0:T(8,128)S(1)} %all_to_all.26.in_ref), channel_id=1, source_target_pairs={{0,16},{8,24},{16,0},{24,8},{1,17},{9,25},{17,1},{25,9},{2,18},{10... | collective-permute-start | bytes 1572872 | tf_op jit(solution)/shard_map/ppermute | solution.py:699
  187.4 0.8 copy-start.11
  188.2 2.6 collective-permute-start.3
  189.5 0.8 copy-start.12
  190.3 2.0 collective-permute-start.4
  190.8 1.5 copy-start.18
  192.4 0.8 copy-start.19
  206.6 2.9 collective-permute-start.5
  209.5 1.2 copy-start
  210.7 10.2 %copy-start.1 = (f32[2,8,4,32,128]{4,3,2,1,0:T(8,128)S(1)}, f32[2,8,4,32,128]{4,3,2,1,0:T(8,128)}, u32[]{:S(2)}) copy-start(f32[2,8,4,32,128]{4,3,2,1,0:T(8,128)} %get-tuple-element.75) | copy-start | bytes 3145732
  211.6 14.4 %collective-permute-start.6 = (f32[8,128,128]{2,1,0:T(8,128)S(1)}, f32[8,128,128]{2,1,0:T(8,128)}, u32[]{:S(2)}, u32[]{:S(2)}) collective-permute-start(f32[8,128,128]{2,1,0:T(8,128)S(1)} %x_forward.6), channel_id=1, source_target_pairs={{0,16},{8,24},{16,0},{24,8},{1,17},{9,25},{17,1},{25,9},{2,18},{10... | collective-permute-start | bytes 1572872 | tf_op jit(solution)/shard_map/ppermute | solution.py:699
  212.5 51.2 %copy-start.4 = (s32[8,80]{1,0:T(8,128)S(1)}, s32[8,80]{1,0:T(8,128)}, u32[]{:S(2)}) copy-start(s32[8,80]{1,0:T(8,128)} %concatenate.26.id_ref.refs_0_) | copy-start | bytes 7684
  212.5 51.2 %copy-start.5 = (s32[8,48]{1,0:T(8,128)S(1)}, s32[8,48]{1,0:T(8,128)}, u32[]{:S(2)}) copy-start(s32[8,48]{1,0:T(8,128)} %concatenate.27.id_ref.refs_1_) | copy-start | bytes 4612
  212.5 51.2 %copy-start.6 = (s32[8]{0:T(128)S(1)}, s32[8]{0:T(128)}, u32[]{:S(2)}) copy-start(s32[8]{0:T(128)} %get-tuple-element.91.num_ref.refs_2_) | copy-start | bytes 100
  212.5 51.2 %copy-start.8 = (s32[8]{0:T(128)S(1)}, s32[8]{0:T(128)}, u32[]{:S(2)}) copy-start(s32[8]{0:T(128)} %get-tuple-element.89.num_ref.refs_3_) | copy-start | bytes 100
  212.5 51.2 %copy-start.9 = (bf16[2048,512]{1,0:T(8,128)(2,1)S(1)}, bf16[2048,512]{1,0:T(8,128)(2,1)}, u32[]{:S(2)}) copy-start(bf16[2048,512]{1,0:T(8,128)(2,1)} %constant.149.clone.refs_11_) | copy-start | bytes 6291460
  212.5 51.2 %copy-start.15 = (bf16[128,96]{1,0:T(8,128)(2,1)S(1)}, bf16[128,96]{1,0:T(8,128)(2,1)}, u32[]{:S(2)}) copy-start(bf16[128,96]{1,0:T(8,128)(2,1)} %constant.143.clone.refs_12_) | copy-start | bytes 73732
  220.9 42.8 %copy-start.3 = (f32[8,64,128]{2,1,0:T(8,128)S(1)}, f32[8,64,128]{2,1,0:T(8,128)}, u32[]{:S(2)}) copy-start(f32[8,64,128]{2,1,0:T(8,128)} %readout.1) | copy-start | bytes 786436
  220.9 42.8 %copy-start.10 = (bf16[2048,512]{1,0:T(8,128)(2,1)S(1)}, bf16[2048,512]{1,0:T(8,128)(2,1)}, u32[]{:S(2)}) copy-start(bf16[2048,512]{1,0:T(8,128)(2,1)} %constant.148.clone.refs_10_) | copy-start | bytes 6291460
  244.7 53.2 %copy-start.7 = (s32[128]{0:T(128)S(1)}, s32[128]{0:T(128)}, u32[]{:S(2)}) copy-start(s32[128]{0:T(128)} %get-tuple-element.51.slot_ref) | copy-start | bytes 1540
  245.3 3.2 %collective-permute-start.9 = (f32[4,1024]{1,0:T(4,128)S(1)}, f32[4,1024]{1,0:T(4,128)S(1)}, u32[]{:S(2)}, u32[]{:S(2)}) collective-permute-start(f32[4,1024]{1,0:T(4,128)S(1)} %y_last.1), channel_id=1, source_target_pairs={{0,24},{8,16},{16,8},{24,0},{1,25},{9,17},{17,9},{25,1},{2,26},{10... | collective-permute-start | bytes 49160 | tf_op jit(solution)/shard_map/ppermute | solution.py:699
  245.4 3.8 %collective-permute-start.8 = (f32[4,1024]{1,0:T(4,128)S(1)}, f32[4,1024]{1,0:T(4,128)S(1)}, u32[]{:S(2)}, u32[]{:S(2)}) collective-permute-start(f32[4,1024]{1,0:T(4,128)S(1)} %y_last.1), channel_id=1, source_target_pairs={{0,16},{8,24},{16,0},{24,8},{1,17},{9,25},{17,1},{25,9},{2,18},{10... | collective-permute-start | bytes 49160 | tf_op jit(solution)/shard_map/ppermute | solution.py:699
  246.2 3.0 %collective-permute-start.7 = (f32[4,1024]{1,0:T(4,128)S(1)}, f32[4,1024]{1,0:T(4,128)S(1)}, u32[]{:S(2)}, u32[]{:S(2)}) collective-permute-start(f32[4,1024]{1,0:T(4,128)S(1)} %y_last.1), channel_id=1, source_target_pairs={{0,8},{8,0},{16,24},{24,16},{1,9},{9,1},{17,25},{25,17},{2,10},{10... | collective-permute-start | bytes 49160 | tf_op jit(solution)/shard_map/ppermute | solution.py:699
  249.2 7.7 %collective-permute-start.16 = (f32[4,1024]{1,0:T(4,128)S(1)}, f32[4,1024]{1,0:T(4,128)S(1)}, u32[]{:S(2)}, u32[]{:S(2)}) collective-permute-start(f32[4,1024]{1,0:T(4,128)S(1)} %add_add_fusion.refs_13_), channel_id=1, source_target_pairs={{0,7},{1,6},{2,5},{3,4},{4,3},{5,2},{6,1},{7,0},{8,15},{9,14},{10,... | collective-permute-start | bytes 49160 | tf_op jit(solution)/shard_map/ppermute | solution.py:702
  251.7 8.3 %collective-permute-start.15 = (f32[4,1024]{1,0:T(4,128)S(1)}, f32[4,1024]{1,0:T(4,128)S(1)}, u32[]{:S(2)}, u32[]{:S(2)}) collective-permute-start(f32[4,1024]{1,0:T(4,128)S(1)} %add_add_fusion.refs_13_), channel_id=1, source_target_pairs={{0,6},{1,7},{2,4},{3,5},{4,2},{5,3},{6,0},{7,1},{8,14},{9,15},{10,... | collective-permute-start | bytes 49160 | tf_op jit(solution)/shard_map/ppermute | solution.py:702
  254.1 6.4 %collective-permute-start.14 = (f32[4,1024]{1,0:T(4,128)S(1)}, f32[4,1024]{1,0:T(4,128)S(1)}, u32[]{:S(2)}, u32[]{:S(2)}) collective-permute-start(f32[4,1024]{1,0:T(4,128)S(1)} %add_add_fusion.refs_13_), channel_id=1, source_target_pairs={{0,5},{1,4},{2,7},{3,6},{4,1},{5,0},{6,3},{7,2},{8,13},{9,12},{10,... | collective-permute-start | bytes 49160 | tf_op jit(solution)/shard_map/ppermute | solution.py:702
  254.1 6.4 %collective-permute-start.13 = (f32[4,1024]{1,0:T(4,128)S(1)}, f32[4,1024]{1,0:T(4,128)S(1)}, u32[]{:S(2)}, u32[]{:S(2)}) collective-permute-start(f32[4,1024]{1,0:T(4,128)S(1)} %add_add_fusion.refs_13_), channel_id=1, source_target_pairs={{0,4},{1,5},{2,6},{3,7},{4,0},{5,1},{6,2},{7,3},{8,12},{9,13},{10,... | collective-permute-start | bytes 49160 | tf_op jit(solution)/shard_map/ppermute | solution.py:702
  257.0 4.6 %collective-permute-start.12 = (f32[4,1024]{1,0:T(4,128)S(1)}, f32[4,1024]{1,0:T(4,128)S(1)}, u32[]{:S(2)}, u32[]{:S(2)}) collective-permute-start(f32[4,1024]{1,0:T(4,128)S(1)} %add_add_fusion.refs_13_), channel_id=1, source_target_pairs={{0,3},{1,2},{2,1},{3,0},{4,7},{5,6},{6,5},{7,4},{8,11},{9,10},{10,... | collective-permute-start | bytes 49160 | tf_op jit(solution)/shard_map/ppermute | solution.py:702
  257.0 4.9 %collective-permute-start.11 = (f32[4,1024]{1,0:T(4,128)S(1)}, f32[4,1024]{1,0:T(4,128)S(1)}, u32[]{:S(2)}, u32[]{:S(2)}) collective-permute-start(f32[4,1024]{1,0:T(4,128)S(1)} %add_add_fusion.refs_13_), channel_id=1, source_target_pairs={{0,2},{1,3},{2,0},{3,1},{4,6},{5,7},{6,4},{7,5},{8,10},{9,11},{10,... | collective-permute-start | bytes 49160 | tf_op jit(solution)/shard_map/ppermute | solution.py:702
  259.9 3.7 %collective-permute-start.10 = (f32[4,1024]{1,0:T(4,128)S(1)}, f32[4,1024]{1,0:T(4,128)S(1)}, u32[]{:S(2)}, u32[]{:S(2)}) collective-permute-start(f32[4,1024]{1,0:T(4,128)S(1)} %add_add_fusion.refs_13_), channel_id=1, source_target_pairs={{0,1},{1,0},{2,3},{3,2},{4,5},{5,4},{6,7},{7,6},{8,9},{9,8},{10,11... | collective-permute-start | bytes 49160 | tf_op jit(solution)/shard_map/ppermute | solution.py:702
  277.7 13.9 %collective-permute-start.17 = (f32[16,128]{1,0:T(8,128)S(1)}, f32[16,128]{1,0:T(8,128)S(1)}, u32[]{:S(2)}, u32[]{:S(2)}) collective-permute-start(f32[16,128]{1,0:T(8,128)S(1)} %get-tuple-element.82), channel_id=1, source_target_pairs={{0,1},{1,0},{2,3},{3,2},{4,5},{5,4},{6,7},{7,6},{8,9},{9,8},{10,11... | collective-permute-start | bytes 24584 | tf_op jit(solution)/shard_map/ppermute | solution.py:702
  285.7 5.9 %collective-permute-start.18 = (f32[16,128]{1,0:T(8,128)S(1)}, f32[16,128]{1,0:T(8,128)S(1)}, u32[]{:S(2)}, u32[]{:S(2)}) collective-permute-start(f32[16,128]{1,0:T(8,128)S(1)} %get-tuple-element.83), channel_id=1, source_target_pairs={{0,2},{1,3},{2,0},{3,1},{4,6},{5,7},{6,4},{7,5},{8,10},{9,11},{10,... | collective-permute-start | bytes 24584 | tf_op jit(solution)/shard_map/ppermute | solution.py:702
  285.7 9.2 %collective-permute-start.19 = (f32[16,128]{1,0:T(8,128)S(1)}, f32[16,128]{1,0:T(8,128)S(1)}, u32[]{:S(2)}, u32[]{:S(2)}) collective-permute-start(f32[16,128]{1,0:T(8,128)S(1)} %get-tuple-element.84), channel_id=1, source_target_pairs={{0,3},{1,2},{2,1},{3,0},{4,7},{5,6},{6,5},{7,4},{8,11},{9,10},{10,... | collective-permute-start | bytes 24584 | tf_op jit(solution)/shard_map/ppermute | solution.py:702
  287.2 7.7 %collective-permute-start.20 = (f32[16,128]{1,0:T(8,128)S(1)}, f32[16,128]{1,0:T(8,128)S(1)}, u32[]{:S(2)}, u32[]{:S(2)}) collective-permute-start(f32[16,128]{1,0:T(8,128)S(1)} %get-tuple-element.85), channel_id=1, source_target_pairs={{0,4},{1,5},{2,6},{3,7},{4,0},{5,1},{6,2},{7,3},{8,12},{9,13},{10,... | collective-permute-start | bytes 24584 | tf_op jit(solution)/shard_map/ppermute | solution.py:702
  287.2 7.7 %collective-permute-start.21 = (f32[16,128]{1,0:T(8,128)S(1)}, f32[16,128]{1,0:T(8,128)S(1)}, u32[]{:S(2)}, u32[]{:S(2)}) collective-permute-start(f32[16,128]{1,0:T(8,128)S(1)} %get-tuple-element.86), channel_id=1, source_target_pairs={{0,5},{1,4},{2,7},{3,6},{4,1},{5,0},{6,3},{7,2},{8,13},{9,12},{10,... | collective-permute-start | bytes 24584 | tf_op jit(solution)/shard_map/ppermute | solution.py:702
  291.5 5.4 %collective-permute-start.22 = (f32[16,128]{1,0:T(8,128)S(1)}, f32[16,128]{1,0:T(8,128)S(1)}, u32[]{:S(2)}, u32[]{:S(2)}) collective-permute-start(f32[16,128]{1,0:T(8,128)S(1)} %get-tuple-element.87), channel_id=1, source_target_pairs={{0,6},{1,7},{2,4},{3,5},{4,2},{5,3},{6,0},{7,1},{8,14},{9,15},{10,... | collective-permute-start | bytes 24584 | tf_op jit(solution)/shard_map/ppermute | solution.py:702
  291.5 6.4 %collective-permute-start.23 = (f32[16,128]{1,0:T(8,128)S(1)}, f32[16,128]{1,0:T(8,128)S(1)}, u32[]{:S(2)}, u32[]{:S(2)}) collective-permute-start(f32[16,128]{1,0:T(8,128)S(1)} %get-tuple-element.88), channel_id=1, source_target_pairs={{0,7},{1,6},{2,5},{3,4},{4,3},{5,2},{6,1},{7,0},{8,15},{9,14},{10,... | collective-permute-start | bytes 24584 | tf_op jit(solution)/shard_map/ppermute | solution.py:702

commit v6 on v4

--- a/solution.py
+++ b/solution.py
@@ -463,10 +463,9 @@
     store_spectrum(s, row, 0, out, keep_ref, send_ref)
 
 
-def decode_kernel(s, caps, *refs):
-    n = len(caps)
-    id_refs, num_refs, in_refs = refs[:n], refs[n : 2 * n], refs[2 * n : 3 * n]
-    base_ref, spec_ref, turn_ref, mix_ref, hi_ref, lo_ref, inv_ref, out_ref, s_ref = refs[3 * n :]
+def decode_kernel(
+    s, id_ref, base_ref, point_ref, spec_ref, turn_ref, mix_ref, hi_ref, lo_ref, inv_ref, out_ref, s_ref, list_ref
+):
     modes = jnp.concatenate([spec_ref[i] for i in range(s.ny)], axis=0)
     real_row = lax.broadcasted_iota(jnp.int32, modes.shape, 0) // s.KL % 2 == 0
 
@@ -481,54 +480,58 @@
     field = dot(inv_ref[...], jnp.concatenate([hi, lo, hi], axis=0))
     width = s.bxn * s.byn
     per = 128 // width
+    fields = []
     for q in range(field.shape[1] // 128):
         tiles = [field[z * B : (z + 1) * B, q * 128 : (q + 1) * 128] for z in range(s.NB)]
         for i, tile in enumerate(block_turn(tiles, per, width)):
             at = (q * per + i) * B
-            s_ref[at : at + B, :] = tile + mix_ref[at : at + B, :] + base_ref[0]
+            fields.append(tile + mix_ref[at : at + B, :] + base_ref[0])
     out_ref[...] = jnp.zeros(out_ref.shape, F32)
     cell = lax.broadcasted_iota(jnp.int32, (s.LB, 128), 0)
 
-    first = 0
-    for cap, id_ref, num_ref, pos_ref in zip(caps, id_refs, num_refs, in_refs):
-        decode_blocks(s, cap, sum(caps), first, id_ref, num_ref, pos_ref, cell, s_ref, out_ref)
-        first += cap
-
-
-def decode_blocks(s, cap, all_caps, first, id_ref, num_ref, pos_ref, cell, s_ref, out_ref):
-    def per_source(src, carry):
-        def per_pair(h, inner):
-            shi, slo = split(s_ref[...])
-            picks = []
-            for i in range(2):
-                at = id_ref[6, src * cap + h * 2 + i]
-                picks.append(jnp.where(cell == at, 1.0, 0.0).astype(BF))
-            pick = jnp.concatenate(picks, axis=1)
-            if s.LB == 128:
-                vals = dot(jnp.concatenate([shi, slo], axis=1), jnp.concatenate([pick, pick], axis=0))
-            else:
-                vals = dot(shi, pick) + dot(slo, pick)
-            for i in range(2):
-                j = h * 2 + i
-                slot = src * cap + j
-                points = [
-                    jnp.broadcast_to(pos_ref[src, pl.ds(d * cap + j, 1), :], (8, 128))
-                    - id_ref[3 + d, slot].astype(F32)
-                    for d in range(3)
-                ]
-                top = jnp.zeros((B, 128), F32)
-                low = jnp.zeros((B, 128), F32)
-                for n, tile in enumerate(kernel_tiles(points)):
-                    top = top + tile * vals[n * B : (n + 1) * B, i * 128 : (i + 1) * 128]
-                    low = low + tile
-                top = jnp.sum(top, axis=0, keepdims=True)
-                low = jnp.sum(low, axis=0, keepdims=True)
-                out_ref[pl.ds(src * all_caps + first + j, 1), :] = top / jnp.where(low > 0.0, low, 1.0)
-            return inner
-
-        return lax.fori_loop(0, (num_ref[src] + 1) // 2, per_pair, carry)
-
-    lax.fori_loop(0, s.ny, per_source, 0)
+    shi, slo = split(jnp.concatenate(fields, axis=0))
+    s_ref[0], s_ref[1] = shi, slo
+    slots = point_ref.shape[1]
+    step = 4
+
+    def collect(n, live):
+        list_ref[live] = n
+        return live + id_ref[1, n]
+
+    live = lax.fori_loop(0, slots, collect, 0, unroll=8)
+    for i in range(step):
+        list_ref[live + i] = 0
+
+    def per_group(h, carry):
+        at = [list_ref[h * step + i] for i in range(step)]
+        pick = jnp.concatenate([jnp.where(cell == id_ref[0, q], 1.0, 0.0).astype(BF) for q in at], axis=1)
+        if s.LB == 128:
+            vals = dot(jnp.concatenate([s_ref[0], s_ref[1]], axis=1), jnp.concatenate([pick, pick], axis=0))
+        else:
+            vals = dot(s_ref[0], pick) + dot(s_ref[1], pick)
+        for i, q in enumerate(at):
+            points = [jnp.broadcast_to(point_ref[d, pl.ds(q, 1), :], (8, 128)) for d in range(3)]
+            top = jnp.zeros((B, 128), F32)
+            low = jnp.zeros((B, 128), F32)
+            for n, tile in enumerate(kernel_tiles(points)):
+                top = top + tile * vals[n * B : (n + 1) * B, i * 128 : (i + 1) * 128]
+                low = low + tile
+            top = jnp.sum(top, axis=0, keepdims=True)
+            low = jnp.sum(low, axis=0, keepdims=True)
+            out_ref[pl.ds(id_ref[2, q], 1), :] = top / jnp.where(low > 0.0, low, 1.0)
+        return carry
+
+    lax.fori_loop(0, (live + step - 1) // step, per_group, 0)
+
+
+def return_kernel(s, slot_ref, in_ref, out_ref):
+    def step(n, carry):
+        slot = slot_ref[n]
+        line = in_ref[pl.ds(jnp.maximum(slot, 0), 1), :]
+        out_ref[pl.ds(n, 1), :] = jnp.where(slot >= 0, line, 0.0)
+        return carry
+
+    lax.fori_loop(0, out_ref.shape[0], step, 0, unroll=8)
 
 
 def per_device(
@@ -567,7 +570,7 @@
         6e6,
         scratch=[pltpu.SMEM((ny,), jnp.int32)],
     )(block_brick, block_count, positions, point_feat, area.reshape(blocks, PB))
-    early, late = (lax.all_to_all(part, "gy", split_axis=0, concat_axis=0, tiled=True) for part in outgoing)
+    early = lax.all_to_all(outgoing[0], "gy", split_axis=0, concat_axis=0, tiled=True)
 
     def placement(incoming, cap):
         in_pos = incoming[:, cap * C :, :]
@@ -636,10 +639,11 @@
     x_fwd = lax.dynamic_index_in_dim(t["x_fwd"], row_x, 0, False)
     x_inv = lax.dynamic_index_in_dim(t["x_inv"], row_x, 0, False)
     row = row_x.astype(jnp.int32).reshape(1)
-    prepared = (early, init, mixing, bias, base, reading, u0, v0, u1, v1, turns, x_fwd, x_inv, row)
-    early, init, mixing, bias, base, reading, u0, v0, u1, v1, turns, x_fwd, x_inv, row = (
+    prepared = (early, outgoing[1], init, mixing, bias, base, reading, u0, v0, u1, v1, turns, x_fwd, x_inv, row)
+    early, second, init, mixing, bias, base, reading, u0, v0, u1, v1, turns, x_fwd, x_inv, row = (
         lax.optimization_barrier(prepared)
     )
+    late = lax.all_to_all(second, "gy", split_axis=0, concat_axis=0, tiled=True)
     ids_a, counts_a, pos_a = placement(early, caps[0])
     ids_b, counts_b, pos_b = placement(late, caps[1])
 
@@ -673,7 +677,7 @@
     def exchange(array, distance):
         return lax.ppermute(array, "gx", [(i, i ^ distance) for i in range(nx)])
 
-    def to_modes(keep, send):
+    def to_modes(keep, send, beside=None):
         recv = exchange(send, 1).reshape(half, s.Xl * s.K2, s.LY)
         keep = keep.reshape(half, s.Xl * s.K2, s.LY)
 
@@ -693,12 +697,14 @@
 
         others = [exchange(part(d), 2 * d) for d in range(1, half)]
         spec = part(0)
+        if beside is not None:
+            beside, *others = lax.optimization_barrier((beside(), *others))
         for other in others:
             spec = spec + other
         spec = lax.all_to_all(spec, "gy", split_axis=0, concat_axis=0, tiled=True)
-        return spec.reshape(G * s.cp, s.LK)
-
-    spec = to_modes(keep, send)
+        return spec.reshape(G * s.cp, s.LK), beside
+
+    spec, unused = to_modes(keep, send)
     mixed = call(
         functools.partial(mix_kernel, s),
         "mix",
@@ -742,41 +748,55 @@
         2.1e7,
         grid=(B,),
     )(row, mixed, t["z_inv"], t["z_fwd"], *fields)
-    spec = to_modes(keep, send)
-    read = call(
-        functools.partial(readout_kernel, s),
-        "readout",
-        shape(B, B * B, s.LB),
-        [grid_block, whole(reading)],
-        pl.BlockSpec((1, B * B, s.LB), lambda a: (a, 0, 0)),
-        2e9,
-        9e6,
-        grid=(B,),
-    )(grid, reading)
+
+    def readout():
+        return call(
+            functools.partial(readout_kernel, s),
+            "readout",
+            shape(B, B * B, s.LB),
+            [grid_block, whole(reading)],
+            pl.BlockSpec((1, B * B, s.LB), lambda a: (a, 0, 0)),
+            2e9,
+            9e6,
+            grid=(B,),
+        )(grid, reading), decode_places()
+
+    def decode_places():
+        points, bricks, live, places = [], [], [], []
+        first = 0
+        for part, ids, pos in ((caps[0], ids_a, pos_a), (caps[1], ids_b, pos_b)):
+            pos = pos.reshape(ny, 3, part, PB).transpose(1, 0, 2, 3).reshape(3, ny * part, PB)
+            points.append(pos - ids[3:6].astype(F32)[:, :, None])
+            bricks.append(ids[6])
+            live.append((ids[0] >= 0).astype(jnp.int32))
+            places.append((jnp.arange(ny)[:, None] * cap + first + jnp.arange(part)[None, :]).reshape(-1))
+            first += part
+        where = [jnp.concatenate(v).astype(jnp.int32) for v in (bricks, live, places)]
+        return jnp.concatenate(points, axis=1), jnp.stack(where)
+
+    spec, (read, (points, where)) = to_modes(keep, send, readout)
     last = call(
         functools.partial(y_last_kernel, s), "y_last", shape(2 * s.KL, M * M), [VM] * 4, VM, 1e9, 1e6, room=16
     )(spec, t["y_fwd"], u1, v1)
 
-    step = 1
-    while step < nx:
-        last = last + lax.ppermute(last, "gx", [(i, i ^ step) for i in range(nx)])
-        step *= 2
+    last = functools.reduce(jnp.add, [last] + [exchange(last, e) for e in range(1, nx)])
     last = jnp.broadcast_to(last[None], (ny,) + last.shape)
     last = lax.all_to_all(last, "gy", split_axis=0, concat_axis=0, tiled=True)
     values = call(
-        functools.partial(decode_kernel, s, caps),
+        functools.partial(decode_kernel, s),
         "decode",
         shape(ny * cap, PB),
-        [SM] * 4 + [VM] * 2 + [SM] + [VM] * 6,
+        [SM, SM] + [VM] * 7,
         VM,
         4e9,
         6e6,
-        scratch=[pltpu.VMEM((B * B * B, s.LB), F32)],
+        scratch=[pltpu.VMEM((2, B * B * B, s.LB), BF), pltpu.SMEM((ny * cap + 8,), jnp.int32)],
         room=32,
-    )(ids_a, ids_b, counts_a, counts_b, pos_a, pos_b, base, last, turns, read.reshape(B * B * B, s.LB), t["xy_hi"], t["xy_lo"], t["z_last"])
+    )(where, base, points, last, turns, read.reshape(B * B * B, s.LB), t["xy_hi"], t["xy_lo"], t["z_last"])
     returned = lax.all_to_all(values.reshape(ny, cap, PB), "gy", split_axis=0, concat_axis=0, tiled=True)
-    choose = (slot_of[:, None] == jnp.arange(ny * cap, dtype=jnp.int32)[None, :]).astype(F32)
-    pressure = jnp.dot(choose, returned.reshape(ny * cap, PB), precision=lax.Precision.HIGHEST)
+    pressure = call(
+        functools.partial(return_kernel, s), "return", shape(blocks, PB), [SM, VM], VM, 1e5, 2e5, room=16
+    )(slot_of, returned.reshape(ny * cap, PB))
     return pressure.reshape(blocks * PB)
 
 

time: 301 us -> 269 us (0.89)
  waiting for transfers between devices: 63.4 us -> 33.5 us
  Pallas kernels: 102 us -> 115 us
  blocking collectives: 82.9 us -> 75.4 us
  starting transfers between devices: 21.6 us -> 16.4 us
  local copies, waits for them, and re-layouts: 21.6 us -> 17.4 us
    all_to_all x3 -> x2, waiting for transfers between devices: 29.7 us -> 8.14 us  [the longest x1 8.14 us: per_device(): lax.all_to_all(outgoing[0], 'gy', split_axis=0, concat_axis=0, tiled=True)]
    all_to_all x1, blocking collectives: 20.4 us -> 9.29 us  [per_device(): lax.all_to_all(values.reshape(ny, cap, PB), 'gy', split_axis=0, concat_ax...]
    all_to_all x0 -> x1, blocking collectives: none -> 10.8 us  [per_device(): last = lax.all_to_all(last, 'gy', split_axis=0, concat_axis=0, tiled=True)]
    all_to_all x2, blocking collectives: 45.1 us -> 37.8 us  [to_modes(): spec = lax.all_to_all(spec, 'gy', split_axis=0, concat_axis=0, tiled=True)]
    pallas_call x1, Pallas kernels: 11.8 us -> 19 us  [per_device(): call(functools.partial(encode_last_kernel, s, caps[1]), 'encode_last', (g...]
    ppermute x7 -> x10, waiting for transfers between devices: 30.1 us -> 25.4 us  [exchange(): return lax.ppermute(array, 'gx', [(i, i ^ distance) for i in range(nx)])]
    all_to_all x3 -> x2, starting transfers between devices: 15.2 us -> 11.2 us  [the longest x1 7.6 us: per_device(): lax.all_to_all(outgoing[0], 'gy', split_axis=0, concat_axis=0, tiled=True)]
    ppermute x2 -> x0, waiting for transfers between devices: 3.63 us -> none  [per_device(): last = last + lax.ppermute(last, 'gx', [(i, i ^ step) for i in range(nx)])]
  transfers between devices with their start and end apart: 12 -> 12, of which waited for: 9 -> 8; matrix products, arithmetic and copies ran while one was open for 6% -> 7% of each run, Pallas kernels for 10% -> 21%
where the time goes in v6:
time: 269 us; the launch traced here: 268 us
  Pallas kernels  115 us (43%)
  blocking collectives  75.4 us (28%)
  waiting for transfers between devices  33.5 us (12%)
  local copies, waits for them, and re-layouts  17.4 us (6%)
  starting transfers between devices  16.4 us (6%)
  other arithmetic  9.58 us (4%)
    all_to_all x2, blocking collectives, to_modes(): spec = lax.all_to_all(spec, 'gy', split_axis=0, concat_axis=0, tiled=True)  37.8 us
    ppermute x10, waiting for transfers between devices, exchange(): return lax.ppermute(array, 'gx', [(i, i ^ distance) for i in range(nx)])  25.4 us
    pallas_call x1, Pallas kernels, per_device(): call(functools.partial(encode_first_kernel, s, caps[0]), 'encode_first',...  24.3 us
    pallas_call x1, Pallas kernels, per_device(): call(functools.partial(encode_last_kernel, s, caps[1]), 'encode_last', (g...  19 us
    all_to_all x1, blocking collectives, per_device(): lax.all_to_all(spec.reshape(ny, s.LY, s.LK), 'gy', split_axis=0, concat_a...  17.5 us
    pallas_call x1, Pallas kernels, per_device(): call(functools.partial(decode_kernel, s), 'decode', shape(ny * cap, PB),...  14.7 us
    pallas_call x1, Pallas kernels, per_device(): call(functools.partial(layer_kernel, s), 'layer', (grid_shape, spec_shape...  13.4 us
    all_to_all x1, blocking collectives, per_device(): last = lax.all_to_all(last, 'gy', split_axis=0, concat_axis=0, tiled=True)  10.8 us
  transfers between devices with their start and end apart: 12, of which 8 were waited for; matrix products, arithmetic and copies ran while one was open for 7% of the time, Pallas kernels for 21%

profile of v6, /device:TPU:0, one launch (start us, length us, event | category | flops | bytes accessed | tf_op | source)
XLA Modules:
  0.0 268.3 jit_solution(15654478742571870153)
XLA Ops:
  0.7 7.0 %pack.1 = (f32[8,350,128]{2,1,0:T(8,128)}, f32[8,210,128]{2,1,0:T(8,128)}, s32[128]{0:T(128)}) custom-call(s32[128]{0:T(128)} %brick_ref.1, s32[1]{0:T(128)S(6)} %copy.63.count_ref, f32[3,16384]{1,0:T(4,128)} %pos_ref.1, f32[32,16384]{1,0:T(8,128)} %feat_ref.1, f32[128,128]{1,0:T(8,128)} %bitcast.106), custom_call_target="tpu_custom_call" | custom-call | flops 1000000 | bytes 6000000 | tf_op jit(solution)/shard_map/pack/pallas_call | solution.py:563
  7.7 7.6 %all-to-all-start = ((f32[8,350,128]{2,1,0:T(8,128)}), f32[8,350,128]{2,1,0:T(8,128)S(1)}, u32[]{:S(2)}, u32[]{:S(2)}) async-start(f32[8,350,128]{2,1,0:T(8,128)} %get-tuple-element.40), calls=%async_computation | async-start | bytes 2883584 | tf_op jit(solution)/shard_map/all_to_all | solution.py:573
  15.3 0.7 slice_bitcast_fusion
  16.0 0.8 fusion
  16.8 0.7 dynamic_slice.11
  18.5 1.0 fusion.12
  20.3 1.1 slice_negate_fusion.1
  24.6 1.7 pad_maximum_fusion
  27.5 1.1 reshape.547
  29.2 0.9 dynamic-slice_bitcast_fusion.1.table_ref
  30.1 0.9 dynamic-slice_bitcast_fusion.table_ref
  31.2 0.7 compare_select_fusion
  31.9 0.8 bitcast_select_fusion.gain_ref
  32.8 8.2 %field.1.init_ref = f32[8,16,128,128]{3,2,1,0:T(8,128)} custom-call(f32[4,8,16,128]{3,2,1,0:T(8,128)} %bitcast.109, f32[64,2048]{1,0:T(8,128)} %bitcast_select_fusion.gain_ref), custom_call_target="tpu_custom_call" | custom-call | flops 3000000000 | bytes 10000000 | tf_op jit(solution)/shard_map/field/pallas_call | solution.py:601
  41.0 8.1 %all-to-all-done.in_ref = f32[8,350,128]{2,1,0:T(8,128)S(1)} async-done(((f32[8,350,128]{2,1,0:T(8,128)}), f32[8,350,128]{2,1,0:T(8,128)S(1)}, u32[]{:S(2)}, u32[]{:S(2)}) %all-to-all-start) | async-done | bytes 1433632 | tf_op jit(solution)/shard_map/all_to_all | solution.py:573
  49.2 3.6 %all-to-all-start.1 = ((f32[8,210,128]{2,1,0:T(8,128)}), f32[8,210,128]{2,1,0:T(8,128)S(1)}, u32[]{:S(2)}, u32[]{:S(2)}) async-start(f32[8,210,128]{2,1,0:T(8,128)} %get-tuple-element.43), calls=%async_computation.1 | async-start | bytes 1769472 | tf_op jit(solution)/shard_map/all_to_all | solution.py:646
  54.7 24.3 %encode_first.1.before_ref = f32[8,16,128,128]{3,2,1,0:T(8,128)} custom-call(s32[8,80]{1,0:T(8,128)} %concatenate.40.id_ref, s32[8]{0:T(128)} %get-tuple-element.83.num_ref, f32[8,350,128]{2,1,0:T(8,128)} %copy-done.12, f32[8,16,128,128]{3,2,1,0:T(8,128)} %field.1.init_ref), custom_call_target="tpu_custom_call" | custom-call | flops 3000000000 | bytes 20000000 | tf_op jit(solution)/shard_map/encode_first/pallas_call | solution.py:652
  81.0 19.0 %encode_last.1 = (f32[8,16,128,128]{3,2,1,0:T(8,128)}, f32[2,8,4,32,128]{4,3,2,1,0:T(8,128)}, f32[2,8,4,32,128]{4,3,2,1,0:T(8,128)}) custom-call(s32[1]{0:T(128)} %bitcast.12.row_ref, s32[8,48]{1,0:T(8,128)} %concatenate.39.id_ref, s32[8]{0:T(128)} %get-tuple-element.85.num_ref, f32[8,210,128]{2,1,0:T(8,128)} %copy-done.13, ...), custom_call_target="tpu_custom_call" | custom-call | flops 4000000000 | bytes 22000000 | tf_op jit(solution)/shard_map/encode_last/pallas_call | solution.py:661
  100.1 2.9 %collective-permute-done = f32[2,8,4,32,128]{4,3,2,1,0:T(8,128)S(1)} collective-permute-done((f32[2,8,4,32,128]{4,3,2,1,0:T(8,128)}, f32[2,8,4,32,128]{4,3,2,1,0:T(8,128)S(1)}, u32[]{:S(2)}, u32[]{:S(2)}) %collective-permute-start) | collective-permute-done | bytes 1048608 | tf_op jit(solution)/shard_map/ppermute | solution.py:678
  102.9 1.2 copy-done.2
  104.1 0.9 x_forward.5
  105.1 0.9 x_forward.4
  106.0 13.0 %collective-permute-done.1 = f32[8,128,128]{2,1,0:T(8,128)S(1)} collective-permute-done((f32[8,128,128]{2,1,0:T(8,128)S(1)}, f32[8,128,128]{2,1,0:T(8,128)S(1)}, u32[]{:S(2)}, u32[]{:S(2)}) %collective-permute-start.1) | collective-permute-done | bytes 524320 | tf_op jit(solution)/shard_map/ppermute | solution.py:678
  119.1 20.2 %all_to_all.35 = f32[8,128,128]{2,1,0:T(8,128)S(1)} all-to-all(f32[8,128,128]{2,1,0:T(8,128)S(1)} %add.223), channel_id=1, replica_groups=mesh['gx'=4,'gy'=8] {'gy'}, dimensions={0} | all-to-all | bytes 1048576 | tf_op jit(solution)/shard_map/all_to_all | solution.py:704
  139.3 1.0 y_both.1
  140.4 17.5 %all_to_all.36.in_ref = f32[8,128,128]{2,1,0:T(8,128)S(1)} all-to-all(f32[8,128,128]{2,1,0:T(8,128)S(1)} %bitcast.91), channel_id=1, replica_groups=mesh['gx'=4,'gy'=8] {'gy'}, dimensions={0} | all-to-all | bytes 1048576 | tf_op jit(solution)/shard_map/all_to_all | solution.py:721
  157.9 1.4 collective-permute-start.2
  159.3 10.6 %mix.1.mixed_ref = f32[8,16,128,128]{3,2,1,0:T(8,128)} custom-call(f32[8,16,128,128]{3,2,1,0:T(8,128)} %get-tuple-element.46.grid_ref, f32[128,128]{1,0:T(8,128)} %get-tuple-element.47.mix_ref, f32[1,128]{1,0:T(1,128)} %reshape.548.bias_ref), custom_call_target="tpu_custom_call" | custom-call | flops 2000000000 | bytes 17000000 | tf_op jit(solution)/shard_map/mix/pallas_call | solution.py:708
  169.9 1.3 x_inverse.2
  171.2 0.8 copy-done.7
  172.0 1.3 x_inverse.3
  173.3 0.8 copy-done.8
  175.0 1.2 collective-permute-done.4
  176.2 0.8 copy-done.18
  177.0 13.4 %layer.1 = (f32[8,16,128,128]{3,2,1,0:T(8,128)}, f32[2,8,4,32,128]{4,3,2,1,0:T(8,128)}, f32[2,8,4,32,128]{4,3,2,1,0:T(8,128)}) custom-call(s32[1]{0:T(128)} %bitcast.12.row_ref, f32[8,16,128,128]{3,2,1,0:T(8,128)} %mix.1.mixed_ref, bf16[128,96]{1,0:T(8,128)(2,1)} %constant.147.clone.inv_ref, bf16[64,256]{1,0:T(8,128)(2,1)} %constant.146.clone.table_ref.fwd_ref, ...), custom_call_target="tpu_custom_call" | custom-call | flops 4000000000 | bytes 21000000 | tf_op jit(solution)/shard_map/layer/pallas_call | solution.py:741
  191.3 2.0 collective-permute-done.5
  193.3 1.2 copy-done
  194.5 0.9 x_forward.6
  196.3 8.2 %readout.1 = f32[8,64,128]{2,1,0:T(8,128)} custom-call(f32[8,16,128,128]{3,2,1,0:T(8,128)} %get-tuple-element.61.grid_ref, f32[128,128]{1,0:T(8,128)} %get-tuple-element.62.mix_ref), custom_call_target="tpu_custom_call" | custom-call | flops 2000000000 | bytes 9000000 | tf_op jit(solution)/shard_map/readout/pallas_call | solution.py:753
  204.5 0.9 x_forward.7
  205.4 4.3 %collective-permute-done.6 = f32[8,128,128]{2,1,0:T(8,128)S(1)} collective-permute-done((f32[8,128,128]{2,1,0:T(8,128)S(1)}, f32[8,128,128]{2,1,0:T(8,128)S(1)}, u32[]{:S(2)}, u32[]{:S(2)}) %collective-permute-start.6) | collective-permute-done | bytes 524320 | tf_op jit(solution)/shard_map/ppermute | solution.py:678
  209.8 17.7 %all_to_all.37 = f32[8,128,128]{2,1,0:T(8,128)S(1)} all-to-all(f32[8,128,128]{2,1,0:T(8,128)S(1)} %add.235), channel_id=1, replica_groups=mesh['gx'=4,'gy'=8] {'gy'}, dimensions={0} | all-to-all | bytes 1048576 | tf_op jit(solution)/shard_map/all_to_all | solution.py:704
  228.8 1.1 collective-permute-start.7
  230.0 1.3 collective-permute-done.9
  232.0 10.8 %all_to_all.38.spec_ref = f32[8,4,1024]{2,1,0:T(4,128)S(1)} all-to-all(f32[8,4,1024]{2,1,0:T(4,128)S(1)} %broadcast_in_dim.115), channel_id=1, replica_groups=mesh['gx'=4,'gy'=8] {'gy'}, dimensions={0} | all-to-all | bytes 262144 | tf_op jit(solution)/shard_map/all_to_all | solution.py:784
  242.8 14.7 %decode.1 = f32[128,128]{1,0:T(8,128)S(1)} custom-call(s32[3,128]{1,0:T(4,128)S(1)} %pad_add_fusion.id_ref, f32[1]{0:T(128)} %bitcast.6.base_ref, f32[3,128,128]{2,1,0:T(8,128)S(1)} %pad_maximum_fusion.4.point_ref, f32[8,4,1024]{2,1,0:T(4,128)S(1)} %all_to_all.38.spec_ref, f32[2,1024]{1,0:T(2,128)S(1)} %pad_maximum_fusion.5.turn_ref, ...), custom_call_target="tpu_custom_call" | custom-call | flops 4000000000 | bytes 6000000 | tf_op jit(solution)/shard_map/decode/pallas_call | solution.py:785
  257.5 9.3 %all_to_all.39 = f32[8,16,128]{2,1,0:T(8,128)S(1)} all-to-all(f32[8,16,128]{2,1,0:T(8,128)S(1)} %bitcast.95), channel_id=1, replica_groups=mesh['gx'=4,'gy'=8] {'gy'}, dimensions={0} | all-to-all | bytes 131072 | tf_op jit(solution)/shard_map/all_to_all | solution.py:796
  266.8 1.5 return.1
  (134 shorter events, 15.4 us)
Async XLA Ops:
  0.0 21.6 %copy-start.19 = (f32[2,32]{1,0:T(2,128)S(1)}, f32[2,32]{1,0:T(2,128)}, u32[]{:S(2)}) copy-start(f32[2,32]{1,0:T(2,128)} %param.31) | copy-start | bytes 772
  0.0 21.8 %copy-start.15 = (f32[32]{0:T(128)S(1)}, f32[32]{0:T(128)}, u32[]{:S(2)}) copy-start(f32[32]{0:T(128)} %param.29) | copy-start | bytes 388
  7.7 41.5 %all-to-all-start = ((f32[8,350,128]{2,1,0:T(8,128)}), f32[8,350,128]{2,1,0:T(8,128)S(1)}, u32[]{:S(2)}, u32[]{:S(2)}) async-start(f32[8,350,128]{2,1,0:T(8,128)} %get-tuple-element.40), calls=%async_computation | async-start | bytes 2883584 | tf_op jit(solution)/shard_map/all_to_all | solution.py:573
  19.5 9.1 %copy-start.16 = (f32[32]{0:T(128)S(1)}, f32[32]{0:T(128)}, u32[]{:S(2)}) copy-start(f32[32]{0:T(128)} %param.33) | copy-start | bytes 388
  27.5 26.6 %copy-start.14 = (s32[3]{0:T(128)S(1)}, s32[3]{0:T(128)}, u32[]{:S(2)}) copy-start(s32[3]{0:T(128)} %constant.156.clone) | copy-start | bytes 40
  49.1 5.6 %copy-start.12 = (f32[8,350,128]{2,1,0:T(8,128)}, f32[8,350,128]{2,1,0:T(8,128)S(1)}, u32[]{:S(2)}) copy-start(f32[8,350,128]{2,1,0:T(8,128)S(1)} %all-to-all-done.in_ref) | copy-start | bytes 4300804
  49.2 29.9 %all-to-all-start.1 = ((f32[8,210,128]{2,1,0:T(8,128)}), f32[8,210,128]{2,1,0:T(8,128)S(1)}, u32[]{:S(2)}, u32[]{:S(2)}) async-start(f32[8,210,128]{2,1,0:T(8,128)} %get-tuple-element.43), calls=%async_computation.1 | async-start | bytes 1769472 | tf_op jit(solution)/shard_map/all_to_all | solution.py:646
  79.1 1.9 copy-start.13
  81.0 58.3 %copy-start.9 = (bf16[128,256]{1,0:T(8,128)(2,1)S(1)}, bf16[128,256]{1,0:T(8,128)(2,1)}, u32[]{:S(2)}) copy-start(bf16[128,256]{1,0:T(8,128)(2,1)} %constant.151.clone.fwd_ref) | copy-start | bytes 196612
  81.0 58.3 %copy-start.10 = (bf16[128,192]{1,0:T(8,128)(2,1)S(1)}, bf16[128,192]{1,0:T(8,128)(2,1)}, u32[]{:S(2)}) copy-start(bf16[128,192]{1,0:T(8,128)(2,1)} %constant.152.clone.inv_ref) | copy-start | bytes 147460
  100.0 2.9 %collective-permute-start = (f32[2,8,4,32,128]{4,3,2,1,0:T(8,128)}, f32[2,8,4,32,128]{4,3,2,1,0:T(8,128)S(1)}, u32[]{:S(2)}, u32[]{:S(2)}) collective-permute-start(f32[2,8,4,32,128]{4,3,2,1,0:T(8,128)} %get-tuple-element.50), channel_id=1, source_target_pairs={{0,8},{8,0},{16,24},{24,16},{1,9},{9,1},{17,25},{25,17},{2,10},{10... | collective-permute-start | bytes 3145736 | tf_op jit(solution)/shard_map/ppermute | solution.py:678
  102.9 1.2 copy-start.2
  105.0 14.0 %collective-permute-start.1 = (f32[8,128,128]{2,1,0:T(8,128)S(1)}, f32[8,128,128]{2,1,0:T(8,128)S(1)}, u32[]{:S(2)}, u32[]{:S(2)}) collective-permute-start(f32[8,128,128]{2,1,0:T(8,128)S(1)} %x_forward.5), channel_id=1, source_target_pairs={{0,16},{8,24},{16,0},{24,8},{1,17},{9,25},{17,1},{25,9},{2,18},{10... | collective-permute-start | bytes 1572872 | tf_op jit(solution)/shard_map/ppermute | solution.py:678
  157.9 14.1 %collective-permute-start.2 = (f32[8,128,128]{2,1,0:T(8,128)S(1)}, f32[8,128,128]{2,1,0:T(8,128)S(1)}, u32[]{:S(2)}, u32[]{:S(2)}) collective-permute-start(f32[8,128,128]{2,1,0:T(8,128)S(1)} %all_to_all.36.in_ref), channel_id=1, source_target_pairs={{0,16},{8,24},{16,0},{24,8},{1,17},{9,25},{17,1},{25,9},{2,18},{10... | collective-permute-start | bytes 1572872 | tf_op jit(solution)/shard_map/ppermute | solution.py:678
  171.2 0.8 copy-start.7
  172.0 2.9 %collective-permute-start.3 = (f32[1024,128]{1,0:T(8,128)S(1)}, f32[1024,128]{1,0:T(8,128)S(1)}, u32[]{:S(2)}, u32[]{:S(2)}) collective-permute-start(f32[1024,128]{1,0:T(8,128)S(1)} %get-tuple-element.57), channel_id=1, source_target_pairs={{0,8},{8,0},{16,24},{24,16},{1,9},{9,1},{17,25},{25,17},{2,10},{10... | collective-permute-start | bytes 1572872 | tf_op jit(solution)/shard_map/ppermute | solution.py:678
  173.3 0.8 copy-start.8
  174.1 2.0 collective-permute-start.4
  174.9 1.2 copy-start.17
  176.2 0.8 copy-start.18
  190.4 14.1 %copy-start.1 = (f32[2,8,4,32,128]{4,3,2,1,0:T(8,128)S(1)}, f32[2,8,4,32,128]{4,3,2,1,0:T(8,128)}, u32[]{:S(2)}) copy-start(f32[2,8,4,32,128]{4,3,2,1,0:T(8,128)} %get-tuple-element.63) | copy-start | bytes 3145732
  190.4 2.9 %collective-permute-start.5 = (f32[2,8,4,32,128]{4,3,2,1,0:T(8,128)}, f32[2,8,4,32,128]{4,3,2,1,0:T(8,128)S(1)}, u32[]{:S(2)}, u32[]{:S(2)}) collective-permute-start(f32[2,8,4,32,128]{4,3,2,1,0:T(8,128)} %get-tuple-element.64), channel_id=1, source_target_pairs={{0,8},{8,0},{16,24},{24,16},{1,9},{9,1},{17,25},{25,17},{2,10},{10... | collective-permute-start | bytes 3145736 | tf_op jit(solution)/shard_map/ppermute | solution.py:678
  193.3 1.2 copy-start
  195.4 14.3 %collective-permute-start.6 = (f32[8,128,128]{2,1,0:T(8,128)S(1)}, f32[8,128,128]{2,1,0:T(8,128)S(1)}, u32[]{:S(2)}, u32[]{:S(2)}) collective-permute-start(f32[8,128,128]{2,1,0:T(8,128)S(1)} %x_forward.6), channel_id=1, source_target_pairs={{0,16},{8,24},{16,0},{24,8},{1,17},{9,25},{17,1},{25,9},{2,18},{10... | collective-permute-start | bytes 1572872 | tf_op jit(solution)/shard_map/ppermute | solution.py:678
  196.3 46.5 %copy-start.11 = (bf16[128,96]{1,0:T(8,128)(2,1)S(1)}, bf16[128,96]{1,0:T(8,128)(2,1)}, u32[]{:S(2)}) copy-start(bf16[128,96]{1,0:T(8,128)(2,1)} %constant.148.clone.inv_ref) | copy-start | bytes 73732
  204.5 38.2 %copy-start.3 = (f32[8,64,128]{2,1,0:T(8,128)S(1)}, f32[8,64,128]{2,1,0:T(8,128)}, u32[]{:S(2)}) copy-start(f32[8,64,128]{2,1,0:T(8,128)} %readout.1) | copy-start | bytes 786436
  204.5 38.2 %copy-start.5 = (bf16[2048,512]{1,0:T(8,128)(2,1)S(1)}, bf16[2048,512]{1,0:T(8,128)(2,1)}, u32[]{:S(2)}) copy-start(bf16[2048,512]{1,0:T(8,128)(2,1)} %constant.154.clone.lo_ref) | copy-start | bytes 6291460
  204.5 38.2 %copy-start.6 = (bf16[2048,512]{1,0:T(8,128)(2,1)S(1)}, bf16[2048,512]{1,0:T(8,128)(2,1)}, u32[]{:S(2)}) copy-start(bf16[2048,512]{1,0:T(8,128)(2,1)} %constant.153.clone.hi_ref) | copy-start | bytes 6291460
  228.0 38.7 %copy-start.4 = (s32[128]{0:T(128)S(1)}, s32[128]{0:T(128)}, u32[]{:S(2)}) copy-start(s32[128]{0:T(128)} %get-tuple-element.39.slot_ref) | copy-start | bytes 1540
  228.1 3.2 %collective-permute-start.9 = (f32[4,1024]{1,0:T(4,128)S(1)}, f32[4,1024]{1,0:T(4,128)S(1)}, u32[]{:S(2)}, u32[]{:S(2)}) collective-permute-start(f32[4,1024]{1,0:T(4,128)S(1)} %y_last.1), channel_id=1, source_target_pairs={{0,24},{8,16},{16,8},{24,0},{1,25},{9,17},{17,9},{25,1},{2,26},{10... | collective-permute-start | bytes 49160 | tf_op jit(solution)/shard_map/ppermute | solution.py:678
  228.1 3.8 %collective-permute-start.8 = (f32[4,1024]{1,0:T(4,128)S(1)}, f32[4,1024]{1,0:T(4,128)S(1)}, u32[]{:S(2)}, u32[]{:S(2)}) collective-permute-start(f32[4,1024]{1,0:T(4,128)S(1)} %y_last.1), channel_id=1, source_target_pairs={{0,16},{8,24},{16,0},{24,8},{1,17},{9,25},{17,1},{25,9},{2,18},{10... | collective-permute-start | bytes 49160 | tf_op jit(solution)/shard_map/ppermute | solution.py:678
  228.8 3.1 %collective-permute-start.7 = (f32[4,1024]{1,0:T(4,128)S(1)}, f32[4,1024]{1,0:T(4,128)S(1)}, u32[]{:S(2)}, u32[]{:S(2)}) collective-permute-start(f32[4,1024]{1,0:T(4,128)S(1)} %y_last.1), channel_id=1, source_target_pairs={{0,8},{8,0},{16,24},{24,16},{1,9},{9,1},{17,25},{25,17},{2,10},{10... | collective-permute-start | bytes 49160 | tf_op jit(solution)/shard_map/ppermute | solution.py:678

commit v7 on v6

--- a/solution.py
+++ b/solution.py
@@ -159,45 +159,39 @@
 
 
 def pack_kernel(s, caps, brick_ref, count_ref, pos_ref, feat_ref, area_ref, *refs):
-    out_refs, (slot_ref, fill_ref) = refs[: len(caps)], refs[len(caps) :]
+    out_refs, (slot_ref, fill_ref, feat_out, pos_out) = refs[: len(caps)], refs[len(caps) :]
     blocks = brick_ref.shape[0]
-    C = s.C
+    C, cap = s.C, sum(caps)
     for i in range(s.ny):
         fill_ref[i] = 0
-        for out_ref in out_refs:
-            out_ref[i] = jnp.full(out_ref.shape[1:], -1.0, F32)
+        pos_out[i] = jnp.full(pos_out.shape[1:], -1.0, F32)
+        feat_out[i] = jnp.zeros(feat_out.shape[1:], F32)
+    fill_ref[s.ny] = 0
     live = count_ref[0]
 
-    def step(n, carry):
-        @pl.when(n < live)
-        def _():
-            brick = brick_ref[n]
-            dest = (brick // s.NB) % s.NB // s.byn
-            order = fill_ref[dest]
-            fill_ref[dest] = order + 1
-            slot_ref[n] = dest * sum(caps) + order
-            lanes = pl.ds(pl.multiple_of(n * 128, 128), 128)
-            first = 0
-            for cap, out_ref in zip(caps, out_refs):
-                place = order - first
-
-                @pl.when((place >= 0) & (place < cap))
-                def _():
-                    feats = feat_ref[:, lanes] * area_ref[pl.ds(n, 1), :]
-                    out_ref[dest, pl.ds(pl.multiple_of(place * C, 8), C), :] = feats
-                    points = pos_ref[:, lanes]
-                    for d in range(3):
-                        out_ref[dest, pl.ds(cap * C + d * cap + place, 1), :] = points[d : d + 1, :]
-
-                first += cap
-
-        @pl.when(n >= live)
-        def _():
-            slot_ref[n] = -1
-
+    def place(n, carry):
+        alive = n < live
+        dest = jnp.where(alive, (brick_ref[n] // s.NB) % s.NB // s.byn, s.ny)
+        order = jnp.where(alive, fill_ref[dest], 0)
+        fill_ref[dest] = order + 1
+        slot_ref[n] = jnp.where(alive, dest * cap + order, -1)
+        lanes = pl.ds(pl.multiple_of(n * 128, 128), 128)
+        feats = feat_ref[:, lanes] * area_ref[pl.ds(n, 1), :]
+        feat_out[dest, pl.ds(pl.multiple_of(order * C, 8), C), :] = feats
+        points = pos_ref[:, lanes]
+        for d in range(3):
+            pos_out[dest, d, pl.ds(order, 1), :] = points[d : d + 1, :]
         return carry
 
-    lax.fori_loop(0, blocks, step, 0)
+    lax.fori_loop(0, blocks, place, 0, unroll=8)
+    first = 0
+    for part, out_ref in zip(caps, out_refs):
+        for i in range(s.ny):
+            out_ref[i, : part * C] = feat_out[i, first * C : (first + part) * C]
+            for d in range(3):
+                at = part * C + d * part
+                out_ref[i, at : at + part] = pos_out[i, d, first : first + part]
+        first += part
 
 
 def field_kernel(s, sdf_ref, gain_ref, out_ref):
@@ -249,74 +243,83 @@
 
 def grid_to_spectrum(s, rows_of, table):
     tiles = []
-    for y in range(0, s.Yl, 2):
-        both = jnp.concatenate([rows_of(y), rows_of(y + 1)], axis=1)
-        hi, lo = split(both)
+    for y in range(0, s.Yl, 4):
+        hi, lo = split(jnp.concatenate([rows_of(y + i) for i in range(4)], axis=1))
         res = dot(table, jnp.concatenate([hi, lo], axis=0))
         res = res[: s.K2] + res[s.K2 :]
-        tiles += [res[:, : s.L], res[:, s.L :]]
+        tiles += [res[:, i * s.L : (i + 1) * s.L] for i in range(4)]
     return block_turn(tiles, s.nx * s.bxn, s.cp)
 
 
-def add_blocks(s, cap, id_ref, num_ref, in_ref, grid_ref):
+def live_list(alive, slots, step, list_ref):
+    def collect(n, live):
+        list_ref[live] = n
+        return live + alive(n)
+
+    live = lax.fori_loop(0, slots, collect, 0, unroll=8)
+    for i in range(step):
+        list_ref[live + i] = 0
+    return live
+
+
+def add_blocks(s, cap, id_ref, in_ref, grid_ref, list_ref):
     C = s.C
+    step = 4
     group = lax.broadcasted_iota(jnp.int32, (s.L, 128), 0) // s.cp % s.bxn
-
-    def per_source(src, carry):
-        def per_pair(h, inner):
-            results = []
-            for i in range(2):
-                j = h * 2 + i
-                slot = src * cap + j
-                points = [
-                    jnp.broadcast_to(in_ref[src, pl.ds(cap * C + d * cap + j, 1), :], (8, 128))
-                    - id_ref[3 + d, slot].astype(F32)
-                    for d in range(3)
-                ]
-                weights = jnp.concatenate(kernel_tiles(points), axis=0)
-                feats = in_ref[src, pl.ds(pl.multiple_of(j * C, 8), C), :]
-                spread = []
-                for g in range(s.nx):
-                    spread += [feats[g * s.cp : (g + 1) * s.cp]] * s.bxn
-                spread = jnp.where(group == id_ref[0, slot], jnp.concatenate(spread, axis=0), 0.0)
-                whi, wlo = split(weights)
-                fhi, flo = split(spread)
-                left = jnp.concatenate([whi, wlo], axis=1)
-                right = jnp.concatenate([fhi, fhi], axis=1)
-                if s.L == 128:
-                    under = jnp.concatenate([flo, jnp.zeros_like(flo)], axis=1)
-                    res = dot(left, jnp.concatenate([right, under], axis=0), NT)
-                    res = res[:, : s.L] + res[:, s.L :]
-                else:
-                    res = dot(left, right, NT) + dot(whi, flo, NT)
-                results.append(res.reshape(B, B, B, s.L))
-            for i in range(2):
-                slot = src * cap + h * 2 + i
-                ys = pl.ds(pl.multiple_of(id_ref[1, slot] * B, B), B)
-                zs = pl.ds(pl.multiple_of(id_ref[2, slot] * B, B), B)
-                grid_ref[:, ys, zs, :] = grid_ref[:, ys, zs, :] + results[i]
-            return inner
-
-        return lax.fori_loop(0, (num_ref[src] + 1) // 2, per_pair, carry)
-
-    lax.fori_loop(0, s.ny, per_source, 0)
-
-
-def encode_first_kernel(s, cap, id_ref, num_ref, in_ref, init_ref, grid_ref):
+    live = live_list(lambda n: jnp.where(id_ref[0, n] >= 0, 1, 0), s.ny * cap, step, list_ref)
+
+    def per_group(h, carry):
+        results = []
+        slots = [list_ref[h * step + i] for i in range(step)]
+        for i, slot in enumerate(slots):
+            src, j = slot // cap, slot % cap
+            points = [
+                jnp.broadcast_to(in_ref[src, pl.ds(cap * C + d * cap + j, 1), :], (8, 128))
+                - id_ref[3 + d, slot].astype(F32)
+                for d in range(3)
+            ]
+            weights = jnp.concatenate(kernel_tiles(points), axis=0)
+            feats = in_ref[src, pl.ds(pl.multiple_of(j * C, 8), C), :]
+            spread = []
+            for g in range(s.nx):
+                spread += [feats[g * s.cp : (g + 1) * s.cp]] * s.bxn
+            mine = jnp.where(h * step + i < live, id_ref[0, slot], -1)
+            spread = jnp.where(group == mine, jnp.concatenate(spread, axis=0), 0.0)
+            whi, wlo = split(weights)
+            fhi, flo = split(spread)
+            left = jnp.concatenate([whi, wlo], axis=1)
+            right = jnp.concatenate([fhi, fhi], axis=1)
+            if s.L == 128:
+                under = jnp.concatenate([flo, jnp.zeros_like(flo)], axis=1)
+                res = dot(left, jnp.concatenate([right, under], axis=0), NT)
+                res = res[:, : s.L] + res[:, s.L :]
+            else:
+                res = dot(left, right, NT) + dot(whi, flo, NT)
+            results.append(res.reshape(B, B, B, s.L))
+        for slot, res in zip(slots, results):
+            ys = pl.ds(pl.multiple_of(id_ref[1, slot] * B, B), B)
+            zs = pl.ds(pl.multiple_of(id_ref[2, slot] * B, B), B)
+            grid_ref[:, ys, zs, :] = grid_ref[:, ys, zs, :] + res
+        return carry
+
+    lax.fori_loop(0, (live + step - 1) // step, per_group, 0)
+
+
+def encode_first_kernel(s, cap, id_ref, in_ref, init_ref, grid_ref, list_ref):
     for a in range(B):
         grid_ref[a] = init_ref[a]
-    add_blocks(s, cap, id_ref, num_ref, in_ref, grid_ref)
+    add_blocks(s, cap, id_ref, in_ref, grid_ref, list_ref)
 
 
 def encode_last_kernel(
-    s, cap, row_ref, id_ref, num_ref, in_ref, before_ref, table_ref, grid_ref, keep_ref, send_ref,
-    sum_ref, held_ref, in_sem, out_sems
+    s, cap, row_ref, id_ref, in_ref, before_ref, table_ref, grid_ref, keep_ref, send_ref,
+    list_ref, sum_ref, held_ref, in_sem, out_sems
 ):
     fetch = pltpu.make_async_copy(before_ref, held_ref, in_sem)
     fetch.start()
     for a in range(B):
         sum_ref[a] = jnp.zeros(sum_ref.shape[1:], F32)
-    add_blocks(s, cap, id_ref, num_ref, in_ref, sum_ref)
+    add_blocks(s, cap, id_ref, in_ref, sum_ref, list_ref)
     fetch.wait()
 
     def transform(a, carry):
@@ -454,10 +457,10 @@
     row = row_ref[0]
     groups = by_distance(s, row, [[ref[0, b] for b in range(s.bxn)] for ref in in_refs])
     tiles = block_turn([tile for group in groups for tile in group], s.Yl, s.cp)
-    for y in range(0, s.Yl, 2):
-        hi, lo = split(jnp.concatenate([tiles[y], tiles[y + 1]], axis=1))
+    for y in range(0, s.Yl, 4):
+        hi, lo = split(jnp.concatenate(tiles[y : y + 4], axis=1))
         res = dot(inv_ref[...], jnp.concatenate([hi, lo, hi], axis=0))
-        for i in range(2):
+        for i in range(4):
             grid_ref[0, y + i] = gelu(mixed_ref[0, y + i] + res[:, i * s.L : (i + 1) * s.L])
     out = grid_to_spectrum(s, lambda y: grid_ref[0, y], fwd_ref[...])
     store_spectrum(s, row, 0, out, keep_ref, send_ref)
@@ -494,13 +497,7 @@
     slots = point_ref.shape[1]
     step = 4
 
-    def collect(n, live):
-        list_ref[live] = n
-        return live + id_ref[1, n]
-
-    live = lax.fori_loop(0, slots, collect, 0, unroll=8)
-    for i in range(step):
-        list_ref[live + i] = 0
+    live = live_list(lambda n: id_ref[1, n], slots, step, list_ref)
 
     def per_group(h, carry):
         at = [list_ref[h * step + i] for i in range(step)]
@@ -522,16 +519,6 @@
         return carry
 
     lax.fori_loop(0, (live + step - 1) // step, per_group, 0)
-
-
-def return_kernel(s, slot_ref, in_ref, out_ref):
-    def step(n, carry):
-        slot = slot_ref[n]
-        line = in_ref[pl.ds(jnp.maximum(slot, 0), 1), :]
-        out_ref[pl.ds(n, 1), :] = jnp.where(slot >= 0, line, 0.0)
-        return carry
-
-    lax.fori_loop(0, out_ref.shape[0], step, 0, unroll=8)
 
 
 def per_device(
@@ -568,14 +555,17 @@
         (VM,) * len(caps) + (SM,),
         1e6,
         6e6,
-        scratch=[pltpu.SMEM((ny,), jnp.int32)],
+        scratch=[
+            pltpu.SMEM((ny + 1,), jnp.int32),
+            pltpu.VMEM((ny + 1, cap * C, PB), F32),
+            pltpu.VMEM((ny + 1, 3, cap, PB), F32),
+        ],
     )(block_brick, block_count, positions, point_feat, area.reshape(blocks, PB))
     early = lax.all_to_all(outgoing[0], "gy", split_axis=0, concat_axis=0, tiled=True)
 
     def placement(incoming, cap):
         in_pos = incoming[:, cap * C :, :]
         first = in_pos.reshape(ny, 3, cap, PB)[..., 0].transpose(1, 0, 2).reshape(3, ny * cap)
-        counts = jnp.sum((first[0].reshape(ny, cap) >= 0.0).astype(jnp.int32), axis=1)
         brick = jnp.floor(first / B).astype(jnp.int32)
         start = jnp.stack([row_x * s.bxn, row_y * s.byn, jnp.zeros_like(row_x)])
         limit = jnp.array([s.bxn - 1, s.byn - 1, s.NB - 1], jnp.int32)
@@ -584,7 +574,7 @@
         flat = local[2] * (s.bxn * s.byn) + local[0] * s.byn + local[1]
         owned = jnp.where(first[0:1] >= 0.0, local[0:1], -1)
         ids = jnp.concatenate([owned, local[1:], corner, flat[None], flat[None]], axis=0)
-        return ids, counts, in_pos
+        return ids, in_pos
 
     lane = jnp.arange(L)
     lane_bx = lane // s.cp % s.bxn
@@ -644,8 +634,8 @@
         lax.optimization_barrier(prepared)
     )
     late = lax.all_to_all(second, "gy", split_axis=0, concat_axis=0, tiled=True)
-    ids_a, counts_a, pos_a = placement(early, caps[0])
-    ids_b, counts_b, pos_b = placement(late, caps[1])
+    ids_a, pos_a = placement(early, caps[0])
+    ids_b, pos_b = placement(late, caps[1])
 
     half = s.nx // 2
     spec_shape = shape(half, B, s.bxn, s.K2, s.LY)
@@ -653,26 +643,28 @@
         functools.partial(encode_first_kernel, s, caps[0]),
         "encode_first",
         grid_shape,
-        [SM, SM, VM, VM],
+        [SM, VM, VM],
         VM,
         3e9,
         2e7,
-    )(ids_a, counts_a, early, init)
+        scratch=[pltpu.SMEM((ny * caps[0] + 8,), jnp.int32)],
+    )(ids_a, early, init)
     grid, keep, send = call(
         functools.partial(encode_last_kernel, s, caps[1]),
         "encode_last",
         (grid_shape, spec_shape, spec_shape),
-        [SM, SM, SM, VM, pl.BlockSpec(memory_space=pl.ANY), VM],
+        [SM, SM, VM, pl.BlockSpec(memory_space=pl.ANY), VM],
         (pl.BlockSpec(memory_space=pl.ANY), VM, VM),
         4e9,
         2.2e7,
         scratch=[
+            pltpu.SMEM((ny * caps[1] + 8,), jnp.int32),
             pltpu.VMEM(grid_shape.shape, F32),
             pltpu.VMEM(grid_shape.shape, F32),
             pltpu.SemaphoreType.DMA,
             pltpu.SemaphoreType.DMA((B,)),
         ],
-    )(row, ids_b, counts_b, late, before, t["z_fwd"])
+    )(row, ids_b, late, before, t["z_fwd"])
 
     def exchange(array, distance):
         return lax.ppermute(array, "gx", [(i, i ^ distance) for i in range(nx)])
@@ -794,9 +786,8 @@
         room=32,
     )(where, base, points, last, turns, read.reshape(B * B * B, s.LB), t["xy_hi"], t["xy_lo"], t["z_last"])
     returned = lax.all_to_all(values.reshape(ny, cap, PB), "gy", split_axis=0, concat_axis=0, tiled=True)
-    pressure = call(
-        functools.partial(return_kernel, s), "return", shape(blocks, PB), [SM, VM], VM, 1e5, 2e5, room=16
-    )(slot_of, returned.reshape(ny * cap, PB))
+    choose = (slot_of[:, None] == jnp.arange(ny * cap, dtype=jnp.int32)[None, :]).astype(F32)
+    pressure = jnp.dot(choose, returned.reshape(ny * cap, PB), precision=lax.Precision.HIGHEST)
     return pressure.reshape(blocks * PB)
 
 

time: 269 us -> 256 us (0.952)
  Pallas kernels: 115 us -> 93.8 us
  blocking collectives: 75.4 us -> 80.5 us
    pallas_call x1, Pallas kernels: 19 us -> 11.7 us  [per_device(): call(functools.partial(encode_last_kernel, s, caps[1]), 'encode_last', (g...]
    pallas_call x1, Pallas kernels: 24.3 us -> 17.7 us  [per_device(): call(functools.partial(encode_first_kernel, s, caps[0]), 'encode_first',...]
    pallas_call x1, Pallas kernels: 14.7 us -> 10.3 us  [per_device(): call(functools.partial(decode_kernel, s), 'decode', shape(ny * cap, PB),...]
    all_to_all x1, waiting for transfers between devices: 0.01 us -> 3.37 us  [per_device(): late = lax.all_to_all(second, 'gy', split_axis=0, concat_axis=0, tiled=True)]
    all_to_all x1, blocking collectives: 9.29 us -> 12.4 us  [per_device(): lax.all_to_all(values.reshape(ny, cap, PB), 'gy', split_axis=0, concat_ax...]
  transfers between devices with their start and end apart: 12 -> 12, of which waited for: 8 -> 9; matrix products, arithmetic and copies ran while one was open for 7% -> 8% of each run, Pallas kernels for 21% -> 19%
where the time goes in v7:
time: 256 us; the launch traced here: 255 us
  Pallas kernels  93.8 us (37%)
  blocking collectives  80.5 us (31%)
  waiting for transfers between devices  35.8 us (14%)
  starting transfers between devices  17.5 us (7%)
  local copies, waits for them, and re-layouts  17.4 us (7%)
  other arithmetic  8.2 us (3%)
    all_to_all x2, blocking collectives, to_modes(): spec = lax.all_to_all(spec, 'gy', split_axis=0, concat_axis=0, tiled=True)  39.8 us
    ppermute x10, waiting for transfers between devices, exchange(): return lax.ppermute(array, 'gx', [(i, i ^ distance) for i in range(nx)])  23.9 us
    pallas_call x1, Pallas kernels, per_device(): call(functools.partial(encode_first_kernel, s, caps[0]), 'encode_first',...  17.7 us
    all_to_all x1, blocking collectives, per_device(): lax.all_to_all(spec.reshape(ny, s.LY, s.LK), 'gy', split_axis=0, concat_a...  17.5 us
    pallas_call x1, Pallas kernels, per_device(): call(functools.partial(layer_kernel, s), 'layer', (grid_shape, spec_shape...  13.4 us
    all_to_all x1, blocking collectives, per_device(): lax.all_to_all(values.reshape(ny, cap, PB), 'gy', split_axis=0, concat_ax...  12.4 us
    pallas_call x1, Pallas kernels, per_device(): call(functools.partial(encode_last_kernel, s, caps[1]), 'encode_last', (g...  11.7 us
    all_to_all x1, blocking collectives, per_device(): last = lax.all_to_all(last, 'gy', split_axis=0, concat_axis=0, tiled=True)  10.8 us
  transfers between devices with their start and end apart: 12, of which 9 were waited for; matrix products, arithmetic and copies ran while one was open for 8% of the time, Pallas kernels for 19%

profile of v7, /device:TPU:0, one launch (start us, length us, event | category | flops | bytes accessed | tf_op | source)
XLA Modules:
  0.0 255.3 jit_solution(2324387926730645915)
XLA Ops:
  0.7 5.8 %pack.1 = (f32[8,350,128]{2,1,0:T(8,128)}, f32[8,210,128]{2,1,0:T(8,128)}, s32[128]{0:T(128)}) custom-call(s32[128]{0:T(128)} %brick_ref.1, s32[1]{0:T(128)S(6)} %copy.63.count_ref, f32[3,16384]{1,0:T(4,128)} %pos_ref.1, f32[32,16384]{1,0:T(8,128)} %feat_ref.1, f32[128,128]{1,0:T(8,128)} %bitcast.108), custom_call_target="tpu_custom_call" | custom-call | flops 1000000 | bytes 6000000 | tf_op jit(solution)/shard_map/pack/pallas_call | solution.py:550
  6.5 7.3 %all-to-all-start = ((f32[8,350,128]{2,1,0:T(8,128)}), f32[8,350,128]{2,1,0:T(8,128)S(1)}, u32[]{:S(2)}, u32[]{:S(2)}) async-start(f32[8,350,128]{2,1,0:T(8,128)} %get-tuple-element.40), calls=%async_computation | async-start | bytes 2883584 | tf_op jit(solution)/shard_map/all_to_all | solution.py:564
  14.5 0.8 fusion.1
  17.0 1.0 fusion.13
  18.8 1.1 slice_negate_fusion.1
  23.1 1.7 pad_maximum_fusion
  25.9 1.1 reshape.540
  27.6 0.9 dynamic-slice_bitcast_fusion.1.table_ref
  28.5 0.9 dynamic-slice_bitcast_fusion.table_ref
  29.6 0.7 compare_select_fusion
  30.3 0.8 bitcast_select_fusion.gain_ref
  31.2 8.2 %field.1.init_ref = f32[8,16,128,128]{3,2,1,0:T(8,128)} custom-call(f32[4,8,16,128]{3,2,1,0:T(8,128)} %bitcast.111, f32[64,2048]{1,0:T(8,128)} %bitcast_select_fusion.gain_ref), custom_call_target="tpu_custom_call" | custom-call | flops 3000000000 | bytes 10000000 | tf_op jit(solution)/shard_map/field/pallas_call | solution.py:591
  39.4 8.6 %all-to-all-done.in_ref = f32[8,350,128]{2,1,0:T(8,128)S(1)} async-done(((f32[8,350,128]{2,1,0:T(8,128)}), f32[8,350,128]{2,1,0:T(8,128)S(1)}, u32[]{:S(2)}, u32[]{:S(2)}) %all-to-all-start) | async-done | bytes 1433632 | tf_op jit(solution)/shard_map/all_to_all | solution.py:564
  48.0 3.6 %all-to-all-start.1 = ((f32[8,210,128]{2,1,0:T(8,128)}), f32[8,210,128]{2,1,0:T(8,128)S(1)}, u32[]{:S(2)}, u32[]{:S(2)}) async-start(f32[8,210,128]{2,1,0:T(8,128)} %get-tuple-element.43), calls=%async_computation.1 | async-start | bytes 1769472 | tf_op jit(solution)/shard_map/all_to_all | solution.py:636
  52.9 17.7 %encode_first.1.before_ref = f32[8,16,128,128]{3,2,1,0:T(8,128)} custom-call(s32[8,80]{1,0:T(8,128)} %concatenate.40.id_ref, f32[8,350,128]{2,1,0:T(8,128)} %copy-done.11, f32[8,16,128,128]{3,2,1,0:T(8,128)} %field.1.init_ref), custom_call_target="tpu_custom_call" | custom-call | flops 3000000000 | bytes 20000000 | tf_op jit(solution)/shard_map/encode_first/pallas_call | solution.py:642
  70.7 3.4 %all-to-all-done.1.in_ref = f32[8,210,128]{2,1,0:T(8,128)S(1)} async-done(((f32[8,210,128]{2,1,0:T(8,128)}), f32[8,210,128]{2,1,0:T(8,128)S(1)}, u32[]{:S(2)}, u32[]{:S(2)}) %all-to-all-start.1) | async-done | bytes 860192 | tf_op jit(solution)/shard_map/all_to_all | solution.py:636
  75.3 11.7 %encode_last.1 = (f32[8,16,128,128]{3,2,1,0:T(8,128)}, f32[2,8,4,32,128]{4,3,2,1,0:T(8,128)}, f32[2,8,4,32,128]{4,3,2,1,0:T(8,128)}) custom-call(s32[1]{0:T(128)} %bitcast.12.row_ref, s32[8,48]{1,0:T(8,128)} %concatenate.39.id_ref, f32[8,210,128]{2,1,0:T(8,128)} %copy-done.12, f32[8,16,128,128]{3,2,1,0:T(8,128)} %encode_first.1.before_ref, ...), custom_call_target="tpu_custom_call" | custom-call | flops 4000000000 | bytes 22000000 | tf_op jit(solution)/shard_map/encode_last/pallas_call | solution.py:652
  87.1 2.9 %collective-permute-done = f32[2,8,4,32,128]{4,3,2,1,0:T(8,128)S(1)} collective-permute-done((f32[2,8,4,32,128]{4,3,2,1,0:T(8,128)}, f32[2,8,4,32,128]{4,3,2,1,0:T(8,128)S(1)}, u32[]{:S(2)}, u32[]{:S(2)}) %collective-permute-start) | collective-permute-done | bytes 1048608 | tf_op jit(solution)/shard_map/ppermute | solution.py:670
  89.9 1.2 copy-done.2
  91.2 0.9 x_forward.5
  92.1 1.6 collective-permute-start.1
  93.6 0.9 x_forward.4
  94.5 11.5 %collective-permute-done.1 = f32[8,128,128]{2,1,0:T(8,128)S(1)} collective-permute-done((f32[8,128,128]{2,1,0:T(8,128)S(1)}, f32[8,128,128]{2,1,0:T(8,128)S(1)}, u32[]{:S(2)}, u32[]{:S(2)}) %collective-permute-start.1) | collective-permute-done | bytes 524320 | tf_op jit(solution)/shard_map/ppermute | solution.py:670
  106.2 22.2 %all_to_all.35 = f32[8,128,128]{2,1,0:T(8,128)S(1)} all-to-all(f32[8,128,128]{2,1,0:T(8,128)S(1)} %add.223), channel_id=1, replica_groups=mesh['gx'=4,'gy'=8] {'gy'}, dimensions={0} | all-to-all | bytes 1048576 | tf_op jit(solution)/shard_map/all_to_all | solution.py:696
  128.4 1.0 y_both.1
  129.4 17.5 %all_to_all.36.in_ref = f32[8,128,128]{2,1,0:T(8,128)S(1)} all-to-all(f32[8,128,128]{2,1,0:T(8,128)S(1)} %bitcast.93), channel_id=1, replica_groups=mesh['gx'=4,'gy'=8] {'gy'}, dimensions={0} | all-to-all | bytes 1048576 | tf_op jit(solution)/shard_map/all_to_all | solution.py:713
  146.9 1.4 collective-permute-start.2
  148.3 10.6 %mix.1.mixed_ref = f32[8,16,128,128]{3,2,1,0:T(8,128)} custom-call(f32[8,16,128,128]{3,2,1,0:T(8,128)} %get-tuple-element.46.grid_ref, f32[128,128]{1,0:T(8,128)} %get-tuple-element.47.mix_ref, f32[1,128]{1,0:T(1,128)} %reshape.541.bias_ref), custom_call_target="tpu_custom_call" | custom-call | flops 2000000000 | bytes 17000000 | tf_op jit(solution)/shard_map/mix/pallas_call | solution.py:700
  158.9 1.3 x_inverse.2
  160.2 0.8 copy-done.6
  161.0 1.3 x_inverse.3
  162.3 0.8 copy-done.7
  164.0 1.2 collective-permute-done.4
  165.2 0.8 copy-done.18
  166.0 13.4 %layer.1 = (f32[8,16,128,128]{3,2,1,0:T(8,128)}, f32[2,8,4,32,128]{4,3,2,1,0:T(8,128)}, f32[2,8,4,32,128]{4,3,2,1,0:T(8,128)}) custom-call(s32[1]{0:T(128)} %bitcast.12.row_ref, f32[8,16,128,128]{3,2,1,0:T(8,128)} %mix.1.mixed_ref, bf16[128,96]{1,0:T(8,128)(2,1)} %constant.145.clone.inv_ref, bf16[64,256]{1,0:T(8,128)(2,1)} %constant.144.clone.table_ref.fwd_ref, ...), custom_call_target="tpu_custom_call" | custom-call | flops 4000000000 | bytes 21000000 | tf_op jit(solution)/shard_map/layer/pallas_call | solution.py:733
  180.3 2.0 collective-permute-done.5
  182.3 1.2 copy-done
  183.6 0.9 x_forward.6
  185.3 8.2 %readout.1 = f32[8,64,128]{2,1,0:T(8,128)} custom-call(f32[8,16,128,128]{3,2,1,0:T(8,128)} %get-tuple-element.61.grid_ref, f32[128,128]{1,0:T(8,128)} %get-tuple-element.62.mix_ref), custom_call_target="tpu_custom_call" | custom-call | flops 2000000000 | bytes 9000000 | tf_op jit(solution)/shard_map/readout/pallas_call | solution.py:745
  193.5 0.9 x_forward.7
  194.4 4.3 %collective-permute-done.6 = f32[8,128,128]{2,1,0:T(8,128)S(1)} collective-permute-done((f32[8,128,128]{2,1,0:T(8,128)S(1)}, f32[8,128,128]{2,1,0:T(8,128)S(1)}, u32[]{:S(2)}, u32[]{:S(2)}) %collective-permute-start.6) | collective-permute-done | bytes 524320 | tf_op jit(solution)/shard_map/ppermute | solution.py:670
  198.8 17.6 %all_to_all.37 = f32[8,128,128]{2,1,0:T(8,128)S(1)} all-to-all(f32[8,128,128]{2,1,0:T(8,128)S(1)} %add.235), channel_id=1, replica_groups=mesh['gx'=4,'gy'=8] {'gy'}, dimensions={0} | all-to-all | bytes 1048576 | tf_op jit(solution)/shard_map/all_to_all | solution.py:696
  217.8 1.1 collective-permute-start.7
  219.0 1.3 collective-permute-done.9
  221.0 10.8 %all_to_all.38.spec_ref = f32[8,4,1024]{2,1,0:T(4,128)S(1)} all-to-all(f32[8,4,1024]{2,1,0:T(4,128)S(1)} %broadcast_in_dim.117), channel_id=1, replica_groups=mesh['gx'=4,'gy'=8] {'gy'}, dimensions={0} | all-to-all | bytes 262144 | tf_op jit(solution)/shard_map/all_to_all | solution.py:776
  231.8 10.3 %decode.1 = f32[128,128]{1,0:T(8,128)S(1)} custom-call(s32[3,128]{1,0:T(4,128)S(1)} %pad_add_fusion.id_ref, f32[1]{0:T(128)} %bitcast.6.base_ref, f32[3,128,128]{2,1,0:T(8,128)S(1)} %pad_maximum_fusion.4.point_ref, f32[8,4,1024]{2,1,0:T(4,128)S(1)} %all_to_all.38.spec_ref, f32[2,1024]{1,0:T(2,128)S(1)} %pad_maximum_fusion.5.turn_ref, ...), custom_call_target="tpu_custom_call" | custom-call | flops 4000000000 | bytes 6000000 | tf_op jit(solution)/shard_map/decode/pallas_call | solution.py:777
  242.0 12.4 %all_to_all.39 = f32[8,16,128]{2,1,0:T(8,128)S(1)} all-to-all(f32[8,16,128]{2,1,0:T(8,128)S(1)} %bitcast.96), channel_id=1, replica_groups=mesh['gx'=4,'gy'=8] {'gy'}, dimensions={0} | all-to-all | bytes 131072 | tf_op jit(solution)/shard_map/all_to_all | solution.py:788
  254.5 0.9 convolution_bitcast_fusion
  (134 shorter events, 15.4 us)
Async XLA Ops:
  0.0 20.1 %copy-start.19 = (f32[2,32]{1,0:T(2,128)S(1)}, f32[2,32]{1,0:T(2,128)}, u32[]{:S(2)}) copy-start(f32[2,32]{1,0:T(2,128)} %param.31) | copy-start | bytes 772
  0.0 20.3 %copy-start.15 = (f32[32]{0:T(128)S(1)}, f32[32]{0:T(128)}, u32[]{:S(2)}) copy-start(f32[32]{0:T(128)} %param.29) | copy-start | bytes 388
  6.5 41.5 %all-to-all-start = ((f32[8,350,128]{2,1,0:T(8,128)}), f32[8,350,128]{2,1,0:T(8,128)S(1)}, u32[]{:S(2)}, u32[]{:S(2)}) async-start(f32[8,350,128]{2,1,0:T(8,128)} %get-tuple-element.40), calls=%async_computation | async-start | bytes 2883584 | tf_op jit(solution)/shard_map/all_to_all | solution.py:564
  18.0 9.0 %copy-start.16 = (f32[32]{0:T(128)S(1)}, f32[32]{0:T(128)}, u32[]{:S(2)}) copy-start(f32[32]{0:T(128)} %param.33) | copy-start | bytes 388
  25.9 26.3 %copy-start.13 = (s32[3]{0:T(128)S(1)}, s32[3]{0:T(128)}, u32[]{:S(2)}) copy-start(s32[3]{0:T(128)} %constant.154.clone) | copy-start | bytes 40
  48.0 5.0 %copy-start.11 = (f32[8,350,128]{2,1,0:T(8,128)}, f32[8,350,128]{2,1,0:T(8,128)S(1)}, u32[]{:S(2)}) copy-start(f32[8,350,128]{2,1,0:T(8,128)S(1)} %all-to-all-done.in_ref) | copy-start | bytes 4300804
  48.0 26.1 %all-to-all-start.1 = ((f32[8,210,128]{2,1,0:T(8,128)}), f32[8,210,128]{2,1,0:T(8,128)S(1)}, u32[]{:S(2)}, u32[]{:S(2)}) async-start(f32[8,210,128]{2,1,0:T(8,128)} %get-tuple-element.43), calls=%async_computation.1 | async-start | bytes 1769472 | tf_op jit(solution)/shard_map/all_to_all | solution.py:636
  74.1 1.2 copy-start.12
  75.3 53.1 %copy-start.8 = (bf16[128,256]{1,0:T(8,128)(2,1)S(1)}, bf16[128,256]{1,0:T(8,128)(2,1)}, u32[]{:S(2)}) copy-start(bf16[128,256]{1,0:T(8,128)(2,1)} %constant.149.clone.fwd_ref) | copy-start | bytes 196612
  75.3 53.1 %copy-start.9 = (bf16[128,192]{1,0:T(8,128)(2,1)S(1)}, bf16[128,192]{1,0:T(8,128)(2,1)}, u32[]{:S(2)}) copy-start(bf16[128,192]{1,0:T(8,128)(2,1)} %constant.150.clone.inv_ref) | copy-start | bytes 147460
  87.0 2.9 %collective-permute-start = (f32[2,8,4,32,128]{4,3,2,1,0:T(8,128)}, f32[2,8,4,32,128]{4,3,2,1,0:T(8,128)S(1)}, u32[]{:S(2)}, u32[]{:S(2)}) collective-permute-start(f32[2,8,4,32,128]{4,3,2,1,0:T(8,128)} %get-tuple-element.50), channel_id=1, source_target_pairs={{0,8},{8,0},{16,24},{24,16},{1,9},{9,1},{17,25},{25,17},{2,10},{10... | collective-permute-start | bytes 3145736 | tf_op jit(solution)/shard_map/ppermute | solution.py:670
  89.9 1.2 copy-start.2
  92.1 14.0 %collective-permute-start.1 = (f32[8,128,128]{2,1,0:T(8,128)S(1)}, f32[8,128,128]{2,1,0:T(8,128)S(1)}, u32[]{:S(2)}, u32[]{:S(2)}) collective-permute-start(f32[8,128,128]{2,1,0:T(8,128)S(1)} %x_forward.5), channel_id=1, source_target_pairs={{0,16},{8,24},{16,0},{24,8},{1,17},{9,25},{17,1},{25,9},{2,18},{10... | collective-permute-start | bytes 1572872 | tf_op jit(solution)/shard_map/ppermute | solution.py:670
  146.9 14.1 %collective-permute-start.2 = (f32[8,128,128]{2,1,0:T(8,128)S(1)}, f32[8,128,128]{2,1,0:T(8,128)S(1)}, u32[]{:S(2)}, u32[]{:S(2)}) collective-permute-start(f32[8,128,128]{2,1,0:T(8,128)S(1)} %all_to_all.36.in_ref), channel_id=1, source_target_pairs={{0,16},{8,24},{16,0},{24,8},{1,17},{9,25},{17,1},{25,9},{2,18},{10... | collective-permute-start | bytes 1572872 | tf_op jit(solution)/shard_map/ppermute | solution.py:670
  160.2 0.8 copy-start.6
  161.0 2.9 %collective-permute-start.3 = (f32[1024,128]{1,0:T(8,128)S(1)}, f32[1024,128]{1,0:T(8,128)S(1)}, u32[]{:S(2)}, u32[]{:S(2)}) collective-permute-start(f32[1024,128]{1,0:T(8,128)S(1)} %get-tuple-element.57), channel_id=1, source_target_pairs={{0,8},{8,0},{16,24},{24,16},{1,9},{9,1},{17,25},{25,17},{2,10},{10... | collective-permute-start | bytes 1572872 | tf_op jit(solution)/shard_map/ppermute | solution.py:670
  162.3 0.8 copy-start.7
  163.1 2.0 collective-permute-start.4
  164.0 1.2 copy-start.17
  165.2 0.8 copy-start.18
  179.4 14.1 %copy-start.1 = (f32[2,8,4,32,128]{4,3,2,1,0:T(8,128)S(1)}, f32[2,8,4,32,128]{4,3,2,1,0:T(8,128)}, u32[]{:S(2)}) copy-start(f32[2,8,4,32,128]{4,3,2,1,0:T(8,128)} %get-tuple-element.63) | copy-start | bytes 3145732
  179.4 2.9 %collective-permute-start.5 = (f32[2,8,4,32,128]{4,3,2,1,0:T(8,128)}, f32[2,8,4,32,128]{4,3,2,1,0:T(8,128)S(1)}, u32[]{:S(2)}, u32[]{:S(2)}) collective-permute-start(f32[2,8,4,32,128]{4,3,2,1,0:T(8,128)} %get-tuple-element.64), channel_id=1, source_target_pairs={{0,8},{8,0},{16,24},{24,16},{1,9},{9,1},{17,25},{25,17},{2,10},{10... | collective-permute-start | bytes 3145736 | tf_op jit(solution)/shard_map/ppermute | solution.py:670
  182.3 1.2 copy-start
  184.5 14.3 %collective-permute-start.6 = (f32[8,128,128]{2,1,0:T(8,128)S(1)}, f32[8,128,128]{2,1,0:T(8,128)S(1)}, u32[]{:S(2)}, u32[]{:S(2)}) collective-permute-start(f32[8,128,128]{2,1,0:T(8,128)S(1)} %x_forward.6), channel_id=1, source_target_pairs={{0,16},{8,24},{16,0},{24,8},{1,17},{9,25},{17,1},{25,9},{2,18},{10... | collective-permute-start | bytes 1572872 | tf_op jit(solution)/shard_map/ppermute | solution.py:670
  185.3 46.5 %copy-start.10 = (bf16[128,96]{1,0:T(8,128)(2,1)S(1)}, bf16[128,96]{1,0:T(8,128)(2,1)}, u32[]{:S(2)}) copy-start(bf16[128,96]{1,0:T(8,128)(2,1)} %constant.146.clone.inv_ref) | copy-start | bytes 73732
  193.5 38.3 %copy-start.3 = (f32[8,64,128]{2,1,0:T(8,128)S(1)}, f32[8,64,128]{2,1,0:T(8,128)}, u32[]{:S(2)}) copy-start(f32[8,64,128]{2,1,0:T(8,128)} %readout.1) | copy-start | bytes 786436
  193.5 38.3 %copy-start.4 = (bf16[2048,512]{1,0:T(8,128)(2,1)S(1)}, bf16[2048,512]{1,0:T(8,128)(2,1)}, u32[]{:S(2)}) copy-start(bf16[2048,512]{1,0:T(8,128)(2,1)} %constant.152.clone.lo_ref) | copy-start | bytes 6291460
  193.5 38.3 %copy-start.5 = (bf16[2048,512]{1,0:T(8,128)(2,1)S(1)}, bf16[2048,512]{1,0:T(8,128)(2,1)}, u32[]{:S(2)}) copy-start(bf16[2048,512]{1,0:T(8,128)(2,1)} %constant.151.clone.hi_ref) | copy-start | bytes 6291460
  217.0 37.4 %copy-start.14 = (s32[128]{0:T(128)S(1)}, s32[128]{0:T(128)}, u32[]{:S(2)}) copy-start(s32[128]{0:T(128)} %get-tuple-element.39) | copy-start | bytes 1540
  217.0 3.2 %collective-permute-start.9 = (f32[4,1024]{1,0:T(4,128)S(1)}, f32[4,1024]{1,0:T(4,128)S(1)}, u32[]{:S(2)}, u32[]{:S(2)}) collective-permute-start(f32[4,1024]{1,0:T(4,128)S(1)} %y_last.1), channel_id=1, source_target_pairs={{0,24},{8,16},{16,8},{24,0},{1,25},{9,17},{17,9},{25,1},{2,26},{10... | collective-permute-start | bytes 49160 | tf_op jit(solution)/shard_map/ppermute | solution.py:670
  217.1 3.8 %collective-permute-start.8 = (f32[4,1024]{1,0:T(4,128)S(1)}, f32[4,1024]{1,0:T(4,128)S(1)}, u32[]{:S(2)}, u32[]{:S(2)}) collective-permute-start(f32[4,1024]{1,0:T(4,128)S(1)} %y_last.1), channel_id=1, source_target_pairs={{0,16},{8,24},{16,0},{24,8},{1,17},{9,25},{17,1},{25,9},{2,18},{10... | collective-permute-start | bytes 49160 | tf_op jit(solution)/shard_map/ppermute | solution.py:670
  217.8 3.1 %collective-permute-start.7 = (f32[4,1024]{1,0:T(4,128)S(1)}, f32[4,1024]{1,0:T(4,128)S(1)}, u32[]{:S(2)}, u32[]{:S(2)}) collective-permute-start(f32[4,1024]{1,0:T(4,128)S(1)} %y_last.1), channel_id=1, source_target_pairs={{0,8},{8,0},{16,24},{24,16},{1,9},{9,1},{17,25},{25,17},{2,10},{10... | collective-permute-start | bytes 49160 | tf_op jit(solution)/shard_map/ppermute | solution.py:670

commit v8 on v7

--- a/solution.py
+++ b/solution.py
@@ -165,7 +165,6 @@
     for i in range(s.ny):
         fill_ref[i] = 0
         pos_out[i] = jnp.full(pos_out.shape[1:], -1.0, F32)
-        feat_out[i] = jnp.zeros(feat_out.shape[1:], F32)
     fill_ref[s.ny] = 0
     live = count_ref[0]
 
@@ -184,14 +183,13 @@
         return carry
 
     lax.fori_loop(0, blocks, place, 0, unroll=8)
-    first = 0
-    for part, out_ref in zip(caps, out_refs):
-        for i in range(s.ny):
-            out_ref[i, : part * C] = feat_out[i, first * C : (first + part) * C]
-            for d in range(3):
-                at = part * C + d * part
-                out_ref[i, at : at + part] = pos_out[i, d, first : first + part]
-        first += part
+    early_ref, late_ref = out_refs
+    at = caps[0] * C
+    for i in range(s.ny):
+        early_ref[i, :at] = feat_out[i, :at]
+        late_ref[i] = feat_out[i, at:]
+        for d in range(3):
+            early_ref[i, at + d * cap : at + (d + 1) * cap] = pos_out[i, d]
 
 
 def field_kernel(s, sdf_ref, gain_ref, out_ref):
@@ -262,11 +260,12 @@
     return live
 
 
-def add_blocks(s, cap, id_ref, in_ref, grid_ref, list_ref):
+def add_blocks(s, caps, turn, id_ref, in_ref, pos_ref, at, grid_ref, list_ref):
     C = s.C
+    cap = sum(caps)
     step = 4
     group = lax.broadcasted_iota(jnp.int32, (s.L, 128), 0) // s.cp % s.bxn
-    live = live_list(lambda n: jnp.where(id_ref[0, n] >= 0, 1, 0), s.ny * cap, step, list_ref)
+    live = live_list(lambda n: jnp.where(id_ref[7, n] == turn, 1, 0), s.ny * cap, step, list_ref)
 
     def per_group(h, carry):
         results = []
@@ -274,12 +273,13 @@
         for i, slot in enumerate(slots):
             src, j = slot // cap, slot % cap
             points = [
-                jnp.broadcast_to(in_ref[src, pl.ds(cap * C + d * cap + j, 1), :], (8, 128))
+                jnp.broadcast_to(pos_ref[src, pl.ds(at + d * cap + j, 1), :], (8, 128))
                 - id_ref[3 + d, slot].astype(F32)
                 for d in range(3)
             ]
             weights = jnp.concatenate(kernel_tiles(points), axis=0)
-            feats = in_ref[src, pl.ds(pl.multiple_of(j * C, 8), C), :]
+            place = jnp.clip(j - turn * caps[0], 0, caps[turn] - 1)
+            feats = in_ref[src, pl.ds(pl.multiple_of(place * C, 8), C), :]
             spread = []
             for g in range(s.nx):
                 spread += [feats[g * s.cp : (g + 1) * s.cp]] * s.bxn
@@ -305,21 +305,21 @@
     lax.fori_loop(0, (live + step - 1) // step, per_group, 0)
 
 
-def encode_first_kernel(s, cap, id_ref, in_ref, init_ref, grid_ref, list_ref):
+def encode_first_kernel(s, caps, id_ref, in_ref, init_ref, grid_ref, list_ref):
     for a in range(B):
         grid_ref[a] = init_ref[a]
-    add_blocks(s, cap, id_ref, in_ref, grid_ref, list_ref)
+    add_blocks(s, caps, 0, id_ref, in_ref, in_ref, caps[0] * s.C, grid_ref, list_ref)
 
 
 def encode_last_kernel(
-    s, cap, row_ref, id_ref, in_ref, before_ref, table_ref, grid_ref, keep_ref, send_ref,
+    s, caps, row_ref, id_ref, in_ref, pos_ref, before_ref, table_ref, grid_ref, keep_ref, send_ref,
     list_ref, sum_ref, held_ref, in_sem, out_sems
 ):
     fetch = pltpu.make_async_copy(before_ref, held_ref, in_sem)
     fetch.start()
     for a in range(B):
         sum_ref[a] = jnp.zeros(sum_ref.shape[1:], F32)
-    add_blocks(s, cap, id_ref, in_ref, sum_ref, list_ref)
+    add_blocks(s, caps, 1, id_ref, in_ref, pos_ref, 0, sum_ref, list_ref)
     fetch.wait()
 
     def transform(a, carry):
@@ -495,7 +495,7 @@
     shi, slo = split(jnp.concatenate(fields, axis=0))
     s_ref[0], s_ref[1] = shi, slo
     slots = point_ref.shape[1]
-    step = 4
+    step = 8
 
     live = live_list(lambda n: id_ref[1, n], slots, step, list_ref)
 
@@ -550,9 +550,13 @@
     *outgoing, slot_of = call(
         functools.partial(pack_kernel, s, caps),
         "pack",
-        tuple(shape(ny, part * (C + 3), PB) for part in caps) + (jax.ShapeDtypeStruct((blocks,), jnp.int32),),
+        (
+            shape(ny, caps[0] * C + 3 * cap, PB),
+            shape(ny, caps[1] * C, PB),
+            jax.ShapeDtypeStruct((blocks,), jnp.int32),
+        ),
         [SM, SM, VM, VM, VM],
-        (VM,) * len(caps) + (SM,),
+        (VM, VM, SM),
         1e6,
         6e6,
         scratch=[
@@ -563,8 +567,8 @@
     )(block_brick, block_count, positions, point_feat, area.reshape(blocks, PB))
     early = lax.all_to_all(outgoing[0], "gy", split_axis=0, concat_axis=0, tiled=True)
 
-    def placement(incoming, cap):
-        in_pos = incoming[:, cap * C :, :]
+    def placement(incoming):
+        in_pos = incoming[:, caps[0] * C :, :]
         first = in_pos.reshape(ny, 3, cap, PB)[..., 0].transpose(1, 0, 2).reshape(3, ny * cap)
         brick = jnp.floor(first / B).astype(jnp.int32)
         start = jnp.stack([row_x * s.bxn, row_y * s.byn, jnp.zeros_like(row_x)])
@@ -573,7 +577,9 @@
         corner = (local + start[:, None]) * B
         flat = local[2] * (s.bxn * s.byn) + local[0] * s.byn + local[1]
         owned = jnp.where(first[0:1] >= 0.0, local[0:1], -1)
-        ids = jnp.concatenate([owned, local[1:], corner, flat[None], flat[None]], axis=0)
+        turn = jnp.where(jnp.arange(ny * cap) % cap < caps[0], 0, 1).astype(jnp.int32)
+        turn = jnp.where(first[0] >= 0.0, turn, -1)
+        ids = jnp.concatenate([owned, local[1:], corner, flat[None], turn[None]], axis=0)
         return ids, in_pos
 
     lane = jnp.arange(L)
@@ -634,37 +640,36 @@
         lax.optimization_barrier(prepared)
     )
     late = lax.all_to_all(second, "gy", split_axis=0, concat_axis=0, tiled=True)
-    ids_a, pos_a = placement(early, caps[0])
-    ids_b, pos_b = placement(late, caps[1])
+    ids, in_pos = placement(early)
 
     half = s.nx // 2
     spec_shape = shape(half, B, s.bxn, s.K2, s.LY)
     before = call(
-        functools.partial(encode_first_kernel, s, caps[0]),
+        functools.partial(encode_first_kernel, s, caps),
         "encode_first",
         grid_shape,
         [SM, VM, VM],
         VM,
         3e9,
         2e7,
-        scratch=[pltpu.SMEM((ny * caps[0] + 8,), jnp.int32)],
-    )(ids_a, early, init)
+        scratch=[pltpu.SMEM((ny * cap + 8,), jnp.int32)],
+    )(ids, early, init)
     grid, keep, send = call(
-        functools.partial(encode_last_kernel, s, caps[1]),
+        functools.partial(encode_last_kernel, s, caps),
         "encode_last",
         (grid_shape, spec_shape, spec_shape),
-        [SM, SM, VM, pl.BlockSpec(memory_space=pl.ANY), VM],
+        [SM, SM, VM, VM, pl.BlockSpec(memory_space=pl.ANY), VM],
         (pl.BlockSpec(memory_space=pl.ANY), VM, VM),
         4e9,
         2.2e7,
         scratch=[
-            pltpu.SMEM((ny * caps[1] + 8,), jnp.int32),
+            pltpu.SMEM((ny * cap + 8,), jnp.int32),
             pltpu.VMEM(grid_shape.shape, F32),
             pltpu.VMEM(grid_shape.shape, F32),
             pltpu.SemaphoreType.DMA,
             pltpu.SemaphoreType.DMA((B,)),
         ],
-    )(row, ids_b, late, before, t["z_fwd"])
+    )(row, ids, late, in_pos, before, t["z_fwd"])
 
     def exchange(array, distance):
         return lax.ppermute(array, "gx", [(i, i ^ distance) for i in range(nx)])
@@ -739,6 +744,7 @@
         4e9,
         2.1e7,
         grid=(B,),
+        room=63,
     )(row, mixed, t["z_inv"], t["z_fwd"], *fields)
 
     def readout():
@@ -754,17 +760,10 @@
         )(grid, reading), decode_places()
 
     def decode_places():
-        points, bricks, live, places = [], [], [], []
-        first = 0
-        for part, ids, pos in ((caps[0], ids_a, pos_a), (caps[1], ids_b, pos_b)):
-            pos = pos.reshape(ny, 3, part, PB).transpose(1, 0, 2, 3).reshape(3, ny * part, PB)
-            points.append(pos - ids[3:6].astype(F32)[:, :, None])
-            bricks.append(ids[6])
-            live.append((ids[0] >= 0).astype(jnp.int32))
-            places.append((jnp.arange(ny)[:, None] * cap + first + jnp.arange(part)[None, :]).reshape(-1))
-            first += part
-        where = [jnp.concatenate(v).astype(jnp.int32) for v in (bricks, live, places)]
-        return jnp.concatenate(points, axis=1), jnp.stack(where)
+        points = in_pos.reshape(ny, 3, cap, PB).transpose(1, 0, 2, 3).reshape(3, ny * cap, PB)
+        live = (ids[7] >= 0).astype(jnp.int32)
+        where = jnp.stack([ids[6], live, jnp.arange(ny * cap, dtype=jnp.int32)])
+        return points - ids[3:6].astype(F32)[:, :, None], where
 
     spec, (read, (points, where)) = to_modes(keep, send, readout)
     last = call(

time: 256 us -> 257 us (level)
  Pallas kernels: 93.8 us -> 104 us
  waiting for transfers between devices: 35.8 us -> 28.9 us
  blocking collectives: 80.5 us -> 74.3 us
    pallas_call x3, Pallas kernels: 35.3 us -> 42.5 us  [the longest x1 20 us: per_device(): call(functools.partial(encode_first_kernel, s, caps), 'encode_first', gri...]
    all_to_all x1, waiting for transfers between devices: 8.58 us -> 3.78 us  [per_device(): lax.all_to_all(outgoing[0], 'gy', split_axis=0, concat_axis=0, tiled=True)]
    all_to_all x2, blocking collectives: 39.8 us -> 36.4 us  [to_modes(): spec = lax.all_to_all(spec, 'gy', split_axis=0, concat_axis=0, tiled=True)]
    all_to_all x1, waiting for transfers between devices: 3.37 us -> 0.01 us  [per_device(): late = lax.all_to_all(second, 'gy', split_axis=0, concat_axis=0, tiled=True)]
    all_to_all x1, blocking collectives: 12.4 us -> 9.29 us  [per_device(): lax.all_to_all(values.reshape(ny, cap, PB), 'gy', split_axis=0, concat_ax...]
    pallas_call x1, Pallas kernels: 10.3 us -> 13 us  [per_device(): call(functools.partial(decode_kernel, s), 'decode', shape(ny * cap, PB),...]
  transfers between devices with their start and end apart: 12 -> 12, of which waited for: 9 -> 8; matrix products, arithmetic and copies ran while one was open for 8% -> 10% of each run, Pallas kernels for 19% -> 20%
where the time goes in v8:
time: 257 us; the launch traced here: 255 us
  Pallas kernels  104 us (40%)
  blocking collectives  74.3 us (29%)
  waiting for transfers between devices  28.9 us (11%)
  local copies, waits for them, and re-layouts  19.6 us (8%)
  starting transfers between devices  16.6 us (6%)
  other arithmetic  10.1 us (4%)
    all_to_all x2, blocking collectives, to_modes(): spec = lax.all_to_all(spec, 'gy', split_axis=0, concat_axis=0, tiled=True)  36.4 us
    ppermute x10, waiting for transfers between devices, exchange(): return lax.ppermute(array, 'gx', [(i, i ^ distance) for i in range(nx)])  25.1 us
    pallas_call x1, Pallas kernels, per_device(): call(functools.partial(encode_first_kernel, s, caps), 'encode_first', gri...  20 us
    all_to_all x1, blocking collectives, per_device(): lax.all_to_all(spec.reshape(ny, s.LY, s.LK), 'gy', split_axis=0, concat_a...  17.5 us
    pallas_call x1, Pallas kernels, per_device(): call(functools.partial(encode_last_kernel, s, caps), 'encode_last', (grid...  16.7 us
    pallas_call x1, Pallas kernels, per_device(): call(functools.partial(layer_kernel, s), 'layer', (grid_shape, spec_shape...  13.4 us
    pallas_call x1, Pallas kernels, per_device(): call(functools.partial(decode_kernel, s), 'decode', shape(ny * cap, PB),...  13 us
    all_to_all x1, blocking collectives, per_device(): last = lax.all_to_all(last, 'gy', split_axis=0, concat_axis=0, tiled=True)  11.2 us
  transfers between devices with their start and end apart: 12, of which 8 were waited for; matrix products, arithmetic and copies ran while one was open for 10% of the time, Pallas kernels for 20%

profile of v8, /device:TPU:0, one launch (start us, length us, event | category | flops | bytes accessed | tf_op | source)
XLA Modules:
  0.0 255.5 jit_solution(15561888175681272211)
XLA Ops:
  0.7 5.7 %pack.1 = (f32[8,368,128]{2,1,0:T(8,128)}, f32[8,192,128]{2,1,0:T(8,128)}, s32[128]{0:T(128)}) custom-call(s32[128]{0:T(128)} %brick_ref.1, s32[1]{0:T(128)S(6)} %copy.37.count_ref, f32[3,16384]{1,0:T(4,128)} %pos_ref.1, f32[32,16384]{1,0:T(8,128)} %feat_ref.1, f32[128,128]{1,0:T(8,128)} %bitcast.85), custom_call_target="tpu_custom_call" | custom-call | flops 1000000 | bytes 6000000 | tf_op jit(solution)/shard_map/pack/pallas_call | solution.py:550
  6.4 7.3 %all-to-all-start = ((f32[8,368,128]{2,1,0:T(8,128)}), f32[8,368,128]{2,1,0:T(8,128)S(1)}, u32[]{:S(2)}, u32[]{:S(2)}) async-start(f32[8,368,128]{2,1,0:T(8,128)} %get-tuple-element.40), calls=%async_computation | async-start | bytes 3014656 | tf_op jit(solution)/shard_map/all_to_all | solution.py:568
  14.4 0.8 fusion.1
  16.9 1.0 fusion.13
  18.2 0.8 slice_negate_fusion
  19.5 1.2 slice_negate_fusion.1
  20.7 1.1 pad_maximum_fusion.2
  25.4 1.7 pad_maximum_fusion
  27.9 2.1 broadcast_in_dim.97
  30.0 2.3 reshape.471
  32.4 1.3 fusion.8
  33.7 0.9 dynamic-slice_bitcast_fusion.1.table_ref
  34.6 0.9 dynamic-slice_bitcast_fusion.table_ref
  36.4 0.8 bitcast_select_fusion.gain_ref
  37.3 8.3 %field.1.init_ref = f32[8,16,128,128]{3,2,1,0:T(8,128)} custom-call(f32[4,8,16,128]{3,2,1,0:T(8,128)} %bitcast.88, f32[64,2048]{1,0:T(8,128)} %bitcast_select_fusion.gain_ref), custom_call_target="tpu_custom_call" | custom-call | flops 3000000000 | bytes 10000000 | tf_op jit(solution)/shard_map/field/pallas_call | solution.py:597
  45.5 3.8 %all-to-all-done.in_ref = f32[8,368,128]{2,1,0:T(8,128)S(1)} async-done(((f32[8,368,128]{2,1,0:T(8,128)}), f32[8,368,128]{2,1,0:T(8,128)S(1)}, u32[]{:S(2)}, u32[]{:S(2)}) %all-to-all-start) | async-done | bytes 1507360 | tf_op jit(solution)/shard_map/all_to_all | solution.py:568
  49.3 4.2 %all-to-all-start.1 = ((f32[8,192,128]{2,1,0:T(8,128)}), f32[8,192,128]{2,1,0:T(8,128)}, u32[]{:S(2)}, u32[]{:S(2)}) async-start(f32[8,192,128]{2,1,0:T(8,128)} %get-tuple-element.44), calls=%async_computation.1 | async-start | bytes 1572864 | tf_op jit(solution)/shard_map/all_to_all | solution.py:642
  54.7 20.0 %encode_first.1.before_ref = f32[8,16,128,128]{3,2,1,0:T(8,128)} custom-call(s32[8,128]{1,0:T(8,128)} %concatenate.23.id_ref, f32[8,368,128]{2,1,0:T(8,128)} %copy-done.11, f32[8,16,128,128]{3,2,1,0:T(8,128)} %field.1.init_ref), custom_call_target="tpu_custom_call" | custom-call | flops 3000000000 | bytes 20000000 | tf_op jit(solution)/shard_map/encode_first/pallas_call | solution.py:647
  74.7 16.7 %encode_last.1 = (f32[8,16,128,128]{3,2,1,0:T(8,128)}, f32[2,8,4,32,128]{4,3,2,1,0:T(8,128)}, f32[2,8,4,32,128]{4,3,2,1,0:T(8,128)}) custom-call(s32[1]{0:T(128)} %bitcast.12.row_ref, s32[8,128]{1,0:T(8,128)} %concatenate.23.id_ref, f32[8,192,128]{2,1,0:T(8,128)} %all-to-all-done.1.in_ref, f32[8,48,128]{2,1,0:T(8,128)} %copy-done.12, ...), custom_call_target="tpu_custom_call" | custom-call | flops 4000000000 | bytes 22000000 | tf_op jit(solution)/shard_map/encode_last/pallas_call | solution.py:657
  91.5 2.9 %collective-permute-done = f32[2,8,4,32,128]{4,3,2,1,0:T(8,128)S(1)} collective-permute-done((f32[2,8,4,32,128]{4,3,2,1,0:T(8,128)}, f32[2,8,4,32,128]{4,3,2,1,0:T(8,128)S(1)}, u32[]{:S(2)}, u32[]{:S(2)}) %collective-permute-start) | collective-permute-done | bytes 1048608 | tf_op jit(solution)/shard_map/ppermute | solution.py:675
  94.4 1.2 copy-done.2
  95.6 0.9 x_forward.5
  96.6 0.9 x_forward.4
  97.5 13.1 %collective-permute-done.1 = f32[8,128,128]{2,1,0:T(8,128)S(1)} collective-permute-done((f32[8,128,128]{2,1,0:T(8,128)S(1)}, f32[8,128,128]{2,1,0:T(8,128)S(1)}, u32[]{:S(2)}, u32[]{:S(2)}) %collective-permute-start.1) | collective-permute-done | bytes 524320 | tf_op jit(solution)/shard_map/ppermute | solution.py:675
  110.6 18.7 %all_to_all.35 = f32[8,128,128]{2,1,0:T(8,128)S(1)} all-to-all(f32[8,128,128]{2,1,0:T(8,128)S(1)} %add.168), channel_id=1, replica_groups=mesh['gx'=4,'gy'=8] {'gy'}, dimensions={0} | all-to-all | bytes 1048576 | tf_op jit(solution)/shard_map/all_to_all | solution.py:701
  129.3 1.0 y_both.1
  130.4 17.5 %all_to_all.36.in_ref = f32[8,128,128]{2,1,0:T(8,128)S(1)} all-to-all(f32[8,128,128]{2,1,0:T(8,128)S(1)} %bitcast.73), channel_id=1, replica_groups=mesh['gx'=4,'gy'=8] {'gy'}, dimensions={0} | all-to-all | bytes 1048576 | tf_op jit(solution)/shard_map/all_to_all | solution.py:718
  148.5 10.6 %mix.1.mixed_ref = f32[8,16,128,128]{3,2,1,0:T(8,128)} custom-call(f32[8,16,128,128]{3,2,1,0:T(8,128)} %get-tuple-element.46.grid_ref, f32[128,128]{1,0:T(8,128)} %get-tuple-element.47.mix_ref, f32[1,128]{1,0:T(1,128)} %reshape.472.bias_ref), custom_call_target="tpu_custom_call" | custom-call | flops 2000000000 | bytes 17000000 | tf_op jit(solution)/shard_map/mix/pallas_call | solution.py:705
  159.0 1.3 x_inverse.2
  160.4 0.8 copy-done.6
  161.2 1.3 x_inverse.3
  163.8 1.5 collective-permute-done.4
  165.3 0.8 copy-done.18
  166.1 13.4 %layer.1 = (f32[8,16,128,128]{3,2,1,0:T(8,128)}, f32[2,8,4,32,128]{4,3,2,1,0:T(8,128)}, f32[2,8,4,32,128]{4,3,2,1,0:T(8,128)}) custom-call(s32[1]{0:T(128)} %bitcast.12.row_ref, f32[8,16,128,128]{3,2,1,0:T(8,128)} %mix.1.mixed_ref, bf16[128,96]{1,0:T(8,128)(2,1)} %constant.149.clone.inv_ref, bf16[64,256]{1,0:T(8,128)(2,1)} %constant.148.clone.table_ref.fwd_ref, ...), custom_call_target="tpu_custom_call" | custom-call | flops 4000000000 | bytes 21000000 | tf_op jit(solution)/shard_map/layer/pallas_call | solution.py:738
  179.9 2.5 collective-permute-done.5
  182.4 1.2 copy-done
  183.7 0.9 x_forward.6
  184.5 1.6 collective-permute-start.6
  186.3 8.4 %readout.1 = f32[8,64,128]{2,1,0:T(8,128)} custom-call(f32[8,16,128,128]{3,2,1,0:T(8,128)} %get-tuple-element.61.grid_ref, f32[128,128]{1,0:T(8,128)} %get-tuple-element.62.mix_ref), custom_call_target="tpu_custom_call" | custom-call | flops 2000000000 | bytes 9000000 | tf_op jit(solution)/shard_map/readout/pallas_call | solution.py:751
  194.7 0.9 x_forward.7
  195.6 3.2 %collective-permute-done.6 = f32[8,128,128]{2,1,0:T(8,128)S(1)} collective-permute-done((f32[8,128,128]{2,1,0:T(8,128)S(1)}, f32[8,128,128]{2,1,0:T(8,128)S(1)}, u32[]{:S(2)}, u32[]{:S(2)}) %collective-permute-start.6) | collective-permute-done | bytes 524320 | tf_op jit(solution)/shard_map/ppermute | solution.py:675
  198.9 17.7 %all_to_all.37 = f32[8,128,128]{2,1,0:T(8,128)S(1)} all-to-all(f32[8,128,128]{2,1,0:T(8,128)S(1)} %add.169), channel_id=1, replica_groups=mesh['gx'=4,'gy'=8] {'gy'}, dimensions={0} | all-to-all | bytes 1048576 | tf_op jit(solution)/shard_map/all_to_all | solution.py:701
  217.3 1.5 collective-permute-start.8
  219.1 1.5 collective-permute-done.9
  221.1 11.2 %all_to_all.38.spec_ref = f32[8,4,1024]{2,1,0:T(4,128)S(1)} all-to-all(f32[8,4,1024]{2,1,0:T(4,128)S(1)} %broadcast_in_dim.105), channel_id=1, replica_groups=mesh['gx'=4,'gy'=8] {'gy'}, dimensions={0} | all-to-all | bytes 262144 | tf_op jit(solution)/shard_map/all_to_all | solution.py:775
  232.3 13.0 %decode.1 = f32[128,128]{1,0:T(8,128)S(1)} custom-call(s32[3,128]{1,0:T(4,128)S(1)} %pad_add_fusion.id_ref, f32[1]{0:T(128)} %bitcast.6.base_ref, f32[3,128,128]{2,1,0:T(8,128)S(1)} %bitcast_subtract_fusion.point_ref, f32[8,4,1024]{2,1,0:T(4,128)S(1)} %all_to_all.38.spec_ref, f32[2,1024]{1,0:T(2,128)S(1)} %pad_maximum_fusion.4.turn_ref, ...), custom_call_target="tpu_custom_call" | custom-call | flops 4000000000 | bytes 6000000 | tf_op jit(solution)/shard_map/decode/pallas_call | solution.py:776
  245.3 9.3 %all_to_all.39 = f32[8,16,128]{2,1,0:T(8,128)S(1)} all-to-all(f32[8,16,128]{2,1,0:T(8,128)S(1)} %bitcast.76), channel_id=1, replica_groups=mesh['gx'=4,'gy'=8] {'gy'}, dimensions={0} | all-to-all | bytes 131072 | tf_op jit(solution)/shard_map/all_to_all | solution.py:787
  254.6 0.9 convolution_bitcast_fusion
  (106 shorter events, 13.9 us)
Async XLA Ops:
  0.0 21.8 %copy-start.19 = (f32[2,32]{1,0:T(2,128)S(1)}, f32[2,32]{1,0:T(2,128)}, u32[]{:S(2)}) copy-start(f32[2,32]{1,0:T(2,128)} %param.30) | copy-start | bytes 772
  0.0 22.0 %copy-start.15 = (f32[32]{0:T(128)S(1)}, f32[32]{0:T(128)}, u32[]{:S(2)}) copy-start(f32[32]{0:T(128)} %param.28) | copy-start | bytes 388
  6.4 42.9 %all-to-all-start = ((f32[8,368,128]{2,1,0:T(8,128)}), f32[8,368,128]{2,1,0:T(8,128)S(1)}, u32[]{:S(2)}, u32[]{:S(2)}) async-start(f32[8,368,128]{2,1,0:T(8,128)} %get-tuple-element.40), calls=%async_computation | async-start | bytes 3014656 | tf_op jit(solution)/shard_map/all_to_all | solution.py:568
  27.9 26.0 %copy-start.16 = (s32[3]{0:T(128)S(1)}, s32[3]{0:T(128)}, u32[]{:S(2)}) copy-start(s32[3]{0:T(128)} %constant.158.clone) | copy-start | bytes 40
  49.3 5.4 %copy-start.11 = (f32[8,368,128]{2,1,0:T(8,128)}, f32[8,368,128]{2,1,0:T(8,128)S(1)}, u32[]{:S(2)}) copy-start(f32[8,368,128]{2,1,0:T(8,128)S(1)} %all-to-all-done.in_ref) | copy-start | bytes 4521988
  49.3 25.4 %all-to-all-start.1 = ((f32[8,192,128]{2,1,0:T(8,128)}), f32[8,192,128]{2,1,0:T(8,128)}, u32[]{:S(2)}, u32[]{:S(2)}) async-start(f32[8,192,128]{2,1,0:T(8,128)} %get-tuple-element.44), calls=%async_computation.1 | async-start | bytes 1572864 | tf_op jit(solution)/shard_map/all_to_all | solution.py:642
  53.5 21.2 %copy-start.12 = (f32[8,48,128]{2,1,0:T(8,128)}, f32[8,48,128]{2,1,0:T(8,128)S(1)}, u32[]{:S(2)}) copy-start(f32[8,48,128]{2,1,0:T(8,128)S(1)} %slice.68.pos_ref) | copy-start | bytes 589828
  74.7 54.6 %copy-start.8 = (bf16[128,256]{1,0:T(8,128)(2,1)S(1)}, bf16[128,256]{1,0:T(8,128)(2,1)}, u32[]{:S(2)}) copy-start(bf16[128,256]{1,0:T(8,128)(2,1)} %constant.153.clone.fwd_ref) | copy-start | bytes 196612
  74.7 54.6 %copy-start.9 = (bf16[128,192]{1,0:T(8,128)(2,1)S(1)}, bf16[128,192]{1,0:T(8,128)(2,1)}, u32[]{:S(2)}) copy-start(bf16[128,192]{1,0:T(8,128)(2,1)} %constant.154.clone.inv_ref) | copy-start | bytes 147460
  91.5 2.9 %collective-permute-start = (f32[2,8,4,32,128]{4,3,2,1,0:T(8,128)}, f32[2,8,4,32,128]{4,3,2,1,0:T(8,128)S(1)}, u32[]{:S(2)}, u32[]{:S(2)}) collective-permute-start(f32[2,8,4,32,128]{4,3,2,1,0:T(8,128)} %get-tuple-element.50), channel_id=1, source_target_pairs={{0,8},{8,0},{16,24},{24,16},{1,9},{9,1},{17,25},{25,17},{2,10},{10... | collective-permute-start | bytes 3145736 | tf_op jit(solution)/shard_map/ppermute | solution.py:675
  94.4 1.2 copy-start.2
  96.5 14.0 %collective-permute-start.1 = (f32[8,128,128]{2,1,0:T(8,128)S(1)}, f32[8,128,128]{2,1,0:T(8,128)S(1)}, u32[]{:S(2)}, u32[]{:S(2)}) collective-permute-start(f32[8,128,128]{2,1,0:T(8,128)S(1)} %x_forward.5), channel_id=1, source_target_pairs={{0,16},{8,24},{16,0},{24,8},{1,17},{9,25},{17,1},{25,9},{2,18},{10... | collective-permute-start | bytes 1572872 | tf_op jit(solution)/shard_map/ppermute | solution.py:675
  147.9 13.3 %collective-permute-start.2 = (f32[8,128,128]{2,1,0:T(8,128)S(1)}, f32[8,128,128]{2,1,0:T(8,128)S(1)}, u32[]{:S(2)}, u32[]{:S(2)}) collective-permute-start(f32[8,128,128]{2,1,0:T(8,128)S(1)} %all_to_all.36.in_ref), channel_id=1, source_target_pairs={{0,16},{8,24},{16,0},{24,8},{1,17},{9,25},{17,1},{25,9},{2,18},{10... | collective-permute-start | bytes 1572872 | tf_op jit(solution)/shard_map/ppermute | solution.py:675
  159.0 20.9 %copy-start.13 = (f32[8,48,128]{2,1,0:T(8,128)S(1)}, f32[8,48,128]{2,1,0:T(8,128)}, u32[]{:S(2)}) copy-start(f32[8,48,128]{2,1,0:T(8,128)} %copy-done.12) | copy-start | bytes 589828
  160.4 0.8 copy-start.6
  161.2 2.6 %collective-permute-start.3 = (f32[1024,128]{1,0:T(8,128)S(1)}, f32[1024,128]{1,0:T(8,128)S(1)}, u32[]{:S(2)}, u32[]{:S(2)}) collective-permute-start(f32[1024,128]{1,0:T(8,128)S(1)} %get-tuple-element.57), channel_id=1, source_target_pairs={{0,8},{8,0},{16,24},{24,16},{1,9},{9,1},{17,25},{25,17},{2,10},{10... | collective-permute-start | bytes 1572872 | tf_op jit(solution)/shard_map/ppermute | solution.py:675
  162.5 0.8 copy-start.7
  163.3 2.0 collective-permute-start.4
  163.8 1.5 copy-start.17
  165.3 0.8 copy-start.18
  179.6 2.9 %collective-permute-start.5 = (f32[2,8,4,32,128]{4,3,2,1,0:T(8,128)}, f32[2,8,4,32,128]{4,3,2,1,0:T(8,128)S(1)}, u32[]{:S(2)}, u32[]{:S(2)}) collective-permute-start(f32[2,8,4,32,128]{4,3,2,1,0:T(8,128)} %get-tuple-element.64), channel_id=1, source_target_pairs={{0,8},{8,0},{16,24},{24,16},{1,9},{9,1},{17,25},{25,17},{2,10},{10... | collective-permute-start | bytes 3145736 | tf_op jit(solution)/shard_map/ppermute | solution.py:675
  182.4 1.2 copy-start
  183.7 11.0 %copy-start.1 = (f32[2,8,4,32,128]{4,3,2,1,0:T(8,128)S(1)}, f32[2,8,4,32,128]{4,3,2,1,0:T(8,128)}, u32[]{:S(2)}) copy-start(f32[2,8,4,32,128]{4,3,2,1,0:T(8,128)} %get-tuple-element.63) | copy-start | bytes 3145732
  184.5 14.3 %collective-permute-start.6 = (f32[8,128,128]{2,1,0:T(8,128)S(1)}, f32[8,128,128]{2,1,0:T(8,128)S(1)}, u32[]{:S(2)}, u32[]{:S(2)}) collective-permute-start(f32[8,128,128]{2,1,0:T(8,128)S(1)} %x_forward.6), channel_id=1, source_target_pairs={{0,16},{8,24},{16,0},{24,8},{1,17},{9,25},{17,1},{25,9},{2,18},{10... | collective-permute-start | bytes 1572872 | tf_op jit(solution)/shard_map/ppermute | solution.py:675
  186.3 46.0 %copy-start.4 = (bf16[2048,512]{1,0:T(8,128)(2,1)S(1)}, bf16[2048,512]{1,0:T(8,128)(2,1)}, u32[]{:S(2)}) copy-start(bf16[2048,512]{1,0:T(8,128)(2,1)} %constant.156.clone.lo_ref) | copy-start | bytes 6291460
  186.3 46.0 %copy-start.10 = (bf16[128,96]{1,0:T(8,128)(2,1)S(1)}, bf16[128,96]{1,0:T(8,128)(2,1)}, u32[]{:S(2)}) copy-start(bf16[128,96]{1,0:T(8,128)(2,1)} %constant.150.clone.inv_ref) | copy-start | bytes 73732
  194.7 37.6 %copy-start.3 = (f32[8,64,128]{2,1,0:T(8,128)S(1)}, f32[8,64,128]{2,1,0:T(8,128)}, u32[]{:S(2)}) copy-start(f32[8,64,128]{2,1,0:T(8,128)} %readout.1) | copy-start | bytes 786436
  194.7 37.6 %copy-start.5 = (bf16[2048,512]{1,0:T(8,128)(2,1)S(1)}, bf16[2048,512]{1,0:T(8,128)(2,1)}, u32[]{:S(2)}) copy-start(bf16[2048,512]{1,0:T(8,128)(2,1)} %constant.155.clone.hi_ref) | copy-start | bytes 6291460
  217.2 37.4 %copy-start.14 = (s32[128]{0:T(128)S(1)}, s32[128]{0:T(128)}, u32[]{:S(2)}) copy-start(s32[128]{0:T(128)} %get-tuple-element.39) | copy-start | bytes 1540
  217.2 3.4 %collective-permute-start.9 = (f32[4,1024]{1,0:T(4,128)S(1)}, f32[4,1024]{1,0:T(4,128)S(1)}, u32[]{:S(2)}, u32[]{:S(2)}) collective-permute-start(f32[4,1024]{1,0:T(4,128)S(1)} %y_last.1), channel_id=1, source_target_pairs={{0,24},{8,16},{16,8},{24,0},{1,25},{9,17},{17,9},{25,1},{2,26},{10... | collective-permute-start | bytes 49160 | tf_op jit(solution)/shard_map/ppermute | solution.py:675
  217.3 3.8 %collective-permute-start.8 = (f32[4,1024]{1,0:T(4,128)S(1)}, f32[4,1024]{1,0:T(4,128)S(1)}, u32[]{:S(2)}, u32[]{:S(2)}) collective-permute-start(f32[4,1024]{1,0:T(4,128)S(1)} %y_last.1), channel_id=1, source_target_pairs={{0,16},{8,24},{16,0},{24,8},{1,17},{9,25},{17,1},{25,9},{2,18},{10... | collective-permute-start | bytes 49160 | tf_op jit(solution)/shard_map/ppermute | solution.py:675
  218.8 2.3 collective-permute-start.7

commit v9 on v8

--- a/solution.py
+++ b/solution.py
@@ -15,6 +15,7 @@
 F32 = jnp.float32
 VM = pl.BlockSpec(memory_space=pltpu.VMEM)
 SM = pl.BlockSpec(memory_space=pltpu.SMEM)
+ANY = pl.BlockSpec(memory_space=pl.ANY)
 MIB = 1024 * 1024
 
 
@@ -158,9 +159,17 @@
     return jnp.where(lane < width // 2, first, -first).astype(F32)
 
 
-def pack_kernel(s, caps, brick_ref, count_ref, pos_ref, feat_ref, area_ref, *refs):
-    out_refs, (slot_ref, fill_ref, feat_out, pos_out) = refs[: len(caps)], refs[len(caps) :]
+def pack_kernel(
+    s, caps, brick_ref, count_ref, pos_ref, feat_hbm, area_ref, early_ref, late_ref, slot_ref,
+    fill_ref, feat_ref, feat_out, pos_out, in_sems, out_sems
+):
     blocks = brick_ref.shape[0]
+    pieces = in_sems.shape[0]
+    fetches = []
+    for i in range(pieces):
+        lanes = pl.ds(i * (blocks // pieces) * 128, blocks // pieces * 128)
+        fetches.append(pltpu.make_async_copy(feat_hbm.at[:, lanes], feat_ref.at[:, lanes], in_sems.at[i]))
+        fetches[-1].start()
     C, cap = s.C, sum(caps)
     for i in range(s.ny):
         fill_ref[i] = 0
@@ -182,14 +191,21 @@
             pos_out[dest, d, pl.ds(order, 1), :] = points[d : d + 1, :]
         return carry
 
-    lax.fori_loop(0, blocks, place, 0, unroll=8)
-    early_ref, late_ref = out_refs
+    for i, fetch in enumerate(fetches):
+        fetch.wait()
+        lax.fori_loop(i * (blocks // pieces), (i + 1) * (blocks // pieces), place, 0, unroll=8)
     at = caps[0] * C
+    copies = []
     for i in range(s.ny):
-        early_ref[i, :at] = feat_out[i, :at]
-        late_ref[i] = feat_out[i, at:]
+        pairs = [(feat_out.at[i, pl.ds(0, at)], early_ref.at[i, pl.ds(0, at)])]
+        pairs.append((feat_out.at[i, pl.ds(at, caps[1] * C)], late_ref.at[i]))
         for d in range(3):
-            early_ref[i, at + d * cap : at + (d + 1) * cap] = pos_out[i, d]
+            pairs.append((pos_out.at[i, d], early_ref.at[i, pl.ds(at + d * cap, cap)]))
+        for k, (src, dst) in enumerate(pairs):
+            copies.append(pltpu.make_async_copy(src, dst, out_sems.at[i, k]))
+            copies[-1].start()
+    for copy in copies:
+        copy.wait()
 
 
 def field_kernel(s, sdf_ref, gain_ref, out_ref):
@@ -544,7 +560,7 @@
     cap = blocks // ny
     PB = positions.shape[1] // blocks
     C, G, M, L = s.C, s.G, s.M, s.L
-    large = cap * 5 // 16 * 2
+    large = cap * 11 // 16
     caps = (large, cap - large)
 
     *outgoing, slot_of = call(
@@ -555,14 +571,17 @@
             shape(ny, caps[1] * C, PB),
             jax.ShapeDtypeStruct((blocks,), jnp.int32),
         ),
-        [SM, SM, VM, VM, VM],
-        (VM, VM, SM),
+        [SM, SM, VM, ANY, VM],
+        (ANY, ANY, SM),
         1e6,
         6e6,
         scratch=[
             pltpu.SMEM((ny + 1,), jnp.int32),
+            pltpu.VMEM(point_feat.shape, F32),
             pltpu.VMEM((ny + 1, cap * C, PB), F32),
             pltpu.VMEM((ny + 1, 3, cap, PB), F32),
+            pltpu.SemaphoreType.DMA((4,)),
+            pltpu.SemaphoreType.DMA((ny, 5)),
         ],
     )(block_brick, block_count, positions, point_feat, area.reshape(blocks, PB))
     early = lax.all_to_all(outgoing[0], "gy", split_axis=0, concat_axis=0, tiled=True)

time: 257 us -> 261 us (1.016)
  Pallas kernels: 104 us -> 94.5 us
  blocking collectives: 74.3 us -> 80.7 us
  starting transfers between devices: 16.6 us -> 22.9 us
  waiting for transfers between devices: 28.9 us -> 34.4 us
  other arithmetic: 10.1 us -> 5.78 us
    all_to_all x1, waiting for transfers between devices: 3.78 us -> 10.6 us  [per_device(): lax.all_to_all(outgoing[0], 'gy', split_axis=0, concat_axis=0, tiled=True)]
    ppermute x10, starting transfers between devices: 5.09 us -> 11.5 us  [exchange(): return lax.ppermute(array, 'gx', [(i, i ^ distance) for i in range(nx)])]
    pallas_call x1, Pallas kernels: 16.7 us -> 11.7 us  [per_device(): call(functools.partial(encode_last_kernel, s, caps), 'encode_last', (grid...]
    all_to_all x1, blocking collectives: 9.29 us -> 13.8 us  [per_device(): lax.all_to_all(values.reshape(ny, cap, PB), 'gy', split_axis=0, concat_ax...]
    pallas_call x1, Pallas kernels: 13 us -> 8.59 us  [per_device(): call(functools.partial(decode_kernel, s), 'decode', shape(ny * cap, PB),...]
  transfers between devices with their start and end apart: 12 -> 12, of which waited for: 8 -> 8; matrix products, arithmetic and copies ran while one was open for 10% -> 8% of each run, Pallas kernels for 20% -> 19%
where the time goes in v9:
time: 261 us; the launch traced here: 260 us
  Pallas kernels  94.5 us (36%)
  blocking collectives  80.7 us (31%)
  waiting for transfers between devices  34.4 us (13%)
  starting transfers between devices  22.9 us (9%)
  local copies, waits for them, and re-layouts  19.9 us (8%)
  other arithmetic  5.78 us (2%)
    all_to_all x2, blocking collectives, to_modes(): spec = lax.all_to_all(spec, 'gy', split_axis=0, concat_axis=0, tiled=True)  38.4 us
    ppermute x10, waiting for transfers between devices, exchange(): return lax.ppermute(array, 'gx', [(i, i ^ distance) for i in range(nx)])  23.8 us
    pallas_call x1, Pallas kernels, per_device(): call(functools.partial(encode_first_kernel, s, caps), 'encode_first', gri...  18.9 us
    all_to_all x1, blocking collectives, per_device(): lax.all_to_all(spec.reshape(ny, s.LY, s.LK), 'gy', split_axis=0, concat_a...  17.4 us
    all_to_all x1, blocking collectives, per_device(): lax.all_to_all(values.reshape(ny, cap, PB), 'gy', split_axis=0, concat_ax...  13.8 us
    pallas_call x1, Pallas kernels, per_device(): call(functools.partial(layer_kernel, s), 'layer', (grid_shape, spec_shape...  13.4 us
    pallas_call x1, Pallas kernels, per_device(): call(functools.partial(encode_last_kernel, s, caps), 'encode_last', (grid...  11.7 us
    ppermute x10, starting transfers between devices, exchange(): return lax.ppermute(array, 'gx', [(i, i ^ distance) for i in range(nx)])  11.5 us
  transfers between devices with their start and end apart: 12, of which 8 were waited for; matrix products, arithmetic and copies ran while one was open for 8% of the time, Pallas kernels for 19%

profile of v9, /device:TPU:0, one launch (start us, length us, event | category | flops | bytes accessed | tf_op | source)
XLA Modules:
  0.0 260.2 jit_solution(12789681541665667002)
XLA Ops:
  0.7 6.8 %pack.1 = (f32[8,400,128]{2,1,0:T(8,128)}, f32[8,160,128]{2,1,0:T(8,128)}, s32[128]{0:T(128)}) custom-call(s32[128]{0:T(128)} %brick_ref.1, s32[1]{0:T(128)S(6)} %copy.37.count_ref, f32[3,16384]{1,0:T(4,128)} %pos_ref.1, f32[32,16384]{1,0:T(8,128)} %feat_hbm.1, f32[128,128]{1,0:T(8,128)} %bitcast.85), custom_call_target="tpu_custom_call" | custom-call | flops 1000000 | bytes 6000000 | tf_op jit(solution)/shard_map/pack/pallas_call | solution.py:566
  7.5 7.3 %all-to-all-start = ((f32[8,400,128]{2,1,0:T(8,128)}), f32[8,400,128]{2,1,0:T(8,128)S(1)}, u32[]{:S(2)}, u32[]{:S(2)}) async-start(f32[8,400,128]{2,1,0:T(8,128)} %get-tuple-element.40), calls=%async_computation | async-start | bytes 3276800 | tf_op jit(solution)/shard_map/all_to_all | solution.py:587
  15.5 0.8 fusion.1
  18.0 1.0 fusion.13
  21.0 1.0 copy.30
  22.0 1.5 reshape.476.u_ref
  26.6 1.2 broadcast_in_dim.97
  27.8 2.3 reshape.471
  30.8 0.9 dynamic-slice_bitcast_fusion.1.table_ref
  31.6 0.9 dynamic-slice_bitcast_fusion.table_ref
  32.7 0.7 compare_select_fusion
  33.5 0.8 bitcast_select_fusion.gain_ref
  34.3 8.2 %field.1.init_ref = f32[8,16,128,128]{3,2,1,0:T(8,128)} custom-call(f32[4,8,16,128]{3,2,1,0:T(8,128)} %bitcast.88, f32[64,2048]{1,0:T(8,128)} %bitcast_select_fusion.gain_ref), custom_call_target="tpu_custom_call" | custom-call | flops 3000000000 | bytes 10000000 | tf_op jit(solution)/shard_map/field/pallas_call | solution.py:616
  42.6 10.6 %all-to-all-done.in_ref = f32[8,400,128]{2,1,0:T(8,128)S(1)} async-done(((f32[8,400,128]{2,1,0:T(8,128)}), f32[8,400,128]{2,1,0:T(8,128)S(1)}, u32[]{:S(2)}, u32[]{:S(2)}) %all-to-all-start) | async-done | bytes 1638432 | tf_op jit(solution)/shard_map/all_to_all | solution.py:587
  53.2 4.2 %all-to-all-start.1 = ((f32[8,160,128]{2,1,0:T(8,128)}), f32[8,160,128]{2,1,0:T(8,128)}, u32[]{:S(2)}, u32[]{:S(2)}) async-start(f32[8,160,128]{2,1,0:T(8,128)} %get-tuple-element.44), calls=%async_computation.1 | async-start | bytes 1310720 | tf_op jit(solution)/shard_map/all_to_all | solution.py:661
  58.5 18.9 %encode_first.1.before_ref = f32[8,16,128,128]{3,2,1,0:T(8,128)} custom-call(s32[8,128]{1,0:T(8,128)} %concatenate.23.id_ref, f32[8,400,128]{2,1,0:T(8,128)} %copy-done.11, f32[8,16,128,128]{3,2,1,0:T(8,128)} %field.1.init_ref), custom_call_target="tpu_custom_call" | custom-call | flops 3000000000 | bytes 20000000 | tf_op jit(solution)/shard_map/encode_first/pallas_call | solution.py:666
  77.4 11.7 %encode_last.1 = (f32[8,16,128,128]{3,2,1,0:T(8,128)}, f32[2,8,4,32,128]{4,3,2,1,0:T(8,128)}, f32[2,8,4,32,128]{4,3,2,1,0:T(8,128)}) custom-call(s32[1]{0:T(128)} %bitcast.12.row_ref, s32[8,128]{1,0:T(8,128)} %concatenate.23.id_ref, f32[8,160,128]{2,1,0:T(8,128)} %all-to-all-done.1.in_ref, f32[8,48,128]{2,1,0:T(8,128)} %copy-done.12, ...), custom_call_target="tpu_custom_call" | custom-call | flops 4000000000 | bytes 22000000 | tf_op jit(solution)/shard_map/encode_last/pallas_call | solution.py:676
  89.3 2.9 %collective-permute-done = f32[2,8,4,32,128]{4,3,2,1,0:T(8,128)S(1)} collective-permute-done((f32[2,8,4,32,128]{4,3,2,1,0:T(8,128)}, f32[2,8,4,32,128]{4,3,2,1,0:T(8,128)S(1)}, u32[]{:S(2)}, u32[]{:S(2)}) %collective-permute-start) | collective-permute-done | bytes 1048608 | tf_op jit(solution)/shard_map/ppermute | solution.py:694
  92.1 1.2 copy-done.2
  93.3 0.9 x_forward.5
  94.2 6.5 %collective-permute-start.1 = (f32[8,128,128]{2,1,0:T(8,128)S(1)}, f32[8,128,128]{2,1,0:T(8,128)S(1)}, u32[]{:S(2)}, u32[]{:S(2)}) collective-permute-start(f32[8,128,128]{2,1,0:T(8,128)S(1)} %x_forward.5), channel_id=1, source_target_pairs={{0,16},{8,24},{16,0},{24,8},{1,17},{9,25},{17,1},{25,9},{2,18},{10... | collective-permute-start | bytes 1572872 | tf_op jit(solution)/shard_map/ppermute | solution.py:694
  100.7 0.9 x_forward.4
  101.6 11.6 %collective-permute-done.1 = f32[8,128,128]{2,1,0:T(8,128)S(1)} collective-permute-done((f32[8,128,128]{2,1,0:T(8,128)S(1)}, f32[8,128,128]{2,1,0:T(8,128)S(1)}, u32[]{:S(2)}, u32[]{:S(2)}) %collective-permute-start.1) | collective-permute-done | bytes 524320 | tf_op jit(solution)/shard_map/ppermute | solution.py:694
  113.3 20.8 %all_to_all.35 = f32[8,128,128]{2,1,0:T(8,128)S(1)} all-to-all(f32[8,128,128]{2,1,0:T(8,128)S(1)} %add.168), channel_id=1, replica_groups=mesh['gx'=4,'gy'=8] {'gy'}, dimensions={0} | all-to-all | bytes 1048576 | tf_op jit(solution)/shard_map/all_to_all | solution.py:720
  134.1 1.0 y_both.1
  135.2 17.4 %all_to_all.36.in_ref = f32[8,128,128]{2,1,0:T(8,128)S(1)} all-to-all(f32[8,128,128]{2,1,0:T(8,128)S(1)} %bitcast.73), channel_id=1, replica_groups=mesh['gx'=4,'gy'=8] {'gy'}, dimensions={0} | all-to-all | bytes 1048576 | tf_op jit(solution)/shard_map/all_to_all | solution.py:737
  153.3 10.6 %mix.1.mixed_ref = f32[8,16,128,128]{3,2,1,0:T(8,128)} custom-call(f32[8,16,128,128]{3,2,1,0:T(8,128)} %get-tuple-element.46.grid_ref, f32[128,128]{1,0:T(8,128)} %get-tuple-element.47.mix_ref, f32[1,128]{1,0:T(1,128)} %reshape.472.bias_ref), custom_call_target="tpu_custom_call" | custom-call | flops 2000000000 | bytes 17000000 | tf_op jit(solution)/shard_map/mix/pallas_call | solution.py:724
  163.9 1.3 x_inverse.2
  165.3 0.8 copy-done.6
  166.1 1.3 x_inverse.3
  167.4 0.8 copy-done.7
  168.7 1.5 collective-permute-done.4
  170.3 0.8 copy-done.19
  171.1 13.4 %layer.1 = (f32[8,16,128,128]{3,2,1,0:T(8,128)}, f32[2,8,4,32,128]{4,3,2,1,0:T(8,128)}, f32[2,8,4,32,128]{4,3,2,1,0:T(8,128)}) custom-call(s32[1]{0:T(128)} %bitcast.12.row_ref, f32[8,16,128,128]{3,2,1,0:T(8,128)} %mix.1.mixed_ref, bf16[128,96]{1,0:T(8,128)(2,1)} %constant.149.clone.inv_ref, bf16[64,256]{1,0:T(8,128)(2,1)} %constant.148.clone.table_ref.fwd_ref, ...), custom_call_target="tpu_custom_call" | custom-call | flops 4000000000 | bytes 21000000 | tf_op jit(solution)/shard_map/layer/pallas_call | solution.py:757
  184.9 2.5 collective-permute-done.5
  187.3 1.2 copy-done
  188.6 0.9 x_forward.6
  189.5 1.4 collective-permute-start.6
  191.0 8.4 %readout.1 = f32[8,64,128]{2,1,0:T(8,128)} custom-call(f32[8,16,128,128]{3,2,1,0:T(8,128)} %get-tuple-element.61.grid_ref, f32[128,128]{1,0:T(8,128)} %get-tuple-element.62.mix_ref), custom_call_target="tpu_custom_call" | custom-call | flops 2000000000 | bytes 9000000 | tf_op jit(solution)/shard_map/readout/pallas_call | solution.py:770
  199.4 0.9 x_forward.7
  200.3 3.5 %collective-permute-done.6 = f32[8,128,128]{2,1,0:T(8,128)S(1)} collective-permute-done((f32[8,128,128]{2,1,0:T(8,128)S(1)}, f32[8,128,128]{2,1,0:T(8,128)S(1)}, u32[]{:S(2)}, u32[]{:S(2)}) %collective-permute-start.6) | collective-permute-done | bytes 524320 | tf_op jit(solution)/shard_map/ppermute | solution.py:694
  203.8 17.6 %all_to_all.37 = f32[8,128,128]{2,1,0:T(8,128)S(1)} all-to-all(f32[8,128,128]{2,1,0:T(8,128)S(1)} %add.169), channel_id=1, replica_groups=mesh['gx'=4,'gy'=8] {'gy'}, dimensions={0} | all-to-all | bytes 1048576 | tf_op jit(solution)/shard_map/all_to_all | solution.py:720
  222.1 1.4 collective-permute-start.8
  224.0 1.3 collective-permute-done.9
  226.0 11.0 %all_to_all.38.spec_ref = f32[8,4,1024]{2,1,0:T(4,128)S(1)} all-to-all(f32[8,4,1024]{2,1,0:T(4,128)S(1)} %broadcast_in_dim.105), channel_id=1, replica_groups=mesh['gx'=4,'gy'=8] {'gy'}, dimensions={0} | all-to-all | bytes 262144 | tf_op jit(solution)/shard_map/all_to_all | solution.py:794
  237.0 8.6 %decode.1 = f32[128,128]{1,0:T(8,128)S(1)} custom-call(s32[3,128]{1,0:T(4,128)S(1)} %pad_add_fusion.id_ref, f32[1]{0:T(128)} %bitcast.6.base_ref, f32[3,128,128]{2,1,0:T(8,128)S(1)} %bitcast_subtract_fusion.point_ref, f32[8,4,1024]{2,1,0:T(4,128)S(1)} %all_to_all.38.spec_ref, f32[2,1024]{1,0:T(2,128)S(1)} %pad_maximum_fusion.4.turn_ref, ...), custom_call_target="tpu_custom_call" | custom-call | flops 4000000000 | bytes 6000000 | tf_op jit(solution)/shard_map/decode/pallas_call | solution.py:795
  245.6 13.8 %all_to_all.39 = f32[8,16,128]{2,1,0:T(8,128)S(1)} all-to-all(f32[8,16,128]{2,1,0:T(8,128)S(1)} %bitcast.76), channel_id=1, replica_groups=mesh['gx'=4,'gy'=8] {'gy'}, dimensions={0} | all-to-all | bytes 131072 | tf_op jit(solution)/shard_map/all_to_all | solution.py:806
  259.4 0.9 convolution_bitcast_fusion
  (108 shorter events, 13.2 us)
Async XLA Ops:
  0.0 19.5 %copy-start.20 = (f32[2,32]{1,0:T(2,128)S(1)}, f32[2,32]{1,0:T(2,128)}, u32[]{:S(2)}) copy-start(f32[2,32]{1,0:T(2,128)} %param.30) | copy-start | bytes 772
  0.0 19.7 %copy-start.15 = (f32[32]{0:T(128)S(1)}, f32[32]{0:T(128)}, u32[]{:S(2)}) copy-start(f32[32]{0:T(128)} %param.28) | copy-start | bytes 388
  7.5 45.7 %all-to-all-start = ((f32[8,400,128]{2,1,0:T(8,128)}), f32[8,400,128]{2,1,0:T(8,128)S(1)}, u32[]{:S(2)}, u32[]{:S(2)}) async-start(f32[8,400,128]{2,1,0:T(8,128)} %get-tuple-element.40), calls=%async_computation | async-start | bytes 3276800 | tf_op jit(solution)/shard_map/all_to_all | solution.py:587
  19.0 11.2 %copy-start.16 = (f32[32]{0:T(128)S(1)}, f32[32]{0:T(128)}, u32[]{:S(2)}) copy-start(f32[32]{0:T(128)} %param.32) | copy-start | bytes 388
  26.6 31.2 %copy-start.17 = (s32[3]{0:T(128)S(1)}, s32[3]{0:T(128)}, u32[]{:S(2)}) copy-start(s32[3]{0:T(128)} %constant.158.clone) | copy-start | bytes 40
  53.2 5.4 %copy-start.11 = (f32[8,400,128]{2,1,0:T(8,128)}, f32[8,400,128]{2,1,0:T(8,128)S(1)}, u32[]{:S(2)}) copy-start(f32[8,400,128]{2,1,0:T(8,128)S(1)} %all-to-all-done.in_ref) | copy-start | bytes 4915204
  53.2 24.3 %all-to-all-start.1 = ((f32[8,160,128]{2,1,0:T(8,128)}), f32[8,160,128]{2,1,0:T(8,128)}, u32[]{:S(2)}, u32[]{:S(2)}) async-start(f32[8,160,128]{2,1,0:T(8,128)} %get-tuple-element.44), calls=%async_computation.1 | async-start | bytes 1310720 | tf_op jit(solution)/shard_map/all_to_all | solution.py:661
  57.4 20.0 %copy-start.12 = (f32[8,48,128]{2,1,0:T(8,128)}, f32[8,48,128]{2,1,0:T(8,128)S(1)}, u32[]{:S(2)}) copy-start(f32[8,48,128]{2,1,0:T(8,128)S(1)} %slice.68.pos_ref) | copy-start | bytes 589828
  77.4 56.7 %copy-start.8 = (bf16[128,256]{1,0:T(8,128)(2,1)S(1)}, bf16[128,256]{1,0:T(8,128)(2,1)}, u32[]{:S(2)}) copy-start(bf16[128,256]{1,0:T(8,128)(2,1)} %constant.153.clone.fwd_ref) | copy-start | bytes 196612
  77.4 56.7 %copy-start.9 = (bf16[128,192]{1,0:T(8,128)(2,1)S(1)}, bf16[128,192]{1,0:T(8,128)(2,1)}, u32[]{:S(2)}) copy-start(bf16[128,192]{1,0:T(8,128)(2,1)} %constant.154.clone.inv_ref) | copy-start | bytes 147460
  89.2 2.9 %collective-permute-start = (f32[2,8,4,32,128]{4,3,2,1,0:T(8,128)}, f32[2,8,4,32,128]{4,3,2,1,0:T(8,128)S(1)}, u32[]{:S(2)}, u32[]{:S(2)}) collective-permute-start(f32[2,8,4,32,128]{4,3,2,1,0:T(8,128)} %get-tuple-element.50), channel_id=1, source_target_pairs={{0,8},{8,0},{16,24},{24,16},{1,9},{9,1},{17,25},{25,17},{2,10},{10... | collective-permute-start | bytes 3145736 | tf_op jit(solution)/shard_map/ppermute | solution.py:694
  92.1 1.2 copy-start.2
  94.2 19.0 %collective-permute-start.1 = (f32[8,128,128]{2,1,0:T(8,128)S(1)}, f32[8,128,128]{2,1,0:T(8,128)S(1)}, u32[]{:S(2)}, u32[]{:S(2)}) collective-permute-start(f32[8,128,128]{2,1,0:T(8,128)S(1)} %x_forward.5), channel_id=1, source_target_pairs={{0,16},{8,24},{16,0},{24,8},{1,17},{9,25},{17,1},{25,9},{2,18},{10... | collective-permute-start | bytes 1572872 | tf_op jit(solution)/shard_map/ppermute | solution.py:694
  152.6 13.5 %collective-permute-start.2 = (f32[8,128,128]{2,1,0:T(8,128)S(1)}, f32[8,128,128]{2,1,0:T(8,128)S(1)}, u32[]{:S(2)}, u32[]{:S(2)}) collective-permute-start(f32[8,128,128]{2,1,0:T(8,128)S(1)} %all_to_all.36.in_ref), channel_id=1, source_target_pairs={{0,16},{8,24},{16,0},{24,8},{1,17},{9,25},{17,1},{25,9},{2,18},{10... | collective-permute-start | bytes 1572872 | tf_op jit(solution)/shard_map/ppermute | solution.py:694
  163.9 20.9 %copy-start.13 = (f32[8,48,128]{2,1,0:T(8,128)S(1)}, f32[8,48,128]{2,1,0:T(8,128)}, u32[]{:S(2)}) copy-start(f32[8,48,128]{2,1,0:T(8,128)} %copy-done.12) | copy-start | bytes 589828
  165.3 0.8 copy-start.6
  166.1 2.6 %collective-permute-start.3 = (f32[1024,128]{1,0:T(8,128)S(1)}, f32[1024,128]{1,0:T(8,128)S(1)}, u32[]{:S(2)}, u32[]{:S(2)}) collective-permute-start(f32[1024,128]{1,0:T(8,128)S(1)} %get-tuple-element.57), channel_id=1, source_target_pairs={{0,8},{8,0},{16,24},{24,16},{1,9},{9,1},{17,25},{25,17},{2,10},{10... | collective-permute-start | bytes 1572872 | tf_op jit(solution)/shard_map/ppermute | solution.py:694
  167.4 0.8 copy-start.7
  168.2 2.0 collective-permute-start.4
  168.7 1.5 copy-start.18
  170.3 0.8 copy-start.19
  184.5 2.9 %collective-permute-start.5 = (f32[2,8,4,32,128]{4,3,2,1,0:T(8,128)}, f32[2,8,4,32,128]{4,3,2,1,0:T(8,128)S(1)}, u32[]{:S(2)}, u32[]{:S(2)}) collective-permute-start(f32[2,8,4,32,128]{4,3,2,1,0:T(8,128)} %get-tuple-element.64), channel_id=1, source_target_pairs={{0,8},{8,0},{16,24},{24,16},{1,9},{9,1},{17,25},{25,17},{2,10},{10... | collective-permute-start | bytes 3145736 | tf_op jit(solution)/shard_map/ppermute | solution.py:694
  187.3 1.2 copy-start
  188.6 10.8 %copy-start.1 = (f32[2,8,4,32,128]{4,3,2,1,0:T(8,128)S(1)}, f32[2,8,4,32,128]{4,3,2,1,0:T(8,128)}, u32[]{:S(2)}) copy-start(f32[2,8,4,32,128]{4,3,2,1,0:T(8,128)} %get-tuple-element.63) | copy-start | bytes 3145732
  189.5 14.3 %collective-permute-start.6 = (f32[8,128,128]{2,1,0:T(8,128)S(1)}, f32[8,128,128]{2,1,0:T(8,128)S(1)}, u32[]{:S(2)}, u32[]{:S(2)}) collective-permute-start(f32[8,128,128]{2,1,0:T(8,128)S(1)} %x_forward.6), channel_id=1, source_target_pairs={{0,16},{8,24},{16,0},{24,8},{1,17},{9,25},{17,1},{25,9},{2,18},{10... | collective-permute-start | bytes 1572872 | tf_op jit(solution)/shard_map/ppermute | solution.py:694
  191.0 46.0 %copy-start.4 = (bf16[2048,512]{1,0:T(8,128)(2,1)S(1)}, bf16[2048,512]{1,0:T(8,128)(2,1)}, u32[]{:S(2)}) copy-start(bf16[2048,512]{1,0:T(8,128)(2,1)} %constant.156.clone.lo_ref) | copy-start | bytes 6291460
  191.0 46.0 %copy-start.10 = (bf16[128,96]{1,0:T(8,128)(2,1)S(1)}, bf16[128,96]{1,0:T(8,128)(2,1)}, u32[]{:S(2)}) copy-start(bf16[128,96]{1,0:T(8,128)(2,1)} %constant.150.clone.inv_ref) | copy-start | bytes 73732
  199.4 37.6 %copy-start.3 = (f32[8,64,128]{2,1,0:T(8,128)S(1)}, f32[8,64,128]{2,1,0:T(8,128)}, u32[]{:S(2)}) copy-start(f32[8,64,128]{2,1,0:T(8,128)} %readout.1) | copy-start | bytes 786436
  199.4 37.6 %copy-start.5 = (bf16[2048,512]{1,0:T(8,128)(2,1)S(1)}, bf16[2048,512]{1,0:T(8,128)(2,1)}, u32[]{:S(2)}) copy-start(bf16[2048,512]{1,0:T(8,128)(2,1)} %constant.155.clone.hi_ref) | copy-start | bytes 6291460
  222.0 37.3 %copy-start.14 = (s32[128]{0:T(128)S(1)}, s32[128]{0:T(128)}, u32[]{:S(2)}) copy-start(s32[128]{0:T(128)} %get-tuple-element.39) | copy-start | bytes 1540
  222.0 3.3 %collective-permute-start.9 = (f32[4,1024]{1,0:T(4,128)S(1)}, f32[4,1024]{1,0:T(4,128)S(1)}, u32[]{:S(2)}, u32[]{:S(2)}) collective-permute-start(f32[4,1024]{1,0:T(4,128)S(1)} %y_last.1), channel_id=1, source_target_pairs={{0,24},{8,16},{16,8},{24,0},{1,25},{9,17},{17,9},{25,1},{2,26},{10... | collective-permute-start | bytes 49160 | tf_op jit(solution)/shard_map/ppermute | solution.py:694
  222.1 3.8 %collective-permute-start.8 = (f32[4,1024]{1,0:T(4,128)S(1)}, f32[4,1024]{1,0:T(4,128)S(1)}, u32[]{:S(2)}, u32[]{:S(2)}) collective-permute-start(f32[4,1024]{1,0:T(4,128)S(1)} %y_last.1), channel_id=1, source_target_pairs={{0,16},{8,24},{16,0},{24,8},{1,17},{9,25},{17,1},{25,9},{2,18},{10... | collective-permute-start | bytes 49160 | tf_op jit(solution)/shard_map/ppermute | solution.py:694
  223.5 2.5 collective-permute-start.7

commit v10 on v8

--- a/solution.py
+++ b/solution.py
@@ -263,7 +263,7 @@
 def add_blocks(s, caps, turn, id_ref, in_ref, pos_ref, at, grid_ref, list_ref):
     C = s.C
     cap = sum(caps)
-    step = 4
+    step = 8
     group = lax.broadcasted_iota(jnp.int32, (s.L, 128), 0) // s.cp % s.bxn
     live = live_list(lambda n: jnp.where(id_ref[7, n] == turn, 1, 0), s.ny * cap, step, list_ref)
 

time: 257 us -> 255 us (level)
  Pallas kernels: 104 us -> 93.3 us
  blocking collectives: 74.3 us -> 81.7 us
    all_to_all x2, blocking collectives: 36.4 us -> 41.4 us  [to_modes(): spec = lax.all_to_all(spec, 'gy', split_axis=0, concat_axis=0, tiled=True)]
    pallas_call x1, Pallas kernels: 16.7 us -> 11.8 us  [per_device(): call(functools.partial(encode_last_kernel, s, caps), 'encode_last', (grid...]
    pallas_call x1, Pallas kernels: 13 us -> 9.22 us  [per_device(): call(functools.partial(decode_kernel, s), 'decode', shape(ny * cap, PB),...]
    all_to_all x1, blocking collectives: 9.29 us -> 12 us  [per_device(): lax.all_to_all(values.reshape(ny, cap, PB), 'gy', split_axis=0, concat_ax...]
  transfers between devices with their start and end apart: 12 -> 12, of which waited for: 8 -> 9; matrix products, arithmetic and copies ran while one was open for 10% -> 10% of each run, Pallas kernels for 20% -> 20%
where the time goes in v10:
time: 255 us; the launch traced here: 254 us
  Pallas kernels  93.3 us (37%)
  blocking collectives  81.7 us (32%)
  waiting for transfers between devices  28.8 us (11%)
  local copies, waits for them, and re-layouts  19.6 us (8%)
  starting transfers between devices  18.1 us (7%)
  other arithmetic  10.1 us (4%)
    all_to_all x2, blocking collectives, to_modes(): spec = lax.all_to_all(spec, 'gy', split_axis=0, concat_axis=0, tiled=True)  41.4 us
    ppermute x10, waiting for transfers between devices, exchange(): return lax.ppermute(array, 'gx', [(i, i ^ distance) for i in range(nx)])  24.4 us
    pallas_call x1, Pallas kernels, per_device(): call(functools.partial(encode_first_kernel, s, caps), 'encode_first', gri...  18.1 us
    all_to_all x1, blocking collectives, per_device(): lax.all_to_all(spec.reshape(ny, s.LY, s.LK), 'gy', split_axis=0, concat_a...  17.6 us
    pallas_call x1, Pallas kernels, per_device(): call(functools.partial(layer_kernel, s), 'layer', (grid_shape, spec_shape...  13.4 us
    all_to_all x1, blocking collectives, per_device(): lax.all_to_all(values.reshape(ny, cap, PB), 'gy', split_axis=0, concat_ax...  12 us
    pallas_call x1, Pallas kernels, per_device(): call(functools.partial(encode_last_kernel, s, caps), 'encode_last', (grid...  11.8 us
    all_to_all x1, blocking collectives, per_device(): last = lax.all_to_all(last, 'gy', split_axis=0, concat_axis=0, tiled=True)  10.8 us
  transfers between devices with their start and end apart: 12, of which 9 were waited for; matrix products, arithmetic and copies ran while one was open for 10% of the time, Pallas kernels for 20%

profile of v10, /device:TPU:0, one launch (start us, length us, event | category | flops | bytes accessed | tf_op | source)
XLA Modules:
  0.0 253.5 jit_solution(1140446187850154745)
XLA Ops:
  0.7 5.7 %pack.1 = (f32[8,368,128]{2,1,0:T(8,128)}, f32[8,192,128]{2,1,0:T(8,128)}, s32[128]{0:T(128)}) custom-call(s32[128]{0:T(128)} %brick_ref.1, s32[1]{0:T(128)S(6)} %copy.37.count_ref, f32[3,16384]{1,0:T(4,128)} %pos_ref.1, f32[32,16384]{1,0:T(8,128)} %feat_ref.1, f32[128,128]{1,0:T(8,128)} %bitcast.85), custom_call_target="tpu_custom_call" | custom-call | flops 1000000 | bytes 6000000 | tf_op jit(solution)/shard_map/pack/pallas_call | solution.py:550
  6.4 7.3 %all-to-all-start = ((f32[8,368,128]{2,1,0:T(8,128)}), f32[8,368,128]{2,1,0:T(8,128)S(1)}, u32[]{:S(2)}, u32[]{:S(2)}) async-start(f32[8,368,128]{2,1,0:T(8,128)} %get-tuple-element.40), calls=%async_computation | async-start | bytes 3014656 | tf_op jit(solution)/shard_map/all_to_all | solution.py:568
  14.4 0.8 fusion.1
  16.9 1.0 fusion.13
  19.5 1.2 slice_negate_fusion.1
  20.7 1.1 pad_maximum_fusion.2
  25.4 1.7 pad_maximum_fusion
  27.9 2.1 broadcast_in_dim.97
  30.0 2.3 reshape.471
  32.4 1.3 fusion.8
  33.7 0.9 dynamic-slice_bitcast_fusion.1.table_ref
  34.6 0.9 dynamic-slice_bitcast_fusion.table_ref
  36.4 0.8 bitcast_select_fusion.gain_ref
  37.3 8.3 %field.1.init_ref = f32[8,16,128,128]{3,2,1,0:T(8,128)} custom-call(f32[4,8,16,128]{3,2,1,0:T(8,128)} %bitcast.88, f32[64,2048]{1,0:T(8,128)} %bitcast_select_fusion.gain_ref), custom_call_target="tpu_custom_call" | custom-call | flops 3000000000 | bytes 10000000 | tf_op jit(solution)/shard_map/field/pallas_call | solution.py:597
  45.5 3.8 %all-to-all-done.in_ref = f32[8,368,128]{2,1,0:T(8,128)S(1)} async-done(((f32[8,368,128]{2,1,0:T(8,128)}), f32[8,368,128]{2,1,0:T(8,128)S(1)}, u32[]{:S(2)}, u32[]{:S(2)}) %all-to-all-start) | async-done | bytes 1507360 | tf_op jit(solution)/shard_map/all_to_all | solution.py:568
  49.3 4.2 %all-to-all-start.1 = ((f32[8,192,128]{2,1,0:T(8,128)}), f32[8,192,128]{2,1,0:T(8,128)}, u32[]{:S(2)}, u32[]{:S(2)}) async-start(f32[8,192,128]{2,1,0:T(8,128)} %get-tuple-element.44), calls=%async_computation.1 | async-start | bytes 1572864 | tf_op jit(solution)/shard_map/all_to_all | solution.py:642
  54.7 18.1 %encode_first.1.before_ref = f32[8,16,128,128]{3,2,1,0:T(8,128)} custom-call(s32[8,128]{1,0:T(8,128)} %concatenate.23.id_ref, f32[8,368,128]{2,1,0:T(8,128)} %copy-done.11, f32[8,16,128,128]{3,2,1,0:T(8,128)} %field.1.init_ref), custom_call_target="tpu_custom_call" | custom-call | flops 3000000000 | bytes 20000000 | tf_op jit(solution)/shard_map/encode_first/pallas_call | solution.py:647
  73.5 11.8 %encode_last.1 = (f32[8,16,128,128]{3,2,1,0:T(8,128)}, f32[2,8,4,32,128]{4,3,2,1,0:T(8,128)}, f32[2,8,4,32,128]{4,3,2,1,0:T(8,128)}) custom-call(s32[1]{0:T(128)} %bitcast.12.row_ref, s32[8,128]{1,0:T(8,128)} %concatenate.23.id_ref, f32[8,192,128]{2,1,0:T(8,128)} %all-to-all-done.1.in_ref, f32[8,48,128]{2,1,0:T(8,128)} %copy-done.12, ...), custom_call_target="tpu_custom_call" | custom-call | flops 4000000000 | bytes 22000000 | tf_op jit(solution)/shard_map/encode_last/pallas_call | solution.py:657
  85.3 2.9 %collective-permute-done = f32[2,8,4,32,128]{4,3,2,1,0:T(8,128)S(1)} collective-permute-done((f32[2,8,4,32,128]{4,3,2,1,0:T(8,128)}, f32[2,8,4,32,128]{4,3,2,1,0:T(8,128)S(1)}, u32[]{:S(2)}, u32[]{:S(2)}) %collective-permute-start) | collective-permute-done | bytes 1048608 | tf_op jit(solution)/shard_map/ppermute | solution.py:675
  88.2 1.2 copy-done.2
  89.4 0.9 x_forward.5
  90.3 1.6 collective-permute-start.1
  91.9 0.9 x_forward.4
  92.8 11.5 %collective-permute-done.1 = f32[8,128,128]{2,1,0:T(8,128)S(1)} collective-permute-done((f32[8,128,128]{2,1,0:T(8,128)S(1)}, f32[8,128,128]{2,1,0:T(8,128)S(1)}, u32[]{:S(2)}, u32[]{:S(2)}) %collective-permute-start.1) | collective-permute-done | bytes 524320 | tf_op jit(solution)/shard_map/ppermute | solution.py:675
  104.4 23.7 %all_to_all.35 = f32[8,128,128]{2,1,0:T(8,128)S(1)} all-to-all(f32[8,128,128]{2,1,0:T(8,128)S(1)} %add.168), channel_id=1, replica_groups=mesh['gx'=4,'gy'=8] {'gy'}, dimensions={0} | all-to-all | bytes 1048576 | tf_op jit(solution)/shard_map/all_to_all | solution.py:701
  128.1 1.0 y_both.1
  129.2 17.6 %all_to_all.36.in_ref = f32[8,128,128]{2,1,0:T(8,128)S(1)} all-to-all(f32[8,128,128]{2,1,0:T(8,128)S(1)} %bitcast.73), channel_id=1, replica_groups=mesh['gx'=4,'gy'=8] {'gy'}, dimensions={0} | all-to-all | bytes 1048576 | tf_op jit(solution)/shard_map/all_to_all | solution.py:718
  146.7 1.3 collective-permute-start.2
  148.0 10.6 %mix.1.mixed_ref = f32[8,16,128,128]{3,2,1,0:T(8,128)} custom-call(f32[8,16,128,128]{3,2,1,0:T(8,128)} %get-tuple-element.46.grid_ref, f32[128,128]{1,0:T(8,128)} %get-tuple-element.47.mix_ref, f32[1,128]{1,0:T(1,128)} %reshape.472.bias_ref), custom_call_target="tpu_custom_call" | custom-call | flops 2000000000 | bytes 17000000 | tf_op jit(solution)/shard_map/mix/pallas_call | solution.py:705
  158.6 1.3 x_inverse.2
  160.8 1.3 x_inverse.3
  163.4 1.5 collective-permute-done.4
  164.9 0.8 copy-done.18
  165.7 13.4 %layer.1 = (f32[8,16,128,128]{3,2,1,0:T(8,128)}, f32[2,8,4,32,128]{4,3,2,1,0:T(8,128)}, f32[2,8,4,32,128]{4,3,2,1,0:T(8,128)}) custom-call(s32[1]{0:T(128)} %bitcast.12.row_ref, f32[8,16,128,128]{3,2,1,0:T(8,128)} %mix.1.mixed_ref, bf16[128,96]{1,0:T(8,128)(2,1)} %constant.149.clone.inv_ref, bf16[64,256]{1,0:T(8,128)(2,1)} %constant.148.clone.table_ref.fwd_ref, ...), custom_call_target="tpu_custom_call" | custom-call | flops 4000000000 | bytes 21000000 | tf_op jit(solution)/shard_map/layer/pallas_call | solution.py:738
  179.5 2.5 collective-permute-done.5
  182.0 1.2 copy-done
  183.2 0.9 x_forward.6
  184.1 0.8 collective-permute-start.6
  185.1 8.4 %readout.1 = f32[8,64,128]{2,1,0:T(8,128)} custom-call(f32[8,16,128,128]{3,2,1,0:T(8,128)} %get-tuple-element.61.grid_ref, f32[128,128]{1,0:T(8,128)} %get-tuple-element.62.mix_ref), custom_call_target="tpu_custom_call" | custom-call | flops 2000000000 | bytes 9000000 | tf_op jit(solution)/shard_map/readout/pallas_call | solution.py:751
  193.5 0.9 x_forward.7
  194.4 4.0 %collective-permute-done.6 = f32[8,128,128]{2,1,0:T(8,128)S(1)} collective-permute-done((f32[8,128,128]{2,1,0:T(8,128)S(1)}, f32[8,128,128]{2,1,0:T(8,128)S(1)}, u32[]{:S(2)}, u32[]{:S(2)}) %collective-permute-start.6) | collective-permute-done | bytes 524320 | tf_op jit(solution)/shard_map/ppermute | solution.py:675
  198.5 17.6 %all_to_all.37 = f32[8,128,128]{2,1,0:T(8,128)S(1)} all-to-all(f32[8,128,128]{2,1,0:T(8,128)S(1)} %add.169), channel_id=1, replica_groups=mesh['gx'=4,'gy'=8] {'gy'}, dimensions={0} | all-to-all | bytes 1048576 | tf_op jit(solution)/shard_map/all_to_all | solution.py:701
  217.6 1.1 collective-permute-start.7
  218.7 1.3 collective-permute-done.9
  220.7 10.8 %all_to_all.38.spec_ref = f32[8,4,1024]{2,1,0:T(4,128)S(1)} all-to-all(f32[8,4,1024]{2,1,0:T(4,128)S(1)} %broadcast_in_dim.105), channel_id=1, replica_groups=mesh['gx'=4,'gy'=8] {'gy'}, dimensions={0} | all-to-all | bytes 262144 | tf_op jit(solution)/shard_map/all_to_all | solution.py:775
  231.5 9.2 %decode.1 = f32[128,128]{1,0:T(8,128)S(1)} custom-call(s32[3,128]{1,0:T(4,128)S(1)} %pad_add_fusion.id_ref, f32[1]{0:T(128)} %bitcast.6.base_ref, f32[3,128,128]{2,1,0:T(8,128)S(1)} %bitcast_subtract_fusion.point_ref, f32[8,4,1024]{2,1,0:T(4,128)S(1)} %all_to_all.38.spec_ref, f32[2,1024]{1,0:T(2,128)S(1)} %pad_maximum_fusion.4.turn_ref, ...), custom_call_target="tpu_custom_call" | custom-call | flops 4000000000 | bytes 6000000 | tf_op jit(solution)/shard_map/decode/pallas_call | solution.py:776
  240.7 12.0 %all_to_all.39 = f32[8,16,128]{2,1,0:T(8,128)S(1)} all-to-all(f32[8,16,128]{2,1,0:T(8,128)S(1)} %bitcast.76), channel_id=1, replica_groups=mesh['gx'=4,'gy'=8] {'gy'}, dimensions={0} | all-to-all | bytes 131072 | tf_op jit(solution)/shard_map/all_to_all | solution.py:787
  252.7 0.9 convolution_bitcast_fusion
  (106 shorter events, 16.1 us)
Async XLA Ops:
  0.0 21.8 %copy-start.19 = (f32[2,32]{1,0:T(2,128)S(1)}, f32[2,32]{1,0:T(2,128)}, u32[]{:S(2)}) copy-start(f32[2,32]{1,0:T(2,128)} %param.30) | copy-start | bytes 772
  0.0 22.0 %copy-start.15 = (f32[32]{0:T(128)S(1)}, f32[32]{0:T(128)}, u32[]{:S(2)}) copy-start(f32[32]{0:T(128)} %param.28) | copy-start | bytes 388
  6.4 42.9 %all-to-all-start = ((f32[8,368,128]{2,1,0:T(8,128)}), f32[8,368,128]{2,1,0:T(8,128)S(1)}, u32[]{:S(2)}, u32[]{:S(2)}) async-start(f32[8,368,128]{2,1,0:T(8,128)} %get-tuple-element.40), calls=%async_computation | async-start | bytes 3014656 | tf_op jit(solution)/shard_map/all_to_all | solution.py:568
  27.9 26.0 %copy-start.16 = (s32[3]{0:T(128)S(1)}, s32[3]{0:T(128)}, u32[]{:S(2)}) copy-start(s32[3]{0:T(128)} %constant.158.clone) | copy-start | bytes 40
  49.3 5.4 %copy-start.11 = (f32[8,368,128]{2,1,0:T(8,128)}, f32[8,368,128]{2,1,0:T(8,128)S(1)}, u32[]{:S(2)}) copy-start(f32[8,368,128]{2,1,0:T(8,128)S(1)} %all-to-all-done.in_ref) | copy-start | bytes 4521988
  49.3 24.2 %all-to-all-start.1 = ((f32[8,192,128]{2,1,0:T(8,128)}), f32[8,192,128]{2,1,0:T(8,128)}, u32[]{:S(2)}, u32[]{:S(2)}) async-start(f32[8,192,128]{2,1,0:T(8,128)} %get-tuple-element.44), calls=%async_computation.1 | async-start | bytes 1572864 | tf_op jit(solution)/shard_map/all_to_all | solution.py:642
  53.5 19.2 %copy-start.12 = (f32[8,48,128]{2,1,0:T(8,128)}, f32[8,48,128]{2,1,0:T(8,128)S(1)}, u32[]{:S(2)}) copy-start(f32[8,48,128]{2,1,0:T(8,128)S(1)} %slice.68.pos_ref) | copy-start | bytes 589828
  72.8 55.4 %copy-start.8 = (bf16[128,256]{1,0:T(8,128)(2,1)S(1)}, bf16[128,256]{1,0:T(8,128)(2,1)}, u32[]{:S(2)}) copy-start(bf16[128,256]{1,0:T(8,128)(2,1)} %constant.153.clone.fwd_ref) | copy-start | bytes 196612
  72.8 55.4 %copy-start.9 = (bf16[128,192]{1,0:T(8,128)(2,1)S(1)}, bf16[128,192]{1,0:T(8,128)(2,1)}, u32[]{:S(2)}) copy-start(bf16[128,192]{1,0:T(8,128)(2,1)} %constant.154.clone.inv_ref) | copy-start | bytes 147460
  85.2 2.9 %collective-permute-start = (f32[2,8,4,32,128]{4,3,2,1,0:T(8,128)}, f32[2,8,4,32,128]{4,3,2,1,0:T(8,128)S(1)}, u32[]{:S(2)}, u32[]{:S(2)}) collective-permute-start(f32[2,8,4,32,128]{4,3,2,1,0:T(8,128)} %get-tuple-element.50), channel_id=1, source_target_pairs={{0,8},{8,0},{16,24},{24,16},{1,9},{9,1},{17,25},{25,17},{2,10},{10... | collective-permute-start | bytes 3145736 | tf_op jit(solution)/shard_map/ppermute | solution.py:675
  88.2 1.2 copy-start.2
  90.3 14.0 %collective-permute-start.1 = (f32[8,128,128]{2,1,0:T(8,128)S(1)}, f32[8,128,128]{2,1,0:T(8,128)S(1)}, u32[]{:S(2)}, u32[]{:S(2)}) collective-permute-start(f32[8,128,128]{2,1,0:T(8,128)S(1)} %x_forward.5), channel_id=1, source_target_pairs={{0,16},{8,24},{16,0},{24,8},{1,17},{9,25},{17,1},{25,9},{2,18},{10... | collective-permute-start | bytes 1572872 | tf_op jit(solution)/shard_map/ppermute | solution.py:675
  146.7 14.0 %collective-permute-start.2 = (f32[8,128,128]{2,1,0:T(8,128)S(1)}, f32[8,128,128]{2,1,0:T(8,128)S(1)}, u32[]{:S(2)}, u32[]{:S(2)}) collective-permute-start(f32[8,128,128]{2,1,0:T(8,128)S(1)} %all_to_all.36.in_ref), channel_id=1, source_target_pairs={{0,16},{8,24},{16,0},{24,8},{1,17},{9,25},{17,1},{25,9},{2,18},{10... | collective-permute-start | bytes 1572872 | tf_op jit(solution)/shard_map/ppermute | solution.py:675
  158.6 20.9 %copy-start.13 = (f32[8,48,128]{2,1,0:T(8,128)S(1)}, f32[8,48,128]{2,1,0:T(8,128)}, u32[]{:S(2)}) copy-start(f32[8,48,128]{2,1,0:T(8,128)} %copy-done.12) | copy-start | bytes 589828
  159.9 0.8 copy-start.6
  160.8 2.6 %collective-permute-start.3 = (f32[1024,128]{1,0:T(8,128)S(1)}, f32[1024,128]{1,0:T(8,128)S(1)}, u32[]{:S(2)}, u32[]{:S(2)}) collective-permute-start(f32[1024,128]{1,0:T(8,128)S(1)} %get-tuple-element.57), channel_id=1, source_target_pairs={{0,8},{8,0},{16,24},{24,16},{1,9},{9,1},{17,25},{25,17},{2,10},{10... | collective-permute-start | bytes 1572872 | tf_op jit(solution)/shard_map/ppermute | solution.py:675
  162.1 0.8 copy-start.7
  162.9 2.0 collective-permute-start.4
  163.4 1.5 copy-start.17
  164.9 0.8 copy-start.18
  179.1 2.9 %collective-permute-start.5 = (f32[2,8,4,32,128]{4,3,2,1,0:T(8,128)}, f32[2,8,4,32,128]{4,3,2,1,0:T(8,128)S(1)}, u32[]{:S(2)}, u32[]{:S(2)}) collective-permute-start(f32[2,8,4,32,128]{4,3,2,1,0:T(8,128)} %get-tuple-element.64), channel_id=1, source_target_pairs={{0,8},{8,0},{16,24},{24,16},{1,9},{9,1},{17,25},{25,17},{2,10},{10... | collective-permute-start | bytes 3145736 | tf_op jit(solution)/shard_map/ppermute | solution.py:675
  182.0 1.2 copy-start
  183.2 10.3 %copy-start.1 = (f32[2,8,4,32,128]{4,3,2,1,0:T(8,128)S(1)}, f32[2,8,4,32,128]{4,3,2,1,0:T(8,128)}, u32[]{:S(2)}) copy-start(f32[2,8,4,32,128]{4,3,2,1,0:T(8,128)} %get-tuple-element.63) | copy-start | bytes 3145732
  184.1 14.3 %collective-permute-start.6 = (f32[8,128,128]{2,1,0:T(8,128)S(1)}, f32[8,128,128]{2,1,0:T(8,128)S(1)}, u32[]{:S(2)}, u32[]{:S(2)}) collective-permute-start(f32[8,128,128]{2,1,0:T(8,128)S(1)} %x_forward.6), channel_id=1, source_target_pairs={{0,16},{8,24},{16,0},{24,8},{1,17},{9,25},{17,1},{25,9},{2,18},{10... | collective-permute-start | bytes 1572872 | tf_op jit(solution)/shard_map/ppermute | solution.py:675
  185.1 46.3 %copy-start.4 = (bf16[2048,512]{1,0:T(8,128)(2,1)S(1)}, bf16[2048,512]{1,0:T(8,128)(2,1)}, u32[]{:S(2)}) copy-start(bf16[2048,512]{1,0:T(8,128)(2,1)} %constant.156.clone.lo_ref) | copy-start | bytes 6291460
  185.1 46.3 %copy-start.10 = (bf16[128,96]{1,0:T(8,128)(2,1)S(1)}, bf16[128,96]{1,0:T(8,128)(2,1)}, u32[]{:S(2)}) copy-start(bf16[128,96]{1,0:T(8,128)(2,1)} %constant.150.clone.inv_ref) | copy-start | bytes 73732
  193.5 37.9 %copy-start.3 = (f32[8,64,128]{2,1,0:T(8,128)S(1)}, f32[8,64,128]{2,1,0:T(8,128)}, u32[]{:S(2)}) copy-start(f32[8,64,128]{2,1,0:T(8,128)} %readout.1) | copy-start | bytes 786436
  193.5 37.9 %copy-start.5 = (bf16[2048,512]{1,0:T(8,128)(2,1)S(1)}, bf16[2048,512]{1,0:T(8,128)(2,1)}, u32[]{:S(2)}) copy-start(bf16[2048,512]{1,0:T(8,128)(2,1)} %constant.155.clone.hi_ref) | copy-start | bytes 6291460
  216.7 35.9 %copy-start.14 = (s32[128]{0:T(128)S(1)}, s32[128]{0:T(128)}, u32[]{:S(2)}) copy-start(s32[128]{0:T(128)} %get-tuple-element.39) | copy-start | bytes 1540
  216.7 3.2 %collective-permute-start.9 = (f32[4,1024]{1,0:T(4,128)S(1)}, f32[4,1024]{1,0:T(4,128)S(1)}, u32[]{:S(2)}, u32[]{:S(2)}) collective-permute-start(f32[4,1024]{1,0:T(4,128)S(1)} %y_last.1), channel_id=1, source_target_pairs={{0,24},{8,16},{16,8},{24,0},{1,25},{9,17},{17,9},{25,1},{2,26},{10... | collective-permute-start | bytes 49160 | tf_op jit(solution)/shard_map/ppermute | solution.py:675
  216.8 3.8 %collective-permute-start.8 = (f32[4,1024]{1,0:T(4,128)S(1)}, f32[4,1024]{1,0:T(4,128)S(1)}, u32[]{:S(2)}, u32[]{:S(2)}) collective-permute-start(f32[4,1024]{1,0:T(4,128)S(1)} %y_last.1), channel_id=1, source_target_pairs={{0,16},{8,24},{16,0},{24,8},{1,17},{9,25},{17,1},{25,9},{2,18},{10... | collective-permute-start | bytes 49160 | tf_op jit(solution)/shard_map/ppermute | solution.py:675
  217.6 3.0 %collective-permute-start.7 = (f32[4,1024]{1,0:T(4,128)S(1)}, f32[4,1024]{1,0:T(4,128)S(1)}, u32[]{:S(2)}, u32[]{:S(2)}) collective-permute-start(f32[4,1024]{1,0:T(4,128)S(1)} %y_last.1), channel_id=1, source_target_pairs={{0,8},{8,0},{16,24},{24,16},{1,9},{9,1},{17,25},{25,17},{2,10},{10... | collective-permute-start | bytes 49160 | tf_op jit(solution)/shard_map/ppermute | solution.py:675
